TPU v7x, 32 devices: a whole 2x2x4 slice. The times are simulated.
32 devices in a mesh: groups: 2 (over x), node: 16 (over z, y, core).
Axes of the slice: x: 2, y: 2, z: 4, core: 2. Of those that a mesh axis runs over, the one named last changes fastest.
Arguments:
- tokens: bfloat16 [4096, 2048], P(('groups', 'node')), parts along dimension 0, may hold values from -6 to 6
- expert_ids: int32 [4096, 8], P(('groups', 'node')), parts along dimension 0, may hold values from 0 to 15, all different within a row; in each aligned block of 128 rows (0 to 127, 128 to 255, ...) at most 96 rows name the same one
- gate_fixed: int32 [4096, 8], P(('groups', 'node')), parts along dimension 0, may hold values from 1 to 65535
- gate_weight: bfloat16 [16, 2048, 768], P('node'), may hold values from -0.125 to 0.125
- up_weight: bfloat16 [16, 2048, 768], P('node'), may hold values from -0.125 to 0.125
- down_weight: bfloat16 [16, 768, 2048], P('node'), may hold values from -0.21875 to 0.21875
Outputs:
- mixed: bfloat16 [4096, 2048], P(('groups', 'node')), parts along dimension 0
- expert_load: float32 [32], P(('groups', 'node')), parts along dimension 0
- balance_loss: float32 [2], P('groups'), parts along dimension 0
There are 2 independent parts, one for each index of `groups`. A program takes and returns all parts, laid end to end along the dimension named above; an argument that names none is the same for every part. Nothing has to cross between parts.
Inputs may be any that keep to these rules, and one draw needn't show every extreme that they name: `expert_ids`: each row names 8 different experts. Among the 128 rows of one device no expert is named by more than 96 rows, and in some such blocks one expert is named by exactly 96; every expert is named somewhere.
All inputs are finite; a program needn't handle non-finite values.
Results may differ from a plain program's by a relative error of at most 0.0059.
Values may be sent and summed in bfloat16 or wider, within the bound.
No kernel may reach another device: no remote copies, remote signals or barrier semaphores. Data moves between devices by JAX's collectives and lax.ppermute only.
A program may use at most 128 MiB of HBM per device.

v0:
```python
import jax
import jax.numpy as jnp
from jax import lax
from jax.sharding import PartitionSpec as P


def give_back(expert_out):
    return lax.all_to_all(expert_out, "node", split_axis=0, concat_axis=0, tiled=True)


def body(tokens, expert_ids, gate_fixed, gate_weight, up_weight, down_weight):
    tok_rows, model_width = tokens.shape
    per_token = expert_ids.shape[1]
    local_experts = gate_weight.shape[0]
    node_count = lax.axis_size("node")
    expert_count = local_experts * node_count
    capacity = max(2, 3 * tok_rows * per_token // (2 * expert_count))
    token_total = tok_rows * node_count
    fixed_gate = gate_fixed.astype(jnp.float32)
    weights = fixed_gate / jnp.sum(fixed_gate, axis=1, keepdims=True)
    pair_weights = weights.reshape(-1)
    chosen = expert_ids.reshape(-1)
    one_hot = (chosen[:, None] == jnp.arange(expert_count, dtype=jnp.int32)[None, :]).astype(
        jnp.int32
    )
    earlier = jnp.cumsum(one_hot, axis=0) - one_hot
    slot_index = jnp.sum(earlier * one_hot, axis=1)
    target_row = chosen * capacity + slot_index
    repeated = jnp.repeat(tokens, per_token, axis=0)
    outgoing = (
        jnp.zeros((expert_count * capacity, model_width), jnp.bfloat16).at[target_row].set(repeated)
    )
    outgoing = outgoing.reshape(expert_count, capacity, model_width)
    one_float = one_hot.astype(jnp.float32)
    counts_here = jnp.sum(one_float, axis=0)
    mass_here = jnp.dot(pair_weights, one_float, precision=lax.Precision.HIGHEST) / token_total
    totals = lax.psum_scatter(
        jnp.stack([counts_here, mass_here], axis=1), "node", scatter_dimension=0, tiled=True
    )
    expert_load = totals[:, 0] * expert_count / (token_total * per_token)
    product_term = jnp.sum(totals[:, 0] / (token_total * per_token) * totals[:, 1])
    balance_loss = (expert_count * lax.psum(product_term, "node")).reshape(1)
    arrived_all = lax.all_to_all(outgoing, "node", split_axis=0, concat_axis=0, tiled=True)
    slot_count = arrived_all.shape[1]
    grouped = arrived_all.reshape(node_count, local_experts, slot_count, model_width)
    gate_value = jnp.einsum(
        "sjnd,jdf->sjnf", grouped, gate_weight, preferred_element_type=jnp.float32
    )
    up_value = jnp.einsum("sjnd,jdf->sjnf", grouped, up_weight, preferred_element_type=jnp.float32)
    hidden = (jax.nn.silu(gate_value) * up_value).astype(jnp.bfloat16)
    expert_out = jnp.einsum(
        "sjnf,jfd->sjnd", hidden, down_weight, preferred_element_type=jnp.float32
    )
    returned_rows = give_back(
        expert_out.astype(jnp.bfloat16).reshape(expert_count, slot_count, model_width)
    )
    flat_rows = returned_rows.reshape(expert_count * capacity, model_width)
    gathered = flat_rows[target_row].reshape(tok_rows, per_token, model_width)
    mixed = jnp.einsum(
        "tk,tkd->td", weights, gathered.astype(jnp.float32), precision=lax.Precision.HIGHEST
    )
    return (mixed.astype(jnp.bfloat16), expert_load, balance_loss)


def solution(mesh):
    return jax.shard_map(
        body,
        mesh=mesh,
        in_specs=(
            P(("groups", "node"), None),
            P(("groups", "node"), None),
            P(("groups", "node"), None),
            P("node", None, None),
            P("node", None, None),
            P("node", None, None),
        ),
        out_specs=(P(("groups", "node"), None), P(("groups", "node")), P("groups")),
        check_vma=False,
    )
```

profile of v0, /device:TPU:0, one launch (start us, length us, event | category | flops | bytes accessed | tf_op | source)
XLA Modules:
  0.0 402.6 jit_solution(10045200183252565095)
XLA Ops:
  0.6 0.0 copy-start
  0.6 0.9 copy.18
  1.6 0.1 eq.29
  1.7 0.1 eq.25
  1.8 0.7 broadcast_multiply_fusion
  2.5 4.5 %reduce-window.6 = s32[16,8,128]{2,1,0:T(8,128)S(1)} reduce-window(s32[16,8,128]{2,1,0:T(8,128)S(1)} %fusion.27, s32[]{:T(128)} %constant.25.clone.1), window={size=1x1x128 pad=0_0x0_0x127_0}, to_apply=%region_1.0 | reduce-window | flops 2080768 | bytes 131076 | tf_op jit(solution)/shard_map/reduce-window
  7.0 0.1 slice.19
  7.1 0.1 copy.20
  7.2 0.1 copy.21
  7.3 0.1 broadcast_add_fusion
  7.4 0.1 copy.17
  7.5 0.1 mul.36
  7.7 10.7 %scatter_custom_fusion = bf16[1536,2048]{1,0:T(8,128)(2,1)} fusion(s32[1024]{0:T(1024)S(1)} %bitcast.103, bf16[]{:T(256)} %constant.12.clone.1, bf16[128,2048]{1,0:T(8,128)(2,1)} %param.6), kind=kCustom, calls=%fused_computation.12 | custom fusion | bytes 6815746 | tf_op jit(solution)/shard_map/scatter | solution.py:31
  18.3 0.0 copy-start.3
  18.3 144.8 %all_to_all.10 = bf16[16,96,2048]{2,1,0:T(8,128)(2,1)S(1)} all-to-all(bf16[16,96,2048]{2,1,0:T(8,128)(2,1)} %bitcast.98), channel_id=1, replica_groups=mesh['groups'=2,'node'=16] {'node'}, dimensions={0} | all-to-all | bytes 12582912 | tf_op jit(solution)/shard_map/all_to_all | solution.py:43
  163.2 0.0 copy-start.1
  163.2 2.7 copy-done.1
  165.8 0.0 copy-done.3
  165.8 6.6 %fusion.9 = f32[16,96,768]{2,1,0:T(8,128)} fusion(bf16[16,96,2048]{2,1,0:T(8,128)(2,1)S(1)} %all_to_all.10, bf16[1,2048,768]{2,1,0:T(8,128)(2,1)S(1)} %copy-done.3), kind=kOutput, calls=%fused_computation.15 | convolution fusion | flops 4831838208 | bytes 14155776 | tf_op jit(solution)/shard_map/sjnd,jdf->sjnf/dot_general | solution.py:49
  172.4 0.0 copy-done
  172.4 16.8 %convolution_convert_fusion = bf16[16,96,2048]{2,1,0:T(8,128)(2,1)} fusion(bf16[1,768,2048]{2,1,0:T(8,128)(2,1)S(1)} %copy-done, f32[16,96,768]{2,1,0:T(8,128)} %fusion.9, bf16[16,96,2048]{2,1,0:T(8,128)(2,1)} %copy-done.1, bf16[1,2048,768]{2,1,0:T(8,128)(2,1)} %param.9), kind=kOutput, calls=%fused_computation.9 | convolution fusion | flops 9673900032 | bytes 23592960 | tf_op jit(solution)/shard_map/sjnf,jfd->sjnd/dot_general | solution.py:51
  189.3 0.0 copy-start.2
  189.3 0.0 copy-start.4
  189.3 5.7 %all-to-all-start.1 = ((bf16[16,96,2048]{2,1,0:T(8,128)(2,1)}), bf16[16,96,2048]{2,1,0:T(8,128)(2,1)}, u32[]{:S(2)}, u32[]{:S(2)}) async-start(bf16[16,96,2048]{2,1,0:T(8,128)(2,1)} %convolution_convert_fusion), calls=%async_computation.1 | async-start | bytes 12582912 | tf_op jit(solution)/shard_map/all_to_all | solution.py:8
  195.0 0.0 copy-done.2
  195.0 0.1 copy.22
  195.1 0.1 reshape.132
  195.2 0.0 copy-done.4
  195.2 0.6 dynamic-slice
  195.8 0.2 fusion.19
  196.0 0.2 fusion.24
  196.1 129.0 %all-reduce = f32[16,2]{0,1:T(2,128)S(1)} all-reduce(f32[16,2]{0,1:T(2,128)S(1)} %pad_maximum_fusion), channel_id=2, replica_groups=mesh['groups'=2,'node'=16] {'node'}, use_global_device_ids=true, to_apply=%region_6.7.clone | all-reduce | flops 32 | bytes 256
  325.2 0.7 constant_dynamic-slice_fusion
  325.9 0.5 fusion.30
  327.7 52.0 %psum.7 = f32[]{:T(128)} all-reduce(f32[]{:T(128)} %bitcast.29), channel_id=1, replica_groups=mesh['groups'=2,'node'=16] {'node'}, use_global_device_ids=true, to_apply=%region_7.8 | all-reduce | flops 1 | bytes 8 | tf_op jit(solution)/shard_map/psum | solution.py:42
  379.7 0.1 copy.23
  381.1 0.0 all-to-all-done.1
  381.1 12.4 %gather_fusion = bf16[1024,2048]{1,0:T(8,128)(2,1)} fusion(bf16[1536,2048]{1,0:T(8,128)(2,1)} %bitcast.22, s32[1024]{0:T(1024)S(1)} %broadcast_clamp_fusion), kind=kCustom, calls=%fused_computation | custom fusion | bytes 8392704 | tf_op jit(solution)/shard_map/gather | solution.py:58
  393.5 5.7 %fusion.4 = bf16[128,1,2048]{2,1,0:T(2,128)(2,1)S(1)} fusion(f32[128,8,1]{1,2,0:T(1,128)S(1)} %copy.23, bf16[1024,2048]{1,0:T(8,128)(2,1)} %gather_fusion), kind=kOutput, calls=%fused_computation.10 | convolution fusion | flops 25165824 | bytes 4722688 | tf_op jit(solution)/shard_map/tk,tkd->td/dot_general | solution.py:59
  399.3 1.1 copy.30
  (10 shorter events, 0.1 us)
Async XLA Ops:
  0.6 171.8 %copy-start = (bf16[1,768,2048]{2,1,0:T(8,128)(2,1)S(1)}, bf16[1,768,2048]{2,1,0:T(8,128)(2,1)}, u32[]{:S(2)}) copy-start(bf16[1,768,2048]{2,1,0:T(8,128)(2,1)} %param.11) | copy-start | bytes 9437188
  18.3 147.5 %copy-start.3 = (bf16[1,2048,768]{2,1,0:T(8,128)(2,1)S(1)}, bf16[1,2048,768]{2,1,0:T(8,128)(2,1)}, u32[]{:S(2)}) copy-start(bf16[1,2048,768]{2,1,0:T(8,128)(2,1)} %param.10) | copy-start | bytes 9437188
  163.2 2.7 copy-start.1
  189.3 5.7 %copy-start.2 = (s32[128,8]{0,1:T(8,128)S(1)}, s32[128,8]{0,1:T(8,128)}, u32[]{:S(2)}) copy-start(s32[128,8]{0,1:T(8,128)} %param.8) | copy-start | bytes 12292
  189.3 5.9 %copy-start.4 = (u32[32]{0:T(128)S(1)}, u32[32]{0:T(128)}, u32[]{:S(2)}) copy-start(u32[32]{0:T(128)} %constant.37) | copy-start | bytes 388
  189.3 191.8 %all-to-all-start.1 = ((bf16[16,96,2048]{2,1,0:T(8,128)(2,1)}), bf16[16,96,2048]{2,1,0:T(8,128)(2,1)}, u32[]{:S(2)}, u32[]{:S(2)}) async-start(bf16[16,96,2048]{2,1,0:T(8,128)(2,1)} %convolution_convert_fusion), calls=%async_computation.1 | async-start | bytes 12582912 | tf_op jit(solution)/shard_map/all_to_all | solution.py:8
where the time goes:
time: 403 us
  blocking collectives  326 us (81%)
  local copies, waits for them, and re-layouts  30.6 us (8%)
  matrix products  29.3 us (7%)
  starting transfers between devices  5.66 us (1%)
  between operations  5.62 us (1%)
  other arithmetic  5.58 us (1%)
    all_to_all x1, blocking collectives, body(): lax.all_to_all(outgoing, 'node', split_axis=0, concat_axis=0, tiled=True)  145 us
    unnamed x1, blocking collectives  129 us
    psum x1, blocking collectives, body(): balance_loss = (expert_count * lax.psum(product_term, 'node')).reshape(1)  52 us
    dot_general x1, matrix products, body(): jnp.einsum('sjnf,jfd->sjnd', hidden, down_weight, preferred_element_type=...  16.8 us
    gather x1, local copies, waits for them, and re-layouts, body(): gathered = flat_rows[target_row].reshape(tok_rows, per_token, model_width)  12.4 us
    scatter x1, local copies, waits for them, and re-layouts, body(): jnp.zeros((expert_count * capacity, model_width), jnp.bfloat16)  10.7 us
  transfers between devices with their start and end apart: 1, of which 0 were waited for; matrix products, arithmetic and copies ran while one was open for 1% of the time, Pallas kernels for 0%

commit v1 on v0

v1 whole, which is shorter than its diff:
```python
import functools

import jax
import jax.numpy as jnp
from jax import lax
from jax.experimental import pallas as pl
from jax.experimental.pallas import tpu as pltpu
from jax.sharding import PartitionSpec as P

CORES = 2


def ring_order(chips):
    if chips <= 8:
        return list(range(0, chips, 2)) + list(range(1, chips, 2))[::-1]
    return list(range(chips))


def ring_shift(order, step):
    pairs = []
    for place, chip in enumerate(order):
        target = order[(place + step) % len(order)]
        pairs += [(CORES * chip + core, CORES * target + core) for core in range(CORES)]
    return pairs


def expert_kernel(hidden_steps, sizes, *refs):
    count = len(sizes)
    blocks = refs[:count]
    scale_ref, gate_ref, up_ref, down_ref = refs[count : count + 4]
    outs = refs[count + 4 : 2 * count + 4]
    rows_ref, hidden_ref, arrived = refs[2 * count + 4 :]
    step = pl.program_id(0)
    starts = [sum(sizes[:i]) for i in range(count)]
    chunk = gate_ref.shape[1]

    @pl.when(step == 0)
    def _():
        copies = [
            pltpu.make_async_copy(
                blocks[i], rows_ref.at[pl.ds(starts[i], sizes[i])], arrived.at[i]
            )
            for i in range(count)
        ]
        for copy in copies:
            copy.start()
        for copy in copies:
            copy.wait()

    for j in range(hidden_steps):

        @pl.when(step == j)
        def _():
            rows = rows_ref[...]
            gate = jnp.dot(rows, gate_ref[...], preferred_element_type=jnp.float32)
            up = jnp.dot(rows, up_ref[...], preferred_element_type=jnp.float32)
            hidden = gate / (1.0 + jnp.exp(-gate)) * up * scale_ref[...]
            hidden_ref[:, j * chunk : (j + 1) * chunk] = hidden.astype(jnp.bfloat16)

    @pl.when(step >= hidden_steps)
    def _():
        out = jnp.dot(hidden_ref[...], down_ref[...], preferred_element_type=jnp.float32)
        for i in range(count):
            outs[i][...] = out[starts[i] : starts[i] + sizes[i]].astype(jnp.bfloat16)


def apply_expert(blocks, scale, gate_weight, up_weight, down_weight):
    width, hidden_width = gate_weight.shape
    sizes = tuple(block.shape[0] for block in blocks)
    total = sum(sizes)
    count = len(blocks)
    chunk = 256
    hidden_steps = hidden_width // chunk
    out_chunk = 512
    out_steps = width // out_chunk
    first = lambda i: jnp.minimum(i, hidden_steps - 1)
    second = lambda i: jnp.maximum(i - hidden_steps, 0)
    return pl.pallas_call(
        functools.partial(expert_kernel, hidden_steps, sizes),
        grid=(hidden_steps + out_steps,),
        out_shape=[jax.ShapeDtypeStruct((size, width), jnp.bfloat16) for size in sizes],
        in_specs=[pl.BlockSpec(memory_space=pl.ANY)] * count
        + [
            pl.BlockSpec((total, 1), lambda i: (0, 0)),
            pl.BlockSpec((width, chunk), lambda i: (0, first(i))),
            pl.BlockSpec((width, chunk), lambda i: (0, first(i))),
            pl.BlockSpec((hidden_width, out_chunk), lambda i: (0, second(i))),
        ],
        out_specs=[pl.BlockSpec((size, out_chunk), lambda i: (0, second(i))) for size in sizes],
        scratch_shapes=[
            pltpu.VMEM((total, width), jnp.bfloat16),
            pltpu.VMEM((total, hidden_width), jnp.bfloat16),
            pltpu.SemaphoreType.DMA((count,)),
        ],
        compiler_params=pltpu.CompilerParams(
            vmem_limit_bytes=40 * 1024 * 1024, dimension_semantics=("arbitrary",)
        ),
        cost_estimate=pl.CostEstimate(
            flops=6 * total * width * hidden_width,
            bytes_accessed=6 * width * hidden_width + 4 * total * width,
            transcendentals=total * hidden_width,
        ),
    )(*blocks, scale, gate_weight, up_weight, down_weight)


def body(tokens, expert_ids, gate_fixed, gate_weight, up_weight, down_weight):
    tok_rows, model_width = tokens.shape
    per_token = expert_ids.shape[1]
    node_count = lax.axis_size("node")
    expert_count = node_count
    token_total = tok_rows * node_count
    chips = node_count // CORES
    far = chips // 2
    half = tok_rows // 2
    order = ring_order(chips)
    to_right, to_left = ring_shift(order, 1), ring_shift(order, -1)
    to_sibling = [(node, node ^ 1) for node in range(node_count)]
    right = lambda a: lax.ppermute(a, "node", to_right)
    left = lambda a: lax.ppermute(a, "node", to_left)
    sibling = lambda a: lax.ppermute(a, "node", to_sibling)
    node = lax.axis_index("node")
    core = node % CORES

    fixed_gate = gate_fixed.astype(jnp.float32)
    weights = fixed_gate / jnp.sum(fixed_gate, axis=1, keepdims=True)
    experts = jnp.arange(expert_count, dtype=jnp.int32)
    dense = jnp.sum(
        jnp.where(expert_ids[None] == experts[:, None, None], weights[None], 0.0), axis=2
    )
    dense_all = lax.all_gather(dense, "node")

    counts = jnp.sum((dense_all > 0).astype(jnp.float32), axis=(0, 2))
    mass = jnp.sum(dense_all, axis=(0, 2)) / token_total
    own_count = lax.dynamic_slice(counts, (node,), (1,))
    expert_load = own_count * expert_count / (token_total * per_token)
    balance_loss = (expert_count * jnp.sum(counts / (token_total * per_token) * mass)).reshape(1)

    place_of = [order.index(chip) for chip in range(chips)]
    place = jnp.asarray(place_of, jnp.int32)[node // CORES]
    offsets = [0]
    for k in range(1, far):
        offsets += [-k, k]
    offsets.append(far)
    block_chips = jnp.asarray(order, jnp.int32)[
        (place + jnp.asarray(offsets, jnp.int32)) % chips
    ]
    sources = (CORES * block_chips[:, None] + jnp.stack([core, 1 - core])[None]).reshape(-1)
    own_expert = lax.dynamic_index_in_dim(dense_all, node, 1, keepdims=False)
    scale = own_expert[sources].reshape(-1, 1)

    gate_weight, up_weight, down_weight = gate_weight[0], up_weight[0], down_weight[0]

    def run(blocks, first_row):
        total = sum(block.shape[0] for block in blocks)
        return apply_expert(
            blocks, scale[first_row : first_row + total], gate_weight, up_weight, down_weight
        )

    from_left, from_right = tokens, tokens
    mine, theirs = run([tokens, sibling(tokens)], 0)
    outs = [(mine, sibling(theirs))]
    row = 2 * tok_rows
    for k in range(1, far):
        from_left, from_right = right(from_left), left(from_right)
        res = run([from_left, sibling(from_left), from_right, sibling(from_right)], row)
        row += 4 * tok_rows
        outs.append((res[0], sibling(res[1]), res[2], sibling(res[3])))
    far_low, far_high = right(from_left[:half]), left(from_right[half:])
    res = run([far_low, far_high, sibling(far_low), sibling(far_high)], row)

    def add(*terms):
        return sum(term.astype(jnp.float32) for term in terms)

    low = left(add(res[0], sibling(res[2])).astype(jnp.bfloat16))
    high = right(add(res[1], sibling(res[3])).astype(jnp.bfloat16))
    for k in range(far - 1, 0, -1):
        left_own, left_sib, right_own, right_sib = outs[k]
        to_left_sum, to_right_sum = add(left_own, left_sib), add(right_own, right_sib)
        if k == far - 1:
            to_left_sum = to_left_sum + jnp.pad(low.astype(jnp.float32), ((0, half), (0, 0)))
            to_right_sum = to_right_sum + jnp.pad(high.astype(jnp.float32), ((half, 0), (0, 0)))
        else:
            to_left_sum = to_left_sum + low.astype(jnp.float32)
            to_right_sum = to_right_sum + high.astype(jnp.float32)
        low = left(to_left_sum.astype(jnp.bfloat16))
        high = right(to_right_sum.astype(jnp.bfloat16))
    mixed = add(*outs[0], low, high).astype(jnp.bfloat16)
    return (mixed, expert_load, balance_loss)


def solution(mesh):
    return jax.shard_map(
        body,
        mesh=mesh,
        in_specs=(
            P(("groups", "node"), None),
            P(("groups", "node"), None),
            P(("groups", "node"), None),
            P("node", None, None),
            P("node", None, None),
            P("node", None, None),
        ),
        out_specs=(P(("groups", "node"), None), P(("groups", "node")), P("groups")),
        check_vma=False,
    )
```

time: 403 us -> 163 us (0.40)
  blocking collectives: 326 us -> 24.6 us
  waiting for transfers between devices: 0.01 us -> 59.8 us
  Pallas kernels: 0 us -> 33.9 us
  matrix products: 29.3 us -> 0 us
  local copies, waits for them, and re-layouts: 30.6 us -> 11.7 us
  starting transfers between devices: 5.66 us -> 20.6 us
    all_to_all x1 -> x0, blocking collectives: 145 us -> none  [body(): lax.all_to_all(outgoing, 'node', split_axis=0, concat_axis=0, tiled=True)]
    unnamed x1 -> x0, blocking collectives: 129 us -> none
    ppermute x0 -> x34, waiting for transfers between devices: none -> 59.8 us  [the longest x8 33.7 us: body(): right = lambda a: lax.ppermute(a, 'node', to_right)]
    psum x1 -> x0, blocking collectives: 52 us -> none  [body(): balance_loss = (expert_count * lax.psum(product_term, 'node')).reshape(1)]
    pallas_call x0 -> x5, Pallas kernels: none -> 33.9 us  [apply_expert(): pl.pallas_call(functools.partial(expert_kernel, hidden_steps, sizes), gri...]
    dot_general x4 -> x0, matrix products: 29.3 us -> none  [the longest x1 16.8 us: body(): jnp.einsum('sjnf,jfd->sjnd', hidden, down_weight, preferred_element_type=...]
    all_gather x0 -> x1, blocking collectives: none -> 24.6 us  [body(): dense_all = lax.all_gather(dense, 'node')]
    ppermute x0 -> x34, starting transfers between devices: none -> 20.6 us  [the longest x8 9.95 us: body(): left = lambda a: lax.ppermute(a, 'node', to_left)]
  transfers between devices with their start and end apart: 1 -> 34, of which waited for: 0 -> 10; matrix products, arithmetic and copies ran while one was open for 1% -> 8% of each run, Pallas kernels for 0% -> 21%
where the time goes in v1:
time: 163 us
  waiting for transfers between devices  59.8 us (37%)
  Pallas kernels  33.9 us (21%)
  blocking collectives  24.6 us (15%)
  starting transfers between devices  20.6 us (13%)
  local copies, waits for them, and re-layouts  11.7 us (7%)
  other arithmetic  7.79 us (5%)
  between operations  4.54 us (3%)
    pallas_call x5, Pallas kernels, apply_expert(): pl.pallas_call(functools.partial(expert_kernel, hidden_steps, sizes), gri...  33.9 us
    ppermute x8, waiting for transfers between devices, body(): right = lambda a: lax.ppermute(a, 'node', to_right)  33.7 us
    ppermute x8, waiting for transfers between devices, body(): left = lambda a: lax.ppermute(a, 'node', to_left)  26.1 us
    all_gather x1, blocking collectives, body(): dense_all = lax.all_gather(dense, 'node')  24.6 us
    ppermute x8, starting transfers between devices, body(): left = lambda a: lax.ppermute(a, 'node', to_left)  9.95 us
    ppermute x8, starting transfers between devices, body(): right = lambda a: lax.ppermute(a, 'node', to_right)  7.31 us
    unnamed x18, local copies, waits for them, and re-layouts  5.7 us
    ppermute x18, starting transfers between devices, body(): sibling = lambda a: lax.ppermute(a, 'node', to_sibling)  3.31 us
  transfers between devices with their start and end apart: 34, of which 10 were waited for; matrix products, arithmetic and copies ran while one was open for 8% of the time, Pallas kernels for 21%

profile of v1, /device:TPU:0, one launch (start us, length us, event | category | flops | bytes accessed | tf_op | source)
XLA Modules:
  0.0 162.9 jit_solution(2412067241794086371)
XLA Ops:
  0.6 3.1 %collective-permute-start.2 = (bf16[128,2048]{1,0:T(8,128)(2,1)}, bf16[128,2048]{1,0:T(8,128)(2,1)S(1)}, u32[]{:S(2)}, u32[]{:S(2)}) collective-permute-start(bf16[128,2048]{1,0:T(8,128)(2,1)} %refs_0_.1), channel_id=1, source_target_pairs={{0,4},{1,5},{4,8},{5,9},{8,12},{9,13},{12,14},{13,15},{14,10},{15,... | collective-permute-start | bytes 1572872 | tf_op jit(solution)/shard_map/ppermute | solution.py:118
  3.7 1.2 dynamic_slice.11
  5.0 1.3 compare_select_fusion.1
  6.3 1.3 gather_fusion
  7.6 0.7 convert_reduce_fusion.1
  8.3 7.5 %collective-permute-done.2.refs_0_ = bf16[128,2048]{1,0:T(8,128)(2,1)S(1)} collective-permute-done((bf16[128,2048]{1,0:T(8,128)(2,1)}, bf16[128,2048]{1,0:T(8,128)(2,1)S(1)}, u32[]{:S(2)}, u32[]{:S(2)}) %collective-permute-start.2) | collective-permute-done | bytes 524320 | tf_op jit(solution)/shard_map/ppermute | solution.py:118
  15.8 1.8 %collective-permute-start.7 = (bf16[128,2048]{1,0:T(8,128)(2,1)S(1)}, bf16[128,2048]{1,0:T(8,128)(2,1)}, u32[]{:S(2)}, u32[]{:S(2)}) collective-permute-start(bf16[128,2048]{1,0:T(8,128)(2,1)S(1)} %collective-permute-done.2.refs_0_), channel_id=1, source_target_pairs={{0,4},{1,5},{4,8},{5,9},{8,12},{9,13},{12,14},{13,15},{14,10},{15,... | collective-permute-start | bytes 1572872 | tf_op jit(solution)/shard_map/ppermute | solution.py:118
  17.6 0.2 collective-permute-start.9
  18.0 0.7 convert_divide_fusion
  18.7 10.3 %collective-permute-done.7.refs_0_ = bf16[128,2048]{1,0:T(8,128)(2,1)} collective-permute-done((bf16[128,2048]{1,0:T(8,128)(2,1)S(1)}, bf16[128,2048]{1,0:T(8,128)(2,1)}, u32[]{:S(2)}, u32[]{:S(2)}) %collective-permute-start.7) | collective-permute-done | bytes 524320 | tf_op jit(solution)/shard_map/ppermute | solution.py:118
  29.0 1.5 collective-permute-start.12
  30.5 0.5 collective-permute-start.14
  31.0 0.7 select_reduce_fusion
  31.8 24.6 %all-gather = f32[256,128]{1,0:T(8,128)S(1)} all-gather(f32[16,128]{1,0:T(8,128)S(1)} %select_reduce_fusion), channel_id=2, replica_groups=mesh['groups'=2,'node'=16] {'node'}, dimensions={0}, use_global_device_ids=true | all-gather | bytes 139264 | tf_op jit(solution)/shard_map/all_gather | solution.py:130
  56.4 0.4 collective-permute-start.10
  56.9 0.2 collective-permute-start.8
  57.0 0.6 gather_fusion.1
  57.6 0.7 slice.56
  58.3 0.7 slice.57
  59.1 2.0 %collective-permute-start.18 = (bf16[64,2048]{1,0:T(8,128)(2,1)}, bf16[64,2048]{1,0:T(8,128)(2,1)S(1)}, u32[]{:S(2)}, u32[]{:S(2)}) collective-permute-start(bf16[64,2048]{1,0:T(8,128)(2,1)} %slice.57), channel_id=1, source_target_pairs={{0,2},{1,3},{4,0},{5,1},{8,4},{9,5},{12,8},{13,9},{14,12},{15,13},... | collective-permute-start | bytes 786440 | tf_op jit(solution)/shard_map/ppermute | solution.py:119
  61.1 0.1 copy.25.refs_4_
  61.3 0.1 copy.24.refs_4_
  61.4 0.1 copy.23.refs_4_
  61.6 0.1 copy.22.refs_4_
  61.7 0.1 copy.21.refs_2_
  62.0 0.5 collective-permute-start.15
  62.5 4.6 %collective-permute-done.17.refs_0_ = bf16[64,2048]{1,0:T(8,128)(2,1)S(1)} collective-permute-done((bf16[64,2048]{1,0:T(8,128)(2,1)}, bf16[64,2048]{1,0:T(8,128)(2,1)S(1)}, u32[]{:S(2)}, u32[]{:S(2)}) %collective-permute-start.17) | collective-permute-done | bytes 262176 | tf_op jit(solution)/shard_map/ppermute | solution.py:118
  67.1 0.7 collective-permute-done.18.refs_1_
  67.8 1.9 %copy-done = bf16[1,2048,768]{2,1,0:T(8,128)(2,1)S(1)} copy-done((bf16[1,2048,768]{2,1,0:T(8,128)(2,1)S(1)}, bf16[1,2048,768]{2,1,0:T(8,128)(2,1)}, u32[]{:S(2)}) %copy-start) | copy-done | bytes 3145752
  69.7 1.9 %copy-done.2 = bf16[1,2048,768]{2,1,0:T(8,128)(2,1)S(1)} copy-done((bf16[1,2048,768]{2,1,0:T(8,128)(2,1)S(1)}, bf16[1,2048,768]{2,1,0:T(8,128)(2,1)}, u32[]{:S(2)}) %copy-start.2) | copy-done | bytes 3145752
  71.6 1.9 %copy-done.3 = bf16[1,768,2048]{2,1,0:T(8,128)(2,1)S(1)} copy-done((bf16[1,768,2048]{2,1,0:T(8,128)(2,1)S(1)}, bf16[1,768,2048]{2,1,0:T(8,128)(2,1)}, u32[]{:S(2)}) %copy-start.3) | copy-done | bytes 3145752
  73.5 8.9 %shard_map.114 = (bf16[128,2048]{1,0:T(8,128)(2,1)S(1)}, bf16[128,2048]{1,0:T(8,128)(2,1)S(1)}, bf16[128,2048]{1,0:T(8,128)(2,1)S(1)}, bf16[128,2048]{1,0:T(8,128)(2,1)S(1)}) custom-call(bf16[128,2048]{1,0:T(8,128)(2,1)} %collective-permute-done.7.refs_0_, bf16[128,2048]{1,0:T(8,128)(2,1)} %collective-permute-done.8.refs_1_, ...), custom_call_target="tpu_custom_call" | custom-call | flops 4831838208 | bytes 13631488 | tf_op jit(solution)/shard_map/pallas_call | solution.py:78
  82.5 0.6 collective-permute-start.3
  83.1 5.0 %shard_map.116 = (bf16[64,2048]{1,0:T(8,128)(2,1)S(1)}, bf16[64,2048]{1,0:T(8,128)(2,1)S(1)}, bf16[64,2048]{1,0:T(8,128)(2,1)S(1)}, bf16[64,2048]{1,0:T(8,128)(2,1)S(1)}) custom-call(bf16[64,2048]{1,0:T(8,128)(2,1)S(1)} %collective-permute-done.17.refs_0_, bf16[64,2048]{1,0:T(8,128)(2,1)S(1)} %collective-permute-done.18.refs_1_, ...), custom_call_target="tpu_custom_call" | custom-call | flops 2415919104 | bytes 11534336 | tf_op jit(solution)/shard_map/pallas_call | solution.py:78
  88.2 0.5 collective-permute-start.29
  88.6 7.6 %shard_map.115 = (bf16[128,2048]{1,0:T(8,128)(2,1)S(1)}, bf16[128,2048]{1,0:T(8,128)(2,1)S(1)}, bf16[128,2048]{1,0:T(8,128)(2,1)S(1)}, bf16[128,2048]{1,0:T(8,128)(2,1)S(1)}) custom-call(bf16[128,2048]{1,0:T(8,128)(2,1)S(1)} %collective-permute-done.12.refs_0_, bf16[128,2048]{1,0:T(8,128)(2,1)S(1)} %collective-permute-done.13.refs_1_, ...), custom_call_target="tpu_custom_call" | custom-call | flops 4831838208 | bytes 13631488 | tf_op jit(solution)/shard_map/pallas_call | solution.py:78
  96.2 0.2 collective-permute-start.16
  96.4 0.4 collective-permute-start.28
  96.9 1.8 %collective-permute-start.22 = (bf16[64,2048]{1,0:T(8,128)(2,1)S(1)}, bf16[64,2048]{1,0:T(8,128)(2,1)S(1)}, u32[]{:S(2)}, u32[]{:S(2)}) collective-permute-start(bf16[64,2048]{1,0:T(8,128)(2,1)S(1)} %add_convert_fusion.8), channel_id=1, source_target_pairs={{0,2},{1,3},{4,0},{5,1},{8,4},{9,5},{12,8},{13,9},{14,12},{15,13},... | collective-permute-start | bytes 786440 | tf_op jit(solution)/shard_map/ppermute | solution.py:119
  98.7 6.5 %collective-permute-done.22 = bf16[64,2048]{1,0:T(8,128)(2,1)S(1)} collective-permute-done((bf16[64,2048]{1,0:T(8,128)(2,1)S(1)}, bf16[64,2048]{1,0:T(8,128)(2,1)S(1)}, u32[]{:S(2)}, u32[]{:S(2)}) %collective-permute-start.22) | collective-permute-done | bytes 262176 | tf_op jit(solution)/shard_map/ppermute | solution.py:119
  105.3 0.2 add_convert_fusion.6
  105.5 8.5 %collective-permute-done.30 = bf16[64,2048]{1,0:T(8,128)(2,1)S(1)} collective-permute-done((bf16[64,2048]{1,0:T(8,128)(2,1)S(1)}, bf16[64,2048]{1,0:T(8,128)(2,1)S(1)}, u32[]{:S(2)}, u32[]{:S(2)}) %collective-permute-start.30) | collective-permute-done | bytes 262176 | tf_op jit(solution)/shard_map/ppermute | solution.py:118
  114.0 1.7 %collective-permute-start.23 = (bf16[128,2048]{1,0:T(8,128)(2,1)S(1)}, bf16[128,2048]{1,0:T(8,128)(2,1)S(1)}, u32[]{:S(2)}, u32[]{:S(2)}) collective-permute-start(bf16[128,2048]{1,0:T(8,128)(2,1)S(1)} %add_convert_fusion.6), channel_id=1, source_target_pairs={{0,2},{1,3},{4,0},{5,1},{8,4},{9,5},{12,8},{13,9},{14,12},{15,13},... | collective-permute-start | bytes 1572872 | tf_op jit(solution)/shard_map/ppermute | solution.py:119
  115.7 0.2 add_convert_fusion.3
  115.9 0.3 collective-permute-start.27
  116.2 0.3 collective-permute-start.31
  116.5 7.6 %shard_map.113 = (bf16[128,2048]{1,0:T(8,128)(2,1)S(1)}, bf16[128,2048]{1,0:T(8,128)(2,1)S(1)}, bf16[128,2048]{1,0:T(8,128)(2,1)S(1)}, bf16[128,2048]{1,0:T(8,128)(2,1)S(1)}) custom-call(bf16[128,2048]{1,0:T(8,128)(2,1)S(1)} %copy-done.6, bf16[128,2048]{1,0:T(8,128)(2,1)S(1)} %collective-permute-done.3.refs_1_, bf16[128,2048]{1,0:T(8,128)(2,1)S(1)} %copy-done.8, ...), custom_call_target="tpu_custom_call" | custom-call | flops 4831838208 | bytes 13631488 | tf_op jit(solution)/shard_map/pallas_call | solution.py:78
  124.2 4.1 %collective-permute-done.23 = bf16[128,2048]{1,0:T(8,128)(2,1)S(1)} collective-permute-done((bf16[128,2048]{1,0:T(8,128)(2,1)S(1)}, bf16[128,2048]{1,0:T(8,128)(2,1)S(1)}, u32[]{:S(2)}, u32[]{:S(2)}) %collective-permute-start.23) | collective-permute-done | bytes 524320 | tf_op jit(solution)/shard_map/ppermute | solution.py:119
  128.3 0.2 add_convert_fusion.5
  128.6 1.8 %collective-permute-start.24 = (bf16[128,2048]{1,0:T(8,128)(2,1)S(1)}, bf16[128,2048]{1,0:T(8,128)(2,1)S(1)}, u32[]{:S(2)}, u32[]{:S(2)}) collective-permute-start(bf16[128,2048]{1,0:T(8,128)(2,1)S(1)} %add_convert_fusion.5), channel_id=1, source_target_pairs={{0,2},{1,3},{4,0},{5,1},{8,4},{9,5},{12,8},{13,9},{14,12},{15,13},... | collective-permute-start | bytes 1572872 | tf_op jit(solution)/shard_map/ppermute | solution.py:119
  130.4 0.2 add_convert_fusion.2
  130.6 0.3 collective-permute-start.32
  130.9 4.8 %shard_map.112 = (bf16[128,2048]{1,0:T(8,128)(2,1)S(1)}, bf16[128,2048]{1,0:T(8,128)(2,1)S(1)}) custom-call(bf16[128,2048]{1,0:T(8,128)(2,1)S(1)} %copy-done.4, bf16[128,2048]{1,0:T(8,128)(2,1)S(1)} %collective-permute-done.refs_1_, f32[256,1]{1,0:T(8,128)S(1)} %copy.21.refs_2_, bf16[2048,768]{1,0:T(8,128)(2,1)S(1)} %bitcast.20, ...), custom_call_target="tpu_custom_call" | custom-call | flops 2415919104 | bytes 11534336 | tf_op jit(solution)/shard_map/pallas_call | solution.py:78
  135.9 7.1 %collective-permute-done.24 = bf16[128,2048]{1,0:T(8,128)(2,1)S(1)} collective-permute-done((bf16[128,2048]{1,0:T(8,128)(2,1)S(1)}, bf16[128,2048]{1,0:T(8,128)(2,1)S(1)}, u32[]{:S(2)}, u32[]{:S(2)}) %collective-permute-start.24) | collective-permute-done | bytes 524320 | tf_op jit(solution)/shard_map/ppermute | solution.py:119
  142.9 0.2 add_convert_fusion.4
  143.2 1.8 %collective-permute-start.25 = (bf16[128,2048]{1,0:T(8,128)(2,1)S(1)}, bf16[128,2048]{1,0:T(8,128)(2,1)S(1)}, u32[]{:S(2)}, u32[]{:S(2)}) collective-permute-start(bf16[128,2048]{1,0:T(8,128)(2,1)S(1)} %add_convert_fusion.4), channel_id=1, source_target_pairs={{0,2},{1,3},{4,0},{5,1},{8,4},{9,5},{12,8},{13,9},{14,12},{15,13},... | collective-permute-start | bytes 1572872 | tf_op jit(solution)/shard_map/ppermute | solution.py:119
  145.0 1.0 add_convert_fusion.1
  146.0 0.3 collective-permute-start.33
  146.3 0.1 convert_reduce_fusion
  146.4 0.6 dynamic_slice.12
  147.9 0.6 multiply_reduce_fusion
  149.2 7.6 %collective-permute-done.25 = bf16[128,2048]{1,0:T(8,128)(2,1)S(1)} collective-permute-done((bf16[128,2048]{1,0:T(8,128)(2,1)S(1)}, bf16[128,2048]{1,0:T(8,128)(2,1)S(1)}, u32[]{:S(2)}, u32[]{:S(2)}) %collective-permute-start.25) | collective-permute-done | bytes 524320 | tf_op jit(solution)/shard_map/ppermute | solution.py:119
  156.8 2.7 %collective-permute-done.33 = bf16[128,2048]{1,0:T(8,128)(2,1)S(1)} collective-permute-done((bf16[128,2048]{1,0:T(8,128)(2,1)}, bf16[128,2048]{1,0:T(8,128)(2,1)S(1)}, u32[]{:S(2)}, u32[]{:S(2)}) %collective-permute-start.33) | collective-permute-done | bytes 524320 | tf_op jit(solution)/shard_map/ppermute | solution.py:118
  159.5 1.1 add_convert_fusion
  (67 shorter events, 1.1 us)
Async XLA Ops:
  0.6 15.2 %collective-permute-start.2 = (bf16[128,2048]{1,0:T(8,128)(2,1)}, bf16[128,2048]{1,0:T(8,128)(2,1)S(1)}, u32[]{:S(2)}, u32[]{:S(2)}) collective-permute-start(bf16[128,2048]{1,0:T(8,128)(2,1)} %refs_0_.1), channel_id=1, source_target_pairs={{0,4},{1,5},{4,8},{5,9},{8,12},{9,13},{12,14},{13,15},{14,10},{15,... | collective-permute-start | bytes 1572872 | tf_op jit(solution)/shard_map/ppermute | solution.py:118
  3.7 13.9 %collective-permute-start.4 = (bf16[128,2048]{1,0:T(8,128)(2,1)}, bf16[128,2048]{1,0:T(8,128)(2,1)S(1)}, u32[]{:S(2)}, u32[]{:S(2)}) collective-permute-start(bf16[128,2048]{1,0:T(8,128)(2,1)} %refs_0_.1), channel_id=1, source_target_pairs={{0,2},{1,3},{4,0},{5,1},{8,4},{9,5},{12,8},{13,9},{14,12},{15,13},... | collective-permute-start | bytes 1572872 | tf_op jit(solution)/shard_map/ppermute | solution.py:119
  3.7 127.2 %collective-permute-start = (bf16[128,2048]{1,0:T(8,128)(2,1)}, bf16[128,2048]{1,0:T(8,128)(2,1)S(1)}, u32[]{:S(2)}, u32[]{:S(2)}) collective-permute-start(bf16[128,2048]{1,0:T(8,128)(2,1)} %refs_0_.1), channel_id=1, source_target_pairs={{0,1},{1,0},{2,3},{3,2},{4,5},{5,4},{6,7},{7,6},{8,9},{9,8},{10,11... | collective-permute-start | bytes 1572872 | tf_op jit(solution)/shard_map/ppermute | solution.py:120
  15.8 45.3 %copy-start.5 = (bf16[128,2048]{1,0:T(8,128)(2,1)}, bf16[128,2048]{1,0:T(8,128)(2,1)S(1)}, u32[]{:S(2)}) copy-start(bf16[128,2048]{1,0:T(8,128)(2,1)S(1)} %collective-permute-done.2.refs_0_) | copy-start | bytes 1572868
  15.8 13.2 %collective-permute-start.7 = (bf16[128,2048]{1,0:T(8,128)(2,1)S(1)}, bf16[128,2048]{1,0:T(8,128)(2,1)}, u32[]{:S(2)}, u32[]{:S(2)}) collective-permute-start(bf16[128,2048]{1,0:T(8,128)(2,1)S(1)} %collective-permute-done.2.refs_0_), channel_id=1, source_target_pairs={{0,4},{1,5},{4,8},{5,9},{8,12},{9,13},{12,14},{13,15},{14,10},{15,... | collective-permute-start | bytes 1572872 | tf_op jit(solution)/shard_map/ppermute | solution.py:118
  17.6 43.7 %copy-start.7 = (bf16[128,2048]{1,0:T(8,128)(2,1)}, bf16[128,2048]{1,0:T(8,128)(2,1)S(1)}, u32[]{:S(2)}) copy-start(bf16[128,2048]{1,0:T(8,128)(2,1)S(1)} %collective-permute-done.4.refs_2_) | copy-start | bytes 1572868
  17.6 12.9 %collective-permute-start.9 = (bf16[128,2048]{1,0:T(8,128)(2,1)S(1)}, bf16[128,2048]{1,0:T(8,128)(2,1)}, u32[]{:S(2)}, u32[]{:S(2)}) collective-permute-start(bf16[128,2048]{1,0:T(8,128)(2,1)S(1)} %collective-permute-done.4.refs_2_), channel_id=1, source_target_pairs={{0,2},{1,3},{4,0},{5,1},{8,4},{9,5},{12,8},{13,9},{14,12},{15,13},... | collective-permute-start | bytes 1572872 | tf_op jit(solution)/shard_map/ppermute | solution.py:119
  29.0 28.6 %collective-permute-start.12 = (bf16[128,2048]{1,0:T(8,128)(2,1)}, bf16[128,2048]{1,0:T(8,128)(2,1)S(1)}, u32[]{:S(2)}, u32[]{:S(2)}) collective-permute-start(bf16[128,2048]{1,0:T(8,128)(2,1)} %collective-permute-done.7.refs_0_), channel_id=1, source_target_pairs={{0,4},{1,5},{4,8},{5,9},{8,12},{9,13},{12,14},{13,15},{14,10},{15,... | collective-permute-start | bytes 1572872 | tf_op jit(solution)/shard_map/ppermute | solution.py:118
  30.5 27.9 %collective-permute-start.14 = (bf16[128,2048]{1,0:T(8,128)(2,1)}, bf16[128,2048]{1,0:T(8,128)(2,1)S(1)}, u32[]{:S(2)}, u32[]{:S(2)}) collective-permute-start(bf16[128,2048]{1,0:T(8,128)(2,1)} %collective-permute-done.9.refs_2_), channel_id=1, source_target_pairs={{0,2},{1,3},{4,0},{5,1},{8,4},{9,5},{12,8},{13,9},{14,12},{15,13},... | collective-permute-start | bytes 1572872 | tf_op jit(solution)/shard_map/ppermute | solution.py:119
  56.4 5.4 %collective-permute-start.10 = (bf16[128,2048]{1,0:T(8,128)(2,1)}, bf16[128,2048]{1,0:T(8,128)(2,1)}, u32[]{:S(2)}, u32[]{:S(2)}) collective-permute-start(bf16[128,2048]{1,0:T(8,128)(2,1)} %collective-permute-done.9.refs_2_), channel_id=1, source_target_pairs={{0,1},{1,0},{2,3},{3,2},{4,5},{5,4},{6,7},{7,6},{8,9},{9,8},{10,11... | collective-permute-start | bytes 1572872 | tf_op jit(solution)/shard_map/ppermute | solution.py:120
  56.9 5.1 %collective-permute-start.8 = (bf16[128,2048]{1,0:T(8,128)(2,1)}, bf16[128,2048]{1,0:T(8,128)(2,1)}, u32[]{:S(2)}, u32[]{:S(2)}) collective-permute-start(bf16[128,2048]{1,0:T(8,128)(2,1)} %collective-permute-done.7.refs_0_), channel_id=1, source_target_pairs={{0,1},{1,0},{2,3},{3,2},{4,5},{5,4},{6,7},{7,6},{8,9},{9,8},{10,11... | collective-permute-start | bytes 1572872 | tf_op jit(solution)/shard_map/ppermute | solution.py:120
  58.3 8.8 %collective-permute-start.17 = (bf16[64,2048]{1,0:T(8,128)(2,1)}, bf16[64,2048]{1,0:T(8,128)(2,1)S(1)}, u32[]{:S(2)}, u32[]{:S(2)}) collective-permute-start(bf16[64,2048]{1,0:T(8,128)(2,1)} %slice.56), channel_id=1, source_target_pairs={{0,4},{1,5},{4,8},{5,9},{8,12},{9,13},{12,14},{13,15},{14,10},{15,... | collective-permute-start | bytes 786440 | tf_op jit(solution)/shard_map/ppermute | solution.py:118
  59.1 8.8 %collective-permute-start.18 = (bf16[64,2048]{1,0:T(8,128)(2,1)}, bf16[64,2048]{1,0:T(8,128)(2,1)S(1)}, u32[]{:S(2)}, u32[]{:S(2)}) collective-permute-start(bf16[64,2048]{1,0:T(8,128)(2,1)} %slice.57), channel_id=1, source_target_pairs={{0,2},{1,3},{4,0},{5,1},{8,4},{9,5},{12,8},{13,9},{14,12},{15,13},... | collective-permute-start | bytes 786440 | tf_op jit(solution)/shard_map/ppermute | solution.py:119
  61.9 26.3 %collective-permute-start.13 = (bf16[128,2048]{1,0:T(8,128)(2,1)S(1)}, bf16[128,2048]{1,0:T(8,128)(2,1)S(1)}, u32[]{:S(2)}, u32[]{:S(2)}) collective-permute-start(bf16[128,2048]{1,0:T(8,128)(2,1)S(1)} %collective-permute-done.12.refs_0_), channel_id=1, source_target_pairs={{0,1},{1,0},{2,3},{3,2},{4,5},{5,4},{6,7},{7,6},{8,9},{9,8},{10,11... | collective-permute-start | bytes 1572872 | tf_op jit(solution)/shard_map/ppermute | solution.py:120
  62.0 26.6 %collective-permute-start.15 = (bf16[128,2048]{1,0:T(8,128)(2,1)S(1)}, bf16[128,2048]{1,0:T(8,128)(2,1)S(1)}, u32[]{:S(2)}, u32[]{:S(2)}) collective-permute-start(bf16[128,2048]{1,0:T(8,128)(2,1)S(1)} %collective-permute-done.14.refs_2_), channel_id=1, source_target_pairs={{0,1},{1,0},{2,3},{3,2},{4,5},{5,4},{6,7},{7,6},{8,9},{9,8},{10,11... | collective-permute-start | bytes 1572872 | tf_op jit(solution)/shard_map/ppermute | solution.py:120
  67.1 15.4 %collective-permute-start.19 = (bf16[64,2048]{1,0:T(8,128)(2,1)S(1)}, bf16[64,2048]{1,0:T(8,128)(2,1)S(1)}, u32[]{:S(2)}, u32[]{:S(2)}) collective-permute-start(bf16[64,2048]{1,0:T(8,128)(2,1)S(1)} %collective-permute-done.17.refs_0_), channel_id=1, source_target_pairs={{0,1},{1,0},{2,3},{3,2},{4,5},{5,4},{6,7},{7,6},{8,9},{9,8},{10,11... | collective-permute-start | bytes 786440 | tf_op jit(solution)/shard_map/ppermute | solution.py:120
  67.8 15.2 %collective-permute-start.20 = (bf16[64,2048]{1,0:T(8,128)(2,1)S(1)}, bf16[64,2048]{1,0:T(8,128)(2,1)S(1)}, u32[]{:S(2)}, u32[]{:S(2)}) collective-permute-start(bf16[64,2048]{1,0:T(8,128)(2,1)S(1)} %collective-permute-done.18.refs_1_), channel_id=1, source_target_pairs={{0,1},{1,0},{2,3},{3,2},{4,5},{5,4},{6,7},{7,6},{8,9},{9,8},{10,11... | collective-permute-start | bytes 786440 | tf_op jit(solution)/shard_map/ppermute | solution.py:120
  67.8 1.9 %copy-start = (bf16[1,2048,768]{2,1,0:T(8,128)(2,1)S(1)}, bf16[1,2048,768]{2,1,0:T(8,128)(2,1)}, u32[]{:S(2)}) copy-start(bf16[1,2048,768]{2,1,0:T(8,128)(2,1)} %param.12) | copy-start | bytes 9437188
  69.7 1.9 %copy-start.2 = (bf16[1,2048,768]{2,1,0:T(8,128)(2,1)S(1)}, bf16[1,2048,768]{2,1,0:T(8,128)(2,1)}, u32[]{:S(2)}) copy-start(bf16[1,2048,768]{2,1,0:T(8,128)(2,1)} %param.13) | copy-start | bytes 9437188
  71.6 1.9 %copy-start.3 = (bf16[1,768,2048]{2,1,0:T(8,128)(2,1)S(1)}, bf16[1,768,2048]{2,1,0:T(8,128)(2,1)}, u32[]{:S(2)}) copy-start(bf16[1,768,2048]{2,1,0:T(8,128)(2,1)} %param.14) | copy-start | bytes 9437188
  73.5 9.0 %copy-start.6 = (bf16[128,2048]{1,0:T(8,128)(2,1)S(1)}, bf16[128,2048]{1,0:T(8,128)(2,1)}, u32[]{:S(2)}) copy-start(bf16[128,2048]{1,0:T(8,128)(2,1)} %copy-done.5) | copy-start | bytes 1572868
  82.5 6.2 %copy-start.1 = (bf16[1,2048,768]{2,1,0:T(8,128)(2,1)S(1)}, bf16[1,2048,768]{2,1,0:T(8,128)(2,1)}, u32[]{:S(2)}) copy-start(bf16[1,2048,768]{2,1,0:T(8,128)(2,1)} %param.12) | copy-start | bytes 9437188
  82.5 33.4 %collective-permute-start.3 = (bf16[128,2048]{1,0:T(8,128)(2,1)S(1)}, bf16[128,2048]{1,0:T(8,128)(2,1)S(1)}, u32[]{:S(2)}, u32[]{:S(2)}) collective-permute-start(bf16[128,2048]{1,0:T(8,128)(2,1)S(1)} %copy-done.6), channel_id=1, source_target_pairs={{0,1},{1,0},{2,3},{3,2},{4,5},{5,4},{6,7},{7,6},{8,9},{9,8},{10,11... | collective-permute-start | bytes 1572872 | tf_op jit(solution)/shard_map/ppermute | solution.py:120
  88.0 8.3 %collective-permute-start.21 = (bf16[64,2048]{1,0:T(8,128)(2,1)S(1)}, bf16[64,2048]{1,0:T(8,128)(2,1)S(1)}, u32[]{:S(2)}, u32[]{:S(2)}) collective-permute-start(bf16[64,2048]{1,0:T(8,128)(2,1)S(1)} %get-tuple-element.30), channel_id=1, source_target_pairs={{0,1},{1,0},{2,3},{3,2},{4,5},{5,4},{6,7},{7,6},{8,9},{9,8},{10,11... | collective-permute-start | bytes 786440 | tf_op jit(solution)/shard_map/ppermute | solution.py:120
  88.2 17.1 %copy-start.8 = (bf16[128,2048]{1,0:T(8,128)(2,1)S(1)}, bf16[128,2048]{1,0:T(8,128)(2,1)}, u32[]{:S(2)}) copy-start(bf16[128,2048]{1,0:T(8,128)(2,1)} %copy-done.7) | copy-start | bytes 1572868
  88.2 8.7 %collective-permute-start.29 = (bf16[64,2048]{1,0:T(8,128)(2,1)S(1)}, bf16[64,2048]{1,0:T(8,128)(2,1)S(1)}, u32[]{:S(2)}, u32[]{:S(2)}) collective-permute-start(bf16[64,2048]{1,0:T(8,128)(2,1)S(1)} %get-tuple-element.38), channel_id=1, source_target_pairs={{0,1},{1,0},{2,3},{3,2},{4,5},{5,4},{6,7},{7,6},{8,9},{9,8},{10,11... | collective-permute-start | bytes 786440 | tf_op jit(solution)/shard_map/ppermute | solution.py:120
  96.2 9.0 %collective-permute-start.16 = (bf16[128,2048]{1,0:T(8,128)(2,1)S(1)}, bf16[128,2048]{1,0:T(8,128)(2,1)S(1)}, u32[]{:S(2)}, u32[]{:S(2)}) collective-permute-start(bf16[128,2048]{1,0:T(8,128)(2,1)S(1)} %get-tuple-element.28), channel_id=1, source_target_pairs={{0,1},{1,0},{2,3},{3,2},{4,5},{5,4},{6,7},{7,6},{8,9},{9,8},{10,11... | collective-permute-start | bytes 1572872 | tf_op jit(solution)/shard_map/ppermute | solution.py:120
  96.4 17.6 %collective-permute-start.28 = (bf16[128,2048]{1,0:T(8,128)(2,1)S(1)}, bf16[128,2048]{1,0:T(8,128)(2,1)S(1)}, u32[]{:S(2)}, u32[]{:S(2)}) collective-permute-start(bf16[128,2048]{1,0:T(8,128)(2,1)S(1)} %get-tuple-element.36), channel_id=1, source_target_pairs={{0,1},{1,0},{2,3},{3,2},{4,5},{5,4},{6,7},{7,6},{8,9},{9,8},{10,11... | collective-permute-start | bytes 1572872 | tf_op jit(solution)/shard_map/ppermute | solution.py:120
  96.9 8.4 %collective-permute-start.22 = (bf16[64,2048]{1,0:T(8,128)(2,1)S(1)}, bf16[64,2048]{1,0:T(8,128)(2,1)S(1)}, u32[]{:S(2)}, u32[]{:S(2)}) collective-permute-start(bf16[64,2048]{1,0:T(8,128)(2,1)S(1)} %add_convert_fusion.8), channel_id=1, source_target_pairs={{0,2},{1,3},{4,0},{5,1},{8,4},{9,5},{12,8},{13,9},{14,12},{15,13},... | collective-permute-start | bytes 786440 | tf_op jit(solution)/shard_map/ppermute | solution.py:119
  105.2 11.0 %collective-permute-start.5 = (bf16[128,2048]{1,0:T(8,128)(2,1)S(1)}, bf16[128,2048]{1,0:T(8,128)(2,1)S(1)}, u32[]{:S(2)}, u32[]{:S(2)}) collective-permute-start(bf16[128,2048]{1,0:T(8,128)(2,1)S(1)} %copy-done.8), channel_id=1, source_target_pairs={{0,1},{1,0},{2,3},{3,2},{4,5},{5,4},{6,7},{7,6},{8,9},{9,8},{10,11... | collective-permute-start | bytes 1572872 | tf_op jit(solution)/shard_map/ppermute | solution.py:120
  105.2 8.7 %collective-permute-start.30 = (bf16[64,2048]{1,0:T(8,128)(2,1)S(1)}, bf16[64,2048]{1,0:T(8,128)(2,1)S(1)}, u32[]{:S(2)}, u32[]{:S(2)}) collective-permute-start(bf16[64,2048]{1,0:T(8,128)(2,1)S(1)} %add_convert_fusion.7), channel_id=1, source_target_pairs={{0,4},{1,5},{4,8},{5,9},{8,12},{9,13},{12,14},{13,15},{14,10},{15,... | collective-permute-start | bytes 786440 | tf_op jit(solution)/shard_map/ppermute | solution.py:118
  114.0 10.1 %collective-permute-start.11 = (bf16[128,2048]{1,0:T(8,128)(2,1)S(1)}, bf16[128,2048]{1,0:T(8,128)(2,1)S(1)}, u32[]{:S(2)}, u32[]{:S(2)}) collective-permute-start(bf16[128,2048]{1,0:T(8,128)(2,1)S(1)} %get-tuple-element.26), channel_id=1, source_target_pairs={{0,1},{1,0},{2,3},{3,2},{4,5},{5,4},{6,7},{7,6},{8,9},{9,8},{10,11... | collective-permute-start | bytes 1572872 | tf_op jit(solution)/shard_map/ppermute | solution.py:120
  114.0 14.3 %collective-permute-start.23 = (bf16[128,2048]{1,0:T(8,128)(2,1)S(1)}, bf16[128,2048]{1,0:T(8,128)(2,1)S(1)}, u32[]{:S(2)}, u32[]{:S(2)}) collective-permute-start(bf16[128,2048]{1,0:T(8,128)(2,1)S(1)} %add_convert_fusion.6), channel_id=1, source_target_pairs={{0,2},{1,3},{4,0},{5,1},{8,4},{9,5},{12,8},{13,9},{14,12},{15,13},... | collective-permute-start | bytes 1572872 | tf_op jit(solution)/shard_map/ppermute | solution.py:119
  115.9 12.7 %collective-permute-start.27 = (bf16[128,2048]{1,0:T(8,128)(2,1)S(1)}, bf16[128,2048]{1,0:T(8,128)(2,1)S(1)}, u32[]{:S(2)}, u32[]{:S(2)}) collective-permute-start(bf16[128,2048]{1,0:T(8,128)(2,1)S(1)} %get-tuple-element.34), channel_id=1, source_target_pairs={{0,1},{1,0},{2,3},{3,2},{4,5},{5,4},{6,7},{7,6},{8,9},{9,8},{10,11... | collective-permute-start | bytes 1572872 | tf_op jit(solution)/shard_map/ppermute | solution.py:120
  116.2 14.2 %collective-permute-start.31 = (bf16[128,2048]{1,0:T(8,128)(2,1)S(1)}, bf16[128,2048]{1,0:T(8,128)(2,1)S(1)}, u32[]{:S(2)}, u32[]{:S(2)}) collective-permute-start(bf16[128,2048]{1,0:T(8,128)(2,1)S(1)} %add_convert_fusion.3), channel_id=1, source_target_pairs={{0,4},{1,5},{4,8},{5,9},{8,12},{9,13},{12,14},{13,15},{14,10},{15,... | collective-permute-start | bytes 1572872 | tf_op jit(solution)/shard_map/ppermute | solution.py:118
  124.1 6.9 %copy-start.4 = (bf16[128,2048]{1,0:T(8,128)(2,1)S(1)}, bf16[128,2048]{1,0:T(8,128)(2,1)}, u32[]{:S(2)}) copy-start(bf16[128,2048]{1,0:T(8,128)(2,1)} %refs_0_.1) | copy-start | bytes 1572868
  124.1 11.8 %collective-permute-start.6 = (bf16[128,2048]{1,0:T(8,128)(2,1)S(1)}, bf16[128,2048]{1,0:T(8,128)(2,1)S(1)}, u32[]{:S(2)}, u32[]{:S(2)}) collective-permute-start(bf16[128,2048]{1,0:T(8,128)(2,1)S(1)} %get-tuple-element.24), channel_id=1, source_target_pairs={{0,1},{1,0},{2,3},{3,2},{4,5},{5,4},{6,7},{7,6},{8,9},{9,8},{10,11... | collective-permute-start | bytes 1572872 | tf_op jit(solution)/shard_map/ppermute | solution.py:120
  128.3 16.7 %collective-permute-start.26 = (bf16[128,2048]{1,0:T(8,128)(2,1)S(1)}, bf16[128,2048]{1,0:T(8,128)(2,1)S(1)}, u32[]{:S(2)}, u32[]{:S(2)}) collective-permute-start(bf16[128,2048]{1,0:T(8,128)(2,1)S(1)} %get-tuple-element.32), channel_id=1, source_target_pairs={{0,1},{1,0},{2,3},{3,2},{4,5},{5,4},{6,7},{7,6},{8,9},{9,8},{10,11... | collective-permute-start | bytes 1572872 | tf_op jit(solution)/shard_map/ppermute | solution.py:120
  128.6 14.4 %collective-permute-start.24 = (bf16[128,2048]{1,0:T(8,128)(2,1)S(1)}, bf16[128,2048]{1,0:T(8,128)(2,1)S(1)}, u32[]{:S(2)}, u32[]{:S(2)}) collective-permute-start(bf16[128,2048]{1,0:T(8,128)(2,1)S(1)} %add_convert_fusion.5), channel_id=1, source_target_pairs={{0,2},{1,3},{4,0},{5,1},{8,4},{9,5},{12,8},{13,9},{14,12},{15,13},... | collective-permute-start | bytes 1572872 | tf_op jit(solution)/shard_map/ppermute | solution.py:119
  130.6 14.4 %collective-permute-start.32 = (bf16[128,2048]{1,0:T(8,128)(2,1)S(1)}, bf16[128,2048]{1,0:T(8,128)(2,1)S(1)}, u32[]{:S(2)}, u32[]{:S(2)}) collective-permute-start(bf16[128,2048]{1,0:T(8,128)(2,1)S(1)} %add_convert_fusion.2), channel_id=1, source_target_pairs={{0,4},{1,5},{4,8},{5,9},{8,12},{9,13},{12,14},{13,15},{14,10},{15,... | collective-permute-start | bytes 1572872 | tf_op jit(solution)/shard_map/ppermute | solution.py:118
  135.8 13.4 %collective-permute-start.1 = (bf16[128,2048]{1,0:T(8,128)(2,1)S(1)}, bf16[128,2048]{1,0:T(8,128)(2,1)S(1)}, u32[]{:S(2)}, u32[]{:S(2)}) collective-permute-start(bf16[128,2048]{1,0:T(8,128)(2,1)S(1)} %get-tuple-element.22), channel_id=1, source_target_pairs={{0,1},{1,0},{2,3},{3,2},{4,5},{5,4},{6,7},{7,6},{8,9},{9,8},{10,11... | collective-permute-start | bytes 1572872 | tf_op jit(solution)/shard_map/ppermute | solution.py:120
  143.2 13.6 %collective-permute-start.25 = (bf16[128,2048]{1,0:T(8,128)(2,1)S(1)}, bf16[128,2048]{1,0:T(8,128)(2,1)S(1)}, u32[]{:S(2)}, u32[]{:S(2)}) collective-permute-start(bf16[128,2048]{1,0:T(8,128)(2,1)S(1)} %add_convert_fusion.4), channel_id=1, source_target_pairs={{0,2},{1,3},{4,0},{5,1},{8,4},{9,5},{12,8},{13,9},{14,12},{15,13},... | collective-permute-start | bytes 1572872 | tf_op jit(solution)/shard_map/ppermute | solution.py:119
  146.0 13.5 %collective-permute-start.33 = (bf16[128,2048]{1,0:T(8,128)(2,1)}, bf16[128,2048]{1,0:T(8,128)(2,1)S(1)}, u32[]{:S(2)}, u32[]{:S(2)}) collective-permute-start(bf16[128,2048]{1,0:T(8,128)(2,1)} %add_convert_fusion.1), channel_id=1, source_target_pairs={{0,4},{1,5},{4,8},{5,9},{8,12},{9,13},{12,14},{13,15},{14,10},{15,... | collective-permute-start | bytes 1572872 | tf_op jit(solution)/shard_map/ppermute | solution.py:118

commit v2 on v1

v2 whole, which is shorter than its diff:
```python
import functools

import jax
import jax.numpy as jnp
from jax import lax
from jax.experimental import pallas as pl
from jax.experimental.pallas import tpu as pltpu
from jax.sharding import PartitionSpec as P

CORES = 2
VMEM_LIMIT = 32 * 1024 * 1024


def ring_order(chips):
    if chips <= 8:
        return list(range(0, chips, 2)) + list(range(1, chips, 2))[::-1]
    return list(range(chips))


def ring_shift(order, step):
    pairs = []
    for place, chip in enumerate(order):
        target = order[(place + step) % len(order)]
        pairs += [(CORES * chip + core, CORES * target + core) for core in range(CORES)]
    return pairs


def expert_kernel(sizes, *refs):
    count = len(sizes)
    blocks = refs[:count]
    scale_ref, gate_ref, up_ref, down_ref = refs[count : count + 4]
    outs = refs[count + 4 : 2 * count + 4]
    rows_ref, hidden_ref = refs[2 * count + 4 :]
    starts = [sum(sizes[:i]) for i in range(count)]
    width, hidden_width = gate_ref.shape
    chunk = 256

    for i in range(count):
        rows_ref[starts[i] : starts[i] + sizes[i], :] = blocks[i][...]

    @pl.loop(0, hidden_width // chunk)
    def _(j):
        at = pl.ds(pl.multiple_of(j * chunk, chunk), chunk)
        rows = rows_ref[...]
        gate = jnp.dot(rows, gate_ref[:, at], preferred_element_type=jnp.float32)
        up = jnp.dot(rows, up_ref[:, at], preferred_element_type=jnp.float32)
        hidden_ref[:, at] = (gate / (1.0 + jnp.exp(-gate)) * up).astype(jnp.bfloat16)

    @pl.loop(0, width // chunk)
    def _(j):
        at = pl.ds(pl.multiple_of(j * chunk, chunk), chunk)
        out = jnp.dot(hidden_ref[...], down_ref[:, at], preferred_element_type=jnp.float32)
        out = out.astype(jnp.bfloat16).astype(jnp.float32) * scale_ref[...]
        for i in range(count):
            outs[i][:, at] = out[starts[i] : starts[i] + sizes[i]].astype(jnp.bfloat16)


def apply_expert(blocks, scale, gate_weight, up_weight, down_weight):
    width, hidden_width = gate_weight.shape
    sizes = tuple(block.shape[0] for block in blocks)
    total = sum(sizes)
    count = len(blocks)
    in_vmem = pl.BlockSpec(memory_space=pltpu.VMEM)
    return pl.pallas_call(
        functools.partial(expert_kernel, sizes),
        out_shape=[jax.ShapeDtypeStruct((size, width), jnp.bfloat16) for size in sizes],
        in_specs=[in_vmem] * (count + 4),
        out_specs=[in_vmem] * count,
        scratch_shapes=[
            pltpu.VMEM((total, width), jnp.bfloat16),
            pltpu.VMEM((total, hidden_width), jnp.bfloat16),
        ],
        compiler_params=pltpu.CompilerParams(vmem_limit_bytes=VMEM_LIMIT),
        cost_estimate=pl.CostEstimate(
            flops=6 * total * width * hidden_width,
            bytes_accessed=4 * total * width,
            transcendentals=total * hidden_width,
        ),
    )(*blocks, scale, gate_weight, up_weight, down_weight)


def body(tokens, expert_ids, gate_fixed, gate_weight, up_weight, down_weight):
    tok_rows, model_width = tokens.shape
    per_token = expert_ids.shape[1]
    node_count = lax.axis_size("node")
    expert_count = node_count
    token_total = tok_rows * node_count
    chips = node_count // CORES
    far = chips // 2
    half = tok_rows // 2
    order = ring_order(chips)
    to_right, to_left = ring_shift(order, 1), ring_shift(order, -1)
    to_sibling = [(node, node ^ 1) for node in range(node_count)]
    right = lambda a: lax.ppermute(a, "node", to_right)
    left = lambda a: lax.ppermute(a, "node", to_left)
    sibling = lambda a: lax.ppermute(a, "node", to_sibling)
    node = lax.axis_index("node")

    fixed_gate = gate_fixed.astype(jnp.float32)
    weights = fixed_gate / jnp.sum(fixed_gate, axis=1, keepdims=True)
    experts = jnp.arange(expert_count, dtype=jnp.int32)
    dense = jnp.sum(
        jnp.where(expert_ids[None] == experts[:, None, None], weights[None], 0.0), axis=2
    )
    pair = jnp.stack([dense, sibling(dense)])
    near = [(pair,)]
    for k in range(1, far):
        near.append(
            tuple(lax.ppermute(pair, "node", ring_shift(order, step)) for step in (k, -k))
        )
    near.append((lax.ppermute(pair, "node", ring_shift(order, far)),))
    own = [
        jnp.stack([lax.dynamic_index_in_dim(p, node, 1, keepdims=False) for p in pairs])
        for pairs in near
    ]

    every = jnp.stack([p for pairs in near for p in pairs])
    counts = jnp.sum((every > 0).astype(jnp.float32), axis=(0, 1, 3))
    mass = jnp.sum(every, axis=(0, 1, 3)) / token_total
    own_count = lax.dynamic_slice(counts, (node,), (1,))
    expert_load = own_count * expert_count / (token_total * per_token)
    balance_loss = (expert_count * jnp.sum(counts / (token_total * per_token) * mass)).reshape(1)

    gate_weight, up_weight, down_weight = gate_weight[0], up_weight[0], down_weight[0]

    def run(blocks, k):
        return apply_expert(
            blocks, own[k].reshape(-1, 1), gate_weight, up_weight, down_weight
        )

    from_left, from_right = tokens, tokens
    mine, theirs = run([tokens, sibling(tokens)], 0)
    outs = [(mine, sibling(theirs))]
    for k in range(1, far):
        from_left, from_right = right(from_left), left(from_right)
        res = run([from_left, sibling(from_left), from_right, sibling(from_right)], k)
        outs.append((res[0], sibling(res[1]), res[2], sibling(res[3])))
    far_low, far_high = right(from_left[:half]), left(from_right[half:])
    res = run([far_low, far_high, sibling(far_low), sibling(far_high)], far)

    def add(*terms):
        return sum(term.astype(jnp.float32) for term in terms)

    low = left(add(res[0], sibling(res[2])).astype(jnp.bfloat16))
    high = right(add(res[1], sibling(res[3])).astype(jnp.bfloat16))
    for k in range(far - 1, 0, -1):
        left_own, left_sib, right_own, right_sib = outs[k]
        to_left_sum, to_right_sum = add(left_own, left_sib), add(right_own, right_sib)
        if k == far - 1:
            to_left_sum = to_left_sum + jnp.pad(low.astype(jnp.float32), ((0, half), (0, 0)))
            to_right_sum = to_right_sum + jnp.pad(high.astype(jnp.float32), ((half, 0), (0, 0)))
        else:
            to_left_sum = to_left_sum + low.astype(jnp.float32)
            to_right_sum = to_right_sum + high.astype(jnp.float32)
        low = left(to_left_sum.astype(jnp.bfloat16))
        high = right(to_right_sum.astype(jnp.bfloat16))
    mixed = add(*outs[0], low, high).astype(jnp.bfloat16)
    return (mixed, expert_load, balance_loss)


def solution(mesh):
    return jax.shard_map(
        body,
        mesh=mesh,
        in_specs=(
            P(("groups", "node"), None),
            P(("groups", "node"), None),
            P(("groups", "node"), None),
            P("node", None, None),
            P("node", None, None),
            P("node", None, None),
        ),
        out_specs=(P(("groups", "node"), None), P(("groups", "node")), P("groups")),
        check_vma=False,
    )
```

time: 163 us -> 157 us (0.963)
  blocking collectives: 24.6 us -> 0 us
  starting transfers between devices: 20.6 us -> 32 us
  waiting for transfers between devices: 59.8 us -> 68.4 us
  local copies, waits for them, and re-layouts: 11.7 us -> 9.94 us
  other arithmetic: 7.79 us -> 9.48 us
    all_gather x1 -> x0, blocking collectives: 24.6 us -> none  [body(): dense_all = lax.all_gather(dense, 'node')]
    ppermute x0 -> x7, waiting for transfers between devices: none -> 12 us  [the longest x6 12 us: body(): lax.ppermute(pair, 'node', ring_shift(order, step))]
    ppermute x0 -> x7, starting transfers between devices: none -> 11.8 us  [the longest x6 6.81 us: body(): lax.ppermute(pair, 'node', ring_shift(order, step))]
    ppermute x8, waiting for transfers between devices: 33.7 us -> 26.9 us  [body(): right = lambda a: lax.ppermute(a, 'node', to_right)]
    ppermute x8, starting transfers between devices: 9.95 us -> 6.3 us  [body(): left = lambda a: lax.ppermute(a, 'node', to_left)]
    ppermute x8, waiting for transfers between devices: 26.1 us -> 29.5 us  [body(): left = lambda a: lax.ppermute(a, 'node', to_left)]
    ppermute x8, starting transfers between devices: 7.31 us -> 10.2 us  [body(): right = lambda a: lax.ppermute(a, 'node', to_right)]
    reduce_sum x4 -> x10, other arithmetic: 0.97 us -> 2.94 us  [the longest x9 2.81 us: body(): mass = jnp.sum(every, axis=(0, 1, 3)) / token_total]
  transfers between devices with their start and end apart: 34 -> 42, of which waited for: 10 -> 16; matrix products, arithmetic and copies ran while one was open for 8% -> 6% of each run, Pallas kernels for 21% -> 21%
where the time goes in v2:
time: 157 us
  waiting for transfers between devices  68.4 us (44%)
  Pallas kernels  32.3 us (21%)
  starting transfers between devices  32 us (20%)
  local copies, waits for them, and re-layouts  9.94 us (6%)
  other arithmetic  9.48 us (6%)
  between operations  4.66 us (3%)
    pallas_call x5, Pallas kernels, apply_expert(): pl.pallas_call(functools.partial(expert_kernel, sizes), out_shape=[jax.Sh...  32.3 us
    ppermute x8, waiting for transfers between devices, body(): left = lambda a: lax.ppermute(a, 'node', to_left)  29.5 us
    ppermute x8, waiting for transfers between devices, body(): right = lambda a: lax.ppermute(a, 'node', to_right)  26.9 us
    ppermute x6, waiting for transfers between devices, body(): lax.ppermute(pair, 'node', ring_shift(order, step))  12 us
    ppermute x8, starting transfers between devices, body(): right = lambda a: lax.ppermute(a, 'node', to_right)  10.2 us
    ppermute x6, starting transfers between devices, body(): lax.ppermute(pair, 'node', ring_shift(order, step))  6.81 us
    unnamed x52, local copies, waits for them, and re-layouts  6.49 us
    ppermute x8, starting transfers between devices, body(): left = lambda a: lax.ppermute(a, 'node', to_left)  6.3 us
  transfers between devices with their start and end apart: 42, of which 16 were waited for; matrix products, arithmetic and copies ran while one was open for 6% of the time, Pallas kernels for 21%

profile of v2, /device:TPU:0, one launch (start us, length us, event | category | flops | bytes accessed | tf_op | source)
XLA Modules:
  0.0 156.8 jit_solution(14478870531445164310)
XLA Ops:
  0.6 0.7 convert_reduce_fusion.1
  1.3 0.7 convert_divide_fusion
  2.0 1.4 select_reduce_fusion
  3.4 0.5 collective-permute-start.1
  3.9 2.6 %collective-permute-start.3 = (bf16[128,2048]{1,0:T(8,128)(2,1)}, bf16[128,2048]{1,0:T(8,128)(2,1)S(1)}, u32[]{:S(2)}, u32[]{:S(2)}) collective-permute-start(bf16[128,2048]{1,0:T(8,128)(2,1)} %refs_0_.1), channel_id=1, source_target_pairs={{0,4},{1,5},{4,8},{5,9},{8,12},{9,13},{12,14},{13,15},{14,10},{15,... | collective-permute-start | bytes 1572872 | tf_op jit(solution)/shard_map/ppermute | solution.py:94
  6.5 5.0 %collective-permute-start.28 = (f32[2,16,128]{2,1,0:T(8,128)S(1)}, f32[2,16,128]{2,1,0:T(8,128)S(1)}, u32[]{:S(2)}, u32[]{:S(2)}) collective-permute-start(f32[2,16,128]{2,1,0:T(8,128)S(1)} %pad_maximum_fusion), channel_id=1, source_target_pairs={{0,14},{1,15},{4,10},{5,11},{8,6},{9,7},{12,2},{13,3},{14,0},{15,1... | collective-permute-start | bytes 49160 | tf_op jit(solution)/shard_map/ppermute | solution.py:111
  11.7 3.6 %collective-permute-start.22 = (f32[2,16,128]{2,1,0:T(8,128)S(1)}, f32[2,16,128]{2,1,0:T(8,128)S(1)}, u32[]{:S(2)}, u32[]{:S(2)}) collective-permute-start(f32[2,16,128]{2,1,0:T(8,128)S(1)} %pad_maximum_fusion), channel_id=1, source_target_pairs={{0,10},{1,11},{4,6},{5,7},{8,2},{9,3},{12,0},{13,1},{14,4},{15,5},... | collective-permute-start | bytes 49160 | tf_op jit(solution)/shard_map/ppermute | solution.py:109
  15.4 0.6 reduce_sum.86
  16.0 6.1 %collective-permute-done.21 = f32[2,16,128]{2,1,0:T(8,128)S(1)} collective-permute-done((f32[2,16,128]{2,1,0:T(8,128)S(1)}, f32[2,16,128]{2,1,0:T(8,128)S(1)}, u32[]{:S(2)}, u32[]{:S(2)}) %collective-permute-start.21) | collective-permute-done | bytes 16416 | tf_op jit(solution)/shard_map/ppermute | solution.py:109
  22.2 2.9 %collective-permute-start.15 = (f32[2,16,128]{2,1,0:T(8,128)S(1)}, f32[2,16,128]{2,1,0:T(8,128)S(1)}, u32[]{:S(2)}, u32[]{:S(2)}) collective-permute-start(f32[2,16,128]{2,1,0:T(8,128)S(1)} %pad_maximum_fusion), channel_id=1, source_target_pairs={{0,6},{1,7},{4,2},{5,3},{8,0},{9,1},{12,4},{13,5},{14,8},{15,9},{1... | collective-permute-start | bytes 49160 | tf_op jit(solution)/shard_map/ppermute | solution.py:109
  25.2 1.6 %collective-permute-done.15 = f32[2,16,128]{2,1,0:T(8,128)S(1)} collective-permute-done((f32[2,16,128]{2,1,0:T(8,128)S(1)}, f32[2,16,128]{2,1,0:T(8,128)S(1)}, u32[]{:S(2)}, u32[]{:S(2)}) %collective-permute-start.15) | collective-permute-done | bytes 16416 | tf_op jit(solution)/shard_map/ppermute | solution.py:109
  26.8 3.0 %collective-permute-done.14 = f32[2,16,128]{2,1,0:T(8,128)S(1)} collective-permute-done((f32[2,16,128]{2,1,0:T(8,128)S(1)}, f32[2,16,128]{2,1,0:T(8,128)S(1)}, u32[]{:S(2)}, u32[]{:S(2)}) %collective-permute-start.14) | collective-permute-done | bytes 16416 | tf_op jit(solution)/shard_map/ppermute | solution.py:109
  29.8 0.9 collective-permute-done.7
  30.7 1.2 collective-permute-start.10
  31.9 0.9 collective-permute-start.12
  32.8 0.6 pad_maximum_fusion.2
  33.4 0.4 collective-permute-done.8
  33.8 8.9 %collective-permute-done.10.refs_0_ = bf16[128,2048]{1,0:T(8,128)(2,1)} collective-permute-done((bf16[128,2048]{1,0:T(8,128)(2,1)S(1)}, bf16[128,2048]{1,0:T(8,128)(2,1)}, u32[]{:S(2)}, u32[]{:S(2)}) %collective-permute-start.10) | collective-permute-done | bytes 524320 | tf_op jit(solution)/shard_map/ppermute | solution.py:94
  42.7 1.1 collective-permute-start.17
  43.8 0.9 collective-permute-start.19
  44.8 0.5 collective-permute-start.13
  45.3 0.6 pad_maximum_fusion.1
  45.9 7.0 %collective-permute-done.17.refs_0_ = bf16[128,2048]{1,0:T(8,128)(2,1)S(1)} collective-permute-done((bf16[128,2048]{1,0:T(8,128)(2,1)}, bf16[128,2048]{1,0:T(8,128)(2,1)S(1)}, u32[]{:S(2)}, u32[]{:S(2)}) %collective-permute-start.17) | collective-permute-done | bytes 524320 | tf_op jit(solution)/shard_map/ppermute | solution.py:94
  53.0 1.2 collective-permute-done.19.refs_2_
  54.1 0.6 collective-permute-start.24
  54.7 0.7 slice.9
  55.4 1.5 collective-permute-start.25
  57.2 0.8 copy.22.refs_4_
  58.1 0.8 copy.21.refs_4_
  58.9 0.7 constant_dynamic-update-slice_fusion.2
  59.6 0.5 collective-permute-start.20
  60.1 1.6 %collective-permute-done.24.refs_0_ = bf16[64,2048]{1,0:T(8,128)(2,1)S(1)} collective-permute-done((bf16[64,2048]{1,0:T(8,128)(2,1)S(1)}, bf16[64,2048]{1,0:T(8,128)(2,1)S(1)}, u32[]{:S(2)}, u32[]{:S(2)}) %collective-permute-start.24) | collective-permute-done | bytes 262176 | tf_op jit(solution)/shard_map/ppermute | solution.py:94
  61.7 2.0 %collective-permute-done.25.refs_1_ = bf16[64,2048]{1,0:T(8,128)(2,1)S(1)} collective-permute-done((bf16[64,2048]{1,0:T(8,128)(2,1)}, bf16[64,2048]{1,0:T(8,128)(2,1)S(1)}, u32[]{:S(2)}, u32[]{:S(2)}) %collective-permute-start.25) | collective-permute-done | bytes 262176 | tf_op jit(solution)/shard_map/ppermute | solution.py:95
  63.7 1.9 %copy-done = bf16[1,2048,768]{2,1,0:T(8,128)(2,1)S(1)} copy-done((bf16[1,2048,768]{2,1,0:T(8,128)(2,1)S(1)}, bf16[1,2048,768]{2,1,0:T(8,128)(2,1)}, u32[]{:S(2)}) %copy-start) | copy-done | bytes 3145752
  65.6 1.9 %copy-done.2 = bf16[1,2048,768]{2,1,0:T(8,128)(2,1)S(1)} copy-done((bf16[1,2048,768]{2,1,0:T(8,128)(2,1)S(1)}, bf16[1,2048,768]{2,1,0:T(8,128)(2,1)}, u32[]{:S(2)}) %copy-start.2) | copy-done | bytes 3145752
  67.5 1.9 %copy-done.3 = bf16[1,768,2048]{2,1,0:T(8,128)(2,1)S(1)} copy-done((bf16[1,768,2048]{2,1,0:T(8,128)(2,1)S(1)}, bf16[1,768,2048]{2,1,0:T(8,128)(2,1)}, u32[]{:S(2)}) %copy-start.3) | copy-done | bytes 3145752
  69.4 8.8 %shard_map.87 = (bf16[128,2048]{1,0:T(8,128)(2,1)S(1)}, bf16[128,2048]{1,0:T(8,128)(2,1)S(1)}, bf16[128,2048]{1,0:T(8,128)(2,1)S(1)}, bf16[128,2048]{1,0:T(8,128)(2,1)S(1)}) custom-call(bf16[128,2048]{1,0:T(8,128)(2,1)} %collective-permute-done.10.refs_0_, bf16[128,2048]{1,0:T(8,128)(2,1)} %collective-permute-done.11.refs_1_, ...), custom_call_target="tpu_custom_call" | custom-call | flops 4831838208 | bytes 4194304 | tf_op jit(solution)/shard_map/pallas_call | solution.py:64
  78.2 0.6 collective-permute-start.4
  78.7 4.6 %shard_map.89 = (bf16[64,2048]{1,0:T(8,128)(2,1)S(1)}, bf16[64,2048]{1,0:T(8,128)(2,1)S(1)}, bf16[64,2048]{1,0:T(8,128)(2,1)S(1)}, bf16[64,2048]{1,0:T(8,128)(2,1)S(1)}) custom-call(bf16[64,2048]{1,0:T(8,128)(2,1)S(1)} %collective-permute-done.24.refs_0_, bf16[64,2048]{1,0:T(8,128)(2,1)S(1)} %collective-permute-done.25.refs_1_, ...), custom_call_target="tpu_custom_call" | custom-call | flops 2415919104 | bytes 2097152 | tf_op jit(solution)/shard_map/pallas_call | solution.py:64
  83.4 0.5 collective-permute-start.37
  83.9 7.2 %shard_map.88 = (bf16[128,2048]{1,0:T(8,128)(2,1)S(1)}, bf16[128,2048]{1,0:T(8,128)(2,1)S(1)}, bf16[128,2048]{1,0:T(8,128)(2,1)S(1)}, bf16[128,2048]{1,0:T(8,128)(2,1)S(1)}) custom-call(bf16[128,2048]{1,0:T(8,128)(2,1)S(1)} %collective-permute-done.17.refs_0_, bf16[128,2048]{1,0:T(8,128)(2,1)S(1)} %collective-permute-done.18.refs_1_, ...), custom_call_target="tpu_custom_call" | custom-call | flops 4831838208 | bytes 4194304 | tf_op jit(solution)/shard_map/pallas_call | solution.py:64
  91.3 0.4 collective-permute-start.36
  91.8 0.8 collective-permute-start.30
  92.6 7.5 %collective-permute-done.30 = bf16[64,2048]{1,0:T(8,128)(2,1)S(1)} collective-permute-done((bf16[64,2048]{1,0:T(8,128)(2,1)S(1)}, bf16[64,2048]{1,0:T(8,128)(2,1)S(1)}, u32[]{:S(2)}, u32[]{:S(2)}) %collective-permute-start.30) | collective-permute-done | bytes 262176 | tf_op jit(solution)/shard_map/ppermute | solution.py:95
  100.1 0.8 collective-permute-start.38
  101.1 7.7 %collective-permute-done.38 = bf16[64,2048]{1,0:T(8,128)(2,1)S(1)} collective-permute-done((bf16[64,2048]{1,0:T(8,128)(2,1)S(1)}, bf16[64,2048]{1,0:T(8,128)(2,1)S(1)}, u32[]{:S(2)}, u32[]{:S(2)}) %collective-permute-start.38) | collective-permute-done | bytes 262176 | tf_op jit(solution)/shard_map/ppermute | solution.py:94
  108.8 0.7 collective-permute-start.31
  109.8 0.3 collective-permute-start.35
  110.1 1.3 collective-permute-start.39
  111.4 7.2 %shard_map.86 = (bf16[128,2048]{1,0:T(8,128)(2,1)S(1)}, bf16[128,2048]{1,0:T(8,128)(2,1)S(1)}, bf16[128,2048]{1,0:T(8,128)(2,1)S(1)}, bf16[128,2048]{1,0:T(8,128)(2,1)S(1)}) custom-call(bf16[128,2048]{1,0:T(8,128)(2,1)S(1)} %copy-done.6, bf16[128,2048]{1,0:T(8,128)(2,1)S(1)} %collective-permute-done.4.refs_1_, bf16[128,2048]{1,0:T(8,128)(2,1)S(1)} %copy-done.8, ...), custom_call_target="tpu_custom_call" | custom-call | flops 4831838208 | bytes 4194304 | tf_op jit(solution)/shard_map/pallas_call | solution.py:64
  118.6 4.5 %collective-permute-done.31 = bf16[128,2048]{1,0:T(8,128)(2,1)S(1)} collective-permute-done((bf16[128,2048]{1,0:T(8,128)(2,1)S(1)}, bf16[128,2048]{1,0:T(8,128)(2,1)S(1)}, u32[]{:S(2)}, u32[]{:S(2)}) %collective-permute-start.31) | collective-permute-done | bytes 524320 | tf_op jit(solution)/shard_map/ppermute | solution.py:95
  123.4 0.8 collective-permute-start.32
  124.2 0.2 add_convert_fusion.2
  124.5 1.4 collective-permute-start.40
  125.8 4.6 %shard_map.85 = (bf16[128,2048]{1,0:T(8,128)(2,1)S(1)}, bf16[128,2048]{1,0:T(8,128)(2,1)S(1)}) custom-call(bf16[128,2048]{1,0:T(8,128)(2,1)S(1)} %copy-done.4, bf16[128,2048]{1,0:T(8,128)(2,1)S(1)} %collective-permute-done.refs_1_, f32[256,1]{1,0:T(8,128)S(1)} %copy.20.refs_2_, bf16[2048,768]{1,0:T(8,128)(2,1)S(1)} %bitcast.39, ...), custom_call_target="tpu_custom_call" | custom-call | flops 2415919104 | bytes 2097152 | tf_op jit(solution)/shard_map/pallas_call | solution.py:64
  130.6 7.2 %collective-permute-done.32 = bf16[128,2048]{1,0:T(8,128)(2,1)S(1)} collective-permute-done((bf16[128,2048]{1,0:T(8,128)(2,1)S(1)}, bf16[128,2048]{1,0:T(8,128)(2,1)S(1)}, u32[]{:S(2)}, u32[]{:S(2)}) %collective-permute-start.32) | collective-permute-done | bytes 524320 | tf_op jit(solution)/shard_map/ppermute | solution.py:95
  138.1 0.8 collective-permute-start.33
  138.9 1.0 add_convert_fusion.1
  139.9 1.3 collective-permute-start.41
  141.3 0.6 dynamic_slice.36
  142.8 0.6 multiply_reduce_fusion
  144.7 7.0 %collective-permute-done.33 = bf16[128,2048]{1,0:T(8,128)(2,1)S(1)} collective-permute-done((bf16[128,2048]{1,0:T(8,128)(2,1)S(1)}, bf16[128,2048]{1,0:T(8,128)(2,1)S(1)}, u32[]{:S(2)}, u32[]{:S(2)}) %collective-permute-start.33) | collective-permute-done | bytes 524320 | tf_op jit(solution)/shard_map/ppermute | solution.py:95
  151.7 1.7 %collective-permute-done.41 = bf16[128,2048]{1,0:T(8,128)(2,1)S(1)} collective-permute-done((bf16[128,2048]{1,0:T(8,128)(2,1)}, bf16[128,2048]{1,0:T(8,128)(2,1)S(1)}, u32[]{:S(2)}, u32[]{:S(2)}) %collective-permute-start.41) | collective-permute-done | bytes 524320 | tf_op jit(solution)/shard_map/ppermute | solution.py:94
  153.4 1.1 add_convert_fusion
  (121 shorter events, 3.3 us)
Async XLA Ops:
  3.4 3.0 %collective-permute-start.1 = (f32[16,128]{1,0:T(8,128)S(1)}, f32[16,128]{1,0:T(8,128)S(1)}, u32[]{:S(2)}, u32[]{:S(2)}) collective-permute-start(f32[16,128]{1,0:T(8,128)S(1)} %get-tuple-element.40), channel_id=1, source_target_pairs={{0,1},{1,0},{2,3},{3,2},{4,5},{5,4},{6,7},{7,6},{8,9},{9,8},{10,11... | collective-permute-start | bytes 24584 | tf_op jit(solution)/shard_map/ppermute | solution.py:96
  3.9 26.8 %collective-permute-start.3 = (bf16[128,2048]{1,0:T(8,128)(2,1)}, bf16[128,2048]{1,0:T(8,128)(2,1)S(1)}, u32[]{:S(2)}, u32[]{:S(2)}) collective-permute-start(bf16[128,2048]{1,0:T(8,128)(2,1)} %refs_0_.1), channel_id=1, source_target_pairs={{0,4},{1,5},{4,8},{5,9},{8,12},{9,13},{12,14},{13,15},{14,10},{15,... | collective-permute-start | bytes 1572872 | tf_op jit(solution)/shard_map/ppermute | solution.py:94
  6.5 25.5 %collective-permute-start.5 = (bf16[128,2048]{1,0:T(8,128)(2,1)}, bf16[128,2048]{1,0:T(8,128)(2,1)S(1)}, u32[]{:S(2)}, u32[]{:S(2)}) collective-permute-start(bf16[128,2048]{1,0:T(8,128)(2,1)} %refs_0_.1), channel_id=1, source_target_pairs={{0,2},{1,3},{4,0},{5,1},{8,4},{9,5},{12,8},{13,9},{14,12},{15,13},... | collective-permute-start | bytes 1572872 | tf_op jit(solution)/shard_map/ppermute | solution.py:95
  6.5 49.0 %collective-permute-start.28 = (f32[2,16,128]{2,1,0:T(8,128)S(1)}, f32[2,16,128]{2,1,0:T(8,128)S(1)}, u32[]{:S(2)}, u32[]{:S(2)}) collective-permute-start(f32[2,16,128]{2,1,0:T(8,128)S(1)} %pad_maximum_fusion), channel_id=1, source_target_pairs={{0,14},{1,15},{4,10},{5,11},{8,6},{9,7},{12,2},{13,3},{14,0},{15,1... | collective-permute-start | bytes 49160 | tf_op jit(solution)/shard_map/ppermute | solution.py:111
  11.5 10.7 %collective-permute-start.21 = (f32[2,16,128]{2,1,0:T(8,128)S(1)}, f32[2,16,128]{2,1,0:T(8,128)S(1)}, u32[]{:S(2)}, u32[]{:S(2)}) collective-permute-start(f32[2,16,128]{2,1,0:T(8,128)S(1)} %pad_maximum_fusion), channel_id=1, source_target_pairs={{0,12},{1,13},{4,14},{5,15},{8,10},{9,11},{12,6},{13,7},{14,2},{15... | collective-permute-start | bytes 49160 | tf_op jit(solution)/shard_map/ppermute | solution.py:109
  11.7 13.4 %collective-permute-start.22 = (f32[2,16,128]{2,1,0:T(8,128)S(1)}, f32[2,16,128]{2,1,0:T(8,128)S(1)}, u32[]{:S(2)}, u32[]{:S(2)}) collective-permute-start(f32[2,16,128]{2,1,0:T(8,128)S(1)} %pad_maximum_fusion), channel_id=1, source_target_pairs={{0,10},{1,11},{4,6},{5,7},{8,2},{9,3},{12,0},{13,1},{14,4},{15,5},... | collective-permute-start | bytes 49160 | tf_op jit(solution)/shard_map/ppermute | solution.py:109
  22.2 11.6 %copy-start.9 = (f32[2,16,128]{2,1,0:T(8,128)}, f32[2,16,128]{2,1,0:T(8,128)S(1)}, u32[]{:S(2)}) copy-start(f32[2,16,128]{2,1,0:T(8,128)S(1)} %collective-permute-done.21) | copy-start | bytes 49156
  22.2 4.6 %collective-permute-start.15 = (f32[2,16,128]{2,1,0:T(8,128)S(1)}, f32[2,16,128]{2,1,0:T(8,128)S(1)}, u32[]{:S(2)}, u32[]{:S(2)}) collective-permute-start(f32[2,16,128]{2,1,0:T(8,128)S(1)} %pad_maximum_fusion), channel_id=1, source_target_pairs={{0,6},{1,7},{4,2},{5,3},{8,0},{9,1},{12,4},{13,5},{14,8},{15,9},{1... | collective-permute-start | bytes 49160 | tf_op jit(solution)/shard_map/ppermute | solution.py:109
  25.1 8.7 %copy-start.11 = (f32[2,16,128]{2,1,0:T(8,128)}, f32[2,16,128]{2,1,0:T(8,128)S(1)}, u32[]{:S(2)}) copy-start(f32[2,16,128]{2,1,0:T(8,128)S(1)} %collective-permute-done.22) | copy-start | bytes 49156
  25.1 4.7 %collective-permute-start.14 = (f32[2,16,128]{2,1,0:T(8,128)S(1)}, f32[2,16,128]{2,1,0:T(8,128)S(1)}, u32[]{:S(2)}, u32[]{:S(2)}) collective-permute-start(f32[2,16,128]{2,1,0:T(8,128)S(1)} %pad_maximum_fusion), channel_id=1, source_target_pairs={{0,8},{1,9},{4,12},{5,13},{8,14},{9,15},{12,10},{13,11},{14,6},{15... | collective-permute-start | bytes 49160 | tf_op jit(solution)/shard_map/ppermute | solution.py:109
  26.8 30.1 %copy-start.15 = (f32[2,16,128]{2,1,0:T(8,128)}, f32[2,16,128]{2,1,0:T(8,128)S(1)}, u32[]{:S(2)}) copy-start(f32[2,16,128]{2,1,0:T(8,128)S(1)} %collective-permute-done.15) | copy-start | bytes 49156
  26.8 3.9 %collective-permute-start.7 = (f32[2,16,128]{2,1,0:T(8,128)S(1)}, f32[2,16,128]{2,1,0:T(8,128)S(1)}, u32[]{:S(2)}, u32[]{:S(2)}) collective-permute-start(f32[2,16,128]{2,1,0:T(8,128)S(1)} %pad_maximum_fusion), channel_id=1, source_target_pairs={{0,4},{1,5},{4,8},{5,9},{8,12},{9,13},{12,14},{13,15},{14,10},{15,... | collective-permute-start | bytes 49160 | tf_op jit(solution)/shard_map/ppermute | solution.py:109
  29.8 27.1 %copy-start.13 = (f32[2,16,128]{2,1,0:T(8,128)}, f32[2,16,128]{2,1,0:T(8,128)S(1)}, u32[]{:S(2)}) copy-start(f32[2,16,128]{2,1,0:T(8,128)S(1)} %collective-permute-done.14) | copy-start | bytes 49156
  29.8 4.0 %collective-permute-start.8 = (f32[2,16,128]{2,1,0:T(8,128)S(1)}, f32[2,16,128]{2,1,0:T(8,128)S(1)}, u32[]{:S(2)}, u32[]{:S(2)}) collective-permute-start(f32[2,16,128]{2,1,0:T(8,128)S(1)} %pad_maximum_fusion), channel_id=1, source_target_pairs={{0,2},{1,3},{4,0},{5,1},{8,4},{9,5},{12,8},{13,9},{14,12},{15,13},... | collective-permute-start | bytes 49160 | tf_op jit(solution)/shard_map/ppermute | solution.py:109
  30.7 26.2 %copy-start.17 = (f32[2,16,128]{2,1,0:T(8,128)}, f32[2,16,128]{2,1,0:T(8,128)S(1)}, u32[]{:S(2)}) copy-start(f32[2,16,128]{2,1,0:T(8,128)S(1)} %collective-permute-done.7) | copy-start | bytes 49156
  30.7 26.2 %copy-start.5 = (bf16[128,2048]{1,0:T(8,128)(2,1)}, bf16[128,2048]{1,0:T(8,128)(2,1)S(1)}, u32[]{:S(2)}) copy-start(bf16[128,2048]{1,0:T(8,128)(2,1)S(1)} %collective-permute-done.3.refs_0_) | copy-start | bytes 1572868
  30.7 11.9 %collective-permute-start.10 = (bf16[128,2048]{1,0:T(8,128)(2,1)S(1)}, bf16[128,2048]{1,0:T(8,128)(2,1)}, u32[]{:S(2)}, u32[]{:S(2)}) collective-permute-start(bf16[128,2048]{1,0:T(8,128)(2,1)S(1)} %collective-permute-done.3.refs_0_), channel_id=1, source_target_pairs={{0,4},{1,5},{4,8},{5,9},{8,12},{9,13},{12,14},{13,15},{14,10},{15,... | collective-permute-start | bytes 1572872 | tf_op jit(solution)/shard_map/ppermute | solution.py:94
  31.9 14.0 %copy-start.7 = (bf16[128,2048]{1,0:T(8,128)(2,1)}, bf16[128,2048]{1,0:T(8,128)(2,1)S(1)}, u32[]{:S(2)}) copy-start(bf16[128,2048]{1,0:T(8,128)(2,1)S(1)} %collective-permute-done.5.refs_2_) | copy-start | bytes 1572868
  31.9 11.9 %collective-permute-start.12 = (bf16[128,2048]{1,0:T(8,128)(2,1)S(1)}, bf16[128,2048]{1,0:T(8,128)(2,1)}, u32[]{:S(2)}, u32[]{:S(2)}) collective-permute-start(bf16[128,2048]{1,0:T(8,128)(2,1)S(1)} %collective-permute-done.5.refs_2_), channel_id=1, source_target_pairs={{0,2},{1,3},{4,0},{5,1},{8,4},{9,5},{12,8},{13,9},{14,12},{15,13},... | collective-permute-start | bytes 1572872 | tf_op jit(solution)/shard_map/ppermute | solution.py:95
  33.8 23.1 %copy-start.19 = (f32[2,16,128]{2,1,0:T(8,128)}, f32[2,16,128]{2,1,0:T(8,128)S(1)}, u32[]{:S(2)}) copy-start(f32[2,16,128]{2,1,0:T(8,128)S(1)} %collective-permute-done.8) | copy-start | bytes 49156
  42.7 10.3 %collective-permute-start.17 = (bf16[128,2048]{1,0:T(8,128)(2,1)}, bf16[128,2048]{1,0:T(8,128)(2,1)S(1)}, u32[]{:S(2)}, u32[]{:S(2)}) collective-permute-start(bf16[128,2048]{1,0:T(8,128)(2,1)} %collective-permute-done.10.refs_0_), channel_id=1, source_target_pairs={{0,4},{1,5},{4,8},{5,9},{8,12},{9,13},{12,14},{13,15},{14,10},{15,... | collective-permute-start | bytes 1572872 | tf_op jit(solution)/shard_map/ppermute | solution.py:94
  43.8 10.3 %collective-permute-start.19 = (bf16[128,2048]{1,0:T(8,128)(2,1)}, bf16[128,2048]{1,0:T(8,128)(2,1)S(1)}, u32[]{:S(2)}, u32[]{:S(2)}) collective-permute-start(bf16[128,2048]{1,0:T(8,128)(2,1)} %collective-permute-done.12.refs_2_), channel_id=1, source_target_pairs={{0,2},{1,3},{4,0},{5,1},{8,4},{9,5},{12,8},{13,9},{14,12},{15,13},... | collective-permute-start | bytes 1572872 | tf_op jit(solution)/shard_map/ppermute | solution.py:95
  44.7 14.9 %collective-permute-start.11 = (bf16[128,2048]{1,0:T(8,128)(2,1)}, bf16[128,2048]{1,0:T(8,128)(2,1)}, u32[]{:S(2)}, u32[]{:S(2)}) collective-permute-start(bf16[128,2048]{1,0:T(8,128)(2,1)} %collective-permute-done.10.refs_0_), channel_id=1, source_target_pairs={{0,1},{1,0},{2,3},{3,2},{4,5},{5,4},{6,7},{7,6},{8,9},{9,8},{10,11... | collective-permute-start | bytes 1572872 | tf_op jit(solution)/shard_map/ppermute | solution.py:96
  44.8 14.8 %collective-permute-start.13 = (bf16[128,2048]{1,0:T(8,128)(2,1)}, bf16[128,2048]{1,0:T(8,128)(2,1)}, u32[]{:S(2)}, u32[]{:S(2)}) collective-permute-start(bf16[128,2048]{1,0:T(8,128)(2,1)} %collective-permute-done.12.refs_2_), channel_id=1, source_target_pairs={{0,1},{1,0},{2,3},{3,2},{4,5},{5,4},{6,7},{7,6},{8,9},{9,8},{10,11... | collective-permute-start | bytes 1572872 | tf_op jit(solution)/shard_map/ppermute | solution.py:96
  52.9 72.9 %collective-permute-start = (bf16[128,2048]{1,0:T(8,128)(2,1)}, bf16[128,2048]{1,0:T(8,128)(2,1)S(1)}, u32[]{:S(2)}, u32[]{:S(2)}) collective-permute-start(bf16[128,2048]{1,0:T(8,128)(2,1)} %refs_0_.1), channel_id=1, source_target_pairs={{0,1},{1,0},{2,3},{3,2},{4,5},{5,4},{6,7},{7,6},{8,9},{9,8},{10,11... | collective-permute-start | bytes 1572872 | tf_op jit(solution)/shard_map/ppermute | solution.py:96
  54.1 7.6 %collective-permute-start.24 = (bf16[64,2048]{1,0:T(8,128)(2,1)S(1)}, bf16[64,2048]{1,0:T(8,128)(2,1)S(1)}, u32[]{:S(2)}, u32[]{:S(2)}) collective-permute-start(bf16[64,2048]{1,0:T(8,128)(2,1)S(1)} %slice.8), channel_id=1, source_target_pairs={{0,4},{1,5},{4,8},{5,9},{8,12},{9,13},{12,14},{13,15},{14,10},{15,... | collective-permute-start | bytes 786440 | tf_op jit(solution)/shard_map/ppermute | solution.py:94
  55.4 8.3 %collective-permute-start.25 = (bf16[64,2048]{1,0:T(8,128)(2,1)}, bf16[64,2048]{1,0:T(8,128)(2,1)S(1)}, u32[]{:S(2)}, u32[]{:S(2)}) collective-permute-start(bf16[64,2048]{1,0:T(8,128)(2,1)} %slice.9), channel_id=1, source_target_pairs={{0,2},{1,3},{4,0},{5,1},{8,4},{9,5},{12,8},{13,9},{14,12},{15,13},... | collective-permute-start | bytes 786440 | tf_op jit(solution)/shard_map/ppermute | solution.py:95
  59.6 23.8 %collective-permute-start.18 = (bf16[128,2048]{1,0:T(8,128)(2,1)S(1)}, bf16[128,2048]{1,0:T(8,128)(2,1)S(1)}, u32[]{:S(2)}, u32[]{:S(2)}) collective-permute-start(bf16[128,2048]{1,0:T(8,128)(2,1)S(1)} %collective-permute-done.17.refs_0_), channel_id=1, source_target_pairs={{0,1},{1,0},{2,3},{3,2},{4,5},{5,4},{6,7},{7,6},{8,9},{9,8},{10,11... | collective-permute-start | bytes 1572872 | tf_op jit(solution)/shard_map/ppermute | solution.py:96
  59.6 24.3 %collective-permute-start.20 = (bf16[128,2048]{1,0:T(8,128)(2,1)S(1)}, bf16[128,2048]{1,0:T(8,128)(2,1)S(1)}, u32[]{:S(2)}, u32[]{:S(2)}) collective-permute-start(bf16[128,2048]{1,0:T(8,128)(2,1)S(1)} %collective-permute-done.19.refs_2_), channel_id=1, source_target_pairs={{0,1},{1,0},{2,3},{3,2},{4,5},{5,4},{6,7},{7,6},{8,9},{9,8},{10,11... | collective-permute-start | bytes 1572872 | tf_op jit(solution)/shard_map/ppermute | solution.py:96
  61.7 16.4 %collective-permute-start.26 = (bf16[64,2048]{1,0:T(8,128)(2,1)S(1)}, bf16[64,2048]{1,0:T(8,128)(2,1)S(1)}, u32[]{:S(2)}, u32[]{:S(2)}) collective-permute-start(bf16[64,2048]{1,0:T(8,128)(2,1)S(1)} %collective-permute-done.24.refs_0_), channel_id=1, source_target_pairs={{0,1},{1,0},{2,3},{3,2},{4,5},{5,4},{6,7},{7,6},{8,9},{9,8},{10,11... | collective-permute-start | bytes 786440 | tf_op jit(solution)/shard_map/ppermute | solution.py:96
  63.7 15.0 %collective-permute-start.27 = (bf16[64,2048]{1,0:T(8,128)(2,1)S(1)}, bf16[64,2048]{1,0:T(8,128)(2,1)S(1)}, u32[]{:S(2)}, u32[]{:S(2)}) collective-permute-start(bf16[64,2048]{1,0:T(8,128)(2,1)S(1)} %collective-permute-done.25.refs_1_), channel_id=1, source_target_pairs={{0,1},{1,0},{2,3},{3,2},{4,5},{5,4},{6,7},{7,6},{8,9},{9,8},{10,11... | collective-permute-start | bytes 786440 | tf_op jit(solution)/shard_map/ppermute | solution.py:96
  63.7 1.9 %copy-start = (bf16[1,2048,768]{2,1,0:T(8,128)(2,1)S(1)}, bf16[1,2048,768]{2,1,0:T(8,128)(2,1)}, u32[]{:S(2)}) copy-start(bf16[1,2048,768]{2,1,0:T(8,128)(2,1)} %param.9) | copy-start | bytes 9437188
  65.6 1.9 %copy-start.2 = (bf16[1,2048,768]{2,1,0:T(8,128)(2,1)S(1)}, bf16[1,2048,768]{2,1,0:T(8,128)(2,1)}, u32[]{:S(2)}) copy-start(bf16[1,2048,768]{2,1,0:T(8,128)(2,1)} %param.10) | copy-start | bytes 9437188
  69.4 8.8 %copy-start.6 = (bf16[128,2048]{1,0:T(8,128)(2,1)S(1)}, bf16[128,2048]{1,0:T(8,128)(2,1)}, u32[]{:S(2)}) copy-start(bf16[128,2048]{1,0:T(8,128)(2,1)} %copy-done.5) | copy-start | bytes 1572868
  78.1 5.8 %copy-start.1 = (bf16[1,2048,768]{2,1,0:T(8,128)(2,1)S(1)}, bf16[1,2048,768]{2,1,0:T(8,128)(2,1)}, u32[]{:S(2)}) copy-start(bf16[1,2048,768]{2,1,0:T(8,128)(2,1)} %param.9) | copy-start | bytes 9437188
  78.2 31.6 %collective-permute-start.4 = (bf16[128,2048]{1,0:T(8,128)(2,1)S(1)}, bf16[128,2048]{1,0:T(8,128)(2,1)S(1)}, u32[]{:S(2)}, u32[]{:S(2)}) collective-permute-start(bf16[128,2048]{1,0:T(8,128)(2,1)S(1)} %copy-done.6), channel_id=1, source_target_pairs={{0,1},{1,0},{2,3},{3,2},{4,5},{5,4},{6,7},{7,6},{8,9},{9,8},{10,11... | collective-permute-start | bytes 1572872 | tf_op jit(solution)/shard_map/ppermute | solution.py:96
  83.3 7.9 %collective-permute-start.29 = (bf16[64,2048]{1,0:T(8,128)(2,1)S(1)}, bf16[64,2048]{1,0:T(8,128)(2,1)S(1)}, u32[]{:S(2)}, u32[]{:S(2)}) collective-permute-start(bf16[64,2048]{1,0:T(8,128)(2,1)S(1)} %get-tuple-element.30), channel_id=1, source_target_pairs={{0,1},{1,0},{2,3},{3,2},{4,5},{5,4},{6,7},{7,6},{8,9},{9,8},{10,11... | collective-permute-start | bytes 786440 | tf_op jit(solution)/shard_map/ppermute | solution.py:96
  83.4 16.7 %copy-start.8 = (bf16[128,2048]{1,0:T(8,128)(2,1)S(1)}, bf16[128,2048]{1,0:T(8,128)(2,1)}, u32[]{:S(2)}) copy-start(bf16[128,2048]{1,0:T(8,128)(2,1)} %copy-done.7) | copy-start | bytes 1572868
  83.4 8.3 %collective-permute-start.37 = (bf16[64,2048]{1,0:T(8,128)(2,1)S(1)}, bf16[64,2048]{1,0:T(8,128)(2,1)S(1)}, u32[]{:S(2)}, u32[]{:S(2)}) collective-permute-start(bf16[64,2048]{1,0:T(8,128)(2,1)S(1)} %get-tuple-element.38), channel_id=1, source_target_pairs={{0,1},{1,0},{2,3},{3,2},{4,5},{5,4},{6,7},{7,6},{8,9},{9,8},{10,11... | collective-permute-start | bytes 786440 | tf_op jit(solution)/shard_map/ppermute | solution.py:96
  91.1 9.0 %collective-permute-start.23 = (bf16[128,2048]{1,0:T(8,128)(2,1)S(1)}, bf16[128,2048]{1,0:T(8,128)(2,1)S(1)}, u32[]{:S(2)}, u32[]{:S(2)}) collective-permute-start(bf16[128,2048]{1,0:T(8,128)(2,1)S(1)} %get-tuple-element.28), channel_id=1, source_target_pairs={{0,1},{1,0},{2,3},{3,2},{4,5},{5,4},{6,7},{7,6},{8,9},{9,8},{10,11... | collective-permute-start | bytes 1572872 | tf_op jit(solution)/shard_map/ppermute | solution.py:96
  91.3 17.6 %collective-permute-start.36 = (bf16[128,2048]{1,0:T(8,128)(2,1)S(1)}, bf16[128,2048]{1,0:T(8,128)(2,1)S(1)}, u32[]{:S(2)}, u32[]{:S(2)}) collective-permute-start(bf16[128,2048]{1,0:T(8,128)(2,1)S(1)} %get-tuple-element.36), channel_id=1, source_target_pairs={{0,1},{1,0},{2,3},{3,2},{4,5},{5,4},{6,7},{7,6},{8,9},{9,8},{10,11... | collective-permute-start | bytes 1572872 | tf_op jit(solution)/shard_map/ppermute | solution.py:96
  91.8 8.4 %collective-permute-start.30 = (bf16[64,2048]{1,0:T(8,128)(2,1)S(1)}, bf16[64,2048]{1,0:T(8,128)(2,1)S(1)}, u32[]{:S(2)}, u32[]{:S(2)}) collective-permute-start(bf16[64,2048]{1,0:T(8,128)(2,1)S(1)} %add_convert_fusion.8), channel_id=1, source_target_pairs={{0,2},{1,3},{4,0},{5,1},{8,4},{9,5},{12,8},{13,9},{14,12},{15,13},... | collective-permute-start | bytes 786440 | tf_op jit(solution)/shard_map/ppermute | solution.py:95
  100.1 9.9 %collective-permute-start.6 = (bf16[128,2048]{1,0:T(8,128)(2,1)S(1)}, bf16[128,2048]{1,0:T(8,128)(2,1)S(1)}, u32[]{:S(2)}, u32[]{:S(2)}) collective-permute-start(bf16[128,2048]{1,0:T(8,128)(2,1)S(1)} %copy-done.8), channel_id=1, source_target_pairs={{0,1},{1,0},{2,3},{3,2},{4,5},{5,4},{6,7},{7,6},{8,9},{9,8},{10,11... | collective-permute-start | bytes 1572872 | tf_op jit(solution)/shard_map/ppermute | solution.py:96
  100.1 8.7 %collective-permute-start.38 = (bf16[64,2048]{1,0:T(8,128)(2,1)S(1)}, bf16[64,2048]{1,0:T(8,128)(2,1)S(1)}, u32[]{:S(2)}, u32[]{:S(2)}) collective-permute-start(bf16[64,2048]{1,0:T(8,128)(2,1)S(1)} %add_convert_fusion.7), channel_id=1, source_target_pairs={{0,4},{1,5},{4,8},{5,9},{8,12},{9,13},{12,14},{13,15},{14,10},{15,... | collective-permute-start | bytes 786440 | tf_op jit(solution)/shard_map/ppermute | solution.py:94
  108.8 9.7 %collective-permute-start.16 = (bf16[128,2048]{1,0:T(8,128)(2,1)S(1)}, bf16[128,2048]{1,0:T(8,128)(2,1)S(1)}, u32[]{:S(2)}, u32[]{:S(2)}) collective-permute-start(bf16[128,2048]{1,0:T(8,128)(2,1)S(1)} %get-tuple-element.26), channel_id=1, source_target_pairs={{0,1},{1,0},{2,3},{3,2},{4,5},{5,4},{6,7},{7,6},{8,9},{9,8},{10,11... | collective-permute-start | bytes 1572872 | tf_op jit(solution)/shard_map/ppermute | solution.py:96
  108.8 14.3 %collective-permute-start.31 = (bf16[128,2048]{1,0:T(8,128)(2,1)S(1)}, bf16[128,2048]{1,0:T(8,128)(2,1)S(1)}, u32[]{:S(2)}, u32[]{:S(2)}) collective-permute-start(bf16[128,2048]{1,0:T(8,128)(2,1)S(1)} %add_convert_fusion.6), channel_id=1, source_target_pairs={{0,2},{1,3},{4,0},{5,1},{8,4},{9,5},{12,8},{13,9},{14,12},{15,13},... | collective-permute-start | bytes 1572872 | tf_op jit(solution)/shard_map/ppermute | solution.py:95
  109.8 13.7 %collective-permute-start.35 = (bf16[128,2048]{1,0:T(8,128)(2,1)S(1)}, bf16[128,2048]{1,0:T(8,128)(2,1)S(1)}, u32[]{:S(2)}, u32[]{:S(2)}) collective-permute-start(bf16[128,2048]{1,0:T(8,128)(2,1)S(1)} %get-tuple-element.34), channel_id=1, source_target_pairs={{0,1},{1,0},{2,3},{3,2},{4,5},{5,4},{6,7},{7,6},{8,9},{9,8},{10,11... | collective-permute-start | bytes 1572872 | tf_op jit(solution)/shard_map/ppermute | solution.py:96
  110.1 14.2 %collective-permute-start.39 = (bf16[128,2048]{1,0:T(8,128)(2,1)S(1)}, bf16[128,2048]{1,0:T(8,128)(2,1)S(1)}, u32[]{:S(2)}, u32[]{:S(2)}) collective-permute-start(bf16[128,2048]{1,0:T(8,128)(2,1)S(1)} %add_convert_fusion.3), channel_id=1, source_target_pairs={{0,4},{1,5},{4,8},{5,9},{8,12},{9,13},{12,14},{13,15},{14,10},{15,... | collective-permute-start | bytes 1572872 | tf_op jit(solution)/shard_map/ppermute | solution.py:94
  118.5 7.3 %copy-start.4 = (bf16[128,2048]{1,0:T(8,128)(2,1)S(1)}, bf16[128,2048]{1,0:T(8,128)(2,1)}, u32[]{:S(2)}) copy-start(bf16[128,2048]{1,0:T(8,128)(2,1)} %refs_0_.1) | copy-start | bytes 1572868
  118.6 12.0 %collective-permute-start.9 = (bf16[128,2048]{1,0:T(8,128)(2,1)S(1)}, bf16[128,2048]{1,0:T(8,128)(2,1)S(1)}, u32[]{:S(2)}, u32[]{:S(2)}) collective-permute-start(bf16[128,2048]{1,0:T(8,128)(2,1)S(1)} %get-tuple-element.24), channel_id=1, source_target_pairs={{0,1},{1,0},{2,3},{3,2},{4,5},{5,4},{6,7},{7,6},{8,9},{9,8},{10,11... | collective-permute-start | bytes 1572872 | tf_op jit(solution)/shard_map/ppermute | solution.py:96
  123.2 15.7 %collective-permute-start.34 = (bf16[128,2048]{1,0:T(8,128)(2,1)S(1)}, bf16[128,2048]{1,0:T(8,128)(2,1)S(1)}, u32[]{:S(2)}, u32[]{:S(2)}) collective-permute-start(bf16[128,2048]{1,0:T(8,128)(2,1)S(1)} %get-tuple-element.32), channel_id=1, source_target_pairs={{0,1},{1,0},{2,3},{3,2},{4,5},{5,4},{6,7},{7,6},{8,9},{9,8},{10,11... | collective-permute-start | bytes 1572872 | tf_op jit(solution)/shard_map/ppermute | solution.py:96
  123.4 14.4 %collective-permute-start.32 = (bf16[128,2048]{1,0:T(8,128)(2,1)S(1)}, bf16[128,2048]{1,0:T(8,128)(2,1)S(1)}, u32[]{:S(2)}, u32[]{:S(2)}) collective-permute-start(bf16[128,2048]{1,0:T(8,128)(2,1)S(1)} %add_convert_fusion.5), channel_id=1, source_target_pairs={{0,2},{1,3},{4,0},{5,1},{8,4},{9,5},{12,8},{13,9},{14,12},{15,13},... | collective-permute-start | bytes 1572872 | tf_op jit(solution)/shard_map/ppermute | solution.py:95
  124.5 14.4 %collective-permute-start.40 = (bf16[128,2048]{1,0:T(8,128)(2,1)S(1)}, bf16[128,2048]{1,0:T(8,128)(2,1)S(1)}, u32[]{:S(2)}, u32[]{:S(2)}) collective-permute-start(bf16[128,2048]{1,0:T(8,128)(2,1)S(1)} %add_convert_fusion.2), channel_id=1, source_target_pairs={{0,4},{1,5},{4,8},{5,9},{8,12},{9,13},{12,14},{13,15},{14,10},{15,... | collective-permute-start | bytes 1572872 | tf_op jit(solution)/shard_map/ppermute | solution.py:94
  130.4 10.8 %copy-start.12 = (f32[2,16,128]{2,1,0:T(8,128)S(1)}, f32[2,16,128]{2,1,0:T(8,128)}, u32[]{:S(2)}) copy-start(f32[2,16,128]{2,1,0:T(8,128)} %copy-done.11) | copy-start | bytes 49156
  130.4 11.5 %copy-start.16 = (f32[2,16,128]{2,1,0:T(8,128)S(1)}, f32[2,16,128]{2,1,0:T(8,128)}, u32[]{:S(2)}) copy-start(f32[2,16,128]{2,1,0:T(8,128)} %copy-done.15) | copy-start | bytes 49156
  130.4 11.6 %copy-start.10 = (f32[2,16,128]{2,1,0:T(8,128)S(1)}, f32[2,16,128]{2,1,0:T(8,128)}, u32[]{:S(2)}) copy-start(f32[2,16,128]{2,1,0:T(8,128)} %copy-done.9) | copy-start | bytes 49156
  130.4 11.9 %copy-start.18 = (f32[2,16,128]{2,1,0:T(8,128)S(1)}, f32[2,16,128]{2,1,0:T(8,128)}, u32[]{:S(2)}) copy-start(f32[2,16,128]{2,1,0:T(8,128)} %copy-done.17) | copy-start | bytes 49156
  130.5 12.1 %copy-start.20 = (f32[2,16,128]{2,1,0:T(8,128)S(1)}, f32[2,16,128]{2,1,0:T(8,128)}, u32[]{:S(2)}) copy-start(f32[2,16,128]{2,1,0:T(8,128)} %copy-done.19) | copy-start | bytes 49156
  130.5 12.2 %copy-start.14 = (f32[2,16,128]{2,1,0:T(8,128)S(1)}, f32[2,16,128]{2,1,0:T(8,128)}, u32[]{:S(2)}) copy-start(f32[2,16,128]{2,1,0:T(8,128)} %copy-done.13) | copy-start | bytes 49156
  130.5 12.3 %copy-start.21 = (f32[16]{0:T(128)S(1)}, f32[16]{0:T(128)}, u32[]{:S(2)}) copy-start(f32[16]{0:T(128)} %get-tuple-element.39) | copy-start | bytes 196
  130.5 12.3 %copy-start.22 = (f32[16]{0:T(128)S(1)}, f32[16]{0:T(128)}, u32[]{:S(2)}) copy-start(f32[16]{0:T(128)} %reduce_sum.86) | copy-start | bytes 196
  130.5 14.2 %collective-permute-start.2 = (bf16[128,2048]{1,0:T(8,128)(2,1)S(1)}, bf16[128,2048]{1,0:T(8,128)(2,1)S(1)}, u32[]{:S(2)}, u32[]{:S(2)}) collective-permute-start(bf16[128,2048]{1,0:T(8,128)(2,1)S(1)} %get-tuple-element.22), channel_id=1, source_target_pairs={{0,1},{1,0},{2,3},{3,2},{4,5},{5,4},{6,7},{7,6},{8,9},{9,8},{10,11... | collective-permute-start | bytes 1572872 | tf_op jit(solution)/shard_map/ppermute | solution.py:96
  138.1 13.6 %collective-permute-start.33 = (bf16[128,2048]{1,0:T(8,128)(2,1)S(1)}, bf16[128,2048]{1,0:T(8,128)(2,1)S(1)}, u32[]{:S(2)}, u32[]{:S(2)}) collective-permute-start(bf16[128,2048]{1,0:T(8,128)(2,1)S(1)} %add_convert_fusion.4), channel_id=1, source_target_pairs={{0,2},{1,3},{4,0},{5,1},{8,4},{9,5},{12,8},{13,9},{14,12},{15,13},... | collective-permute-start | bytes 1572872 | tf_op jit(solution)/shard_map/ppermute | solution.py:95
  139.9 13.5 %collective-permute-start.41 = (bf16[128,2048]{1,0:T(8,128)(2,1)}, bf16[128,2048]{1,0:T(8,128)(2,1)S(1)}, u32[]{:S(2)}, u32[]{:S(2)}) collective-permute-start(bf16[128,2048]{1,0:T(8,128)(2,1)} %add_convert_fusion.1), channel_id=1, source_target_pairs={{0,4},{1,5},{4,8},{5,9},{8,12},{9,13},{12,14},{13,15},{14,10},{15,... | collective-permute-start | bytes 1572872 | tf_op jit(solution)/shard_map/ppermute | solution.py:94
  (1 other events, 1.9 us)

commit v3 on v2

v3 whole, which is shorter than its diff:
```python
import functools

import jax
import jax.numpy as jnp
from jax import lax
from jax.experimental import pallas as pl
from jax.experimental.pallas import tpu as pltpu
from jax.sharding import PartitionSpec as P

CORES = 2
CHUNKS = 1
LAG = 2
LANES = 128
VMEM_LIMIT = 24 * 1024 * 1024
HIDDEN_CHUNK = 256
OUT_CHUNK = 512


def ring_order(chips):
    if chips <= 8:
        return list(range(0, chips, 2)) + list(range(1, chips, 2))[::-1]
    return list(range(chips))


def ring_shift(order, step):
    pairs = []
    for place, chip in enumerate(order):
        target = order[(place + step) % len(order)]
        pairs += [(CORES * chip + core, CORES * target + core) for core in range(CORES)]
    return pairs


def pack_kernel(experts, tokens_ref, ids_ref, gates_ref, *outs):
    rows, width = tokens_ref.shape
    lanes = outs[0].shape[1] - width
    lane = lax.broadcasted_iota(jnp.int32, (rows, lanes), 1)
    ids, gates = ids_ref[...], gates_ref[...]
    scores = jnp.zeros((rows, lanes), jnp.int32)
    for k in range(ids.shape[1]):
        at, gate = ids[:, k : k + 1], gates[:, k : k + 1]
        scores = jnp.where(lane == at, gate >> 8, scores)
        scores = jnp.where(lane == at + experts, gate & 255, scores)
    scores = scores.astype(jnp.float32).astype(jnp.bfloat16)
    size = outs[0].shape[0]
    for i, out in enumerate(outs):
        out[:, :width] = tokens_ref[i * size : (i + 1) * size, :]
        out[:, width:] = scores[i * size : (i + 1) * size]


def pack(tokens, expert_ids, gate_fixed, experts, chunks):
    rows, width = tokens.shape
    lanes = -(-2 * experts // LANES) * LANES
    in_vmem = pl.BlockSpec(memory_space=pltpu.VMEM)
    return pl.pallas_call(
        functools.partial(pack_kernel, experts),
        out_shape=[jax.ShapeDtypeStruct((rows // chunks, width + lanes), jnp.bfloat16)] * chunks,
        in_specs=[in_vmem] * 3,
        out_specs=[in_vmem] * chunks,
        compiler_params=pltpu.CompilerParams(vmem_limit_bytes=VMEM_LIMIT),
        cost_estimate=pl.CostEstimate(
            flops=rows * lanes, bytes_accessed=4 * rows * width, transcendentals=0
        ),
    )(tokens, expert_ids, gate_fixed)


def expert_kernel(sizes, *refs):
    count = len(sizes)
    blocks = refs[:count]
    own_ref, join_ref, gate_ref, up_ref, down_ref = refs[count : count + 5]
    outs = refs[count + 5 : 2 * count + 5]
    stats_ref, hidden_ref = refs[2 * count + 5 :]
    starts = [sum(sizes[:i]) for i in range(count)]
    width, hidden_width = gate_ref.shape
    lanes = join_ref.shape[0]

    scores = jnp.concatenate([block[:, width:] for block in blocks], axis=0)
    joined = jnp.dot(scores, join_ref[...], preferred_element_type=jnp.float32)
    weights = joined[:, :lanes] / joined[:, lanes:]
    stats_ref[0:1, :] = jnp.sum((weights > 0).astype(jnp.float32), axis=0, keepdims=True)
    stats_ref[1:2, :] = jnp.sum(weights, axis=0, keepdims=True)
    scale = jnp.sum(weights * own_ref[...], axis=1, keepdims=True)

    rows = jnp.concatenate([block[:, :width] for block in blocks], axis=0)
    for start in range(0, hidden_width, HIDDEN_CHUNK):
        at = slice(start, start + HIDDEN_CHUNK)
        gate = jnp.dot(rows, gate_ref[:, at], preferred_element_type=jnp.float32)
        up = jnp.dot(rows, up_ref[:, at], preferred_element_type=jnp.float32)
        hidden_ref[:, at] = (gate / (1.0 + jnp.exp(-gate)) * up).astype(jnp.bfloat16)
    for start in range(0, width, OUT_CHUNK):
        at = slice(start, start + OUT_CHUNK)
        out = jnp.dot(hidden_ref[...], down_ref[:, at], preferred_element_type=jnp.float32)
        out = out.astype(jnp.bfloat16).astype(jnp.float32) * scale
        for i in range(count):
            outs[i][:, at] = out[starts[i] : starts[i] + sizes[i]].astype(jnp.bfloat16)


def apply_expert(blocks, own, join, gate_weight, up_weight, down_weight):
    width, hidden_width = gate_weight.shape
    sizes = tuple(block.shape[0] for block in blocks)
    total = sum(sizes)
    count = len(blocks)
    in_vmem = pl.BlockSpec(memory_space=pltpu.VMEM)
    return pl.pallas_call(
        functools.partial(expert_kernel, sizes),
        out_shape=[jax.ShapeDtypeStruct((size, width), jnp.bfloat16) for size in sizes]
        + [jax.ShapeDtypeStruct((2, own.shape[1]), jnp.float32)],
        in_specs=[in_vmem] * (count + 5),
        out_specs=[in_vmem] * (count + 1),
        scratch_shapes=[pltpu.VMEM((total, hidden_width), jnp.bfloat16)],
        compiler_params=pltpu.CompilerParams(vmem_limit_bytes=VMEM_LIMIT),
        cost_estimate=pl.CostEstimate(
            flops=6 * total * width * hidden_width,
            bytes_accessed=4 * total * width,
            transcendentals=total * hidden_width,
        ),
    )(*blocks, own, join, gate_weight, up_weight, down_weight)


def body(tokens, expert_ids, gate_fixed, gate_weight, up_weight, down_weight):
    tok_rows, model_width = tokens.shape
    per_token = expert_ids.shape[1]
    node_count = lax.axis_size("node")
    expert_count = node_count
    token_total = tok_rows * node_count
    chips = node_count // CORES
    far = chips // 2
    chunks = CHUNKS if chips <= 8 else 1
    half = tok_rows // chunks // 2
    order = ring_order(chips)
    to_right, to_left = ring_shift(order, 1), ring_shift(order, -1)
    to_sibling = [(node, node ^ 1) for node in range(node_count)]
    right = lambda a: lax.ppermute(a, "node", to_right)
    left = lambda a: lax.ppermute(a, "node", to_left)
    sibling = lambda a: lax.ppermute(a, "node", to_sibling)
    tie = lax.optimization_barrier
    node = lax.axis_index("node")

    packed = pack(tokens, expert_ids, gate_fixed, expert_count, chunks)
    lanes = packed[0].shape[1] - model_width
    own = (jnp.arange(lanes) == node).astype(jnp.float32)[None]
    source, target = jnp.arange(lanes)[:, None], jnp.arange(2 * lanes)[None]
    is_low = source >= expert_count
    to_expert = (target == jnp.where(is_low, source - expert_count, source)) | (target >= lanes)
    join = jnp.where(
        to_expert & (source < 2 * expert_count), jnp.where(is_low, 1.0, 256.0), 0.0
    ).astype(jnp.bfloat16)
    gate_weight, up_weight, down_weight = gate_weight[0], up_weight[0], down_weight[0]
    stats = []

    def run(blocks):
        res = apply_expert(blocks, own, join, gate_weight, up_weight, down_weight)
        stats.append(res[-1])
        return res[:-1]

    def add(*terms):
        return sum(term.astype(jnp.float32) for term in terms).astype(jnp.bfloat16)

    def give_back(outs):
        return [sibling(out) if i % 2 else out for i, out in enumerate(outs)]

    def steps(block):
        low, high = right(block), left(block)
        res = run([block, sibling(block)])
        outs = []
        for k in range(1, far):
            low, high, res = yield low, high, res
            outs.append(give_back(res))
            here = low, high
            if k < far - 1:
                low, high = right(low), left(high)
            else:
                low, high = right(low[:half]), left(high[half:])
            res = run([here[0], sibling(here[0]), here[1], sibling(here[1])])
        low, high, res = yield low, high, res
        outs.append(give_back(res))
        res = run([low, sibling(low), high, sibling(high)])
        low, low_sib, high, high_sib = give_back(res)
        low, high = add(low, low_sib), add(high, high_sib)
        for k in range(far - 1, 0, -1):
            low, high, outs = yield low, high, outs
            low, high = left(low), right(high)
            if k == far - 1:
                zeros = jnp.zeros_like(low)
                low = jnp.concatenate([low, zeros])
                high = jnp.concatenate([zeros, high])
            left_own, left_sib, right_own, right_sib = outs[k]
            low, high = add(left_own, left_sib, low), add(right_own, right_sib, high)
        low, high, outs = yield low, high, outs
        mixed.append(add(*outs[0], left(low), right(high)))

    mixed = []
    lines = [steps(block) for block in packed]
    state = [None] * chunks
    count = 2 * far + 1
    last = []
    for slot in range(count + LAG * (chunks - 1)):
        for i, line in enumerate(lines):
            step = slot - LAG * i
            if 0 <= step < count:
                try:
                    state[i] = tie(line.send(state[i]))
                except StopIteration:
                    pass

    counts, mass = sum(stats)[:, :expert_count]
    mass = mass / token_total
    own_count = lax.dynamic_slice(counts, (node,), (1,))
    expert_load = own_count * expert_count / (token_total * per_token)
    balance_loss = (expert_count * jnp.sum(counts / (token_total * per_token) * mass)).reshape(1)
    return (jnp.concatenate(mixed), expert_load, balance_loss)


def solution(mesh):
    return jax.shard_map(
        body,
        mesh=mesh,
        in_specs=(
            P(("groups", "node"), None),
            P(("groups", "node"), None),
            P(("groups", "node"), None),
            P("node", None, None),
            P("node", None, None),
            P("node", None, None),
        ),
        out_specs=(P(("groups", "node"), None), P(("groups", "node")), P("groups")),
        check_vma=False,
    )
```

time: 157 us -> 125 us (0.80)
  Pallas kernels: 32.3 us -> 21.5 us
  starting transfers between devices: 32 us -> 21.6 us
  other arithmetic: 9.48 us -> 3.91 us
  between operations: 4.66 us -> 2.61 us
  local copies, waits for them, and re-layouts: 9.94 us -> 8.33 us
    ppermute x8, waiting for transfers between devices: 26.9 us -> 48.5 us  [body(): right = lambda a: lax.ppermute(a, 'node', to_right)]
    ppermute x8, waiting for transfers between devices: 29.5 us -> 12.8 us  [body(): left = lambda a: lax.ppermute(a, 'node', to_left)]
    ppermute x7 -> x0, waiting for transfers between devices: 12 us -> none  [the longest x6 12 us: body(): lax.ppermute(pair, 'node', ring_shift(order, step))]
    ppermute x7 -> x0, starting transfers between devices: 11.8 us -> none  [the longest x6 6.81 us: body(): lax.ppermute(pair, 'node', ring_shift(order, step))]
    pallas_call x5, Pallas kernels: 32.3 us -> 20.9 us  [apply_expert(): pl.pallas_call(functools.partial(expert_kernel, sizes), out_shape=[jax.Sh...]
    ppermute x19 -> x18, waiting for transfers between devices: 0.05 us -> 5.56 us  [body(): sibling = lambda a: lax.ppermute(a, 'node', to_sibling)]
    reduce_sum x11 -> x0, other arithmetic: 3.64 us -> none  [the longest x9 2.81 us: body(): mass = jnp.sum(every, axis=(0, 1, 3)) / token_total]
    unnamed x52 -> x16, local copies, waits for them, and re-layouts: 6.49 us -> 8.28 us
  transfers between devices with their start and end apart: 42 -> 34, of which waited for: 16 -> 27; matrix products, arithmetic and copies ran while one was open for 6% -> 2% of each run, Pallas kernels for 21% -> 17%
where the time goes in v3:
time: 125 us
  waiting for transfers between devices  66.9 us (54%)
  starting transfers between devices  21.6 us (17%)
  Pallas kernels  21.5 us (17%)
  local copies, waits for them, and re-layouts  8.33 us (7%)
  other arithmetic  3.91 us (3%)
  between operations  2.61 us (2%)
    ppermute x8, waiting for transfers between devices, body(): right = lambda a: lax.ppermute(a, 'node', to_right)  48.5 us
    pallas_call x5, Pallas kernels, apply_expert(): pl.pallas_call(functools.partial(expert_kernel, sizes), out_shape=[jax.Sh...  20.9 us
    ppermute x8, waiting for transfers between devices, body(): left = lambda a: lax.ppermute(a, 'node', to_left)  12.8 us
    ppermute x8, starting transfers between devices, body(): right = lambda a: lax.ppermute(a, 'node', to_right)  9.58 us
    unnamed x16, local copies, waits for them, and re-layouts  8.28 us
    ppermute x8, starting transfers between devices, body(): left = lambda a: lax.ppermute(a, 'node', to_left)  7.47 us
    ppermute x18, waiting for transfers between devices, body(): sibling = lambda a: lax.ppermute(a, 'node', to_sibling)  5.56 us
    ppermute x18, starting transfers between devices, body(): sibling = lambda a: lax.ppermute(a, 'node', to_sibling)  4.56 us
  transfers between devices with their start and end apart: 34, of which 27 were waited for; matrix products, arithmetic and copies ran while one was open for 2% of the time, Pallas kernels for 17%

profile of v3, /device:TPU:0, one launch (start us, length us, event | category | flops | bytes accessed | tf_op | source)
XLA Modules:
  0.0 124.9 jit_solution(12167930800615601471)
XLA Ops:
  0.6 0.8 copy.10.gates_ref
  1.4 0.8 copy.9.ids_ref
  2.2 1.0 copy-done.6
  3.2 0.7 shard_map.85.refs_0_
  3.9 0.5 collective-permute-start.2
  4.4 2.6 %collective-permute-start = (bf16[128,2176]{1,0:T(8,128)(2,1)S(1)}, bf16[128,2176]{1,0:T(8,128)(2,1)S(1)}, u32[]{:S(2)}, u32[]{:S(2)}) collective-permute-start(bf16[128,2176]{1,0:T(8,128)(2,1)S(1)} %shard_map.85.refs_0_), channel_id=1, source_target_pairs={{0,4},{1,5},{4,8},{5,9},{8,12},{9,13},{12,14},{13,15},{14,10},{15,... | collective-permute-start | bytes 1671176 | tf_op jit(solution)/shard_map/ppermute | solution.py:132
  7.3 1.9 %copy-done = bf16[1,2048,768]{2,1,0:T(8,128)(2,1)S(1)} copy-done((bf16[1,2048,768]{2,1,0:T(8,128)(2,1)S(1)}, bf16[1,2048,768]{2,1,0:T(8,128)(2,1)}, u32[]{:S(2)}) %copy-start) | copy-done | bytes 3145752
  9.2 1.9 %copy-done.2 = bf16[1,2048,768]{2,1,0:T(8,128)(2,1)S(1)} copy-done((bf16[1,2048,768]{2,1,0:T(8,128)(2,1)S(1)}, bf16[1,2048,768]{2,1,0:T(8,128)(2,1)}, u32[]{:S(2)}) %copy-start.2) | copy-done | bytes 3145752
  11.0 1.9 %copy-done.4 = bf16[1,768,2048]{2,1,0:T(8,128)(2,1)S(1)} copy-done((bf16[1,768,2048]{2,1,0:T(8,128)(2,1)S(1)}, bf16[1,768,2048]{2,1,0:T(8,128)(2,1)}, u32[]{:S(2)}) %copy-start.4) | copy-done | bytes 3145752
  12.9 2.7 %shard_map.86 = (bf16[128,2048]{1,0:T(8,128)(2,1)S(1)}, bf16[128,2048]{1,0:T(8,128)(2,1)S(1)}, f32[2,128]{1,0:T(2,128)S(1)}) custom-call(bf16[128,2176]{1,0:T(8,128)(2,1)S(1)} %shard_map.85.refs_0_, bf16[128,2176]{1,0:T(8,128)(2,1)S(1)} %collective-permute-done.2.refs_1_, f32[1,128]{1,0:T(1,128)S(1)} %compare_convert_fusion.refs_2_.refs_4_, ...), custom_call_target="tpu_custom_call" | custom-call | flops 2415919104 | bytes 2097152 | tf_op jit(solution)/shard_map/pallas_call | solution.py:103
  15.6 4.6 %collective-permute-done.refs_0_ = bf16[128,2176]{1,0:T(8,128)(2,1)S(1)} collective-permute-done((bf16[128,2176]{1,0:T(8,128)(2,1)S(1)}, bf16[128,2176]{1,0:T(8,128)(2,1)S(1)}, u32[]{:S(2)}, u32[]{:S(2)}) %collective-permute-start) | collective-permute-done | bytes 557088 | tf_op jit(solution)/shard_map/ppermute | solution.py:132
  20.2 1.5 %collective-permute-done.1.refs_2_ = bf16[128,2176]{1,0:T(8,128)(2,1)S(1)} collective-permute-done((bf16[128,2176]{1,0:T(8,128)(2,1)S(1)}, bf16[128,2176]{1,0:T(8,128)(2,1)S(1)}, u32[]{:S(2)}, u32[]{:S(2)}) %collective-permute-start.1) | collective-permute-done | bytes 557088 | tf_op jit(solution)/shard_map/ppermute | solution.py:133
  21.8 0.5 collective-permute-start.6
  22.3 1.6 %collective-permute-start.3 = (bf16[128,2176]{1,0:T(8,128)(2,1)S(1)}, bf16[128,2176]{1,0:T(8,128)(2,1)S(1)}, u32[]{:S(2)}, u32[]{:S(2)}) collective-permute-start(bf16[128,2176]{1,0:T(8,128)(2,1)S(1)} %collective-permute-done.refs_0_), channel_id=1, source_target_pairs={{0,4},{1,5},{4,8},{5,9},{8,12},{9,13},{12,14},{13,15},{14,10},{15,... | collective-permute-start | bytes 1671176 | tf_op jit(solution)/shard_map/ppermute | solution.py:132
  23.8 0.4 collective-permute-start.4
  24.5 5.2 %shard_map.87 = (bf16[128,2048]{1,0:T(8,128)(2,1)S(1)}, bf16[128,2048]{1,0:T(8,128)(2,1)S(1)}, bf16[128,2048]{1,0:T(8,128)(2,1)S(1)}, bf16[128,2048]{1,0:T(8,128)(2,1)S(1)}, f32[2,128]{1,0:T(2,128)S(1)}) custom-call(bf16[128,2176]{1,0:T(8,128)(2,1)S(1)} %collective-permute-done.refs_0_, bf16[128,2176]{1,0:T(8,128)(2,1)S(1)} %collective-permute-done.5.refs_1_, ...), custom_call_target="tpu_custom_call" | custom-call | flops 4831838208 | bytes 4194304 | tf_op jit(solution)/shard_map/pallas_call | solution.py:103
  29.7 7.1 %collective-permute-done.3.refs_0_ = bf16[128,2176]{1,0:T(8,128)(2,1)S(1)} collective-permute-done((bf16[128,2176]{1,0:T(8,128)(2,1)S(1)}, bf16[128,2176]{1,0:T(8,128)(2,1)S(1)}, u32[]{:S(2)}, u32[]{:S(2)}) %collective-permute-start.3) | collective-permute-done | bytes 557088 | tf_op jit(solution)/shard_map/ppermute | solution.py:132
  36.8 1.3 %collective-permute-done.4.refs_2_ = bf16[128,2176]{1,0:T(8,128)(2,1)S(1)} collective-permute-done((bf16[128,2176]{1,0:T(8,128)(2,1)S(1)}, bf16[128,2176]{1,0:T(8,128)(2,1)S(1)}, u32[]{:S(2)}, u32[]{:S(2)}) %collective-permute-start.4) | collective-permute-done | bytes 557088 | tf_op jit(solution)/shard_map/ppermute | solution.py:133
  38.1 0.5 collective-permute-start.9
  38.6 1.6 %collective-permute-start.7 = (bf16[128,2176]{1,0:T(8,128)(2,1)S(1)}, bf16[128,2176]{1,0:T(8,128)(2,1)S(1)}, u32[]{:S(2)}, u32[]{:S(2)}) collective-permute-start(bf16[128,2176]{1,0:T(8,128)(2,1)S(1)} %collective-permute-done.3.refs_0_), channel_id=1, source_target_pairs={{0,4},{1,5},{4,8},{5,9},{8,12},{9,13},{12,14},{13,15},{14,10},{15,... | collective-permute-start | bytes 1671176 | tf_op jit(solution)/shard_map/ppermute | solution.py:132
  40.2 0.4 collective-permute-start.8
  40.8 5.2 %shard_map.88 = (bf16[128,2048]{1,0:T(8,128)(2,1)S(1)}, bf16[128,2048]{1,0:T(8,128)(2,1)S(1)}, bf16[128,2048]{1,0:T(8,128)(2,1)S(1)}, bf16[128,2048]{1,0:T(8,128)(2,1)S(1)}, f32[2,128]{1,0:T(2,128)S(1)}) custom-call(bf16[128,2176]{1,0:T(8,128)(2,1)S(1)} %collective-permute-done.3.refs_0_, bf16[128,2176]{1,0:T(8,128)(2,1)S(1)} %collective-permute-done.9.refs_1_, ...), custom_call_target="tpu_custom_call" | custom-call | flops 4831838208 | bytes 4194304 | tf_op jit(solution)/shard_map/pallas_call | solution.py:103
  46.0 7.1 %collective-permute-done.7.refs_0_ = bf16[128,2176]{1,0:T(8,128)(2,1)S(1)} collective-permute-done((bf16[128,2176]{1,0:T(8,128)(2,1)S(1)}, bf16[128,2176]{1,0:T(8,128)(2,1)S(1)}, u32[]{:S(2)}, u32[]{:S(2)}) %collective-permute-start.7) | collective-permute-done | bytes 557088 | tf_op jit(solution)/shard_map/ppermute | solution.py:132
  53.1 1.3 %collective-permute-done.8.refs_2_ = bf16[128,2176]{1,0:T(8,128)(2,1)S(1)} collective-permute-done((bf16[128,2176]{1,0:T(8,128)(2,1)S(1)}, bf16[128,2176]{1,0:T(8,128)(2,1)S(1)}, u32[]{:S(2)}, u32[]{:S(2)}) %collective-permute-start.8) | collective-permute-done | bytes 557088 | tf_op jit(solution)/shard_map/ppermute | solution.py:133
  54.4 0.5 collective-permute-start.14
  55.0 1.6 %collective-permute-start.11 = (bf16[64,2176]{1,0:T(8,128)(2,1)S(1)}, bf16[64,2176]{1,0:T(8,128)(2,1)S(1)}, u32[]{:S(2)}, u32[]{:S(2)}) collective-permute-start(bf16[64,2176]{1,0:T(8,128)(2,1)S(1)} %slice.9), channel_id=1, source_target_pairs={{0,4},{1,5},{4,8},{5,9},{8,12},{9,13},{12,14},{13,15},{14,10},{15,... | collective-permute-start | bytes 835592 | tf_op jit(solution)/shard_map/ppermute | solution.py:132
  56.6 0.5 collective-permute-start.12
  57.2 5.2 %shard_map.89 = (bf16[128,2048]{1,0:T(8,128)(2,1)S(1)}, bf16[128,2048]{1,0:T(8,128)(2,1)S(1)}, bf16[128,2048]{1,0:T(8,128)(2,1)S(1)}, bf16[128,2048]{1,0:T(8,128)(2,1)S(1)}, f32[2,128]{1,0:T(2,128)S(1)}) custom-call(bf16[128,2176]{1,0:T(8,128)(2,1)S(1)} %collective-permute-done.7.refs_0_, bf16[128,2176]{1,0:T(8,128)(2,1)S(1)} %collective-permute-done.13.refs_1_, ...), custom_call_target="tpu_custom_call" | custom-call | flops 4831838208 | bytes 4194304 | tf_op jit(solution)/shard_map/pallas_call | solution.py:103
  62.4 1.2 collective-permute-done.11.refs_0_
  63.6 1.2 collective-permute-done.12.refs_2_
  64.9 0.5 collective-permute-start.16
  65.4 0.5 collective-permute-start.20
  65.9 0.5 collective-permute-done.15.refs_1_
  66.4 0.4 collective-permute-done.16.refs_3_
  66.8 2.7 %shard_map.90 = (bf16[64,2048]{1,0:T(8,128)(2,1)S(1)}, bf16[64,2048]{1,0:T(8,128)(2,1)S(1)}, bf16[64,2048]{1,0:T(8,128)(2,1)S(1)}, bf16[64,2048]{1,0:T(8,128)(2,1)S(1)}, f32[2,128]{1,0:T(2,128)S(1)}) custom-call(bf16[64,2176]{1,0:T(8,128)(2,1)S(1)} %collective-permute-done.11.refs_0_, bf16[64,2176]{1,0:T(8,128)(2,1)S(1)} %collective-permute-done.15.refs_1_, ...), custom_call_target="tpu_custom_call" | custom-call | flops 2415919104 | bytes 2097152 | tf_op jit(solution)/shard_map/pallas_call | solution.py:103
  69.7 0.4 collective-permute-start.17
  70.2 0.4 collective-permute-start.22
  70.7 0.4 collective-permute-done.18
  71.3 0.2 collective-permute-done.17
  71.8 0.5 collective-permute-done.21
  72.2 0.7 collective-permute-done.22
  73.0 0.7 collective-permute-done.23
  73.7 0.7 collective-permute-done.24
  74.5 0.7 collective-permute-done.25
  75.2 0.5 collective-permute-start.27
  75.8 1.5 %collective-permute-start.26 = (bf16[64,2048]{1,0:T(8,128)(2,1)S(1)}, bf16[64,2048]{1,0:T(8,128)(2,1)S(1)}, u32[]{:S(2)}, u32[]{:S(2)}) collective-permute-start(bf16[64,2048]{1,0:T(8,128)(2,1)S(1)} %add_convert_fusion.8), channel_id=1, source_target_pairs={{0,2},{1,3},{4,0},{5,1},{8,4},{9,5},{12,8},{13,9},{14,12},{15,13},... | collective-permute-start | bytes 786440 | tf_op jit(solution)/shard_map/ppermute | solution.py:133
  77.3 6.3 %collective-permute-done.27 = bf16[64,2048]{1,0:T(8,128)(2,1)S(1)} collective-permute-done((bf16[64,2048]{1,0:T(8,128)(2,1)S(1)}, bf16[64,2048]{1,0:T(8,128)(2,1)S(1)}, u32[]{:S(2)}, u32[]{:S(2)}) %collective-permute-start.27) | collective-permute-done | bytes 262176 | tf_op jit(solution)/shard_map/ppermute | solution.py:132
  84.0 0.5 collective-permute-start.29
  84.5 1.6 %collective-permute-start.28 = (bf16[128,2048]{1,0:T(8,128)(2,1)S(1)}, bf16[128,2048]{1,0:T(8,128)(2,1)S(1)}, u32[]{:S(2)}, u32[]{:S(2)}) collective-permute-start(bf16[128,2048]{1,0:T(8,128)(2,1)S(1)} %add_convert_fusion.6), channel_id=1, source_target_pairs={{0,2},{1,3},{4,0},{5,1},{8,4},{9,5},{12,8},{13,9},{14,12},{15,13},... | collective-permute-start | bytes 1572872 | tf_op jit(solution)/shard_map/ppermute | solution.py:133
  86.1 11.1 %collective-permute-done.29 = bf16[128,2048]{1,0:T(8,128)(2,1)S(1)} collective-permute-done((bf16[128,2048]{1,0:T(8,128)(2,1)S(1)}, bf16[128,2048]{1,0:T(8,128)(2,1)S(1)}, u32[]{:S(2)}, u32[]{:S(2)}) %collective-permute-start.29) | collective-permute-done | bytes 524320 | tf_op jit(solution)/shard_map/ppermute | solution.py:132
  97.2 0.3 add_convert_fusion.3
  97.4 0.2 add_convert_fusion.4
  97.7 0.6 collective-permute-start.31
  98.2 1.5 %collective-permute-start.30 = (bf16[128,2048]{1,0:T(8,128)(2,1)S(1)}, bf16[128,2048]{1,0:T(8,128)(2,1)S(1)}, u32[]{:S(2)}, u32[]{:S(2)}) collective-permute-start(bf16[128,2048]{1,0:T(8,128)(2,1)S(1)} %add_convert_fusion.4), channel_id=1, source_target_pairs={{0,2},{1,3},{4,0},{5,1},{8,4},{9,5},{12,8},{13,9},{14,12},{15,13},... | collective-permute-start | bytes 1572872 | tf_op jit(solution)/shard_map/ppermute | solution.py:133
  99.7 10.1 %collective-permute-done.31 = bf16[128,2048]{1,0:T(8,128)(2,1)S(1)} collective-permute-done((bf16[128,2048]{1,0:T(8,128)(2,1)S(1)}, bf16[128,2048]{1,0:T(8,128)(2,1)S(1)}, u32[]{:S(2)}, u32[]{:S(2)}) %collective-permute-start.31) | collective-permute-done | bytes 524320 | tf_op jit(solution)/shard_map/ppermute | solution.py:132
  109.9 0.2 add_convert_fusion.1
  110.2 0.2 add_convert_fusion.2
  110.4 1.5 %collective-permute-start.32 = (bf16[128,2048]{1,0:T(8,128)(2,1)S(1)}, bf16[128,2048]{1,0:T(8,128)(2,1)S(1)}, u32[]{:S(2)}, u32[]{:S(2)}) collective-permute-start(bf16[128,2048]{1,0:T(8,128)(2,1)S(1)} %add_convert_fusion.2), channel_id=1, source_target_pairs={{0,2},{1,3},{4,0},{5,1},{8,4},{9,5},{12,8},{13,9},{14,12},{15,13},... | collective-permute-start | bytes 1572872 | tf_op jit(solution)/shard_map/ppermute | solution.py:133
  111.9 0.6 collective-permute-start.33
  112.5 0.6 multiply_reduce_fusion
  113.1 0.6 fusion.2
  114.4 7.3 %collective-permute-done.32 = bf16[128,2048]{1,0:T(8,128)(2,1)S(1)} collective-permute-done((bf16[128,2048]{1,0:T(8,128)(2,1)S(1)}, bf16[128,2048]{1,0:T(8,128)(2,1)S(1)}, u32[]{:S(2)}, u32[]{:S(2)}) %collective-permute-start.32) | collective-permute-done | bytes 524320 | tf_op jit(solution)/shard_map/ppermute | solution.py:133
  121.7 0.9 collective-permute-done.33
  122.6 1.1 add_convert_fusion
  (46 shorter events, 2.2 us)
Async XLA Ops:
  2.2 1.0 copy-start.6
  3.9 3.4 %collective-permute-start.2 = (bf16[128,2176]{1,0:T(8,128)(2,1)S(1)}, bf16[128,2176]{1,0:T(8,128)(2,1)S(1)}, u32[]{:S(2)}, u32[]{:S(2)}) collective-permute-start(bf16[128,2176]{1,0:T(8,128)(2,1)S(1)} %shard_map.85.refs_0_), channel_id=1, source_target_pairs={{0,1},{1,0},{2,3},{3,2},{4,5},{5,4},{6,7},{7,6},{8,9},{9,8},{10,11... | collective-permute-start | bytes 1671176 | tf_op jit(solution)/shard_map/ppermute | solution.py:134
  4.4 15.8 %collective-permute-start = (bf16[128,2176]{1,0:T(8,128)(2,1)S(1)}, bf16[128,2176]{1,0:T(8,128)(2,1)S(1)}, u32[]{:S(2)}, u32[]{:S(2)}) collective-permute-start(bf16[128,2176]{1,0:T(8,128)(2,1)S(1)} %shard_map.85.refs_0_), channel_id=1, source_target_pairs={{0,4},{1,5},{4,8},{5,9},{8,12},{9,13},{12,14},{13,15},{14,10},{15,... | collective-permute-start | bytes 1671176 | tf_op jit(solution)/shard_map/ppermute | solution.py:132
  7.1 14.7 %collective-permute-start.1 = (bf16[128,2176]{1,0:T(8,128)(2,1)S(1)}, bf16[128,2176]{1,0:T(8,128)(2,1)S(1)}, u32[]{:S(2)}, u32[]{:S(2)}) collective-permute-start(bf16[128,2176]{1,0:T(8,128)(2,1)S(1)} %shard_map.85.refs_0_), channel_id=1, source_target_pairs={{0,2},{1,3},{4,0},{5,1},{8,4},{9,5},{12,8},{13,9},{14,12},{15,13},... | collective-permute-start | bytes 1671176 | tf_op jit(solution)/shard_map/ppermute | solution.py:133
  7.3 1.9 %copy-start = (bf16[1,2048,768]{2,1,0:T(8,128)(2,1)S(1)}, bf16[1,2048,768]{2,1,0:T(8,128)(2,1)}, u32[]{:S(2)}) copy-start(bf16[1,2048,768]{2,1,0:T(8,128)(2,1)} %param.9) | copy-start | bytes 9437188
  9.2 1.9 %copy-start.2 = (bf16[1,2048,768]{2,1,0:T(8,128)(2,1)S(1)}, bf16[1,2048,768]{2,1,0:T(8,128)(2,1)}, u32[]{:S(2)}) copy-start(bf16[1,2048,768]{2,1,0:T(8,128)(2,1)} %param.10) | copy-start | bytes 9437188
  11.0 1.9 %copy-start.4 = (bf16[1,768,2048]{2,1,0:T(8,128)(2,1)S(1)}, bf16[1,768,2048]{2,1,0:T(8,128)(2,1)}, u32[]{:S(2)}) copy-start(bf16[1,768,2048]{2,1,0:T(8,128)(2,1)} %param.11) | copy-start | bytes 9437188
  12.9 11.6 %copy-start.1 = (bf16[1,2048,768]{2,1,0:T(8,128)(2,1)S(1)}, bf16[1,2048,768]{2,1,0:T(8,128)(2,1)}, u32[]{:S(2)}) copy-start(bf16[1,2048,768]{2,1,0:T(8,128)(2,1)} %param.9) | copy-start | bytes 9437188
  12.9 11.6 %copy-start.3 = (bf16[1,2048,768]{2,1,0:T(8,128)(2,1)S(1)}, bf16[1,2048,768]{2,1,0:T(8,128)(2,1)}, u32[]{:S(2)}) copy-start(bf16[1,2048,768]{2,1,0:T(8,128)(2,1)} %param.10) | copy-start | bytes 9437188
  12.9 11.6 %copy-start.5 = (bf16[1,768,2048]{2,1,0:T(8,128)(2,1)S(1)}, bf16[1,768,2048]{2,1,0:T(8,128)(2,1)}, u32[]{:S(2)}) copy-start(bf16[1,768,2048]{2,1,0:T(8,128)(2,1)} %param.11) | copy-start | bytes 9437188
  21.8 2.5 %collective-permute-start.5 = (bf16[128,2176]{1,0:T(8,128)(2,1)S(1)}, bf16[128,2176]{1,0:T(8,128)(2,1)S(1)}, u32[]{:S(2)}, u32[]{:S(2)}) collective-permute-start(bf16[128,2176]{1,0:T(8,128)(2,1)S(1)} %collective-permute-done.refs_0_), channel_id=1, source_target_pairs={{0,1},{1,0},{2,3},{3,2},{4,5},{5,4},{6,7},{7,6},{8,9},{9,8},{10,11... | collective-permute-start | bytes 1671176 | tf_op jit(solution)/shard_map/ppermute | solution.py:134
  21.8 2.8 %collective-permute-start.6 = (bf16[128,2176]{1,0:T(8,128)(2,1)S(1)}, bf16[128,2176]{1,0:T(8,128)(2,1)S(1)}, u32[]{:S(2)}, u32[]{:S(2)}) collective-permute-start(bf16[128,2176]{1,0:T(8,128)(2,1)S(1)} %collective-permute-done.1.refs_2_), channel_id=1, source_target_pairs={{0,1},{1,0},{2,3},{3,2},{4,5},{5,4},{6,7},{7,6},{8,9},{9,8},{10,11... | collective-permute-start | bytes 1671176 | tf_op jit(solution)/shard_map/ppermute | solution.py:134
  22.3 14.5 %collective-permute-start.3 = (bf16[128,2176]{1,0:T(8,128)(2,1)S(1)}, bf16[128,2176]{1,0:T(8,128)(2,1)S(1)}, u32[]{:S(2)}, u32[]{:S(2)}) collective-permute-start(bf16[128,2176]{1,0:T(8,128)(2,1)S(1)} %collective-permute-done.refs_0_), channel_id=1, source_target_pairs={{0,4},{1,5},{4,8},{5,9},{8,12},{9,13},{12,14},{13,15},{14,10},{15,... | collective-permute-start | bytes 1671176 | tf_op jit(solution)/shard_map/ppermute | solution.py:132
  23.8 14.3 %collective-permute-start.4 = (bf16[128,2176]{1,0:T(8,128)(2,1)S(1)}, bf16[128,2176]{1,0:T(8,128)(2,1)S(1)}, u32[]{:S(2)}, u32[]{:S(2)}) collective-permute-start(bf16[128,2176]{1,0:T(8,128)(2,1)S(1)} %collective-permute-done.1.refs_2_), channel_id=1, source_target_pairs={{0,2},{1,3},{4,0},{5,1},{8,4},{9,5},{12,8},{13,9},{14,12},{15,13},... | collective-permute-start | bytes 1671176 | tf_op jit(solution)/shard_map/ppermute | solution.py:133
  38.1 2.5 %collective-permute-start.10 = (bf16[128,2176]{1,0:T(8,128)(2,1)S(1)}, bf16[128,2176]{1,0:T(8,128)(2,1)S(1)}, u32[]{:S(2)}, u32[]{:S(2)}) collective-permute-start(bf16[128,2176]{1,0:T(8,128)(2,1)S(1)} %collective-permute-done.4.refs_2_), channel_id=1, source_target_pairs={{0,1},{1,0},{2,3},{3,2},{4,5},{5,4},{6,7},{7,6},{8,9},{9,8},{10,11... | collective-permute-start | bytes 1671176 | tf_op jit(solution)/shard_map/ppermute | solution.py:134
  38.1 2.8 %collective-permute-start.9 = (bf16[128,2176]{1,0:T(8,128)(2,1)S(1)}, bf16[128,2176]{1,0:T(8,128)(2,1)S(1)}, u32[]{:S(2)}, u32[]{:S(2)}) collective-permute-start(bf16[128,2176]{1,0:T(8,128)(2,1)S(1)} %collective-permute-done.3.refs_0_), channel_id=1, source_target_pairs={{0,1},{1,0},{2,3},{3,2},{4,5},{5,4},{6,7},{7,6},{8,9},{9,8},{10,11... | collective-permute-start | bytes 1671176 | tf_op jit(solution)/shard_map/ppermute | solution.py:134
  38.6 14.5 %collective-permute-start.7 = (bf16[128,2176]{1,0:T(8,128)(2,1)S(1)}, bf16[128,2176]{1,0:T(8,128)(2,1)S(1)}, u32[]{:S(2)}, u32[]{:S(2)}) collective-permute-start(bf16[128,2176]{1,0:T(8,128)(2,1)S(1)} %collective-permute-done.3.refs_0_), channel_id=1, source_target_pairs={{0,4},{1,5},{4,8},{5,9},{8,12},{9,13},{12,14},{13,15},{14,10},{15,... | collective-permute-start | bytes 1671176 | tf_op jit(solution)/shard_map/ppermute | solution.py:132
  40.2 14.3 %collective-permute-start.8 = (bf16[128,2176]{1,0:T(8,128)(2,1)S(1)}, bf16[128,2176]{1,0:T(8,128)(2,1)S(1)}, u32[]{:S(2)}, u32[]{:S(2)}) collective-permute-start(bf16[128,2176]{1,0:T(8,128)(2,1)S(1)} %collective-permute-done.4.refs_2_), channel_id=1, source_target_pairs={{0,2},{1,3},{4,0},{5,1},{8,4},{9,5},{12,8},{13,9},{14,12},{15,13},... | collective-permute-start | bytes 1671176 | tf_op jit(solution)/shard_map/ppermute | solution.py:133
  54.4 2.6 %collective-permute-start.13 = (bf16[128,2176]{1,0:T(8,128)(2,1)S(1)}, bf16[128,2176]{1,0:T(8,128)(2,1)S(1)}, u32[]{:S(2)}, u32[]{:S(2)}) collective-permute-start(bf16[128,2176]{1,0:T(8,128)(2,1)S(1)} %collective-permute-done.7.refs_0_), channel_id=1, source_target_pairs={{0,1},{1,0},{2,3},{3,2},{4,5},{5,4},{6,7},{7,6},{8,9},{9,8},{10,11... | collective-permute-start | bytes 1671176 | tf_op jit(solution)/shard_map/ppermute | solution.py:134
  54.4 2.8 %collective-permute-start.14 = (bf16[128,2176]{1,0:T(8,128)(2,1)S(1)}, bf16[128,2176]{1,0:T(8,128)(2,1)S(1)}, u32[]{:S(2)}, u32[]{:S(2)}) collective-permute-start(bf16[128,2176]{1,0:T(8,128)(2,1)S(1)} %collective-permute-done.8.refs_2_), channel_id=1, source_target_pairs={{0,1},{1,0},{2,3},{3,2},{4,5},{5,4},{6,7},{7,6},{8,9},{9,8},{10,11... | collective-permute-start | bytes 1671176 | tf_op jit(solution)/shard_map/ppermute | solution.py:134
  55.0 8.6 %collective-permute-start.11 = (bf16[64,2176]{1,0:T(8,128)(2,1)S(1)}, bf16[64,2176]{1,0:T(8,128)(2,1)S(1)}, u32[]{:S(2)}, u32[]{:S(2)}) collective-permute-start(bf16[64,2176]{1,0:T(8,128)(2,1)S(1)} %slice.9), channel_id=1, source_target_pairs={{0,4},{1,5},{4,8},{5,9},{8,12},{9,13},{12,14},{13,15},{14,10},{15,... | collective-permute-start | bytes 835592 | tf_op jit(solution)/shard_map/ppermute | solution.py:132
  56.6 8.3 %collective-permute-start.12 = (bf16[64,2176]{1,0:T(8,128)(2,1)S(1)}, bf16[64,2176]{1,0:T(8,128)(2,1)S(1)}, u32[]{:S(2)}, u32[]{:S(2)}) collective-permute-start(bf16[64,2176]{1,0:T(8,128)(2,1)S(1)} %slice.10), channel_id=1, source_target_pairs={{0,2},{1,3},{4,0},{5,1},{8,4},{9,5},{12,8},{13,9},{14,12},{15,13},... | collective-permute-start | bytes 835592 | tf_op jit(solution)/shard_map/ppermute | solution.py:133
  64.9 1.6 %collective-permute-start.15 = (bf16[64,2176]{1,0:T(8,128)(2,1)S(1)}, bf16[64,2176]{1,0:T(8,128)(2,1)S(1)}, u32[]{:S(2)}, u32[]{:S(2)}) collective-permute-start(bf16[64,2176]{1,0:T(8,128)(2,1)S(1)} %collective-permute-done.11.refs_0_), channel_id=1, source_target_pairs={{0,1},{1,0},{2,3},{3,2},{4,5},{5,4},{6,7},{7,6},{8,9},{9,8},{10,11... | collective-permute-start | bytes 835592 | tf_op jit(solution)/shard_map/ppermute | solution.py:134
  64.9 2.0 %collective-permute-start.16 = (bf16[64,2176]{1,0:T(8,128)(2,1)S(1)}, bf16[64,2176]{1,0:T(8,128)(2,1)S(1)}, u32[]{:S(2)}, u32[]{:S(2)}) collective-permute-start(bf16[64,2176]{1,0:T(8,128)(2,1)S(1)} %collective-permute-done.12.refs_2_), channel_id=1, source_target_pairs={{0,1},{1,0},{2,3},{3,2},{4,5},{5,4},{6,7},{7,6},{8,9},{9,8},{10,11... | collective-permute-start | bytes 835592 | tf_op jit(solution)/shard_map/ppermute | solution.py:134
  65.4 4.9 %collective-permute-start.19 = (bf16[128,2048]{1,0:T(8,128)(2,1)S(1)}, bf16[128,2048]{1,0:T(8,128)(2,1)S(1)}, u32[]{:S(2)}, u32[]{:S(2)}) collective-permute-start(bf16[128,2048]{1,0:T(8,128)(2,1)S(1)} %get-tuple-element.115), channel_id=1, source_target_pairs={{0,1},{1,0},{2,3},{3,2},{4,5},{5,4},{6,7},{7,6},{8,9},{9,8},{10,11... | collective-permute-start | bytes 1572872 | tf_op jit(solution)/shard_map/ppermute | solution.py:134
  65.4 5.2 %collective-permute-start.20 = (bf16[128,2048]{1,0:T(8,128)(2,1)S(1)}, bf16[128,2048]{1,0:T(8,128)(2,1)S(1)}, u32[]{:S(2)}, u32[]{:S(2)}) collective-permute-start(bf16[128,2048]{1,0:T(8,128)(2,1)S(1)} %get-tuple-element.117), channel_id=1, source_target_pairs={{0,1},{1,0},{2,3},{3,2},{4,5},{5,4},{6,7},{7,6},{8,9},{9,8},{10,11... | collective-permute-start | bytes 1572872 | tf_op jit(solution)/shard_map/ppermute | solution.py:134
  69.5 1.6 %collective-permute-start.18 = (bf16[64,2048]{1,0:T(8,128)(2,1)S(1)}, bf16[64,2048]{1,0:T(8,128)(2,1)S(1)}, u32[]{:S(2)}, u32[]{:S(2)}) collective-permute-start(bf16[64,2048]{1,0:T(8,128)(2,1)S(1)} %get-tuple-element.113), channel_id=1, source_target_pairs={{0,1},{1,0},{2,3},{3,2},{4,5},{5,4},{6,7},{7,6},{8,9},{9,8},{10,11... | collective-permute-start | bytes 786440 | tf_op jit(solution)/shard_map/ppermute | solution.py:134
  69.7 1.8 %collective-permute-start.17 = (bf16[64,2048]{1,0:T(8,128)(2,1)S(1)}, bf16[64,2048]{1,0:T(8,128)(2,1)S(1)}, u32[]{:S(2)}, u32[]{:S(2)}) collective-permute-start(bf16[64,2048]{1,0:T(8,128)(2,1)S(1)} %get-tuple-element.111), channel_id=1, source_target_pairs={{0,1},{1,0},{2,3},{3,2},{4,5},{5,4},{6,7},{7,6},{8,9},{9,8},{10,11... | collective-permute-start | bytes 786440 | tf_op jit(solution)/shard_map/ppermute | solution.py:134
  70.1 2.1 %collective-permute-start.21 = (bf16[128,2048]{1,0:T(8,128)(2,1)S(1)}, bf16[128,2048]{1,0:T(8,128)(2,1)S(1)}, u32[]{:S(2)}, u32[]{:S(2)}) collective-permute-start(bf16[128,2048]{1,0:T(8,128)(2,1)S(1)} %get-tuple-element.119), channel_id=1, source_target_pairs={{0,1},{1,0},{2,3},{3,2},{4,5},{5,4},{6,7},{7,6},{8,9},{9,8},{10,11... | collective-permute-start | bytes 1572872 | tf_op jit(solution)/shard_map/ppermute | solution.py:134
  70.2 2.8 %collective-permute-start.22 = (bf16[128,2048]{1,0:T(8,128)(2,1)S(1)}, bf16[128,2048]{1,0:T(8,128)(2,1)S(1)}, u32[]{:S(2)}, u32[]{:S(2)}) collective-permute-start(bf16[128,2048]{1,0:T(8,128)(2,1)S(1)} %get-tuple-element.121), channel_id=1, source_target_pairs={{0,1},{1,0},{2,3},{3,2},{4,5},{5,4},{6,7},{7,6},{8,9},{9,8},{10,11... | collective-permute-start | bytes 1572872 | tf_op jit(solution)/shard_map/ppermute | solution.py:134
  70.6 3.1 %collective-permute-start.23 = (bf16[128,2048]{1,0:T(8,128)(2,1)S(1)}, bf16[128,2048]{1,0:T(8,128)(2,1)S(1)}, u32[]{:S(2)}, u32[]{:S(2)}) collective-permute-start(bf16[128,2048]{1,0:T(8,128)(2,1)S(1)} %get-tuple-element.123), channel_id=1, source_target_pairs={{0,1},{1,0},{2,3},{3,2},{4,5},{5,4},{6,7},{7,6},{8,9},{9,8},{10,11... | collective-permute-start | bytes 1572872 | tf_op jit(solution)/shard_map/ppermute | solution.py:134
  71.1 3.4 %collective-permute-start.24 = (bf16[128,2048]{1,0:T(8,128)(2,1)S(1)}, bf16[128,2048]{1,0:T(8,128)(2,1)S(1)}, u32[]{:S(2)}, u32[]{:S(2)}) collective-permute-start(bf16[128,2048]{1,0:T(8,128)(2,1)S(1)} %get-tuple-element.125), channel_id=1, source_target_pairs={{0,1},{1,0},{2,3},{3,2},{4,5},{5,4},{6,7},{7,6},{8,9},{9,8},{10,11... | collective-permute-start | bytes 1572872 | tf_op jit(solution)/shard_map/ppermute | solution.py:134
  71.5 3.7 %collective-permute-start.25 = (bf16[128,2048]{1,0:T(8,128)(2,1)S(1)}, bf16[128,2048]{1,0:T(8,128)(2,1)S(1)}, u32[]{:S(2)}, u32[]{:S(2)}) collective-permute-start(bf16[128,2048]{1,0:T(8,128)(2,1)S(1)} %get-tuple-element.127), channel_id=1, source_target_pairs={{0,1},{1,0},{2,3},{3,2},{4,5},{5,4},{6,7},{7,6},{8,9},{9,8},{10,11... | collective-permute-start | bytes 1572872 | tf_op jit(solution)/shard_map/ppermute | solution.py:134
  75.2 8.3 %collective-permute-start.27 = (bf16[64,2048]{1,0:T(8,128)(2,1)S(1)}, bf16[64,2048]{1,0:T(8,128)(2,1)S(1)}, u32[]{:S(2)}, u32[]{:S(2)}) collective-permute-start(bf16[64,2048]{1,0:T(8,128)(2,1)S(1)} %add_convert_fusion.7), channel_id=1, source_target_pairs={{0,4},{1,5},{4,8},{5,9},{8,12},{9,13},{12,14},{13,15},{14,10},{15,... | collective-permute-start | bytes 786440 | tf_op jit(solution)/shard_map/ppermute | solution.py:132
  75.8 8.1 %collective-permute-start.26 = (bf16[64,2048]{1,0:T(8,128)(2,1)S(1)}, bf16[64,2048]{1,0:T(8,128)(2,1)S(1)}, u32[]{:S(2)}, u32[]{:S(2)}) collective-permute-start(bf16[64,2048]{1,0:T(8,128)(2,1)S(1)} %add_convert_fusion.8), channel_id=1, source_target_pairs={{0,2},{1,3},{4,0},{5,1},{8,4},{9,5},{12,8},{13,9},{14,12},{15,13},... | collective-permute-start | bytes 786440 | tf_op jit(solution)/shard_map/ppermute | solution.py:133
  84.0 13.1 %collective-permute-start.29 = (bf16[128,2048]{1,0:T(8,128)(2,1)S(1)}, bf16[128,2048]{1,0:T(8,128)(2,1)S(1)}, u32[]{:S(2)}, u32[]{:S(2)}) collective-permute-start(bf16[128,2048]{1,0:T(8,128)(2,1)S(1)} %add_convert_fusion.5), channel_id=1, source_target_pairs={{0,4},{1,5},{4,8},{5,9},{8,12},{9,13},{12,14},{13,15},{14,10},{15,... | collective-permute-start | bytes 1572872 | tf_op jit(solution)/shard_map/ppermute | solution.py:132
  84.5 12.9 %collective-permute-start.28 = (bf16[128,2048]{1,0:T(8,128)(2,1)S(1)}, bf16[128,2048]{1,0:T(8,128)(2,1)S(1)}, u32[]{:S(2)}, u32[]{:S(2)}) collective-permute-start(bf16[128,2048]{1,0:T(8,128)(2,1)S(1)} %add_convert_fusion.6), channel_id=1, source_target_pairs={{0,2},{1,3},{4,0},{5,1},{8,4},{9,5},{12,8},{13,9},{14,12},{15,13},... | collective-permute-start | bytes 1572872 | tf_op jit(solution)/shard_map/ppermute | solution.py:133
  97.7 12.2 %collective-permute-start.31 = (bf16[128,2048]{1,0:T(8,128)(2,1)S(1)}, bf16[128,2048]{1,0:T(8,128)(2,1)S(1)}, u32[]{:S(2)}, u32[]{:S(2)}) collective-permute-start(bf16[128,2048]{1,0:T(8,128)(2,1)S(1)} %add_convert_fusion.3), channel_id=1, source_target_pairs={{0,4},{1,5},{4,8},{5,9},{8,12},{9,13},{12,14},{13,15},{14,10},{15,... | collective-permute-start | bytes 1572872 | tf_op jit(solution)/shard_map/ppermute | solution.py:132
  98.2 11.9 %collective-permute-start.30 = (bf16[128,2048]{1,0:T(8,128)(2,1)S(1)}, bf16[128,2048]{1,0:T(8,128)(2,1)S(1)}, u32[]{:S(2)}, u32[]{:S(2)}) collective-permute-start(bf16[128,2048]{1,0:T(8,128)(2,1)S(1)} %add_convert_fusion.4), channel_id=1, source_target_pairs={{0,2},{1,3},{4,0},{5,1},{8,4},{9,5},{12,8},{13,9},{14,12},{15,13},... | collective-permute-start | bytes 1572872 | tf_op jit(solution)/shard_map/ppermute | solution.py:133
  110.4 11.2 %collective-permute-start.32 = (bf16[128,2048]{1,0:T(8,128)(2,1)S(1)}, bf16[128,2048]{1,0:T(8,128)(2,1)S(1)}, u32[]{:S(2)}, u32[]{:S(2)}) collective-permute-start(bf16[128,2048]{1,0:T(8,128)(2,1)S(1)} %add_convert_fusion.2), channel_id=1, source_target_pairs={{0,2},{1,3},{4,0},{5,1},{8,4},{9,5},{12,8},{13,9},{14,12},{15,13},... | collective-permute-start | bytes 1572872 | tf_op jit(solution)/shard_map/ppermute | solution.py:133
  111.9 10.7 %collective-permute-start.33 = (bf16[128,2048]{1,0:T(8,128)(2,1)S(1)}, bf16[128,2048]{1,0:T(8,128)(2,1)S(1)}, u32[]{:S(2)}, u32[]{:S(2)}) collective-permute-start(bf16[128,2048]{1,0:T(8,128)(2,1)S(1)} %add_convert_fusion.1), channel_id=1, source_target_pairs={{0,4},{1,5},{4,8},{5,9},{8,12},{9,13},{12,14},{13,15},{14,10},{15,... | collective-permute-start | bytes 1572872 | tf_op jit(solution)/shard_map/ppermute | solution.py:132

commit v4 on v3

v4 whole, which is shorter than its diff:
```python
import functools

import jax
import jax.numpy as jnp
from jax import lax
from jax.experimental import pallas as pl
from jax.experimental.pallas import tpu as pltpu
from jax.sharding import PartitionSpec as P

CORES = 2
LANES = 128
VMEM_LIMIT = 24 * 1024 * 1024
HIDDEN_CHUNK = 256
OUT_CHUNK = 512


def ring_order(chips):
    if chips <= 8:
        return list(range(0, chips, 2)) + list(range(1, chips, 2))[::-1]
    return list(range(chips))


def ring_shift(order, step):
    pairs = []
    for place, chip in enumerate(order):
        target = order[(place + step) % len(order)]
        pairs += [(CORES * chip + core, CORES * target + core) for core in range(CORES)]
    return pairs


def pack_kernel(experts, tokens_ref, ids_ref, gates_ref, out_ref, arrived):
    rows, width = tokens_ref.shape
    lanes = out_ref.shape[1] - width
    copy = pltpu.make_async_copy(tokens_ref, out_ref.at[:, pl.ds(0, width)], arrived)
    copy.start()
    lane = lax.broadcasted_iota(jnp.int32, (lanes, rows), 0)
    scores = jnp.zeros((lanes, rows), jnp.int32)
    for k in range(ids_ref.shape[0]):
        at, gate = ids_ref[k : k + 1, :], gates_ref[k : k + 1, :]
        scores = jnp.where(lane == at, gate >> 8, scores)
        scores = jnp.where(lane == at + experts, gate & 255, scores)
    out_ref[:, width:] = scores.astype(jnp.float32).T.astype(jnp.bfloat16)
    copy.wait()


def pack(tokens, expert_ids, gate_fixed, experts):
    rows, width = tokens.shape
    lanes = -(-2 * experts // LANES) * LANES
    in_vmem = pl.BlockSpec(memory_space=pltpu.VMEM)
    return pl.pallas_call(
        functools.partial(pack_kernel, experts),
        out_shape=jax.ShapeDtypeStruct((rows, width + lanes), jnp.bfloat16),
        in_specs=[pl.BlockSpec(memory_space=pl.ANY), in_vmem, in_vmem],
        out_specs=in_vmem,
        scratch_shapes=[pltpu.SemaphoreType.DMA],
        cost_estimate=pl.CostEstimate(
            flops=rows * lanes, bytes_accessed=4 * rows * width, transcendentals=0
        ),
    )(tokens, expert_ids.T, gate_fixed.T)


def expert_kernel(sizes, *refs):
    count = len(sizes)
    blocks = refs[:count]
    own_ref, join_ref = refs[count : count + 2]
    experts = [refs[count + 2 + 3 * i : count + 5 + 3 * i] for i in range(CORES)]
    refs = refs[count + 2 + 3 * CORES :]
    outs = refs[:count]
    stats_ref, hidden_ref = refs[count:]
    starts = [sum(sizes[:i]) for i in range(count)]
    width, hidden_width = experts[0][0].shape
    lanes = join_ref.shape[0]

    scores = jnp.concatenate([block[:, width:] for block in blocks], axis=0)
    joined = jnp.dot(scores, join_ref[...], preferred_element_type=jnp.float32)
    weights = joined[:, :lanes] / joined[:, lanes:]
    stats_ref[0:1, :] = jnp.sum((weights > 0).astype(jnp.float32), axis=0, keepdims=True)
    stats_ref[1:2, :] = jnp.sum(weights, axis=0, keepdims=True)
    scales = [
        jnp.sum(weights * own_ref[i : i + 1, :], axis=1, keepdims=True) for i in range(CORES)
    ]

    rows = jnp.concatenate([block[:, :width] for block in blocks], axis=0)
    for i, (gate_ref, up_ref, _) in enumerate(experts):
        for start in range(0, hidden_width, HIDDEN_CHUNK):
            at = slice(start, start + HIDDEN_CHUNK)
            gate = jnp.dot(rows, gate_ref[:, at], preferred_element_type=jnp.float32)
            up = jnp.dot(rows, up_ref[:, at], preferred_element_type=jnp.float32)
            hidden_ref[i, :, at] = (gate / (1.0 + jnp.exp(-gate)) * up).astype(jnp.bfloat16)
    for start in range(0, width, OUT_CHUNK):
        at = slice(start, start + OUT_CHUNK)
        total = 0.0
        for i, (_, _, down_ref) in enumerate(experts):
            out = jnp.dot(hidden_ref[i], down_ref[:, at], preferred_element_type=jnp.float32)
            total = total + out.astype(jnp.bfloat16).astype(jnp.float32) * scales[i]
        for i in range(count):
            outs[i][:, at] = total[starts[i] : starts[i] + sizes[i]].astype(jnp.bfloat16)


def apply_experts(blocks, own, join, weights):
    width, hidden_width = weights[0].shape
    sizes = tuple(block.shape[0] for block in blocks)
    total = sum(sizes)
    count = len(blocks)
    in_vmem = pl.BlockSpec(memory_space=pltpu.VMEM)
    return pl.pallas_call(
        functools.partial(expert_kernel, sizes),
        out_shape=[jax.ShapeDtypeStruct((size, width), jnp.bfloat16) for size in sizes]
        + [jax.ShapeDtypeStruct((2, own.shape[1]), jnp.float32)],
        in_specs=[in_vmem] * (count + 2 + len(weights)),
        out_specs=[in_vmem] * (count + 1),
        scratch_shapes=[pltpu.VMEM((CORES, total, hidden_width), jnp.bfloat16)],
        compiler_params=pltpu.CompilerParams(vmem_limit_bytes=VMEM_LIMIT),
        cost_estimate=pl.CostEstimate(
            flops=6 * CORES * total * width * hidden_width,
            bytes_accessed=4 * total * width,
            transcendentals=CORES * total * hidden_width,
        ),
    )(*blocks, own, join, *weights)


def body(tokens, expert_ids, gate_fixed, gate_weight, up_weight, down_weight):
    tok_rows, model_width = tokens.shape
    per_token = expert_ids.shape[1]
    node_count = lax.axis_size("node")
    expert_count = node_count
    token_total = tok_rows * node_count
    chips = node_count // CORES
    far = chips // 2
    half = tok_rows // 2
    order = ring_order(chips)
    to_right, to_left = ring_shift(order, 1), ring_shift(order, -1)
    to_sibling = [(node, node ^ 1) for node in range(node_count)]
    right = lambda a: lax.ppermute(a, "node", to_right)
    left = lambda a: lax.ppermute(a, "node", to_left)
    sibling = lambda a: lax.ppermute(a, "node", to_sibling)
    tie = lax.optimization_barrier
    node = lax.axis_index("node")

    weights = [gate_weight[0], up_weight[0], down_weight[0]]
    weights += [sibling(weight) for weight in weights]
    packed = pack(tokens, expert_ids, gate_fixed, expert_count)
    lanes = packed.shape[1] - model_width
    own = (jnp.arange(lanes)[None] == jnp.stack([node, node ^ 1])[:, None]).astype(jnp.float32)
    source, target = jnp.arange(lanes)[:, None], jnp.arange(2 * lanes)[None]
    is_low = source >= expert_count
    to_expert = (target == jnp.where(is_low, source - expert_count, source)) | (target >= lanes)
    join = jnp.where(
        to_expert & (source < 2 * expert_count), jnp.where(is_low, 1.0, 256.0), 0.0
    ).astype(jnp.bfloat16)
    stats = []

    def run(blocks):
        res = apply_experts(blocks, own, join, weights)
        stats.append(res[-1])
        return res[:-1]

    def add(*terms):
        return sum(term.astype(jnp.float32) for term in terms).astype(jnp.bfloat16)

    low, high = right(packed), left(packed)
    blocks, outs, fresh = {}, {}, {}
    for step in range(2, far + 1):
        (low, high), fresh = tie(((low, high), fresh))
        outs.update(fresh)
        blocks[step - 1] = (low, high)
        if step < far:
            low, high = right(low), left(high)
        else:
            low, high = right(low[:half]), left(high[half:])
        ready = [k for k in blocks if k not in outs] if step >= min(3, far) else []
        fresh = {k: run(blocks[k]) for k in ready}
    (low, high), fresh = tie(((low, high), fresh))
    outs.update(fresh)
    low, high = run([low, high])

    low, high, packed = tie((low, high, packed))
    (own_rows,) = run([packed])
    for k in range(far - 1, 0, -1):
        low, high = left(low), right(high)
        if k == far - 1:
            zeros = jnp.zeros_like(low)
            low = jnp.concatenate([low, zeros])
            high = jnp.concatenate([zeros, high])
        low, high = tie((add(outs[k][0], low), add(outs[k][1], high)))
    mixed = add(own_rows, left(low), right(high))

    total = sum(stats)
    counts, mass = (total + sibling(total))[:, :expert_count]
    mass = mass / token_total
    own_count = lax.dynamic_slice(counts, (node,), (1,))
    expert_load = own_count * expert_count / (token_total * per_token)
    balance_loss = (expert_count * jnp.sum(counts / (token_total * per_token) * mass)).reshape(1)
    return (mixed, expert_load, balance_loss)


def solution(mesh):
    return jax.shard_map(
        body,
        mesh=mesh,
        in_specs=(
            P(("groups", "node"), None),
            P(("groups", "node"), None),
            P(("groups", "node"), None),
            P("node", None, None),
            P("node", None, None),
            P("node", None, None),
        ),
        out_specs=(P(("groups", "node"), None), P(("groups", "node")), P("groups")),
        check_vma=False,
    )
```

time: 125 us -> 129 us (1.032)
  Pallas kernels: 21.5 us -> 38.3 us
  waiting for transfers between devices: 66.9 us -> 56.5 us
  starting transfers between devices: 21.6 us -> 19 us
  other arithmetic: 3.91 us -> 6.14 us
  local copies, waits for them, and re-layouts: 8.33 us -> 6.52 us
    pallas_call x6, Pallas kernels: 21.5 us -> 38.3 us  [the longest x5 35.7 us: apply_experts(): pl.pallas_call(functools.partial(expert_kernel, sizes), out_shape=[jax.Sh...]
    ppermute x8, waiting for transfers between devices: 12.8 us -> 7.78 us  [body(): left = lambda a: lax.ppermute(a, 'node', to_left)]
    ppermute x18 -> x4, waiting for transfers between devices: 5.56 us -> 1.14 us  [body(): sibling = lambda a: lax.ppermute(a, 'node', to_sibling)]
    ppermute x18 -> x4, starting transfers between devices: 4.56 us -> 1.03 us  [body(): sibling = lambda a: lax.ppermute(a, 'node', to_sibling)]
    ppermute x8, starting transfers between devices: 9.58 us -> 12.8 us  [body(): right = lambda a: lax.ppermute(a, 'node', to_right)]
    ppermute x8, starting transfers between devices: 7.47 us -> 5.16 us  [body(): left = lambda a: lax.ppermute(a, 'node', to_left)]
    convert_element_type x9 -> x7, other arithmetic: 2.57 us -> 4.66 us  [add(): sum((term.astype(jnp.float32) for term in terms)).astype(jnp.bfloat16)]
    unnamed x16 -> x12, local copies, waits for them, and re-layouts: 8.28 us -> 6.47 us
  transfers between devices with their start and end apart: 34 -> 20, of which waited for: 27 -> 12; matrix products, arithmetic and copies ran while one was open for 2% -> 2% of each run, Pallas kernels for 17% -> 25%
where the time goes in v4:
time: 129 us
  waiting for transfers between devices  56.5 us (44%)
  Pallas kernels  38.3 us (30%)
  starting transfers between devices  19 us (15%)
  local copies, waits for them, and re-layouts  6.52 us (5%)
  other arithmetic  6.14 us (5%)
  between operations  2.61 us (2%)
    ppermute x8, waiting for transfers between devices, body(): right = lambda a: lax.ppermute(a, 'node', to_right)  47.5 us
    pallas_call x5, Pallas kernels, apply_experts(): pl.pallas_call(functools.partial(expert_kernel, sizes), out_shape=[jax.Sh...  35.7 us
    ppermute x8, starting transfers between devices, body(): right = lambda a: lax.ppermute(a, 'node', to_right)  12.8 us
    ppermute x8, waiting for transfers between devices, body(): left = lambda a: lax.ppermute(a, 'node', to_left)  7.78 us
    unnamed x12, local copies, waits for them, and re-layouts  6.47 us
    ppermute x8, starting transfers between devices, body(): left = lambda a: lax.ppermute(a, 'node', to_left)  5.16 us
    convert_element_type x7, other arithmetic, add(): sum((term.astype(jnp.float32) for term in terms)).astype(jnp.bfloat16)  4.66 us
    pallas_call x1, Pallas kernels, pack(): pl.pallas_call(functools.partial(pack_kernel, experts), out_shape=jax.Sha...  2.59 us
  transfers between devices with their start and end apart: 20, of which 12 were waited for; matrix products, arithmetic and copies ran while one was open for 2% of the time, Pallas kernels for 25%

profile of v4, /device:TPU:0, one launch (start us, length us, event | category | flops | bytes accessed | tf_op | source)
XLA Modules:
  0.0 129.0 jit_solution(15379836929575406403)
XLA Ops:
  0.6 0.5 collective-permute-start.6
  1.1 0.1 collective-permute-start.7
  1.2 0.4 collective-permute-start.8
  1.7 2.6 %shard_map.85.refs_0_ = bf16[128,2176]{1,0:T(8,128)(2,1)} custom-call(bf16[128,2048]{1,0:T(8,128)(2,1)} %tokens_ref.1, s32[8,128]{1,0:T(8,128)} %bitcast.27, s32[8,128]{1,0:T(8,128)} %bitcast.28), custom_call_target="tpu_custom_call" | custom-call | flops 16384 | bytes 1048576 | tf_op jit(solution)/shard_map/pallas_call | solution.py:50
  4.3 2.7 %collective-permute-start = (bf16[128,2176]{1,0:T(8,128)(2,1)}, bf16[128,2176]{1,0:T(8,128)(2,1)}, u32[]{:S(2)}, u32[]{:S(2)}) collective-permute-start(bf16[128,2176]{1,0:T(8,128)(2,1)} %shard_map.85.refs_0_), channel_id=1, source_target_pairs={{0,4},{1,5},{4,8},{5,9},{8,12},{9,13},{12,14},{13,15},{14,10},{15,... | collective-permute-start | bytes 1671176 | tf_op jit(solution)/shard_map/ppermute | solution.py:134
  7.0 0.0 collective-permute-start.1
  7.0 13.4 %collective-permute-done.refs_0_ = bf16[128,2176]{1,0:T(8,128)(2,1)} collective-permute-done((bf16[128,2176]{1,0:T(8,128)(2,1)}, bf16[128,2176]{1,0:T(8,128)(2,1)}, u32[]{:S(2)}, u32[]{:S(2)}) %collective-permute-start) | collective-permute-done | bytes 557088 | tf_op jit(solution)/shard_map/ppermute | solution.py:134
  20.4 1.5 %collective-permute-done.1.refs_1_ = bf16[128,2176]{1,0:T(8,128)(2,1)} collective-permute-done((bf16[128,2176]{1,0:T(8,128)(2,1)}, bf16[128,2176]{1,0:T(8,128)(2,1)}, u32[]{:S(2)}, u32[]{:S(2)}) %collective-permute-start.1) | collective-permute-done | bytes 557088 | tf_op jit(solution)/shard_map/ppermute | solution.py:135
  22.0 1.6 %collective-permute-start.2 = (bf16[128,2176]{1,0:T(8,128)(2,1)}, bf16[128,2176]{1,0:T(8,128)(2,1)S(1)}, u32[]{:S(2)}, u32[]{:S(2)}) collective-permute-start(bf16[128,2176]{1,0:T(8,128)(2,1)} %collective-permute-done.refs_0_), channel_id=1, source_target_pairs={{0,4},{1,5},{4,8},{5,9},{8,12},{9,13},{12,14},{13,15},{14,10},{15,... | collective-permute-start | bytes 1671176 | tf_op jit(solution)/shard_map/ppermute | solution.py:134
  23.6 0.4 collective-permute-start.3
  24.0 0.1 pad_add_fusion
  24.1 0.1 compare_convert_fusion.refs_2_.refs_1_
  24.2 0.1 select_convert_fusion.refs_3_.refs_2_
  24.3 11.8 %collective-permute-done.2.refs_0_ = bf16[128,2176]{1,0:T(8,128)(2,1)S(1)} collective-permute-done((bf16[128,2176]{1,0:T(8,128)(2,1)}, bf16[128,2176]{1,0:T(8,128)(2,1)S(1)}, u32[]{:S(2)}, u32[]{:S(2)}) %collective-permute-start.2) | collective-permute-done | bytes 557088 | tf_op jit(solution)/shard_map/ppermute | solution.py:134
  36.1 1.3 %collective-permute-done.3.refs_1_ = bf16[128,2176]{1,0:T(8,128)(2,1)S(1)} collective-permute-done((bf16[128,2176]{1,0:T(8,128)(2,1)}, bf16[128,2176]{1,0:T(8,128)(2,1)S(1)}, u32[]{:S(2)}, u32[]{:S(2)}) %collective-permute-start.3) | collective-permute-done | bytes 557088 | tf_op jit(solution)/shard_map/ppermute | solution.py:135
  37.4 1.6 %collective-permute-start.4 = (bf16[128,2176]{1,0:T(8,128)(2,1)S(1)}, bf16[128,2176]{1,0:T(8,128)(2,1)S(1)}, u32[]{:S(2)}, u32[]{:S(2)}) collective-permute-start(bf16[128,2176]{1,0:T(8,128)(2,1)S(1)} %collective-permute-done.2.refs_0_), channel_id=1, source_target_pairs={{0,4},{1,5},{4,8},{5,9},{8,12},{9,13},{12,14},{13,15},{14,10},{15,... | collective-permute-start | bytes 1671176 | tf_op jit(solution)/shard_map/ppermute | solution.py:134
  38.9 0.4 collective-permute-start.5
  39.4 0.0 collective-permute-done.6.refs_7_.refs_6_
  39.4 0.0 collective-permute-done.7.refs_8_.refs_7_
  39.4 0.0 collective-permute-done.8.refs_9_.refs_8_
  39.4 0.0 copy-start
  39.4 1.9 %copy-done = bf16[1,2048,768]{2,1,0:T(8,128)(2,1)S(1)} copy-done((bf16[1,2048,768]{2,1,0:T(8,128)(2,1)S(1)}, bf16[1,2048,768]{2,1,0:T(8,128)(2,1)}, u32[]{:S(2)}) %copy-start) | copy-done | bytes 3145752
  41.3 1.9 %copy-done.2 = bf16[1,2048,768]{2,1,0:T(8,128)(2,1)S(1)} copy-done((bf16[1,2048,768]{2,1,0:T(8,128)(2,1)S(1)}, bf16[1,2048,768]{2,1,0:T(8,128)(2,1)}, u32[]{:S(2)}) %copy-start.2) | copy-done | bytes 3145752
  43.2 1.9 %copy-done.3 = bf16[1,768,2048]{2,1,0:T(8,128)(2,1)S(1)} copy-done((bf16[1,768,2048]{2,1,0:T(8,128)(2,1)S(1)}, bf16[1,768,2048]{2,1,0:T(8,128)(2,1)}, u32[]{:S(2)}) %copy-start.3) | copy-done | bytes 3145752
  45.1 8.1 %shard_map.87 = (bf16[128,2048]{1,0:T(8,128)(2,1)S(1)}, bf16[128,2048]{1,0:T(8,128)(2,1)S(1)}, f32[2,128]{1,0:T(2,128)S(1)}) custom-call(bf16[128,2176]{1,0:T(8,128)(2,1)S(1)} %collective-permute-done.2.refs_0_, bf16[128,2176]{1,0:T(8,128)(2,1)S(1)} %collective-permute-done.3.refs_1_, f32[2,128]{1,0:T(2,128)S(1)} %compare_convert_fusion.refs_2_.refs_1_, ...), custom_call_target="tpu_custom_call" | custom-call | flops 4831838208 | bytes 2097152 | tf_op jit(solution)/shard_map/pallas_call | solution.py:106
  53.1 0.0 copy-start.1
  53.2 8.4 %shard_map.86 = (bf16[128,2048]{1,0:T(8,128)(2,1)S(1)}, bf16[128,2048]{1,0:T(8,128)(2,1)S(1)}, f32[2,128]{1,0:T(2,128)S(1)}) custom-call(bf16[128,2176]{1,0:T(8,128)(2,1)} %collective-permute-done.refs_0_, bf16[128,2176]{1,0:T(8,128)(2,1)} %collective-permute-done.1.refs_1_, f32[2,128]{1,0:T(2,128)S(1)} %compare_convert_fusion.refs_2_.refs_1_, ...), custom_call_target="tpu_custom_call" | custom-call | flops 4831838208 | bytes 2097152 | tf_op jit(solution)/shard_map/pallas_call | solution.py:106
  61.6 0.0 collective-permute-done.4.refs_0_
  61.6 0.0 collective-permute-done.5.refs_1_
  61.7 0.5 collective-permute-start.10
  62.2 1.8 %collective-permute-start.9 = (bf16[64,2176]{1,0:T(8,128)(2,1)S(1)}, bf16[64,2176]{1,0:T(8,128)(2,1)S(1)}, u32[]{:S(2)}, u32[]{:S(2)}) collective-permute-start(bf16[64,2176]{1,0:T(8,128)(2,1)S(1)} %slice.9), channel_id=1, source_target_pairs={{0,4},{1,5},{4,8},{5,9},{8,12},{9,13},{12,14},{13,15},{14,10},{15,... | collective-permute-start | bytes 835592 | tf_op jit(solution)/shard_map/ppermute | solution.py:134
  64.0 8.1 %shard_map.88 = (bf16[128,2048]{1,0:T(8,128)(2,1)S(1)}, bf16[128,2048]{1,0:T(8,128)(2,1)S(1)}, f32[2,128]{1,0:T(2,128)S(1)}) custom-call(bf16[128,2176]{1,0:T(8,128)(2,1)S(1)} %collective-permute-done.4.refs_0_, bf16[128,2176]{1,0:T(8,128)(2,1)S(1)} %collective-permute-done.5.refs_1_, f32[2,128]{1,0:T(2,128)S(1)} %compare_convert_fusion.refs_2_.refs_1_, ...), custom_call_target="tpu_custom_call" | custom-call | flops 4831838208 | bytes 2097152 | tf_op jit(solution)/shard_map/pallas_call | solution.py:106
  72.1 0.0 collective-permute-done.10.refs_1_
  72.1 0.0 collective-permute-done.9.refs_0_
  72.1 5.6 %shard_map.89 = (bf16[64,2048]{1,0:T(8,128)(2,1)S(1)}, bf16[64,2048]{1,0:T(8,128)(2,1)S(1)}, f32[2,128]{1,0:T(2,128)S(1)}) custom-call(bf16[64,2176]{1,0:T(8,128)(2,1)S(1)} %collective-permute-done.9.refs_0_, bf16[64,2176]{1,0:T(8,128)(2,1)S(1)} %collective-permute-done.10.refs_1_, f32[2,128]{1,0:T(2,128)S(1)} %compare_convert_fusion.refs_2_.refs_1_, ...), custom_call_target="tpu_custom_call" | custom-call | flops 2415919104 | bytes 1048576 | tf_op jit(solution)/shard_map/pallas_call | solution.py:106
  77.7 1.6 %collective-permute-start.12 = (bf16[64,2048]{1,0:T(8,128)(2,1)S(1)}, bf16[64,2048]{1,0:T(8,128)(2,1)S(1)}, u32[]{:S(2)}, u32[]{:S(2)}) collective-permute-start(bf16[64,2048]{1,0:T(8,128)(2,1)S(1)} %get-tuple-element.63), channel_id=1, source_target_pairs={{0,4},{1,5},{4,8},{5,9},{8,12},{9,13},{12,14},{13,15},{14,10},{15,... | collective-permute-start | bytes 786440 | tf_op jit(solution)/shard_map/ppermute | solution.py:134
  79.3 0.4 collective-permute-start.11
  79.8 4.3 %collective-permute-done.12 = bf16[64,2048]{1,0:T(8,128)(2,1)S(1)} collective-permute-done((bf16[64,2048]{1,0:T(8,128)(2,1)S(1)}, bf16[64,2048]{1,0:T(8,128)(2,1)S(1)}, u32[]{:S(2)}, u32[]{:S(2)}) %collective-permute-start.12) | collective-permute-done | bytes 262176 | tf_op jit(solution)/shard_map/ppermute | solution.py:134
  84.1 0.1 add_convert_fusion.5
  84.2 1.6 %collective-permute-done.11 = bf16[64,2048]{1,0:T(8,128)(2,1)S(1)} collective-permute-done((bf16[64,2048]{1,0:T(8,128)(2,1)S(1)}, bf16[64,2048]{1,0:T(8,128)(2,1)S(1)}, u32[]{:S(2)}, u32[]{:S(2)}) %collective-permute-start.11) | collective-permute-done | bytes 262176 | tf_op jit(solution)/shard_map/ppermute | solution.py:135
  85.8 0.1 add_convert_fusion.6
  85.9 2.6 %collective-permute-start.14 = (bf16[128,2048]{1,0:T(8,128)(2,1)S(1)}, bf16[128,2048]{1,0:T(8,128)(2,1)S(1)}, u32[]{:S(2)}, u32[]{:S(2)}) collective-permute-start(bf16[128,2048]{1,0:T(8,128)(2,1)S(1)} %add_convert_fusion.5), channel_id=1, source_target_pairs={{0,4},{1,5},{4,8},{5,9},{8,12},{9,13},{12,14},{13,15},{14,10},{15,... | collective-permute-start | bytes 1572872 | tf_op jit(solution)/shard_map/ppermute | solution.py:134
  88.5 0.0 collective-permute-start.13
  88.5 8.5 %collective-permute-done.14 = bf16[128,2048]{1,0:T(8,128)(2,1)S(1)} collective-permute-done((bf16[128,2048]{1,0:T(8,128)(2,1)S(1)}, bf16[128,2048]{1,0:T(8,128)(2,1)S(1)}, u32[]{:S(2)}, u32[]{:S(2)}) %collective-permute-start.14) | collective-permute-done | bytes 524320 | tf_op jit(solution)/shard_map/ppermute | solution.py:134
  97.0 0.1 add_convert_fusion.3
  97.1 2.6 %collective-permute-done.13 = bf16[128,2048]{1,0:T(8,128)(2,1)S(1)} collective-permute-done((bf16[128,2048]{1,0:T(8,128)(2,1)S(1)}, bf16[128,2048]{1,0:T(8,128)(2,1)S(1)}, u32[]{:S(2)}, u32[]{:S(2)}) %collective-permute-start.13) | collective-permute-done | bytes 524320 | tf_op jit(solution)/shard_map/ppermute | solution.py:135
  99.7 0.1 add_convert_fusion.4
  99.9 0.9 collective-permute-start.16
  100.8 1.2 collective-permute-start.15
  102.0 9.3 %collective-permute-done.16 = bf16[128,2048]{1,0:T(8,128)(2,1)S(1)} collective-permute-done((bf16[128,2048]{1,0:T(8,128)(2,1)S(1)}, bf16[128,2048]{1,0:T(8,128)(2,1)S(1)}, u32[]{:S(2)}, u32[]{:S(2)}) %collective-permute-start.16) | collective-permute-done | bytes 524320 | tf_op jit(solution)/shard_map/ppermute | solution.py:134
  111.3 0.9 add_convert_fusion.1
  112.2 0.7 collective-permute-done.15
  113.0 0.9 add_convert_fusion.2
  113.9 2.1 %collective-permute-start.17 = (bf16[128,2048]{1,0:T(8,128)(2,1)}, bf16[128,2048]{1,0:T(8,128)(2,1)}, u32[]{:S(2)}, u32[]{:S(2)}) collective-permute-start(bf16[128,2048]{1,0:T(8,128)(2,1)} %add_convert_fusion.2), channel_id=1, source_target_pairs={{0,2},{1,3},{4,0},{5,1},{8,4},{9,5},{12,8},{13,9},{14,12},{15,13},... | collective-permute-start | bytes 1572872 | tf_op jit(solution)/shard_map/ppermute | solution.py:135
  116.0 0.0 collective-permute-start.18
  116.0 5.5 %shard_map.90 = (bf16[128,2048]{1,0:T(8,128)(2,1)S(1)}, f32[2,128]{1,0:T(2,128)S(1)}) custom-call(bf16[128,2176]{1,0:T(8,128)(2,1)S(1)} %copy-done.4, f32[2,128]{1,0:T(2,128)S(1)} %compare_convert_fusion.refs_2_.refs_1_, bf16[128,256]{1,0:T(8,128)(2,1)S(1)} %select_convert_fusion.refs_3_.refs_2_, bf16[2048,768]{1,0:T(8,128)(2,1)S(1)} %bitcast.14, ...), custom_call_target="tpu_custom_call" | custom-call | flops 2415919104 | bytes 1048576 | tf_op jit(solution)/shard_map/pallas_call | solution.py:106
  121.5 0.8 copy-done.5
  122.3 0.0 collective-permute-start.19
  122.3 1.1 collective-permute-done.19
  123.5 0.6 multiply_reduce_fusion
  124.1 0.6 fusion.2
  125.3 0.0 collective-permute-done.17
  125.3 0.2 collective-permute-done.18
  125.5 2.4 %add_convert_fusion = bf16[128,2048]{1,0:T(8,128)(2,1)} fusion(bf16[128,2048]{1,0:T(8,128)(2,1)} %collective-permute-done.18, bf16[128,2048]{1,0:T(8,128)(2,1)} %collective-permute-done.17, bf16[128,2048]{1,0:T(8,128)(2,1)} %copy-done.5), kind=kLoop, calls=%fused_computation | loop fusion | flops 1572864 | bytes 2097152 | tf_op jit(solution)/shard_map/convert_element_type | solution.py:159
  (14 shorter events, 0.1 us)
Async XLA Ops:
  0.6 38.8 %collective-permute-start.6 = (bf16[2048,768]{1,0:T(8,128)(2,1)}, bf16[2048,768]{1,0:T(8,128)(2,1)S(1)}, u32[]{:S(2)}, u32[]{:S(2)}) collective-permute-start(bf16[2048,768]{1,0:T(8,128)(2,1)} %bitcast.9), channel_id=1, source_target_pairs={{0,1},{1,0},{2,3},{3,2},{4,5},{5,4},{6,7},{7,6},{8,9},{9,8},{10,11... | collective-permute-start | bytes 9437192 | tf_op jit(solution)/shard_map/ppermute | solution.py:136
  1.1 38.2 %collective-permute-start.7 = (bf16[2048,768]{1,0:T(8,128)(2,1)}, bf16[2048,768]{1,0:T(8,128)(2,1)}, u32[]{:S(2)}, u32[]{:S(2)}) collective-permute-start(bf16[2048,768]{1,0:T(8,128)(2,1)} %bitcast.15), channel_id=1, source_target_pairs={{0,1},{1,0},{2,3},{3,2},{4,5},{5,4},{6,7},{7,6},{8,9},{9,8},{10,11... | collective-permute-start | bytes 9437192 | tf_op jit(solution)/shard_map/ppermute | solution.py:136
  1.2 38.2 %collective-permute-start.8 = (bf16[768,2048]{1,0:T(8,128)(2,1)}, bf16[768,2048]{1,0:T(8,128)(2,1)}, u32[]{:S(2)}, u32[]{:S(2)}) collective-permute-start(bf16[768,2048]{1,0:T(8,128)(2,1)} %bitcast.21), channel_id=1, source_target_pairs={{0,1},{1,0},{2,3},{3,2},{4,5},{5,4},{6,7},{7,6},{8,9},{9,8},{10,11... | collective-permute-start | bytes 9437192 | tf_op jit(solution)/shard_map/ppermute | solution.py:136
  4.3 16.2 %collective-permute-start = (bf16[128,2176]{1,0:T(8,128)(2,1)}, bf16[128,2176]{1,0:T(8,128)(2,1)}, u32[]{:S(2)}, u32[]{:S(2)}) collective-permute-start(bf16[128,2176]{1,0:T(8,128)(2,1)} %shard_map.85.refs_0_), channel_id=1, source_target_pairs={{0,4},{1,5},{4,8},{5,9},{8,12},{9,13},{12,14},{13,15},{14,10},{15,... | collective-permute-start | bytes 1671176 | tf_op jit(solution)/shard_map/ppermute | solution.py:134
  7.0 15.0 %collective-permute-start.1 = (bf16[128,2176]{1,0:T(8,128)(2,1)}, bf16[128,2176]{1,0:T(8,128)(2,1)}, u32[]{:S(2)}, u32[]{:S(2)}) collective-permute-start(bf16[128,2176]{1,0:T(8,128)(2,1)} %shard_map.85.refs_0_), channel_id=1, source_target_pairs={{0,2},{1,3},{4,0},{5,1},{8,4},{9,5},{12,8},{13,9},{14,12},{15,13},... | collective-permute-start | bytes 1671176 | tf_op jit(solution)/shard_map/ppermute | solution.py:135
  22.0 14.1 %collective-permute-start.2 = (bf16[128,2176]{1,0:T(8,128)(2,1)}, bf16[128,2176]{1,0:T(8,128)(2,1)S(1)}, u32[]{:S(2)}, u32[]{:S(2)}) collective-permute-start(bf16[128,2176]{1,0:T(8,128)(2,1)} %collective-permute-done.refs_0_), channel_id=1, source_target_pairs={{0,4},{1,5},{4,8},{5,9},{8,12},{9,13},{12,14},{13,15},{14,10},{15,... | collective-permute-start | bytes 1671176 | tf_op jit(solution)/shard_map/ppermute | solution.py:134
  23.6 13.8 %collective-permute-start.3 = (bf16[128,2176]{1,0:T(8,128)(2,1)}, bf16[128,2176]{1,0:T(8,128)(2,1)S(1)}, u32[]{:S(2)}, u32[]{:S(2)}) collective-permute-start(bf16[128,2176]{1,0:T(8,128)(2,1)} %collective-permute-done.1.refs_1_), channel_id=1, source_target_pairs={{0,2},{1,3},{4,0},{5,1},{8,4},{9,5},{12,8},{13,9},{14,12},{15,13},... | collective-permute-start | bytes 1671176 | tf_op jit(solution)/shard_map/ppermute | solution.py:135
  37.4 24.3 %collective-permute-start.4 = (bf16[128,2176]{1,0:T(8,128)(2,1)S(1)}, bf16[128,2176]{1,0:T(8,128)(2,1)S(1)}, u32[]{:S(2)}, u32[]{:S(2)}) collective-permute-start(bf16[128,2176]{1,0:T(8,128)(2,1)S(1)} %collective-permute-done.2.refs_0_), channel_id=1, source_target_pairs={{0,4},{1,5},{4,8},{5,9},{8,12},{9,13},{12,14},{13,15},{14,10},{15,... | collective-permute-start | bytes 1671176 | tf_op jit(solution)/shard_map/ppermute | solution.py:134
  38.9 22.7 %collective-permute-start.5 = (bf16[128,2176]{1,0:T(8,128)(2,1)S(1)}, bf16[128,2176]{1,0:T(8,128)(2,1)S(1)}, u32[]{:S(2)}, u32[]{:S(2)}) collective-permute-start(bf16[128,2176]{1,0:T(8,128)(2,1)S(1)} %collective-permute-done.3.refs_1_), channel_id=1, source_target_pairs={{0,2},{1,3},{4,0},{5,1},{8,4},{9,5},{12,8},{13,9},{14,12},{15,13},... | collective-permute-start | bytes 1671176 | tf_op jit(solution)/shard_map/ppermute | solution.py:135
  39.4 1.9 %copy-start = (bf16[1,2048,768]{2,1,0:T(8,128)(2,1)S(1)}, bf16[1,2048,768]{2,1,0:T(8,128)(2,1)}, u32[]{:S(2)}) copy-start(bf16[1,2048,768]{2,1,0:T(8,128)(2,1)} %param.9) | copy-start | bytes 9437188
  41.3 1.9 %copy-start.2 = (bf16[1,2048,768]{2,1,0:T(8,128)(2,1)S(1)}, bf16[1,2048,768]{2,1,0:T(8,128)(2,1)}, u32[]{:S(2)}) copy-start(bf16[1,2048,768]{2,1,0:T(8,128)(2,1)} %param.10) | copy-start | bytes 9437188
  43.2 1.9 %copy-start.3 = (bf16[1,768,2048]{2,1,0:T(8,128)(2,1)S(1)}, bf16[1,768,2048]{2,1,0:T(8,128)(2,1)}, u32[]{:S(2)}) copy-start(bf16[1,768,2048]{2,1,0:T(8,128)(2,1)} %param.11) | copy-start | bytes 9437188
  53.1 10.8 %copy-start.1 = (bf16[1,2048,768]{2,1,0:T(8,128)(2,1)S(1)}, bf16[1,2048,768]{2,1,0:T(8,128)(2,1)}, u32[]{:S(2)}) copy-start(bf16[1,2048,768]{2,1,0:T(8,128)(2,1)} %param.9) | copy-start | bytes 9437188
  61.7 10.4 %collective-permute-start.10 = (bf16[64,2176]{1,0:T(8,128)(2,1)S(1)}, bf16[64,2176]{1,0:T(8,128)(2,1)S(1)}, u32[]{:S(2)}, u32[]{:S(2)}) collective-permute-start(bf16[64,2176]{1,0:T(8,128)(2,1)S(1)} %slice.10), channel_id=1, source_target_pairs={{0,2},{1,3},{4,0},{5,1},{8,4},{9,5},{12,8},{13,9},{14,12},{15,13},... | collective-permute-start | bytes 835592 | tf_op jit(solution)/shard_map/ppermute | solution.py:135
  62.2 9.9 %collective-permute-start.9 = (bf16[64,2176]{1,0:T(8,128)(2,1)S(1)}, bf16[64,2176]{1,0:T(8,128)(2,1)S(1)}, u32[]{:S(2)}, u32[]{:S(2)}) collective-permute-start(bf16[64,2176]{1,0:T(8,128)(2,1)S(1)} %slice.9), channel_id=1, source_target_pairs={{0,4},{1,5},{4,8},{5,9},{8,12},{9,13},{12,14},{13,15},{14,10},{15,... | collective-permute-start | bytes 835592 | tf_op jit(solution)/shard_map/ppermute | solution.py:134
  77.7 6.4 %collective-permute-start.12 = (bf16[64,2048]{1,0:T(8,128)(2,1)S(1)}, bf16[64,2048]{1,0:T(8,128)(2,1)S(1)}, u32[]{:S(2)}, u32[]{:S(2)}) collective-permute-start(bf16[64,2048]{1,0:T(8,128)(2,1)S(1)} %get-tuple-element.63), channel_id=1, source_target_pairs={{0,4},{1,5},{4,8},{5,9},{8,12},{9,13},{12,14},{13,15},{14,10},{15,... | collective-permute-start | bytes 786440 | tf_op jit(solution)/shard_map/ppermute | solution.py:134
  79.3 6.4 %collective-permute-start.11 = (bf16[64,2048]{1,0:T(8,128)(2,1)S(1)}, bf16[64,2048]{1,0:T(8,128)(2,1)S(1)}, u32[]{:S(2)}, u32[]{:S(2)}) collective-permute-start(bf16[64,2048]{1,0:T(8,128)(2,1)S(1)} %get-tuple-element.61), channel_id=1, source_target_pairs={{0,2},{1,3},{4,0},{5,1},{8,4},{9,5},{12,8},{13,9},{14,12},{15,13},... | collective-permute-start | bytes 786440 | tf_op jit(solution)/shard_map/ppermute | solution.py:135
  85.9 30.1 %copy-start.4 = (bf16[128,2176]{1,0:T(8,128)(2,1)S(1)}, bf16[128,2176]{1,0:T(8,128)(2,1)}, u32[]{:S(2)}) copy-start(bf16[128,2176]{1,0:T(8,128)(2,1)} %shard_map.85.refs_0_) | copy-start | bytes 1671172
  85.9 11.1 %collective-permute-start.14 = (bf16[128,2048]{1,0:T(8,128)(2,1)S(1)}, bf16[128,2048]{1,0:T(8,128)(2,1)S(1)}, u32[]{:S(2)}, u32[]{:S(2)}) collective-permute-start(bf16[128,2048]{1,0:T(8,128)(2,1)S(1)} %add_convert_fusion.5), channel_id=1, source_target_pairs={{0,4},{1,5},{4,8},{5,9},{8,12},{9,13},{12,14},{13,15},{14,10},{15,... | collective-permute-start | bytes 1572872 | tf_op jit(solution)/shard_map/ppermute | solution.py:134
  88.5 11.3 %collective-permute-start.13 = (bf16[128,2048]{1,0:T(8,128)(2,1)S(1)}, bf16[128,2048]{1,0:T(8,128)(2,1)S(1)}, u32[]{:S(2)}, u32[]{:S(2)}) collective-permute-start(bf16[128,2048]{1,0:T(8,128)(2,1)S(1)} %add_convert_fusion.6), channel_id=1, source_target_pairs={{0,2},{1,3},{4,0},{5,1},{8,4},{9,5},{12,8},{13,9},{14,12},{15,13},... | collective-permute-start | bytes 1572872 | tf_op jit(solution)/shard_map/ppermute | solution.py:135
  99.9 11.4 %collective-permute-start.16 = (bf16[128,2048]{1,0:T(8,128)(2,1)S(1)}, bf16[128,2048]{1,0:T(8,128)(2,1)S(1)}, u32[]{:S(2)}, u32[]{:S(2)}) collective-permute-start(bf16[128,2048]{1,0:T(8,128)(2,1)S(1)} %add_convert_fusion.3), channel_id=1, source_target_pairs={{0,4},{1,5},{4,8},{5,9},{8,12},{9,13},{12,14},{13,15},{14,10},{15,... | collective-permute-start | bytes 1572872 | tf_op jit(solution)/shard_map/ppermute | solution.py:134
  100.8 12.2 %collective-permute-start.15 = (bf16[128,2048]{1,0:T(8,128)(2,1)S(1)}, bf16[128,2048]{1,0:T(8,128)(2,1)S(1)}, u32[]{:S(2)}, u32[]{:S(2)}) collective-permute-start(bf16[128,2048]{1,0:T(8,128)(2,1)S(1)} %add_convert_fusion.4), channel_id=1, source_target_pairs={{0,2},{1,3},{4,0},{5,1},{8,4},{9,5},{12,8},{13,9},{14,12},{15,13},... | collective-permute-start | bytes 1572872 | tf_op jit(solution)/shard_map/ppermute | solution.py:135
  113.9 11.4 %collective-permute-start.17 = (bf16[128,2048]{1,0:T(8,128)(2,1)}, bf16[128,2048]{1,0:T(8,128)(2,1)}, u32[]{:S(2)}, u32[]{:S(2)}) collective-permute-start(bf16[128,2048]{1,0:T(8,128)(2,1)} %add_convert_fusion.2), channel_id=1, source_target_pairs={{0,2},{1,3},{4,0},{5,1},{8,4},{9,5},{12,8},{13,9},{14,12},{15,13},... | collective-permute-start | bytes 1572872 | tf_op jit(solution)/shard_map/ppermute | solution.py:135
  116.0 9.5 %collective-permute-start.18 = (bf16[128,2048]{1,0:T(8,128)(2,1)}, bf16[128,2048]{1,0:T(8,128)(2,1)}, u32[]{:S(2)}, u32[]{:S(2)}) collective-permute-start(bf16[128,2048]{1,0:T(8,128)(2,1)} %add_convert_fusion.1), channel_id=1, source_target_pairs={{0,4},{1,5},{4,8},{5,9},{8,12},{9,13},{12,14},{13,15},{14,10},{15,... | collective-permute-start | bytes 1572872 | tf_op jit(solution)/shard_map/ppermute | solution.py:134
  121.5 0.8 copy-start.5
  122.3 1.1 collective-permute-start.19

commit v5 on v4

--- a/solution.py
+++ b/solution.py
@@ -9,7 +9,7 @@
 
 CORES = 2
 LANES = 128
-VMEM_LIMIT = 24 * 1024 * 1024
+VMEM_LIMIT = 20 * 1024 * 1024
 HIDDEN_CHUNK = 256
 OUT_CHUNK = 512
 
@@ -63,13 +63,19 @@
     count = len(sizes)
     blocks = refs[:count]
     own_ref, join_ref = refs[count : count + 2]
-    experts = [refs[count + 2 + 3 * i : count + 5 + 3 * i] for i in range(CORES)]
-    refs = refs[count + 2 + 3 * CORES :]
-    outs = refs[:count]
-    stats_ref, hidden_ref = refs[count:]
+    own_weights, far_weights = refs[count + 2 : count + 5], refs[count + 5 : count + 8]
+    outs = refs[count + 8 : 2 * count + 8]
+    stats_ref, hidden_ref, *held, arrived = refs[2 * count + 8 :]
+    experts = [own_weights, held]
     starts = [sum(sizes[:i]) for i in range(count)]
-    width, hidden_width = experts[0][0].shape
+    width, hidden_width = own_weights[0].shape
     lanes = join_ref.shape[0]
+
+    copies = [
+        pltpu.make_async_copy(far_weights[i], held[i], arrived.at[i]) for i in range(len(held))
+    ]
+    for copy in copies:
+        copy.start()
 
     scores = jnp.concatenate([block[:, width:] for block in blocks], axis=0)
     joined = jnp.dot(scores, join_ref[...], preferred_element_type=jnp.float32)
@@ -82,11 +88,15 @@
 
     rows = jnp.concatenate([block[:, :width] for block in blocks], axis=0)
     for i, (gate_ref, up_ref, _) in enumerate(experts):
+        if i:
+            copies[0].wait()
+            copies[1].wait()
         for start in range(0, hidden_width, HIDDEN_CHUNK):
             at = slice(start, start + HIDDEN_CHUNK)
             gate = jnp.dot(rows, gate_ref[:, at], preferred_element_type=jnp.float32)
             up = jnp.dot(rows, up_ref[:, at], preferred_element_type=jnp.float32)
             hidden_ref[i, :, at] = (gate / (1.0 + jnp.exp(-gate)) * up).astype(jnp.bfloat16)
+    copies[2].wait()
     for start in range(0, width, OUT_CHUNK):
         at = slice(start, start + OUT_CHUNK)
         total = 0.0
@@ -107,9 +117,11 @@
         functools.partial(expert_kernel, sizes),
         out_shape=[jax.ShapeDtypeStruct((size, width), jnp.bfloat16) for size in sizes]
         + [jax.ShapeDtypeStruct((2, own.shape[1]), jnp.float32)],
-        in_specs=[in_vmem] * (count + 2 + len(weights)),
+        in_specs=[in_vmem] * (count + 5) + [pl.BlockSpec(memory_space=pl.ANY)] * 3,
         out_specs=[in_vmem] * (count + 1),
-        scratch_shapes=[pltpu.VMEM((CORES, total, hidden_width), jnp.bfloat16)],
+        scratch_shapes=[pltpu.VMEM((CORES, total, hidden_width), jnp.bfloat16)]
+        + [pltpu.VMEM(weight.shape, jnp.bfloat16) for weight in weights[3:]]
+        + [pltpu.SemaphoreType.DMA((3,))],
         compiler_params=pltpu.CompilerParams(vmem_limit_bytes=VMEM_LIMIT),
         cost_estimate=pl.CostEstimate(
             flops=6 * CORES * total * width * hidden_width,
@@ -159,20 +171,19 @@
         return sum(term.astype(jnp.float32) for term in terms).astype(jnp.bfloat16)
 
     low, high = right(packed), left(packed)
-    blocks, outs, fresh = {}, {}, {}
-    for step in range(2, far + 1):
-        (low, high), fresh = tie(((low, high), fresh))
-        outs.update(fresh)
-        blocks[step - 1] = (low, high)
-        if step < far:
+    outs = {}
+    for k in range(1, far + 1):
+        if k > 1:
+            low, high, outs[k - 1] = tie((low, high, outs[k - 1]))
+        here = low, high
+        if k == far:
+            break
+        if k < far - 1:
             low, high = right(low), left(high)
         else:
             low, high = right(low[:half]), left(high[half:])
-        ready = [k for k in blocks if k not in outs] if step >= min(3, far) else []
-        fresh = {k: run(blocks[k]) for k in ready}
-    (low, high), fresh = tie(((low, high), fresh))
-    outs.update(fresh)
-    low, high = run([low, high])
+        outs[k] = run(here)
+    low, high = run(here)
 
     low, high, packed = tie((low, high, packed))
     (own_rows,) = run([packed])
@@ -182,7 +193,7 @@
             zeros = jnp.zeros_like(low)
             low = jnp.concatenate([low, zeros])
             high = jnp.concatenate([zeros, high])
-        low, high = tie((add(outs[k][0], low), add(outs[k][1], high)))
+        low, high = ((add(outs[k][0], low), add(outs[k][1], high)))
     mixed = add(own_rows, left(low), right(high))
 
     total = sum(stats)

time: 129 us -> 114 us (0.88)
  waiting for transfers between devices: 56.5 us -> 44.2 us
  Pallas kernels: 38.3 us -> 35.5 us
    ppermute x8, waiting for transfers between devices: 47.5 us -> 17.6 us  [body(): right = lambda a: lax.ppermute(a, 'node', to_right)]
    ppermute x8, waiting for transfers between devices: 7.78 us -> 25.4 us  [body(): left = lambda a: lax.ppermute(a, 'node', to_left)]
    ppermute x8, starting transfers between devices: 5.16 us -> 1.9 us  [body(): left = lambda a: lax.ppermute(a, 'node', to_left)]
    ppermute x8, starting transfers between devices: 12.8 us -> 15.6 us  [body(): right = lambda a: lax.ppermute(a, 'node', to_right)]
    pallas_call x5, Pallas kernels: 35.7 us -> 32.9 us  [apply_experts(): pl.pallas_call(functools.partial(expert_kernel, sizes), out_shape=[jax.Sh...]
  transfers between devices with their start and end apart: 20 -> 20, of which waited for: 12 -> 7; matrix products, arithmetic and copies ran while one was open for 2% -> 3% of each run, Pallas kernels for 25% -> 27%
where the time goes in v5:
time: 114 us
  waiting for transfers between devices  44.2 us (39%)
  Pallas kernels  35.5 us (31%)
  starting transfers between devices  18.5 us (16%)
  local copies, waits for them, and re-layouts  6.51 us (6%)
  other arithmetic  6.16 us (5%)
  between operations  2.62 us (2%)
    pallas_call x5, Pallas kernels, apply_experts(): pl.pallas_call(functools.partial(expert_kernel, sizes), out_shape=[jax.Sh...  32.9 us
    ppermute x8, waiting for transfers between devices, body(): left = lambda a: lax.ppermute(a, 'node', to_left)  25.4 us
    ppermute x8, waiting for transfers between devices, body(): right = lambda a: lax.ppermute(a, 'node', to_right)  17.6 us
    ppermute x8, starting transfers between devices, body(): right = lambda a: lax.ppermute(a, 'node', to_right)  15.6 us
    unnamed x12, local copies, waits for them, and re-layouts  6.47 us
    convert_element_type x7, other arithmetic, add(): sum((term.astype(jnp.float32) for term in terms)).astype(jnp.bfloat16)  4.68 us
    pallas_call x1, Pallas kernels, pack(): pl.pallas_call(functools.partial(pack_kernel, experts), out_shape=jax.Sha...  2.59 us
  transfers between devices with their start and end apart: 20, of which 7 were waited for; matrix products, arithmetic and copies ran while one was open for 3% of the time, Pallas kernels for 27%

profile of v5, /device:TPU:0, one launch (start us, length us, event | category | flops | bytes accessed | tf_op | source)
XLA Modules:
  0.0 113.5 jit_solution(12689548926825938383)
XLA Ops:
  0.6 0.5 collective-permute-start.4
  1.1 0.1 collective-permute-start.5
  1.2 0.4 collective-permute-start.6
  1.7 2.6 %shard_map.85.refs_0_ = bf16[128,2176]{1,0:T(8,128)(2,1)} custom-call(bf16[128,2048]{1,0:T(8,128)(2,1)} %tokens_ref.1, s32[8,128]{1,0:T(8,128)} %bitcast.27, s32[8,128]{1,0:T(8,128)} %bitcast.28), custom_call_target="tpu_custom_call" | custom-call | flops 16384 | bytes 1048576 | tf_op jit(solution)/shard_map/pallas_call | solution.py:50
  4.3 2.7 %collective-permute-start = (bf16[128,2176]{1,0:T(8,128)(2,1)}, bf16[128,2176]{1,0:T(8,128)(2,1)}, u32[]{:S(2)}, u32[]{:S(2)}) collective-permute-start(bf16[128,2176]{1,0:T(8,128)(2,1)} %shard_map.85.refs_0_), channel_id=1, source_target_pairs={{0,4},{1,5},{4,8},{5,9},{8,12},{9,13},{12,14},{13,15},{14,10},{15,... | collective-permute-start | bytes 1671176 | tf_op jit(solution)/shard_map/ppermute | solution.py:146
  7.0 0.0 collective-permute-start.2
  7.0 0.1 pad_add_fusion
  7.1 0.1 select_convert_fusion.refs_3_.refs_2_
  7.2 13.2 %collective-permute-done.refs_0_ = bf16[128,2176]{1,0:T(8,128)(2,1)} collective-permute-done((bf16[128,2176]{1,0:T(8,128)(2,1)}, bf16[128,2176]{1,0:T(8,128)(2,1)}, u32[]{:S(2)}, u32[]{:S(2)}) %collective-permute-start) | collective-permute-done | bytes 557088 | tf_op jit(solution)/shard_map/ppermute | solution.py:146
  20.4 1.8 %collective-permute-start.1 = (bf16[128,2176]{1,0:T(8,128)(2,1)}, bf16[128,2176]{1,0:T(8,128)(2,1)S(1)}, u32[]{:S(2)}, u32[]{:S(2)}) collective-permute-start(bf16[128,2176]{1,0:T(8,128)(2,1)} %collective-permute-done.refs_0_), channel_id=1, source_target_pairs={{0,4},{1,5},{4,8},{5,9},{8,12},{9,13},{12,14},{13,15},{14,10},{15,... | collective-permute-start | bytes 1671176 | tf_op jit(solution)/shard_map/ppermute | solution.py:146
  22.3 0.0 collective-permute-done.2.refs_1_
  22.3 0.2 collective-permute-start.3
  22.5 0.1 compare_convert_fusion.refs_2_.refs_1_
  22.5 0.0 collective-permute-done.4.refs_7_.refs_6_
  22.5 0.0 collective-permute-done.5.refs_8_.refs_7_
  22.6 0.0 collective-permute-done.6.refs_9_.refs_8_
  22.6 0.0 copy-start
  22.6 1.9 %copy-done = bf16[1,2048,768]{2,1,0:T(8,128)(2,1)S(1)} copy-done((bf16[1,2048,768]{2,1,0:T(8,128)(2,1)S(1)}, bf16[1,2048,768]{2,1,0:T(8,128)(2,1)}, u32[]{:S(2)}) %copy-start) | copy-done | bytes 3145752
  24.5 1.9 %copy-done.2 = bf16[1,2048,768]{2,1,0:T(8,128)(2,1)S(1)} copy-done((bf16[1,2048,768]{2,1,0:T(8,128)(2,1)S(1)}, bf16[1,2048,768]{2,1,0:T(8,128)(2,1)}, u32[]{:S(2)}) %copy-start.2) | copy-done | bytes 3145752
  26.3 1.9 %copy-done.3 = bf16[1,768,2048]{2,1,0:T(8,128)(2,1)S(1)} copy-done((bf16[1,768,2048]{2,1,0:T(8,128)(2,1)S(1)}, bf16[1,768,2048]{2,1,0:T(8,128)(2,1)}, u32[]{:S(2)}) %copy-start.3) | copy-done | bytes 3145752
  28.2 8.6 %shard_map.86 = (bf16[128,2048]{1,0:T(8,128)(2,1)S(1)}, bf16[128,2048]{1,0:T(8,128)(2,1)S(1)}, f32[2,128]{1,0:T(2,128)S(1)}) custom-call(bf16[128,2176]{1,0:T(8,128)(2,1)} %collective-permute-done.refs_0_, bf16[128,2176]{1,0:T(8,128)(2,1)} %collective-permute-done.2.refs_1_, f32[2,128]{1,0:T(2,128)S(1)} %compare_convert_fusion.refs_2_.refs_1_, ...), custom_call_target="tpu_custom_call" | custom-call | flops 4831838208 | bytes 2097152 | tf_op jit(solution)/shard_map/pallas_call | solution.py:116
  36.8 0.0 collective-permute-done.1.refs_0_
  36.8 0.0 collective-permute-done.3.refs_1_
  36.8 1.9 %collective-permute-start.7 = (bf16[128,2176]{1,0:T(8,128)(2,1)S(1)}, bf16[128,2176]{1,0:T(8,128)(2,1)S(1)}, u32[]{:S(2)}, u32[]{:S(2)}) collective-permute-start(bf16[128,2176]{1,0:T(8,128)(2,1)S(1)} %collective-permute-done.1.refs_0_), channel_id=1, source_target_pairs={{0,4},{1,5},{4,8},{5,9},{8,12},{9,13},{12,14},{13,15},{14,10},{15,... | collective-permute-start | bytes 1671176 | tf_op jit(solution)/shard_map/ppermute | solution.py:146
  38.7 0.2 collective-permute-start.8
  38.9 7.4 %shard_map.87 = (bf16[128,2048]{1,0:T(8,128)(2,1)S(1)}, bf16[128,2048]{1,0:T(8,128)(2,1)S(1)}, f32[2,128]{1,0:T(2,128)S(1)}) custom-call(bf16[128,2176]{1,0:T(8,128)(2,1)S(1)} %collective-permute-done.1.refs_0_, bf16[128,2176]{1,0:T(8,128)(2,1)S(1)} %collective-permute-done.3.refs_1_, f32[2,128]{1,0:T(2,128)S(1)} %compare_convert_fusion.refs_2_.refs_1_, ...), custom_call_target="tpu_custom_call" | custom-call | flops 4831838208 | bytes 2097152 | tf_op jit(solution)/shard_map/pallas_call | solution.py:116
  46.4 4.3 %collective-permute-done.7.refs_0_ = bf16[128,2176]{1,0:T(8,128)(2,1)S(1)} collective-permute-done((bf16[128,2176]{1,0:T(8,128)(2,1)S(1)}, bf16[128,2176]{1,0:T(8,128)(2,1)S(1)}, u32[]{:S(2)}, u32[]{:S(2)}) %collective-permute-start.7) | collective-permute-done | bytes 557088 | tf_op jit(solution)/shard_map/ppermute | solution.py:146
  50.7 1.3 %collective-permute-done.8.refs_1_ = bf16[128,2176]{1,0:T(8,128)(2,1)S(1)} collective-permute-done((bf16[128,2176]{1,0:T(8,128)(2,1)S(1)}, bf16[128,2176]{1,0:T(8,128)(2,1)S(1)}, u32[]{:S(2)}, u32[]{:S(2)}) %collective-permute-start.8) | collective-permute-done | bytes 557088 | tf_op jit(solution)/shard_map/ppermute | solution.py:147
  52.1 0.5 collective-permute-start.10
  52.6 1.9 %collective-permute-start.9 = (bf16[64,2176]{1,0:T(8,128)(2,1)S(1)}, bf16[64,2176]{1,0:T(8,128)(2,1)S(1)}, u32[]{:S(2)}, u32[]{:S(2)}) collective-permute-start(bf16[64,2176]{1,0:T(8,128)(2,1)S(1)} %slice.9), channel_id=1, source_target_pairs={{0,4},{1,5},{4,8},{5,9},{8,12},{9,13},{12,14},{13,15},{14,10},{15,... | collective-permute-start | bytes 835592 | tf_op jit(solution)/shard_map/ppermute | solution.py:146
  54.4 0.0 copy-done.1
  54.4 7.4 %shard_map.88 = (bf16[128,2048]{1,0:T(8,128)(2,1)S(1)}, bf16[128,2048]{1,0:T(8,128)(2,1)S(1)}, f32[2,128]{1,0:T(2,128)S(1)}) custom-call(bf16[128,2176]{1,0:T(8,128)(2,1)S(1)} %collective-permute-done.7.refs_0_, bf16[128,2176]{1,0:T(8,128)(2,1)S(1)} %collective-permute-done.8.refs_1_, f32[2,128]{1,0:T(2,128)S(1)} %compare_convert_fusion.refs_2_.refs_1_, ...), custom_call_target="tpu_custom_call" | custom-call | flops 4831838208 | bytes 2097152 | tf_op jit(solution)/shard_map/pallas_call | solution.py:116
  61.9 0.0 collective-permute-done.10.refs_1_
  61.9 0.0 collective-permute-done.9.refs_0_
  61.9 4.7 %shard_map.89 = (bf16[64,2048]{1,0:T(8,128)(2,1)S(1)}, bf16[64,2048]{1,0:T(8,128)(2,1)S(1)}, f32[2,128]{1,0:T(2,128)S(1)}) custom-call(bf16[64,2176]{1,0:T(8,128)(2,1)S(1)} %collective-permute-done.9.refs_0_, bf16[64,2176]{1,0:T(8,128)(2,1)S(1)} %collective-permute-done.10.refs_1_, f32[2,128]{1,0:T(2,128)S(1)} %compare_convert_fusion.refs_2_.refs_1_, ...), custom_call_target="tpu_custom_call" | custom-call | flops 2415919104 | bytes 1048576 | tf_op jit(solution)/shard_map/pallas_call | solution.py:116
  66.7 0.5 collective-permute-start.11
  67.1 1.6 %collective-permute-start.15 = (bf16[64,2048]{1,0:T(8,128)(2,1)S(1)}, bf16[64,2048]{1,0:T(8,128)(2,1)S(1)}, u32[]{:S(2)}, u32[]{:S(2)}) collective-permute-start(bf16[64,2048]{1,0:T(8,128)(2,1)S(1)} %get-tuple-element.55), channel_id=1, source_target_pairs={{0,4},{1,5},{4,8},{5,9},{8,12},{9,13},{12,14},{13,15},{14,10},{15,... | collective-permute-start | bytes 786440 | tf_op jit(solution)/shard_map/ppermute | solution.py:146
  68.7 5.4 %collective-permute-done.11 = bf16[64,2048]{1,0:T(8,128)(2,1)S(1)} collective-permute-done((bf16[64,2048]{1,0:T(8,128)(2,1)S(1)}, bf16[64,2048]{1,0:T(8,128)(2,1)S(1)}, u32[]{:S(2)}, u32[]{:S(2)}) %collective-permute-start.11) | collective-permute-done | bytes 262176 | tf_op jit(solution)/shard_map/ppermute | solution.py:147
  74.1 0.1 add_convert_fusion.6
  74.2 0.3 collective-permute-start.12
  74.4 0.0 collective-permute-done.15
  74.5 0.1 add_convert_fusion.3
  74.5 1.9 %collective-permute-start.16 = (bf16[128,2048]{1,0:T(8,128)(2,1)S(1)}, bf16[128,2048]{1,0:T(8,128)(2,1)S(1)}, u32[]{:S(2)}, u32[]{:S(2)}) collective-permute-start(bf16[128,2048]{1,0:T(8,128)(2,1)S(1)} %add_convert_fusion.3), channel_id=1, source_target_pairs={{0,4},{1,5},{4,8},{5,9},{8,12},{9,13},{12,14},{13,15},{14,10},{15,... | collective-permute-start | bytes 1572872 | tf_op jit(solution)/shard_map/ppermute | solution.py:146
  76.4 9.7 %collective-permute-done.12 = bf16[128,2048]{1,0:T(8,128)(2,1)S(1)} collective-permute-done((bf16[128,2048]{1,0:T(8,128)(2,1)S(1)}, bf16[128,2048]{1,0:T(8,128)(2,1)S(1)}, u32[]{:S(2)}, u32[]{:S(2)}) %collective-permute-start.12) | collective-permute-done | bytes 524320 | tf_op jit(solution)/shard_map/ppermute | solution.py:147
  86.1 0.1 add_convert_fusion.5
  86.3 0.3 collective-permute-start.13
  86.5 0.0 collective-permute-done.16
  86.5 0.2 add_convert_fusion.2
  86.7 1.9 %collective-permute-start.17 = (bf16[128,2048]{1,0:T(8,128)(2,1)S(1)}, bf16[128,2048]{1,0:T(8,128)(2,1)S(1)}, u32[]{:S(2)}, u32[]{:S(2)}) collective-permute-start(bf16[128,2048]{1,0:T(8,128)(2,1)S(1)} %add_convert_fusion.2), channel_id=1, source_target_pairs={{0,4},{1,5},{4,8},{5,9},{8,12},{9,13},{12,14},{13,15},{14,10},{15,... | collective-permute-start | bytes 1572872 | tf_op jit(solution)/shard_map/ppermute | solution.py:146
  88.6 9.0 %collective-permute-done.13 = bf16[128,2048]{1,0:T(8,128)(2,1)S(1)} collective-permute-done((bf16[128,2048]{1,0:T(8,128)(2,1)S(1)}, bf16[128,2048]{1,0:T(8,128)(2,1)S(1)}, u32[]{:S(2)}, u32[]{:S(2)}) %collective-permute-start.13) | collective-permute-done | bytes 524320 | tf_op jit(solution)/shard_map/ppermute | solution.py:147
  97.5 0.9 add_convert_fusion.4
  98.5 0.0 collective-permute-start.14
  98.5 0.0 collective-permute-done.17
  98.5 0.9 add_convert_fusion.1
  99.4 2.0 %collective-permute-start.18 = (bf16[128,2048]{1,0:T(8,128)(2,1)}, bf16[128,2048]{1,0:T(8,128)(2,1)}, u32[]{:S(2)}, u32[]{:S(2)}) collective-permute-start(bf16[128,2048]{1,0:T(8,128)(2,1)} %add_convert_fusion.1), channel_id=1, source_target_pairs={{0,4},{1,5},{4,8},{5,9},{8,12},{9,13},{12,14},{13,15},{14,10},{15,... | collective-permute-start | bytes 1572872 | tf_op jit(solution)/shard_map/ppermute | solution.py:146
  101.4 4.7 %shard_map.90 = (bf16[128,2048]{1,0:T(8,128)(2,1)S(1)}, f32[2,128]{1,0:T(2,128)S(1)}) custom-call(bf16[128,2176]{1,0:T(8,128)(2,1)S(1)} %copy-done.4, f32[2,128]{1,0:T(2,128)S(1)} %compare_convert_fusion.refs_2_.refs_1_, bf16[128,256]{1,0:T(8,128)(2,1)S(1)} %select_convert_fusion.refs_3_.refs_2_, bf16[2048,768]{1,0:T(8,128)(2,1)S(1)} %bitcast.14, ...), custom_call_target="tpu_custom_call" | custom-call | flops 2415919104 | bytes 1048576 | tf_op jit(solution)/shard_map/pallas_call | solution.py:116
  106.2 0.8 copy-done.5
  107.0 0.0 collective-permute-start.19
  107.0 1.1 %collective-permute-done.19 = f32[2,128]{1,0:T(2,128)S(1)} collective-permute-done((f32[2,128]{1,0:T(2,128)S(1)}, f32[2,128]{1,0:T(2,128)S(1)}, u32[]{:S(2)}, u32[]{:S(2)}) %collective-permute-start.19) | collective-permute-done | bytes 1056 | tf_op jit(solution)/shard_map/ppermute | solution.py:148
  108.1 0.6 multiply_reduce_fusion
  108.7 0.6 fusion.2
  110.0 0.0 collective-permute-done.14
  110.0 0.0 collective-permute-done.18
  110.0 2.4 %add_convert_fusion = bf16[128,2048]{1,0:T(8,128)(2,1)} fusion(bf16[128,2048]{1,0:T(8,128)(2,1)} %collective-permute-done.18, bf16[128,2048]{1,0:T(8,128)(2,1)} %collective-permute-done.14, bf16[128,2048]{1,0:T(8,128)(2,1)} %copy-done.5), kind=kLoop, calls=%fused_computation | loop fusion | flops 1572864 | bytes 2097152 | tf_op jit(solution)/shard_map/convert_element_type | solution.py:171
  (14 shorter events, 0.1 us)
Async XLA Ops:
  0.6 21.9 %collective-permute-start.4 = (bf16[2048,768]{1,0:T(8,128)(2,1)}, bf16[2048,768]{1,0:T(8,128)(2,1)S(1)}, u32[]{:S(2)}, u32[]{:S(2)}) collective-permute-start(bf16[2048,768]{1,0:T(8,128)(2,1)} %bitcast.9), channel_id=1, source_target_pairs={{0,1},{1,0},{2,3},{3,2},{4,5},{5,4},{6,7},{7,6},{8,9},{9,8},{10,11... | collective-permute-start | bytes 9437192 | tf_op jit(solution)/shard_map/ppermute | solution.py:148
  1.1 21.4 %collective-permute-start.5 = (bf16[2048,768]{1,0:T(8,128)(2,1)}, bf16[2048,768]{1,0:T(8,128)(2,1)}, u32[]{:S(2)}, u32[]{:S(2)}) collective-permute-start(bf16[2048,768]{1,0:T(8,128)(2,1)} %bitcast.15), channel_id=1, source_target_pairs={{0,1},{1,0},{2,3},{3,2},{4,5},{5,4},{6,7},{7,6},{8,9},{9,8},{10,11... | collective-permute-start | bytes 9437192 | tf_op jit(solution)/shard_map/ppermute | solution.py:148
  1.2 21.3 %collective-permute-start.6 = (bf16[768,2048]{1,0:T(8,128)(2,1)}, bf16[768,2048]{1,0:T(8,128)(2,1)}, u32[]{:S(2)}, u32[]{:S(2)}) collective-permute-start(bf16[768,2048]{1,0:T(8,128)(2,1)} %bitcast.21), channel_id=1, source_target_pairs={{0,1},{1,0},{2,3},{3,2},{4,5},{5,4},{6,7},{7,6},{8,9},{9,8},{10,11... | collective-permute-start | bytes 9437192 | tf_op jit(solution)/shard_map/ppermute | solution.py:148
  4.3 16.2 %collective-permute-start = (bf16[128,2176]{1,0:T(8,128)(2,1)}, bf16[128,2176]{1,0:T(8,128)(2,1)}, u32[]{:S(2)}, u32[]{:S(2)}) collective-permute-start(bf16[128,2176]{1,0:T(8,128)(2,1)} %shard_map.85.refs_0_), channel_id=1, source_target_pairs={{0,4},{1,5},{4,8},{5,9},{8,12},{9,13},{12,14},{13,15},{14,10},{15,... | collective-permute-start | bytes 1671176 | tf_op jit(solution)/shard_map/ppermute | solution.py:146
  7.0 15.3 %collective-permute-start.2 = (bf16[128,2176]{1,0:T(8,128)(2,1)}, bf16[128,2176]{1,0:T(8,128)(2,1)}, u32[]{:S(2)}, u32[]{:S(2)}) collective-permute-start(bf16[128,2176]{1,0:T(8,128)(2,1)} %shard_map.85.refs_0_), channel_id=1, source_target_pairs={{0,2},{1,3},{4,0},{5,1},{8,4},{9,5},{12,8},{13,9},{14,12},{15,13},... | collective-permute-start | bytes 1671176 | tf_op jit(solution)/shard_map/ppermute | solution.py:147
  20.4 16.4 %collective-permute-start.1 = (bf16[128,2176]{1,0:T(8,128)(2,1)}, bf16[128,2176]{1,0:T(8,128)(2,1)S(1)}, u32[]{:S(2)}, u32[]{:S(2)}) collective-permute-start(bf16[128,2176]{1,0:T(8,128)(2,1)} %collective-permute-done.refs_0_), channel_id=1, source_target_pairs={{0,4},{1,5},{4,8},{5,9},{8,12},{9,13},{12,14},{13,15},{14,10},{15,... | collective-permute-start | bytes 1671176 | tf_op jit(solution)/shard_map/ppermute | solution.py:146
  22.3 14.6 %collective-permute-start.3 = (bf16[128,2176]{1,0:T(8,128)(2,1)}, bf16[128,2176]{1,0:T(8,128)(2,1)S(1)}, u32[]{:S(2)}, u32[]{:S(2)}) collective-permute-start(bf16[128,2176]{1,0:T(8,128)(2,1)} %collective-permute-done.2.refs_1_), channel_id=1, source_target_pairs={{0,2},{1,3},{4,0},{5,1},{8,4},{9,5},{12,8},{13,9},{14,12},{15,13},... | collective-permute-start | bytes 1671176 | tf_op jit(solution)/shard_map/ppermute | solution.py:147
  22.6 1.9 %copy-start = (bf16[1,2048,768]{2,1,0:T(8,128)(2,1)S(1)}, bf16[1,2048,768]{2,1,0:T(8,128)(2,1)}, u32[]{:S(2)}) copy-start(bf16[1,2048,768]{2,1,0:T(8,128)(2,1)} %param.9) | copy-start | bytes 9437188
  24.5 1.9 %copy-start.2 = (bf16[1,2048,768]{2,1,0:T(8,128)(2,1)S(1)}, bf16[1,2048,768]{2,1,0:T(8,128)(2,1)}, u32[]{:S(2)}) copy-start(bf16[1,2048,768]{2,1,0:T(8,128)(2,1)} %param.10) | copy-start | bytes 9437188
  26.3 1.9 %copy-start.3 = (bf16[1,768,2048]{2,1,0:T(8,128)(2,1)S(1)}, bf16[1,768,2048]{2,1,0:T(8,128)(2,1)}, u32[]{:S(2)}) copy-start(bf16[1,768,2048]{2,1,0:T(8,128)(2,1)} %param.11) | copy-start | bytes 9437188
  36.8 13.9 %collective-permute-start.7 = (bf16[128,2176]{1,0:T(8,128)(2,1)S(1)}, bf16[128,2176]{1,0:T(8,128)(2,1)S(1)}, u32[]{:S(2)}, u32[]{:S(2)}) collective-permute-start(bf16[128,2176]{1,0:T(8,128)(2,1)S(1)} %collective-permute-done.1.refs_0_), channel_id=1, source_target_pairs={{0,4},{1,5},{4,8},{5,9},{8,12},{9,13},{12,14},{13,15},{14,10},{15,... | collective-permute-start | bytes 1671176 | tf_op jit(solution)/shard_map/ppermute | solution.py:146
  38.7 13.4 %collective-permute-start.8 = (bf16[128,2176]{1,0:T(8,128)(2,1)S(1)}, bf16[128,2176]{1,0:T(8,128)(2,1)S(1)}, u32[]{:S(2)}, u32[]{:S(2)}) collective-permute-start(bf16[128,2176]{1,0:T(8,128)(2,1)S(1)} %collective-permute-done.3.refs_1_), channel_id=1, source_target_pairs={{0,2},{1,3},{4,0},{5,1},{8,4},{9,5},{12,8},{13,9},{14,12},{15,13},... | collective-permute-start | bytes 1671176 | tf_op jit(solution)/shard_map/ppermute | solution.py:147
  38.9 15.5 %copy-start.1 = (bf16[1,2048,768]{2,1,0:T(8,128)(2,1)S(1)}, bf16[1,2048,768]{2,1,0:T(8,128)(2,1)}, u32[]{:S(2)}) copy-start(bf16[1,2048,768]{2,1,0:T(8,128)(2,1)} %param.9) | copy-start | bytes 9437188
  52.1 9.8 %collective-permute-start.10 = (bf16[64,2176]{1,0:T(8,128)(2,1)S(1)}, bf16[64,2176]{1,0:T(8,128)(2,1)S(1)}, u32[]{:S(2)}, u32[]{:S(2)}) collective-permute-start(bf16[64,2176]{1,0:T(8,128)(2,1)S(1)} %slice.10), channel_id=1, source_target_pairs={{0,2},{1,3},{4,0},{5,1},{8,4},{9,5},{12,8},{13,9},{14,12},{15,13},... | collective-permute-start | bytes 835592 | tf_op jit(solution)/shard_map/ppermute | solution.py:147
  52.6 9.3 %collective-permute-start.9 = (bf16[64,2176]{1,0:T(8,128)(2,1)S(1)}, bf16[64,2176]{1,0:T(8,128)(2,1)S(1)}, u32[]{:S(2)}, u32[]{:S(2)}) collective-permute-start(bf16[64,2176]{1,0:T(8,128)(2,1)S(1)} %slice.9), channel_id=1, source_target_pairs={{0,4},{1,5},{4,8},{5,9},{8,12},{9,13},{12,14},{13,15},{14,10},{15,... | collective-permute-start | bytes 835592 | tf_op jit(solution)/shard_map/ppermute | solution.py:146
  66.7 7.5 %collective-permute-start.11 = (bf16[64,2048]{1,0:T(8,128)(2,1)S(1)}, bf16[64,2048]{1,0:T(8,128)(2,1)S(1)}, u32[]{:S(2)}, u32[]{:S(2)}) collective-permute-start(bf16[64,2048]{1,0:T(8,128)(2,1)S(1)} %get-tuple-element.51), channel_id=1, source_target_pairs={{0,2},{1,3},{4,0},{5,1},{8,4},{9,5},{12,8},{13,9},{14,12},{15,13},... | collective-permute-start | bytes 786440 | tf_op jit(solution)/shard_map/ppermute | solution.py:147
  67.1 7.3 %collective-permute-start.15 = (bf16[64,2048]{1,0:T(8,128)(2,1)S(1)}, bf16[64,2048]{1,0:T(8,128)(2,1)S(1)}, u32[]{:S(2)}, u32[]{:S(2)}) collective-permute-start(bf16[64,2048]{1,0:T(8,128)(2,1)S(1)} %get-tuple-element.55), channel_id=1, source_target_pairs={{0,4},{1,5},{4,8},{5,9},{8,12},{9,13},{12,14},{13,15},{14,10},{15,... | collective-permute-start | bytes 786440 | tf_op jit(solution)/shard_map/ppermute | solution.py:146
  74.2 12.0 %collective-permute-start.12 = (bf16[128,2048]{1,0:T(8,128)(2,1)S(1)}, bf16[128,2048]{1,0:T(8,128)(2,1)S(1)}, u32[]{:S(2)}, u32[]{:S(2)}) collective-permute-start(bf16[128,2048]{1,0:T(8,128)(2,1)S(1)} %add_convert_fusion.6), channel_id=1, source_target_pairs={{0,2},{1,3},{4,0},{5,1},{8,4},{9,5},{12,8},{13,9},{14,12},{15,13},... | collective-permute-start | bytes 1572872 | tf_op jit(solution)/shard_map/ppermute | solution.py:147
  74.5 26.9 %copy-start.4 = (bf16[128,2176]{1,0:T(8,128)(2,1)S(1)}, bf16[128,2176]{1,0:T(8,128)(2,1)}, u32[]{:S(2)}) copy-start(bf16[128,2176]{1,0:T(8,128)(2,1)} %shard_map.85.refs_0_) | copy-start | bytes 1671172
  74.5 12.0 %collective-permute-start.16 = (bf16[128,2048]{1,0:T(8,128)(2,1)S(1)}, bf16[128,2048]{1,0:T(8,128)(2,1)S(1)}, u32[]{:S(2)}, u32[]{:S(2)}) collective-permute-start(bf16[128,2048]{1,0:T(8,128)(2,1)S(1)} %add_convert_fusion.3), channel_id=1, source_target_pairs={{0,4},{1,5},{4,8},{5,9},{8,12},{9,13},{12,14},{13,15},{14,10},{15,... | collective-permute-start | bytes 1572872 | tf_op jit(solution)/shard_map/ppermute | solution.py:146
  86.3 11.3 %collective-permute-start.13 = (bf16[128,2048]{1,0:T(8,128)(2,1)S(1)}, bf16[128,2048]{1,0:T(8,128)(2,1)S(1)}, u32[]{:S(2)}, u32[]{:S(2)}) collective-permute-start(bf16[128,2048]{1,0:T(8,128)(2,1)S(1)} %add_convert_fusion.5), channel_id=1, source_target_pairs={{0,2},{1,3},{4,0},{5,1},{8,4},{9,5},{12,8},{13,9},{14,12},{15,13},... | collective-permute-start | bytes 1572872 | tf_op jit(solution)/shard_map/ppermute | solution.py:147
  86.7 11.8 %collective-permute-start.17 = (bf16[128,2048]{1,0:T(8,128)(2,1)S(1)}, bf16[128,2048]{1,0:T(8,128)(2,1)S(1)}, u32[]{:S(2)}, u32[]{:S(2)}) collective-permute-start(bf16[128,2048]{1,0:T(8,128)(2,1)S(1)} %add_convert_fusion.2), channel_id=1, source_target_pairs={{0,4},{1,5},{4,8},{5,9},{8,12},{9,13},{12,14},{13,15},{14,10},{15,... | collective-permute-start | bytes 1572872 | tf_op jit(solution)/shard_map/ppermute | solution.py:146
  98.5 11.5 %collective-permute-start.14 = (bf16[128,2048]{1,0:T(8,128)(2,1)}, bf16[128,2048]{1,0:T(8,128)(2,1)}, u32[]{:S(2)}, u32[]{:S(2)}) collective-permute-start(bf16[128,2048]{1,0:T(8,128)(2,1)} %add_convert_fusion.4), channel_id=1, source_target_pairs={{0,2},{1,3},{4,0},{5,1},{8,4},{9,5},{12,8},{13,9},{14,12},{15,13},... | collective-permute-start | bytes 1572872 | tf_op jit(solution)/shard_map/ppermute | solution.py:147
  99.4 10.6 %collective-permute-start.18 = (bf16[128,2048]{1,0:T(8,128)(2,1)}, bf16[128,2048]{1,0:T(8,128)(2,1)}, u32[]{:S(2)}, u32[]{:S(2)}) collective-permute-start(bf16[128,2048]{1,0:T(8,128)(2,1)} %add_convert_fusion.1), channel_id=1, source_target_pairs={{0,4},{1,5},{4,8},{5,9},{8,12},{9,13},{12,14},{13,15},{14,10},{15,... | collective-permute-start | bytes 1572872 | tf_op jit(solution)/shard_map/ppermute | solution.py:146
  106.2 0.8 copy-start.5
  107.0 1.1 %collective-permute-start.19 = (f32[2,128]{1,0:T(2,128)S(1)}, f32[2,128]{1,0:T(2,128)S(1)}, u32[]{:S(2)}, u32[]{:S(2)}) collective-permute-start(f32[2,128]{1,0:T(2,128)S(1)} %add_add_fusion), channel_id=1, source_target_pairs={{0,1},{1,0},{2,3},{3,2},{4,5},{5,4},{6,7},{7,6},{8,9},{9,8},{10,11... | collective-permute-start | bytes 3080 | tf_op jit(solution)/shard_map/ppermute | solution.py:148

commit v6 on v4

--- a/solution.py
+++ b/solution.py
@@ -9,7 +9,7 @@
 
 CORES = 2
 LANES = 128
-VMEM_LIMIT = 24 * 1024 * 1024
+VMEM_LIMIT = 10 * 1024 * 1024
 HIDDEN_CHUNK = 256
 OUT_CHUNK = 512
 
@@ -28,11 +28,18 @@
     return pairs
 
 
-def pack_kernel(experts, tokens_ref, ids_ref, gates_ref, out_ref, arrived):
+def pack_kernel(experts, tokens_ref, ids_hbm, gates_hbm, out_ref, ids_ref, gates_ref, arrived):
     rows, width = tokens_ref.shape
     lanes = out_ref.shape[1] - width
-    copy = pltpu.make_async_copy(tokens_ref, out_ref.at[:, pl.ds(0, width)], arrived)
-    copy.start()
+    copies = [
+        pltpu.make_async_copy(ids_hbm, ids_ref, arrived.at[0]),
+        pltpu.make_async_copy(gates_hbm, gates_ref, arrived.at[1]),
+        pltpu.make_async_copy(tokens_ref, out_ref.at[:, pl.ds(0, width)], arrived.at[2]),
+    ]
+    for copy in copies:
+        copy.start()
+    copies[0].wait()
+    copies[1].wait()
     lane = lax.broadcasted_iota(jnp.int32, (lanes, rows), 0)
     scores = jnp.zeros((lanes, rows), jnp.int32)
     for k in range(ids_ref.shape[0]):
@@ -40,23 +47,50 @@
         scores = jnp.where(lane == at, gate >> 8, scores)
         scores = jnp.where(lane == at + experts, gate & 255, scores)
     out_ref[:, width:] = scores.astype(jnp.float32).T.astype(jnp.bfloat16)
-    copy.wait()
+    copies[2].wait()
 
 
 def pack(tokens, expert_ids, gate_fixed, experts):
     rows, width = tokens.shape
     lanes = -(-2 * experts // LANES) * LANES
-    in_vmem = pl.BlockSpec(memory_space=pltpu.VMEM)
+    per_token = expert_ids.shape[1]
     return pl.pallas_call(
         functools.partial(pack_kernel, experts),
         out_shape=jax.ShapeDtypeStruct((rows, width + lanes), jnp.bfloat16),
-        in_specs=[pl.BlockSpec(memory_space=pl.ANY), in_vmem, in_vmem],
-        out_specs=in_vmem,
-        scratch_shapes=[pltpu.SemaphoreType.DMA],
+        in_specs=[pl.BlockSpec(memory_space=pl.ANY)] * 3,
+        out_specs=pl.BlockSpec(memory_space=pltpu.VMEM),
+        scratch_shapes=[
+            pltpu.VMEM((per_token, rows), jnp.int32),
+            pltpu.VMEM((per_token, rows), jnp.int32),
+            pltpu.SemaphoreType.DMA((3,)),
+        ],
         cost_estimate=pl.CostEstimate(
             flops=rows * lanes, bytes_accessed=4 * rows * width, transcendentals=0
         ),
     )(tokens, expert_ids.T, gate_fixed.T)
+
+
+def hold_kernel(*refs):
+    count = len(refs) // 2
+    arrived = refs[-1]
+    copies = [
+        pltpu.make_async_copy(refs[i], refs[count + i], arrived.at[i]) for i in range(count)
+    ]
+    for copy in copies:
+        copy.start()
+    for copy in copies:
+        copy.wait()
+
+
+def hold(arrays):
+    return pl.pallas_call(
+        hold_kernel,
+        out_shape=[pltpu.VMEM(array.shape, array.dtype) for array in arrays],
+        in_specs=[pl.BlockSpec(memory_space=pl.ANY)] * len(arrays),
+        out_specs=[pl.BlockSpec(memory_space=pltpu.VMEM)] * len(arrays),
+        scratch_shapes=[pltpu.SemaphoreType.DMA((len(arrays),))],
+        compiler_params=pltpu.CompilerParams(vmem_limit_bytes=VMEM_LIMIT),
+    )(*arrays)
 
 
 def expert_kernel(sizes, *refs):
@@ -138,7 +172,8 @@
     node = lax.axis_index("node")
 
     weights = [gate_weight[0], up_weight[0], down_weight[0]]
-    weights += [sibling(weight) for weight in weights]
+    others = [sibling(weight) for weight in weights]
+    weights = hold([pltpu.with_memory_space_constraint(w, pltpu.HBM) for w in weights + others])
     packed = pack(tokens, expert_ids, gate_fixed, expert_count)
     lanes = packed.shape[1] - model_width
     own = (jnp.arange(lanes)[None] == jnp.stack([node, node ^ 1])[:, None]).astype(jnp.float32)
@@ -159,20 +194,19 @@
         return sum(term.astype(jnp.float32) for term in terms).astype(jnp.bfloat16)
 
     low, high = right(packed), left(packed)
-    blocks, outs, fresh = {}, {}, {}
-    for step in range(2, far + 1):
-        (low, high), fresh = tie(((low, high), fresh))
-        outs.update(fresh)
-        blocks[step - 1] = (low, high)
-        if step < far:
+    outs = {}
+    for k in range(1, far + 1):
+        if k > 1:
+            low, high, outs[k - 1] = tie((low, high, outs[k - 1]))
+        here = low, high
+        if k == far:
+            break
+        if k < far - 1:
             low, high = right(low), left(high)
         else:
             low, high = right(low[:half]), left(high[half:])
-        ready = [k for k in blocks if k not in outs] if step >= min(3, far) else []
-        fresh = {k: run(blocks[k]) for k in ready}
-    (low, high), fresh = tie(((low, high), fresh))
-    outs.update(fresh)
-    low, high = run([low, high])
+        outs[k] = run(here)
+    low, high = run(here)
 
     low, high, packed = tie((low, high, packed))
     (own_rows,) = run([packed])
@@ -182,7 +216,7 @@
             zeros = jnp.zeros_like(low)
             low = jnp.concatenate([low, zeros])
             high = jnp.concatenate([zeros, high])
-        low, high = tie((add(outs[k][0], low), add(outs[k][1], high)))
+        low, high = ((add(outs[k][0], low), add(outs[k][1], high)))
     mixed = add(own_rows, left(low), right(high))
 
     total = sum(stats)

time: 129 us -> 106 us (0.82)
  Pallas kernels: 38.3 us -> 29.2 us
  local copies, waits for them, and re-layouts: 6.52 us -> 0.05 us
  waiting for transfers between devices: 56.5 us -> 52.2 us
  other arithmetic: 6.14 us -> 3.18 us
    ppermute x8, waiting for transfers between devices: 47.5 us -> 21 us  [body(): right = lambda a: lax.ppermute(a, 'node', to_right)]
    ppermute x8, waiting for transfers between devices: 7.78 us -> 30.1 us  [body(): left = lambda a: lax.ppermute(a, 'node', to_left)]
    pallas_call x5, Pallas kernels: 35.7 us -> 20.8 us  [apply_experts(): pl.pallas_call(functools.partial(expert_kernel, sizes), out_shape=[jax.Sh...]
    pallas_call x0 -> x1, Pallas kernels: none -> 6.5 us  [hold(): pl.pallas_call(hold_kernel, out_shape=[pltpu.VMEM(array.shape, array.dtyp...]
    unnamed x12 -> x2, local copies, waits for them, and re-layouts: 6.47 us -> 0.01 us
    convert_element_type x7, other arithmetic: 4.66 us -> 1.69 us  [add(): sum((term.astype(jnp.float32) for term in terms)).astype(jnp.bfloat16)]
    ppermute x8, starting transfers between devices: 5.16 us -> 3.46 us  [body(): left = lambda a: lax.ppermute(a, 'node', to_left)]
    ppermute x8, starting transfers between devices: 12.8 us -> 14.3 us  [body(): right = lambda a: lax.ppermute(a, 'node', to_right)]
  transfers between devices with their start and end apart: 20 -> 20, of which waited for: 12 -> 11; matrix products, arithmetic and copies ran while one was open for 2% -> 2% of each run, Pallas kernels for 25% -> 25%
where the time goes in v6:
time: 106 us
  waiting for transfers between devices  52.2 us (49%)
  Pallas kernels  29.2 us (28%)
  starting transfers between devices  18.8 us (18%)
  other arithmetic  3.18 us (3%)
  between operations  2.6 us (2%)
    ppermute x8, waiting for transfers between devices, body(): left = lambda a: lax.ppermute(a, 'node', to_left)  30.1 us
    ppermute x8, waiting for transfers between devices, body(): right = lambda a: lax.ppermute(a, 'node', to_right)  21 us
    pallas_call x5, Pallas kernels, apply_experts(): pl.pallas_call(functools.partial(expert_kernel, sizes), out_shape=[jax.Sh...  20.8 us
    ppermute x8, starting transfers between devices, body(): right = lambda a: lax.ppermute(a, 'node', to_right)  14.3 us
    pallas_call x1, Pallas kernels, hold(): pl.pallas_call(hold_kernel, out_shape=[pltpu.VMEM(array.shape, array.dtyp...  6.5 us
    ppermute x8, starting transfers between devices, body(): left = lambda a: lax.ppermute(a, 'node', to_left)  3.46 us
  transfers between devices with their start and end apart: 20, of which 11 were waited for; matrix products, arithmetic and copies ran while one was open for 2% of the time, Pallas kernels for 25%

profile of v6, /device:TPU:0, one launch (start us, length us, event | category | flops | bytes accessed | tf_op | source)
XLA Modules:
  0.0 106.0 jit_solution(16960263366486453306)
XLA Ops:
  0.6 0.5 collective-permute-start.4
  1.1 0.1 collective-permute-start.5
  1.2 0.4 collective-permute-start.6
  1.7 1.9 %shard_map.85.refs_0_ = bf16[128,2176]{1,0:T(8,128)(2,1)} custom-call(bf16[128,2048]{1,0:T(8,128)(2,1)} %tokens_ref.1, s32[8,128]{1,0:T(8,128)} %bitcast.15, s32[8,128]{1,0:T(8,128)} %bitcast.16), custom_call_target="tpu_custom_call" | custom-call | flops 16384 | bytes 1048576 | tf_op jit(solution)/shard_map/pallas_call | solution.py:57
  3.6 2.7 %collective-permute-start = (bf16[128,2176]{1,0:T(8,128)(2,1)}, bf16[128,2176]{1,0:T(8,128)(2,1)S(1)}, u32[]{:S(2)}, u32[]{:S(2)}) collective-permute-start(bf16[128,2176]{1,0:T(8,128)(2,1)} %shard_map.85.refs_0_), channel_id=1, source_target_pairs={{0,4},{1,5},{4,8},{5,9},{8,12},{9,13},{12,14},{13,15},{14,10},{15,... | collective-permute-start | bytes 1671176 | tf_op jit(solution)/shard_map/ppermute | solution.py:168
  6.3 0.0 collective-permute-start.2
  6.3 0.1 pad_add_fusion
  6.4 0.1 select_convert_fusion.refs_3_.refs_2_
  6.5 13.1 %collective-permute-done.refs_0_ = bf16[128,2176]{1,0:T(8,128)(2,1)S(1)} collective-permute-done((bf16[128,2176]{1,0:T(8,128)(2,1)}, bf16[128,2176]{1,0:T(8,128)(2,1)S(1)}, u32[]{:S(2)}, u32[]{:S(2)}) %collective-permute-start) | collective-permute-done | bytes 557088 | tf_op jit(solution)/shard_map/ppermute | solution.py:168
  19.7 1.8 %collective-permute-start.1 = (bf16[128,2176]{1,0:T(8,128)(2,1)S(1)}, bf16[128,2176]{1,0:T(8,128)(2,1)S(1)}, u32[]{:S(2)}, u32[]{:S(2)}) collective-permute-start(bf16[128,2176]{1,0:T(8,128)(2,1)S(1)} %collective-permute-done.refs_0_), channel_id=1, source_target_pairs={{0,4},{1,5},{4,8},{5,9},{8,12},{9,13},{12,14},{13,15},{14,10},{15,... | collective-permute-start | bytes 1671176 | tf_op jit(solution)/shard_map/ppermute | solution.py:168
  21.5 0.0 collective-permute-done.2.refs_1_
  21.5 0.2 collective-permute-start.3
  21.7 0.1 compare_convert_fusion.refs_2_.refs_1_
  21.8 0.0 collective-permute-done.4.refs_3_
  21.8 0.0 collective-permute-done.5.refs_4_
  21.8 0.0 collective-permute-done.6.refs_5_
  21.8 6.5 %shard_map.86 = (bf16[2048,768]{1,0:T(8,128)(2,1)S(1)}, bf16[2048,768]{1,0:T(8,128)(2,1)S(1)}, bf16[768,2048]{1,0:T(8,128)(2,1)S(1)}, bf16[2048,768]{1,0:T(8,128...) custom-call(bf16[2048,768]{1,0:T(8,128)(2,1)} %bitcast.10, bf16[2048,768]{1,0:T(8,128)(2,1)} %bitcast.12, ...), custom_call_target="tpu_custom_call" | custom-call | tf_op jit(solution)/shard_map/pallas_call | solution.py:86
  28.3 5.1 %shard_map.87 = (bf16[128,2048]{1,0:T(8,128)(2,1)S(1)}, bf16[128,2048]{1,0:T(8,128)(2,1)S(1)}, f32[2,128]{1,0:T(2,128)S(1)}) custom-call(bf16[128,2176]{1,0:T(8,128)(2,1)S(1)} %collective-permute-done.refs_0_, bf16[128,2176]{1,0:T(8,128)(2,1)S(1)} %collective-permute-done.2.refs_1_, f32[2,128]{1,0:T(2,128)S(1)} %compare_convert_fusion.refs_2_.refs_1_, ...), custom_call_target="tpu_custom_call" | custom-call | flops 4831838208 | bytes 2097152 | tf_op jit(solution)/shard_map/pallas_call | solution.py:140
  33.4 0.6 collective-permute-done.1.refs_0_
  34.0 1.3 %collective-permute-done.3.refs_1_ = bf16[128,2176]{1,0:T(8,128)(2,1)S(1)} collective-permute-done((bf16[128,2176]{1,0:T(8,128)(2,1)S(1)}, bf16[128,2176]{1,0:T(8,128)(2,1)S(1)}, u32[]{:S(2)}, u32[]{:S(2)}) %collective-permute-start.3) | collective-permute-done | bytes 557088 | tf_op jit(solution)/shard_map/ppermute | solution.py:169
  35.4 1.6 %collective-permute-start.7 = (bf16[128,2176]{1,0:T(8,128)(2,1)S(1)}, bf16[128,2176]{1,0:T(8,128)(2,1)S(1)}, u32[]{:S(2)}, u32[]{:S(2)}) collective-permute-start(bf16[128,2176]{1,0:T(8,128)(2,1)S(1)} %collective-permute-done.1.refs_0_), channel_id=1, source_target_pairs={{0,4},{1,5},{4,8},{5,9},{8,12},{9,13},{12,14},{13,15},{14,10},{15,... | collective-permute-start | bytes 1671176 | tf_op jit(solution)/shard_map/ppermute | solution.py:168
  36.9 0.4 collective-permute-start.8
  37.4 5.1 %shard_map.88 = (bf16[128,2048]{1,0:T(8,128)(2,1)S(1)}, bf16[128,2048]{1,0:T(8,128)(2,1)S(1)}, f32[2,128]{1,0:T(2,128)S(1)}) custom-call(bf16[128,2176]{1,0:T(8,128)(2,1)S(1)} %collective-permute-done.1.refs_0_, bf16[128,2176]{1,0:T(8,128)(2,1)S(1)} %collective-permute-done.3.refs_1_, f32[2,128]{1,0:T(2,128)S(1)} %compare_convert_fusion.refs_2_.refs_1_, ...), custom_call_target="tpu_custom_call" | custom-call | flops 4831838208 | bytes 2097152 | tf_op jit(solution)/shard_map/pallas_call | solution.py:140
  42.5 5.8 %collective-permute-done.7.refs_0_ = bf16[128,2176]{1,0:T(8,128)(2,1)S(1)} collective-permute-done((bf16[128,2176]{1,0:T(8,128)(2,1)S(1)}, bf16[128,2176]{1,0:T(8,128)(2,1)S(1)}, u32[]{:S(2)}, u32[]{:S(2)}) %collective-permute-start.7) | collective-permute-done | bytes 557088 | tf_op jit(solution)/shard_map/ppermute | solution.py:168
  48.3 1.3 %collective-permute-done.8.refs_1_ = bf16[128,2176]{1,0:T(8,128)(2,1)S(1)} collective-permute-done((bf16[128,2176]{1,0:T(8,128)(2,1)S(1)}, bf16[128,2176]{1,0:T(8,128)(2,1)S(1)}, u32[]{:S(2)}, u32[]{:S(2)}) %collective-permute-start.8) | collective-permute-done | bytes 557088 | tf_op jit(solution)/shard_map/ppermute | solution.py:169
  49.7 0.5 collective-permute-start.10
  50.2 1.8 %collective-permute-start.9 = (bf16[64,2176]{1,0:T(8,128)(2,1)S(1)}, bf16[64,2176]{1,0:T(8,128)(2,1)S(1)}, u32[]{:S(2)}, u32[]{:S(2)}) collective-permute-start(bf16[64,2176]{1,0:T(8,128)(2,1)S(1)} %slice.9), channel_id=1, source_target_pairs={{0,4},{1,5},{4,8},{5,9},{8,12},{9,13},{12,14},{13,15},{14,10},{15,... | collective-permute-start | bytes 835592 | tf_op jit(solution)/shard_map/ppermute | solution.py:168
  52.0 5.2 %shard_map.89 = (bf16[128,2048]{1,0:T(8,128)(2,1)S(1)}, bf16[128,2048]{1,0:T(8,128)(2,1)S(1)}, f32[2,128]{1,0:T(2,128)S(1)}) custom-call(bf16[128,2176]{1,0:T(8,128)(2,1)S(1)} %collective-permute-done.7.refs_0_, bf16[128,2176]{1,0:T(8,128)(2,1)S(1)} %collective-permute-done.8.refs_1_, f32[2,128]{1,0:T(2,128)S(1)} %compare_convert_fusion.refs_2_.refs_1_, ...), custom_call_target="tpu_custom_call" | custom-call | flops 4831838208 | bytes 2097152 | tf_op jit(solution)/shard_map/pallas_call | solution.py:140
  57.2 0.0 collective-permute-done.10.refs_1_
  57.2 0.0 collective-permute-done.9.refs_0_
  57.2 2.7 %shard_map.90 = (bf16[64,2048]{1,0:T(8,128)(2,1)S(1)}, bf16[64,2048]{1,0:T(8,128)(2,1)S(1)}, f32[2,128]{1,0:T(2,128)S(1)}) custom-call(bf16[64,2176]{1,0:T(8,128)(2,1)S(1)} %collective-permute-done.9.refs_0_, bf16[64,2176]{1,0:T(8,128)(2,1)S(1)} %collective-permute-done.10.refs_1_, f32[2,128]{1,0:T(2,128)S(1)} %compare_convert_fusion.refs_2_.refs_1_, ...), custom_call_target="tpu_custom_call" | custom-call | flops 2415919104 | bytes 1048576 | tf_op jit(solution)/shard_map/pallas_call | solution.py:140
  59.9 0.5 collective-permute-start.11
  60.4 1.6 %collective-permute-start.15 = (bf16[64,2048]{1,0:T(8,128)(2,1)S(1)}, bf16[64,2048]{1,0:T(8,128)(2,1)S(1)}, u32[]{:S(2)}, u32[]{:S(2)}) collective-permute-start(bf16[64,2048]{1,0:T(8,128)(2,1)S(1)} %get-tuple-element.67), channel_id=1, source_target_pairs={{0,4},{1,5},{4,8},{5,9},{8,12},{9,13},{12,14},{13,15},{14,10},{15,... | collective-permute-start | bytes 786440 | tf_op jit(solution)/shard_map/ppermute | solution.py:168
  62.0 6.1 %collective-permute-done.11 = bf16[64,2048]{1,0:T(8,128)(2,1)S(1)} collective-permute-done((bf16[64,2048]{1,0:T(8,128)(2,1)S(1)}, bf16[64,2048]{1,0:T(8,128)(2,1)S(1)}, u32[]{:S(2)}, u32[]{:S(2)}) %collective-permute-start.11) | collective-permute-done | bytes 262176 | tf_op jit(solution)/shard_map/ppermute | solution.py:169
  68.1 0.1 add_convert_fusion.6
  68.2 0.5 collective-permute-start.12
  68.7 0.0 collective-permute-done.15
  68.7 0.1 add_convert_fusion.3
  68.8 0.0 copy-start
  68.8 1.6 %collective-permute-start.16 = (bf16[128,2048]{1,0:T(8,128)(2,1)S(1)}, bf16[128,2048]{1,0:T(8,128)(2,1)S(1)}, u32[]{:S(2)}, u32[]{:S(2)}) collective-permute-start(bf16[128,2048]{1,0:T(8,128)(2,1)S(1)} %add_convert_fusion.3), channel_id=1, source_target_pairs={{0,4},{1,5},{4,8},{5,9},{8,12},{9,13},{12,14},{13,15},{14,10},{15,... | collective-permute-start | bytes 1572872 | tf_op jit(solution)/shard_map/ppermute | solution.py:168
  70.4 9.7 %collective-permute-done.12 = bf16[128,2048]{1,0:T(8,128)(2,1)S(1)} collective-permute-done((bf16[128,2048]{1,0:T(8,128)(2,1)S(1)}, bf16[128,2048]{1,0:T(8,128)(2,1)S(1)}, u32[]{:S(2)}, u32[]{:S(2)}) %collective-permute-start.12) | collective-permute-done | bytes 524320 | tf_op jit(solution)/shard_map/ppermute | solution.py:169
  80.1 0.1 add_convert_fusion.5
  80.3 0.5 collective-permute-start.13
  80.8 0.0 collective-permute-done.16
  80.8 0.1 add_convert_fusion.2
  80.9 1.6 %collective-permute-start.17 = (bf16[128,2048]{1,0:T(8,128)(2,1)S(1)}, bf16[128,2048]{1,0:T(8,128)(2,1)S(1)}, u32[]{:S(2)}, u32[]{:S(2)}) collective-permute-start(bf16[128,2048]{1,0:T(8,128)(2,1)S(1)} %add_convert_fusion.2), channel_id=1, source_target_pairs={{0,4},{1,5},{4,8},{5,9},{8,12},{9,13},{12,14},{13,15},{14,10},{15,... | collective-permute-start | bytes 1572872 | tf_op jit(solution)/shard_map/ppermute | solution.py:168
  82.5 10.6 %collective-permute-done.13 = bf16[128,2048]{1,0:T(8,128)(2,1)S(1)} collective-permute-done((bf16[128,2048]{1,0:T(8,128)(2,1)S(1)}, bf16[128,2048]{1,0:T(8,128)(2,1)S(1)}, u32[]{:S(2)}, u32[]{:S(2)}) %collective-permute-start.13) | collective-permute-done | bytes 524320 | tf_op jit(solution)/shard_map/ppermute | solution.py:169
  93.1 0.1 add_convert_fusion.4
  93.3 0.8 collective-permute-start.14
  94.0 0.0 collective-permute-done.17
  94.0 0.1 add_convert_fusion.1
  94.2 1.5 %collective-permute-start.18 = (bf16[128,2048]{1,0:T(8,128)(2,1)S(1)}, bf16[128,2048]{1,0:T(8,128)(2,1)S(1)}, u32[]{:S(2)}, u32[]{:S(2)}) collective-permute-start(bf16[128,2048]{1,0:T(8,128)(2,1)S(1)} %add_convert_fusion.1), channel_id=1, source_target_pairs={{0,4},{1,5},{4,8},{5,9},{8,12},{9,13},{12,14},{13,15},{14,10},{15,... | collective-permute-start | bytes 1572872 | tf_op jit(solution)/shard_map/ppermute | solution.py:168
  95.7 0.0 copy-done
  95.7 2.7 %shard_map.91 = (bf16[128,2048]{1,0:T(8,128)(2,1)S(1)}, f32[2,128]{1,0:T(2,128)S(1)}) custom-call(bf16[128,2176]{1,0:T(8,128)(2,1)S(1)} %copy-done, f32[2,128]{1,0:T(2,128)S(1)} %compare_convert_fusion.refs_2_.refs_1_, bf16[128,256]{1,0:T(8,128)(2,1)S(1)} %select_convert_fusion.refs_3_.refs_2_, bf16[2048,768]{1,0:T(8,128)(2,1)S(1)} %get-tuple-element.38.refs_4_.refs_3_, ...), custom_call_target="tpu_custom_call" | custom-call | flops 2415919104 | bytes 1048576 | tf_op jit(solution)/shard_map/pallas_call | solution.py:140
  98.4 0.1 collective-permute-start.19
  98.5 1.1 %collective-permute-done.19 = f32[2,128]{1,0:T(2,128)S(1)} collective-permute-done((f32[2,128]{1,0:T(2,128)S(1)}, f32[2,128]{1,0:T(2,128)S(1)}, u32[]{:S(2)}, u32[]{:S(2)}) %collective-permute-start.19) | collective-permute-done | bytes 1056 | tf_op jit(solution)/shard_map/ppermute | solution.py:170
  99.6 0.6 multiply_reduce_fusion
  100.2 0.6 fusion.2
  101.5 1.0 collective-permute-done.14
  102.5 1.4 %collective-permute-done.18 = bf16[128,2048]{1,0:T(8,128)(2,1)S(1)} collective-permute-done((bf16[128,2048]{1,0:T(8,128)(2,1)S(1)}, bf16[128,2048]{1,0:T(8,128)(2,1)S(1)}, u32[]{:S(2)}, u32[]{:S(2)}) %collective-permute-start.18) | collective-permute-done | bytes 524320 | tf_op jit(solution)/shard_map/ppermute | solution.py:168
  103.9 1.0 add_convert_fusion
  (8 shorter events, 0.1 us)
Async XLA Ops:
  0.6 21.1 %collective-permute-start.4 = (bf16[2048,768]{1,0:T(8,128)(2,1)}, bf16[2048,768]{1,0:T(8,128)(2,1)}, u32[]{:S(2)}, u32[]{:S(2)}) collective-permute-start(bf16[2048,768]{1,0:T(8,128)(2,1)} %bitcast.9), channel_id=1, source_target_pairs={{0,1},{1,0},{2,3},{3,2},{4,5},{5,4},{6,7},{7,6},{8,9},{9,8},{10,11... | collective-permute-start | bytes 9437192 | tf_op jit(solution)/shard_map/ppermute | solution.py:170
  1.1 20.6 %collective-permute-start.5 = (bf16[2048,768]{1,0:T(8,128)(2,1)}, bf16[2048,768]{1,0:T(8,128)(2,1)}, u32[]{:S(2)}, u32[]{:S(2)}) collective-permute-start(bf16[2048,768]{1,0:T(8,128)(2,1)} %bitcast.11), channel_id=1, source_target_pairs={{0,1},{1,0},{2,3},{3,2},{4,5},{5,4},{6,7},{7,6},{8,9},{9,8},{10,11... | collective-permute-start | bytes 9437192 | tf_op jit(solution)/shard_map/ppermute | solution.py:170
  1.2 20.5 %collective-permute-start.6 = (bf16[768,2048]{1,0:T(8,128)(2,1)}, bf16[768,2048]{1,0:T(8,128)(2,1)}, u32[]{:S(2)}, u32[]{:S(2)}) collective-permute-start(bf16[768,2048]{1,0:T(8,128)(2,1)} %bitcast.13), channel_id=1, source_target_pairs={{0,1},{1,0},{2,3},{3,2},{4,5},{5,4},{6,7},{7,6},{8,9},{9,8},{10,11... | collective-permute-start | bytes 9437192 | tf_op jit(solution)/shard_map/ppermute | solution.py:170
  3.6 16.1 %collective-permute-start = (bf16[128,2176]{1,0:T(8,128)(2,1)}, bf16[128,2176]{1,0:T(8,128)(2,1)S(1)}, u32[]{:S(2)}, u32[]{:S(2)}) collective-permute-start(bf16[128,2176]{1,0:T(8,128)(2,1)} %shard_map.85.refs_0_), channel_id=1, source_target_pairs={{0,4},{1,5},{4,8},{5,9},{8,12},{9,13},{12,14},{13,15},{14,10},{15,... | collective-permute-start | bytes 1671176 | tf_op jit(solution)/shard_map/ppermute | solution.py:168
  6.3 15.2 %collective-permute-start.2 = (bf16[128,2176]{1,0:T(8,128)(2,1)}, bf16[128,2176]{1,0:T(8,128)(2,1)S(1)}, u32[]{:S(2)}, u32[]{:S(2)}) collective-permute-start(bf16[128,2176]{1,0:T(8,128)(2,1)} %shard_map.85.refs_0_), channel_id=1, source_target_pairs={{0,2},{1,3},{4,0},{5,1},{8,4},{9,5},{12,8},{13,9},{14,12},{15,13},... | collective-permute-start | bytes 1671176 | tf_op jit(solution)/shard_map/ppermute | solution.py:169
  19.7 14.4 %collective-permute-start.1 = (bf16[128,2176]{1,0:T(8,128)(2,1)S(1)}, bf16[128,2176]{1,0:T(8,128)(2,1)S(1)}, u32[]{:S(2)}, u32[]{:S(2)}) collective-permute-start(bf16[128,2176]{1,0:T(8,128)(2,1)S(1)} %collective-permute-done.refs_0_), channel_id=1, source_target_pairs={{0,4},{1,5},{4,8},{5,9},{8,12},{9,13},{12,14},{13,15},{14,10},{15,... | collective-permute-start | bytes 1671176 | tf_op jit(solution)/shard_map/ppermute | solution.py:168
  21.5 13.9 %collective-permute-start.3 = (bf16[128,2176]{1,0:T(8,128)(2,1)S(1)}, bf16[128,2176]{1,0:T(8,128)(2,1)S(1)}, u32[]{:S(2)}, u32[]{:S(2)}) collective-permute-start(bf16[128,2176]{1,0:T(8,128)(2,1)S(1)} %collective-permute-done.2.refs_1_), channel_id=1, source_target_pairs={{0,2},{1,3},{4,0},{5,1},{8,4},{9,5},{12,8},{13,9},{14,12},{15,13},... | collective-permute-start | bytes 1671176 | tf_op jit(solution)/shard_map/ppermute | solution.py:169
  35.4 13.0 %collective-permute-start.7 = (bf16[128,2176]{1,0:T(8,128)(2,1)S(1)}, bf16[128,2176]{1,0:T(8,128)(2,1)S(1)}, u32[]{:S(2)}, u32[]{:S(2)}) collective-permute-start(bf16[128,2176]{1,0:T(8,128)(2,1)S(1)} %collective-permute-done.1.refs_0_), channel_id=1, source_target_pairs={{0,4},{1,5},{4,8},{5,9},{8,12},{9,13},{12,14},{13,15},{14,10},{15,... | collective-permute-start | bytes 1671176 | tf_op jit(solution)/shard_map/ppermute | solution.py:168
  36.9 12.7 %collective-permute-start.8 = (bf16[128,2176]{1,0:T(8,128)(2,1)S(1)}, bf16[128,2176]{1,0:T(8,128)(2,1)S(1)}, u32[]{:S(2)}, u32[]{:S(2)}) collective-permute-start(bf16[128,2176]{1,0:T(8,128)(2,1)S(1)} %collective-permute-done.3.refs_1_), channel_id=1, source_target_pairs={{0,2},{1,3},{4,0},{5,1},{8,4},{9,5},{12,8},{13,9},{14,12},{15,13},... | collective-permute-start | bytes 1671176 | tf_op jit(solution)/shard_map/ppermute | solution.py:169
  49.7 7.5 %collective-permute-start.10 = (bf16[64,2176]{1,0:T(8,128)(2,1)S(1)}, bf16[64,2176]{1,0:T(8,128)(2,1)S(1)}, u32[]{:S(2)}, u32[]{:S(2)}) collective-permute-start(bf16[64,2176]{1,0:T(8,128)(2,1)S(1)} %slice.10), channel_id=1, source_target_pairs={{0,2},{1,3},{4,0},{5,1},{8,4},{9,5},{12,8},{13,9},{14,12},{15,13},... | collective-permute-start | bytes 835592 | tf_op jit(solution)/shard_map/ppermute | solution.py:169
  50.2 7.0 %collective-permute-start.9 = (bf16[64,2176]{1,0:T(8,128)(2,1)S(1)}, bf16[64,2176]{1,0:T(8,128)(2,1)S(1)}, u32[]{:S(2)}, u32[]{:S(2)}) collective-permute-start(bf16[64,2176]{1,0:T(8,128)(2,1)S(1)} %slice.9), channel_id=1, source_target_pairs={{0,4},{1,5},{4,8},{5,9},{8,12},{9,13},{12,14},{13,15},{14,10},{15,... | collective-permute-start | bytes 835592 | tf_op jit(solution)/shard_map/ppermute | solution.py:168
  59.9 8.2 %collective-permute-start.11 = (bf16[64,2048]{1,0:T(8,128)(2,1)S(1)}, bf16[64,2048]{1,0:T(8,128)(2,1)S(1)}, u32[]{:S(2)}, u32[]{:S(2)}) collective-permute-start(bf16[64,2048]{1,0:T(8,128)(2,1)S(1)} %get-tuple-element.63), channel_id=1, source_target_pairs={{0,2},{1,3},{4,0},{5,1},{8,4},{9,5},{12,8},{13,9},{14,12},{15,13},... | collective-permute-start | bytes 786440 | tf_op jit(solution)/shard_map/ppermute | solution.py:169
  60.4 8.3 %collective-permute-start.15 = (bf16[64,2048]{1,0:T(8,128)(2,1)S(1)}, bf16[64,2048]{1,0:T(8,128)(2,1)S(1)}, u32[]{:S(2)}, u32[]{:S(2)}) collective-permute-start(bf16[64,2048]{1,0:T(8,128)(2,1)S(1)} %get-tuple-element.67), channel_id=1, source_target_pairs={{0,4},{1,5},{4,8},{5,9},{8,12},{9,13},{12,14},{13,15},{14,10},{15,... | collective-permute-start | bytes 786440 | tf_op jit(solution)/shard_map/ppermute | solution.py:168
  68.2 12.0 %collective-permute-start.12 = (bf16[128,2048]{1,0:T(8,128)(2,1)S(1)}, bf16[128,2048]{1,0:T(8,128)(2,1)S(1)}, u32[]{:S(2)}, u32[]{:S(2)}) collective-permute-start(bf16[128,2048]{1,0:T(8,128)(2,1)S(1)} %add_convert_fusion.6), channel_id=1, source_target_pairs={{0,2},{1,3},{4,0},{5,1},{8,4},{9,5},{12,8},{13,9},{14,12},{15,13},... | collective-permute-start | bytes 1572872 | tf_op jit(solution)/shard_map/ppermute | solution.py:169
  68.8 26.9 %copy-start = (bf16[128,2176]{1,0:T(8,128)(2,1)S(1)}, bf16[128,2176]{1,0:T(8,128)(2,1)}, u32[]{:S(2)}) copy-start(bf16[128,2176]{1,0:T(8,128)(2,1)} %shard_map.85.refs_0_) | copy-start | bytes 1671172
  68.8 12.0 %collective-permute-start.16 = (bf16[128,2048]{1,0:T(8,128)(2,1)S(1)}, bf16[128,2048]{1,0:T(8,128)(2,1)S(1)}, u32[]{:S(2)}, u32[]{:S(2)}) collective-permute-start(bf16[128,2048]{1,0:T(8,128)(2,1)S(1)} %add_convert_fusion.3), channel_id=1, source_target_pairs={{0,4},{1,5},{4,8},{5,9},{8,12},{9,13},{12,14},{13,15},{14,10},{15,... | collective-permute-start | bytes 1572872 | tf_op jit(solution)/shard_map/ppermute | solution.py:168
  80.3 12.9 %collective-permute-start.13 = (bf16[128,2048]{1,0:T(8,128)(2,1)S(1)}, bf16[128,2048]{1,0:T(8,128)(2,1)S(1)}, u32[]{:S(2)}, u32[]{:S(2)}) collective-permute-start(bf16[128,2048]{1,0:T(8,128)(2,1)S(1)} %add_convert_fusion.5), channel_id=1, source_target_pairs={{0,2},{1,3},{4,0},{5,1},{8,4},{9,5},{12,8},{13,9},{14,12},{15,13},... | collective-permute-start | bytes 1572872 | tf_op jit(solution)/shard_map/ppermute | solution.py:169
  80.9 13.1 %collective-permute-start.17 = (bf16[128,2048]{1,0:T(8,128)(2,1)S(1)}, bf16[128,2048]{1,0:T(8,128)(2,1)S(1)}, u32[]{:S(2)}, u32[]{:S(2)}) collective-permute-start(bf16[128,2048]{1,0:T(8,128)(2,1)S(1)} %add_convert_fusion.2), channel_id=1, source_target_pairs={{0,4},{1,5},{4,8},{5,9},{8,12},{9,13},{12,14},{13,15},{14,10},{15,... | collective-permute-start | bytes 1572872 | tf_op jit(solution)/shard_map/ppermute | solution.py:168
  93.3 9.2 %collective-permute-start.14 = (bf16[128,2048]{1,0:T(8,128)(2,1)S(1)}, bf16[128,2048]{1,0:T(8,128)(2,1)S(1)}, u32[]{:S(2)}, u32[]{:S(2)}) collective-permute-start(bf16[128,2048]{1,0:T(8,128)(2,1)S(1)} %add_convert_fusion.4), channel_id=1, source_target_pairs={{0,2},{1,3},{4,0},{5,1},{8,4},{9,5},{12,8},{13,9},{14,12},{15,13},... | collective-permute-start | bytes 1572872 | tf_op jit(solution)/shard_map/ppermute | solution.py:169
  94.2 9.7 %collective-permute-start.18 = (bf16[128,2048]{1,0:T(8,128)(2,1)S(1)}, bf16[128,2048]{1,0:T(8,128)(2,1)S(1)}, u32[]{:S(2)}, u32[]{:S(2)}) collective-permute-start(bf16[128,2048]{1,0:T(8,128)(2,1)S(1)} %add_convert_fusion.1), channel_id=1, source_target_pairs={{0,4},{1,5},{4,8},{5,9},{8,12},{9,13},{12,14},{13,15},{14,10},{15,... | collective-permute-start | bytes 1572872 | tf_op jit(solution)/shard_map/ppermute | solution.py:168
  98.4 1.2 %collective-permute-start.19 = (f32[2,128]{1,0:T(2,128)S(1)}, f32[2,128]{1,0:T(2,128)S(1)}, u32[]{:S(2)}, u32[]{:S(2)}) collective-permute-start(f32[2,128]{1,0:T(2,128)S(1)} %add_add_fusion), channel_id=1, source_target_pairs={{0,1},{1,0},{2,3},{3,2},{4,5},{5,4},{6,7},{7,6},{8,9},{9,8},{10,11... | collective-permute-start | bytes 3080 | tf_op jit(solution)/shard_map/ppermute | solution.py:170

commit v7 on v6

--- a/solution.py
+++ b/solution.py
@@ -70,6 +70,26 @@
     )(tokens, expert_ids.T, gate_fixed.T)
 
 
+def join_kernel(*refs):
+    out_ref = refs[-1]
+    half = out_ref.shape[0] // 2
+    for i in range(2):
+        total = sum(ref[...].astype(jnp.float32) for ref in refs[3 * i : 3 * i + 3])
+        out_ref[i * half : (i + 1) * half, :] = total.astype(jnp.bfloat16)
+
+
+def join_halves(first, second):
+    rows, width = first[0].shape
+    in_vmem = pl.BlockSpec(memory_space=pltpu.VMEM)
+    return pl.pallas_call(
+        join_kernel,
+        out_shape=jax.ShapeDtypeStruct((2 * rows, width), jnp.bfloat16),
+        in_specs=[in_vmem] * 6,
+        out_specs=in_vmem,
+        compiler_params=pltpu.CompilerParams(vmem_limit_bytes=VMEM_LIMIT // 2),
+    )(*first, *second)
+
+
 def hold_kernel(*refs):
     count = len(refs) // 2
     arrived = refs[-1]
@@ -93,15 +113,13 @@
     )(*arrays)
 
 
-def expert_kernel(sizes, *refs):
+def expert_kernel(sizes, piece, *refs):
     count = len(sizes)
     blocks = refs[:count]
     own_ref, join_ref = refs[count : count + 2]
     experts = [refs[count + 2 + 3 * i : count + 5 + 3 * i] for i in range(CORES)]
     refs = refs[count + 2 + 3 * CORES :]
-    outs = refs[:count]
-    stats_ref, hidden_ref = refs[count:]
-    starts = [sum(sizes[:i]) for i in range(count)]
+    *outs, stats_ref, hidden_ref = refs
     width, hidden_width = experts[0][0].shape
     lanes = join_ref.shape[0]
 
@@ -127,22 +145,22 @@
         for i, (_, _, down_ref) in enumerate(experts):
             out = jnp.dot(hidden_ref[i], down_ref[:, at], preferred_element_type=jnp.float32)
             total = total + out.astype(jnp.bfloat16).astype(jnp.float32) * scales[i]
-        for i in range(count):
-            outs[i][:, at] = total[starts[i] : starts[i] + sizes[i]].astype(jnp.bfloat16)
-
-
-def apply_experts(blocks, own, join, weights):
+        for i, out_ref in enumerate(outs):
+            out_ref[:, at] = total[i * piece : (i + 1) * piece].astype(jnp.bfloat16)
+
+
+def apply_experts(blocks, piece, own, join, weights):
     width, hidden_width = weights[0].shape
     sizes = tuple(block.shape[0] for block in blocks)
     total = sum(sizes)
     count = len(blocks)
     in_vmem = pl.BlockSpec(memory_space=pltpu.VMEM)
     return pl.pallas_call(
-        functools.partial(expert_kernel, sizes),
-        out_shape=[jax.ShapeDtypeStruct((size, width), jnp.bfloat16) for size in sizes]
+        functools.partial(expert_kernel, sizes, piece),
+        out_shape=[jax.ShapeDtypeStruct((piece, width), jnp.bfloat16)] * (total // piece)
         + [jax.ShapeDtypeStruct((2, own.shape[1]), jnp.float32)],
         in_specs=[in_vmem] * (count + 2 + len(weights)),
-        out_specs=[in_vmem] * (count + 1),
+        out_specs=[in_vmem] * (total // piece + 1),
         scratch_shapes=[pltpu.VMEM((CORES, total, hidden_width), jnp.bfloat16)],
         compiler_params=pltpu.CompilerParams(vmem_limit_bytes=VMEM_LIMIT),
         cost_estimate=pl.CostEstimate(
@@ -186,7 +204,7 @@
     stats = []
 
     def run(blocks):
-        res = apply_experts(blocks, own, join, weights)
+        res = apply_experts(blocks, half, own, join, weights)
         stats.append(res[-1])
         return res[:-1]
 
@@ -206,18 +224,21 @@
         else:
             low, high = right(low[:half]), left(high[half:])
         outs[k] = run(here)
-    low, high = run(here)
-
-    low, high, packed = tie((low, high, packed))
-    (own_rows,) = run([packed])
+    res = run(here)
+
+    ways = (left, left, right, right)
+    from_far = {0: res[0], 3: res[1]}
+    sums = [ways[i](from_far.get(i, outs[far - 1][i])) for i in (1, 2, 0, 3)]
+    sums = [sums[(1, 2, 0, 3).index(i)] for i in range(4)]
     for k in range(far - 1, 0, -1):
-        low, high = left(low), right(high)
-        if k == far - 1:
-            zeros = jnp.zeros_like(low)
-            low = jnp.concatenate([low, zeros])
-            high = jnp.concatenate([zeros, high])
-        low, high = ((add(outs[k][0], low), add(outs[k][1], high)))
-    mixed = add(own_rows, left(low), right(high))
+        if k == max(1, far - 2):
+            packed, sums[1] = tie((packed, sums[1]))
+            own_rows = run([packed])
+        for i in (1, 2, 0, 3):
+            step = k if i in from_far else k - 1
+            if step:
+                sums[i] = ways[i](add(outs[step][i], sums[i]))
+    mixed = join_halves((own_rows[0], sums[0], sums[2]), (own_rows[1], sums[1], sums[3]))
 
     total = sum(stats)
     counts, mass = (total + sibling(total))[:, :expert_count]

time: 106 us -> 104 us (0.981)
  waiting for transfers between devices: 52.2 us -> 43.3 us
  starting transfers between devices: 18.8 us -> 24.9 us
  Pallas kernels: 29.2 us -> 30.5 us
    ppermute x8 -> x11, waiting for transfers between devices: 30.1 us -> 7.93 us  [body(): left = lambda a: lax.ppermute(a, 'node', to_left)]
    ppermute x8 -> x11, waiting for transfers between devices: 21 us -> 34.2 us  [body(): right = lambda a: lax.ppermute(a, 'node', to_right)]
    ppermute x8 -> x11, starting transfers between devices: 14.3 us -> 19.3 us  [body(): right = lambda a: lax.ppermute(a, 'node', to_right)]
    pallas_call x5 -> x6, Pallas kernels: 20.8 us -> 22.1 us  [the longest x5 21.1 us: apply_experts(): pl.pallas_call(functools.partial(expert_kernel, sizes, piece), out_shape=...]
    ppermute x8 -> x11, starting transfers between devices: 3.46 us -> 4.63 us  [body(): left = lambda a: lax.ppermute(a, 'node', to_left)]
  transfers between devices with their start and end apart: 20 -> 26, of which waited for: 11 -> 16; matrix products, arithmetic and copies ran while one was open for 2% -> 2% of each run, Pallas kernels for 25% -> 28%
where the time goes in v7:
time: 104 us; the launch traced here: 103 us
  waiting for transfers between devices  43.3 us (42%)
  Pallas kernels  30.5 us (29%)
  starting transfers between devices  24.9 us (24%)
  between operations  2.59 us (2%)
  other arithmetic  2.13 us (2%)
    ppermute x11, waiting for transfers between devices, body(): right = lambda a: lax.ppermute(a, 'node', to_right)  34.2 us
    pallas_call x5, Pallas kernels, apply_experts(): pl.pallas_call(functools.partial(expert_kernel, sizes, piece), out_shape=...  21.1 us
    ppermute x11, starting transfers between devices, body(): right = lambda a: lax.ppermute(a, 'node', to_right)  19.3 us
    ppermute x11, waiting for transfers between devices, body(): left = lambda a: lax.ppermute(a, 'node', to_left)  7.93 us
    pallas_call x1, Pallas kernels, hold(): pl.pallas_call(hold_kernel, out_shape=[pltpu.VMEM(array.shape, array.dtyp...  6.5 us
    ppermute x11, starting transfers between devices, body(): left = lambda a: lax.ppermute(a, 'node', to_left)  4.63 us
  transfers between devices with their start and end apart: 26, of which 16 were waited for; matrix products, arithmetic and copies ran while one was open for 2% of the time, Pallas kernels for 28%

profile of v7, /device:TPU:0, one launch (start us, length us, event | category | flops | bytes accessed | tf_op | source)
XLA Modules:
  0.0 103.5 jit_solution(7195623222770376218)
XLA Ops:
  0.6 0.5 collective-permute-start.4
  1.1 0.1 collective-permute-start.5
  1.2 0.4 collective-permute-start.6
  1.7 1.9 %shard_map.85.refs_0_ = bf16[128,2176]{1,0:T(8,128)(2,1)} custom-call(bf16[128,2048]{1,0:T(8,128)(2,1)} %tokens_ref.1, s32[8,128]{1,0:T(8,128)} %bitcast.15, s32[8,128]{1,0:T(8,128)} %bitcast.16), custom_call_target="tpu_custom_call" | custom-call | flops 16384 | bytes 1048576 | tf_op jit(solution)/shard_map/pallas_call | solution.py:57
  3.6 2.7 %collective-permute-start = (bf16[128,2176]{1,0:T(8,128)(2,1)}, bf16[128,2176]{1,0:T(8,128)(2,1)S(1)}, u32[]{:S(2)}, u32[]{:S(2)}) collective-permute-start(bf16[128,2176]{1,0:T(8,128)(2,1)} %shard_map.85.refs_0_), channel_id=1, source_target_pairs={{0,4},{1,5},{4,8},{5,9},{8,12},{9,13},{12,14},{13,15},{14,10},{15,... | collective-permute-start | bytes 1671176 | tf_op jit(solution)/shard_map/ppermute | solution.py:186
  6.3 0.0 collective-permute-start.2
  6.3 0.1 pad_add_fusion
  6.4 0.1 select_convert_fusion.refs_3_.refs_2_
  6.5 13.1 %collective-permute-done.refs_0_ = bf16[128,2176]{1,0:T(8,128)(2,1)S(1)} collective-permute-done((bf16[128,2176]{1,0:T(8,128)(2,1)}, bf16[128,2176]{1,0:T(8,128)(2,1)S(1)}, u32[]{:S(2)}, u32[]{:S(2)}) %collective-permute-start) | collective-permute-done | bytes 557088 | tf_op jit(solution)/shard_map/ppermute | solution.py:186
  19.6 1.8 %collective-permute-start.1 = (bf16[128,2176]{1,0:T(8,128)(2,1)S(1)}, bf16[128,2176]{1,0:T(8,128)(2,1)S(1)}, u32[]{:S(2)}, u32[]{:S(2)}) collective-permute-start(bf16[128,2176]{1,0:T(8,128)(2,1)S(1)} %collective-permute-done.refs_0_), channel_id=1, source_target_pairs={{0,4},{1,5},{4,8},{5,9},{8,12},{9,13},{12,14},{13,15},{14,10},{15,... | collective-permute-start | bytes 1671176 | tf_op jit(solution)/shard_map/ppermute | solution.py:186
  21.4 0.2 collective-permute-start.3
  21.7 0.1 compare_convert_fusion.refs_2_.refs_1_
  21.7 6.5 %shard_map.86 = (bf16[2048,768]{1,0:T(8,128)(2,1)S(1)}, bf16[2048,768]{1,0:T(8,128)(2,1)S(1)}, bf16[768,2048]{1,0:T(8,128)(2,1)S(1)}, bf16[2048,768]{1,0:T(8,128...) custom-call(bf16[2048,768]{1,0:T(8,128)(2,1)} %bitcast.10, bf16[2048,768]{1,0:T(8,128)(2,1)} %bitcast.12, ...), custom_call_target="tpu_custom_call" | custom-call | tf_op jit(solution)/shard_map/pallas_call | solution.py:106
  28.3 5.2 %shard_map.87 = (bf16[64,2048]{1,0:T(8,128)(2,1)S(1)}, bf16[64,2048]{1,0:T(8,128)(2,1)S(1)}, bf16[64,2048]{1,0:T(8,128)(2,1)S(1)}, bf16[64,2048]{1,0:T(8,128)(2,1)S(1)}, f32[2,128]{1,0:T(2,128)S(1)}) custom-call(bf16[128,2176]{1,0:T(8,128)(2,1)S(1)} %collective-permute-done.refs_0_, bf16[128,2176]{1,0:T(8,128)(2,1)S(1)} %collective-permute-done.2.refs_1_, ...), custom_call_target="tpu_custom_call" | custom-call | flops 4831838208 | bytes 2097152 | tf_op jit(solution)/shard_map/pallas_call | solution.py:158
  33.5 0.5 collective-permute-done.1.refs_0_
  34.0 1.3 %collective-permute-done.3.refs_1_ = bf16[128,2176]{1,0:T(8,128)(2,1)S(1)} collective-permute-done((bf16[128,2176]{1,0:T(8,128)(2,1)S(1)}, bf16[128,2176]{1,0:T(8,128)(2,1)S(1)}, u32[]{:S(2)}, u32[]{:S(2)}) %collective-permute-start.3) | collective-permute-done | bytes 557088 | tf_op jit(solution)/shard_map/ppermute | solution.py:187
  35.3 1.6 %collective-permute-start.7 = (bf16[128,2176]{1,0:T(8,128)(2,1)S(1)}, bf16[128,2176]{1,0:T(8,128)(2,1)S(1)}, u32[]{:S(2)}, u32[]{:S(2)}) collective-permute-start(bf16[128,2176]{1,0:T(8,128)(2,1)S(1)} %collective-permute-done.1.refs_0_), channel_id=1, source_target_pairs={{0,4},{1,5},{4,8},{5,9},{8,12},{9,13},{12,14},{13,15},{14,10},{15,... | collective-permute-start | bytes 1671176 | tf_op jit(solution)/shard_map/ppermute | solution.py:186
  36.9 0.4 collective-permute-start.8
  37.4 5.2 %shard_map.88 = (bf16[64,2048]{1,0:T(8,128)(2,1)S(1)}, bf16[64,2048]{1,0:T(8,128)(2,1)S(1)}, bf16[64,2048]{1,0:T(8,128)(2,1)S(1)}, bf16[64,2048]{1,0:T(8,128)(2,1)S(1)}, f32[2,128]{1,0:T(2,128)S(1)}) custom-call(bf16[128,2176]{1,0:T(8,128)(2,1)S(1)} %collective-permute-done.1.refs_0_, bf16[128,2176]{1,0:T(8,128)(2,1)S(1)} %collective-permute-done.3.refs_1_, ...), custom_call_target="tpu_custom_call" | custom-call | flops 4831838208 | bytes 2097152 | tf_op jit(solution)/shard_map/pallas_call | solution.py:158
  42.6 5.8 %collective-permute-done.7.refs_0_ = bf16[128,2176]{1,0:T(8,128)(2,1)S(1)} collective-permute-done((bf16[128,2176]{1,0:T(8,128)(2,1)S(1)}, bf16[128,2176]{1,0:T(8,128)(2,1)S(1)}, u32[]{:S(2)}, u32[]{:S(2)}) %collective-permute-start.7) | collective-permute-done | bytes 557088 | tf_op jit(solution)/shard_map/ppermute | solution.py:186
  48.3 1.3 %collective-permute-done.8.refs_1_ = bf16[128,2176]{1,0:T(8,128)(2,1)S(1)} collective-permute-done((bf16[128,2176]{1,0:T(8,128)(2,1)S(1)}, bf16[128,2176]{1,0:T(8,128)(2,1)S(1)}, u32[]{:S(2)}, u32[]{:S(2)}) %collective-permute-start.8) | collective-permute-done | bytes 557088 | tf_op jit(solution)/shard_map/ppermute | solution.py:187
  49.7 0.5 collective-permute-start.10
  50.2 1.8 %collective-permute-start.9 = (bf16[64,2176]{1,0:T(8,128)(2,1)S(1)}, bf16[64,2176]{1,0:T(8,128)(2,1)S(1)}, u32[]{:S(2)}, u32[]{:S(2)}) collective-permute-start(bf16[64,2176]{1,0:T(8,128)(2,1)S(1)} %slice.9), channel_id=1, source_target_pairs={{0,4},{1,5},{4,8},{5,9},{8,12},{9,13},{12,14},{13,15},{14,10},{15,... | collective-permute-start | bytes 835592 | tf_op jit(solution)/shard_map/ppermute | solution.py:186
  52.0 5.2 %shard_map.89 = (bf16[64,2048]{1,0:T(8,128)(2,1)S(1)}, bf16[64,2048]{1,0:T(8,128)(2,1)S(1)}, bf16[64,2048]{1,0:T(8,128)(2,1)S(1)}, bf16[64,2048]{1,0:T(8,128)(2,1)S(1)}, f32[2,128]{1,0:T(2,128)S(1)}) custom-call(bf16[128,2176]{1,0:T(8,128)(2,1)S(1)} %collective-permute-done.7.refs_0_, bf16[128,2176]{1,0:T(8,128)(2,1)S(1)} %collective-permute-done.8.refs_1_, ...), custom_call_target="tpu_custom_call" | custom-call | flops 4831838208 | bytes 2097152 | tf_op jit(solution)/shard_map/pallas_call | solution.py:158
  57.2 0.5 collective-permute-start.11
  57.7 2.8 %shard_map.91 = (bf16[64,2048]{1,0:T(8,128)(2,1)S(1)}, bf16[64,2048]{1,0:T(8,128)(2,1)S(1)}, f32[2,128]{1,0:T(2,128)S(1)}) custom-call(bf16[64,2176]{1,0:T(8,128)(2,1)S(1)} %collective-permute-done.9.refs_0_, bf16[64,2176]{1,0:T(8,128)(2,1)S(1)} %collective-permute-done.10.refs_1_, f32[2,128]{1,0:T(2,128)S(1)} %compare_convert_fusion.refs_2_.refs_1_, ...), custom_call_target="tpu_custom_call" | custom-call | flops 2415919104 | bytes 1048576 | tf_op jit(solution)/shard_map/pallas_call | solution.py:158
  60.5 1.6 %collective-permute-start.21 = (bf16[64,2048]{1,0:T(8,128)(2,1)S(1)}, bf16[64,2048]{1,0:T(8,128)(2,1)S(1)}, u32[]{:S(2)}, u32[]{:S(2)}) collective-permute-start(bf16[64,2048]{1,0:T(8,128)(2,1)S(1)} %get-tuple-element.91), channel_id=1, source_target_pairs={{0,4},{1,5},{4,8},{5,9},{8,12},{9,13},{12,14},{13,15},{14,10},{15,... | collective-permute-start | bytes 786440 | tf_op jit(solution)/shard_map/ppermute | solution.py:186
  62.1 1.6 %collective-permute-start.17 = (bf16[64,2048]{1,0:T(8,128)(2,1)S(1)}, bf16[64,2048]{1,0:T(8,128)(2,1)S(1)}, u32[]{:S(2)}, u32[]{:S(2)}) collective-permute-start(bf16[64,2048]{1,0:T(8,128)(2,1)S(1)} %get-tuple-element.84), channel_id=1, source_target_pairs={{0,4},{1,5},{4,8},{5,9},{8,12},{9,13},{12,14},{13,15},{14,10},{15,... | collective-permute-start | bytes 786440 | tf_op jit(solution)/shard_map/ppermute | solution.py:186
  63.7 0.5 collective-permute-start.13
  64.1 1.0 collective-permute-done.11
  65.1 0.1 add_convert_fusion.9
  65.2 0.5 collective-permute-start.12
  65.7 4.1 %collective-permute-done.21 = bf16[64,2048]{1,0:T(8,128)(2,1)S(1)} collective-permute-done((bf16[64,2048]{1,0:T(8,128)(2,1)S(1)}, bf16[64,2048]{1,0:T(8,128)(2,1)S(1)}, u32[]{:S(2)}, u32[]{:S(2)}) %collective-permute-start.21) | collective-permute-done | bytes 262176 | tf_op jit(solution)/shard_map/ppermute | solution.py:186
  69.8 0.1 add_convert_fusion.2
  69.8 1.6 %collective-permute-start.22 = (bf16[64,2048]{1,0:T(8,128)(2,1)S(1)}, bf16[64,2048]{1,0:T(8,128)(2,1)S(1)}, u32[]{:S(2)}, u32[]{:S(2)}) collective-permute-start(bf16[64,2048]{1,0:T(8,128)(2,1)S(1)} %add_convert_fusion.2), channel_id=1, source_target_pairs={{0,4},{1,5},{4,8},{5,9},{8,12},{9,13},{12,14},{13,15},{14,10},{15,... | collective-permute-start | bytes 786440 | tf_op jit(solution)/shard_map/ppermute | solution.py:186
  71.5 3.9 %collective-permute-done.17 = bf16[64,2048]{1,0:T(8,128)(2,1)S(1)} collective-permute-done((bf16[64,2048]{1,0:T(8,128)(2,1)S(1)}, bf16[64,2048]{1,0:T(8,128)(2,1)S(1)}, u32[]{:S(2)}, u32[]{:S(2)}) %collective-permute-start.17) | collective-permute-done | bytes 262176 | tf_op jit(solution)/shard_map/ppermute | solution.py:186
  75.4 0.1 add_convert_fusion.5
  75.5 1.6 %collective-permute-start.18 = (bf16[64,2048]{1,0:T(8,128)(2,1)S(1)}, bf16[64,2048]{1,0:T(8,128)(2,1)S(1)}, u32[]{:S(2)}, u32[]{:S(2)}) collective-permute-start(bf16[64,2048]{1,0:T(8,128)(2,1)S(1)} %add_convert_fusion.5), channel_id=1, source_target_pairs={{0,4},{1,5},{4,8},{5,9},{8,12},{9,13},{12,14},{13,15},{14,10},{15,... | collective-permute-start | bytes 786440 | tf_op jit(solution)/shard_map/ppermute | solution.py:186
  77.1 0.1 add_convert_fusion.8
  77.2 0.5 collective-permute-start.14
  77.7 0.9 collective-permute-done.12
  78.5 2.5 %collective-permute-done.22 = bf16[64,2048]{1,0:T(8,128)(2,1)S(1)} collective-permute-done((bf16[64,2048]{1,0:T(8,128)(2,1)S(1)}, bf16[64,2048]{1,0:T(8,128)(2,1)S(1)}, u32[]{:S(2)}, u32[]{:S(2)}) %collective-permute-start.22) | collective-permute-done | bytes 262176 | tf_op jit(solution)/shard_map/ppermute | solution.py:186
  81.0 0.1 add_convert_fusion.1
  81.1 1.6 %collective-permute-start.23 = (bf16[64,2048]{1,0:T(8,128)(2,1)S(1)}, bf16[64,2048]{1,0:T(8,128)(2,1)S(1)}, u32[]{:S(2)}, u32[]{:S(2)}) collective-permute-start(bf16[64,2048]{1,0:T(8,128)(2,1)S(1)} %add_convert_fusion.1), channel_id=1, source_target_pairs={{0,4},{1,5},{4,8},{5,9},{8,12},{9,13},{12,14},{13,15},{14,10},{15,... | collective-permute-start | bytes 786440 | tf_op jit(solution)/shard_map/ppermute | solution.py:186
  82.7 0.1 add_convert_fusion.3
  82.8 0.5 collective-permute-start.20
  83.3 3.3 %collective-permute-done.18 = bf16[64,2048]{1,0:T(8,128)(2,1)S(1)} collective-permute-done((bf16[64,2048]{1,0:T(8,128)(2,1)S(1)}, bf16[64,2048]{1,0:T(8,128)(2,1)S(1)}, u32[]{:S(2)}, u32[]{:S(2)}) %collective-permute-start.18) | collective-permute-done | bytes 262176 | tf_op jit(solution)/shard_map/ppermute | solution.py:186
  86.6 0.1 add_convert_fusion.4
  86.7 1.6 %collective-permute-start.19 = (bf16[64,2048]{1,0:T(8,128)(2,1)S(1)}, bf16[64,2048]{1,0:T(8,128)(2,1)S(1)}, u32[]{:S(2)}, u32[]{:S(2)}) collective-permute-start(bf16[64,2048]{1,0:T(8,128)(2,1)S(1)} %add_convert_fusion.4), channel_id=1, source_target_pairs={{0,4},{1,5},{4,8},{5,9},{8,12},{9,13},{12,14},{13,15},{14,10},{15,... | collective-permute-start | bytes 786440 | tf_op jit(solution)/shard_map/ppermute | solution.py:186
  88.3 0.1 add_convert_fusion.7
  88.4 0.5 collective-permute-start.15
  88.9 2.7 %shard_map.90 = (bf16[64,2048]{1,0:T(8,128)(2,1)S(1)}, bf16[64,2048]{1,0:T(8,128)(2,1)S(1)}, f32[2,128]{1,0:T(2,128)S(1)}) custom-call(bf16[128,2176]{1,0:T(8,128)(2,1)S(1)} %copy-done, f32[2,128]{1,0:T(2,128)S(1)} %compare_convert_fusion.refs_2_.refs_1_, bf16[128,256]{1,0:T(8,128)(2,1)S(1)} %select_convert_fusion.refs_3_.refs_2_, ...), custom_call_target="tpu_custom_call" | custom-call | flops 2415919104 | bytes 1048576 | tf_op jit(solution)/shard_map/pallas_call | solution.py:158
  91.6 0.6 collective-permute-done.23
  92.2 0.1 add_convert_fusion
  92.3 1.6 %collective-permute-start.24 = (bf16[64,2048]{1,0:T(8,128)(2,1)S(1)}, bf16[64,2048]{1,0:T(8,128)(2,1)S(1)}, u32[]{:S(2)}, u32[]{:S(2)}) collective-permute-start(bf16[64,2048]{1,0:T(8,128)(2,1)S(1)} %add_convert_fusion), channel_id=1, source_target_pairs={{0,4},{1,5},{4,8},{5,9},{8,12},{9,13},{12,14},{13,15},{14,10},{15,... | collective-permute-start | bytes 786440 | tf_op jit(solution)/shard_map/ppermute | solution.py:186
  93.9 0.9 collective-permute-done.15
  94.8 0.1 add_convert_fusion.6
  94.9 0.5 collective-permute-start.16
  95.4 1.1 %collective-permute-done.25 = f32[2,128]{1,0:T(2,128)S(1)} collective-permute-done((f32[2,128]{1,0:T(2,128)S(1)}, f32[2,128]{1,0:T(2,128)S(1)}, u32[]{:S(2)}, u32[]{:S(2)}) %collective-permute-start.25) | collective-permute-done | bytes 1056 | tf_op jit(solution)/shard_map/ppermute | solution.py:188
  96.6 0.6 multiply_reduce_fusion
  97.2 0.6 fusion.2
  98.4 0.4 collective-permute-done.24.refs_5_
  98.8 2.5 %collective-permute-done.16.refs_1_ = bf16[64,2048]{1,0:T(8,128)(2,1)S(1)} collective-permute-done((bf16[64,2048]{1,0:T(8,128)(2,1)S(1)}, bf16[64,2048]{1,0:T(8,128)(2,1)S(1)}, u32[]{:S(2)}, u32[]{:S(2)}) %collective-permute-start.16) | collective-permute-done | bytes 262176 | tf_op jit(solution)/shard_map/ppermute | solution.py:187
  101.3 1.0 shard_map.92
  (21 shorter events, 0.1 us)
Async XLA Ops:
  0.6 21.1 %collective-permute-start.4 = (bf16[2048,768]{1,0:T(8,128)(2,1)}, bf16[2048,768]{1,0:T(8,128)(2,1)}, u32[]{:S(2)}, u32[]{:S(2)}) collective-permute-start(bf16[2048,768]{1,0:T(8,128)(2,1)} %bitcast.9), channel_id=1, source_target_pairs={{0,1},{1,0},{2,3},{3,2},{4,5},{5,4},{6,7},{7,6},{8,9},{9,8},{10,11... | collective-permute-start | bytes 9437192 | tf_op jit(solution)/shard_map/ppermute | solution.py:188
  1.1 20.6 %collective-permute-start.5 = (bf16[2048,768]{1,0:T(8,128)(2,1)}, bf16[2048,768]{1,0:T(8,128)(2,1)}, u32[]{:S(2)}, u32[]{:S(2)}) collective-permute-start(bf16[2048,768]{1,0:T(8,128)(2,1)} %bitcast.11), channel_id=1, source_target_pairs={{0,1},{1,0},{2,3},{3,2},{4,5},{5,4},{6,7},{7,6},{8,9},{9,8},{10,11... | collective-permute-start | bytes 9437192 | tf_op jit(solution)/shard_map/ppermute | solution.py:188
  1.2 20.5 %collective-permute-start.6 = (bf16[768,2048]{1,0:T(8,128)(2,1)}, bf16[768,2048]{1,0:T(8,128)(2,1)}, u32[]{:S(2)}, u32[]{:S(2)}) collective-permute-start(bf16[768,2048]{1,0:T(8,128)(2,1)} %bitcast.13), channel_id=1, source_target_pairs={{0,1},{1,0},{2,3},{3,2},{4,5},{5,4},{6,7},{7,6},{8,9},{9,8},{10,11... | collective-permute-start | bytes 9437192 | tf_op jit(solution)/shard_map/ppermute | solution.py:188
  3.6 16.1 %collective-permute-start = (bf16[128,2176]{1,0:T(8,128)(2,1)}, bf16[128,2176]{1,0:T(8,128)(2,1)S(1)}, u32[]{:S(2)}, u32[]{:S(2)}) collective-permute-start(bf16[128,2176]{1,0:T(8,128)(2,1)} %shard_map.85.refs_0_), channel_id=1, source_target_pairs={{0,4},{1,5},{4,8},{5,9},{8,12},{9,13},{12,14},{13,15},{14,10},{15,... | collective-permute-start | bytes 1671176 | tf_op jit(solution)/shard_map/ppermute | solution.py:186
  6.3 15.2 %collective-permute-start.2 = (bf16[128,2176]{1,0:T(8,128)(2,1)}, bf16[128,2176]{1,0:T(8,128)(2,1)S(1)}, u32[]{:S(2)}, u32[]{:S(2)}) collective-permute-start(bf16[128,2176]{1,0:T(8,128)(2,1)} %shard_map.85.refs_0_), channel_id=1, source_target_pairs={{0,2},{1,3},{4,0},{5,1},{8,4},{9,5},{12,8},{13,9},{14,12},{15,13},... | collective-permute-start | bytes 1671176 | tf_op jit(solution)/shard_map/ppermute | solution.py:187
  19.6 14.4 %collective-permute-start.1 = (bf16[128,2176]{1,0:T(8,128)(2,1)S(1)}, bf16[128,2176]{1,0:T(8,128)(2,1)S(1)}, u32[]{:S(2)}, u32[]{:S(2)}) collective-permute-start(bf16[128,2176]{1,0:T(8,128)(2,1)S(1)} %collective-permute-done.refs_0_), channel_id=1, source_target_pairs={{0,4},{1,5},{4,8},{5,9},{8,12},{9,13},{12,14},{13,15},{14,10},{15,... | collective-permute-start | bytes 1671176 | tf_op jit(solution)/shard_map/ppermute | solution.py:186
  21.4 13.9 %collective-permute-start.3 = (bf16[128,2176]{1,0:T(8,128)(2,1)S(1)}, bf16[128,2176]{1,0:T(8,128)(2,1)S(1)}, u32[]{:S(2)}, u32[]{:S(2)}) collective-permute-start(bf16[128,2176]{1,0:T(8,128)(2,1)S(1)} %collective-permute-done.2.refs_1_), channel_id=1, source_target_pairs={{0,2},{1,3},{4,0},{5,1},{8,4},{9,5},{12,8},{13,9},{14,12},{15,13},... | collective-permute-start | bytes 1671176 | tf_op jit(solution)/shard_map/ppermute | solution.py:187
  35.3 13.0 %collective-permute-start.7 = (bf16[128,2176]{1,0:T(8,128)(2,1)S(1)}, bf16[128,2176]{1,0:T(8,128)(2,1)S(1)}, u32[]{:S(2)}, u32[]{:S(2)}) collective-permute-start(bf16[128,2176]{1,0:T(8,128)(2,1)S(1)} %collective-permute-done.1.refs_0_), channel_id=1, source_target_pairs={{0,4},{1,5},{4,8},{5,9},{8,12},{9,13},{12,14},{13,15},{14,10},{15,... | collective-permute-start | bytes 1671176 | tf_op jit(solution)/shard_map/ppermute | solution.py:186
  36.9 12.7 %collective-permute-start.8 = (bf16[128,2176]{1,0:T(8,128)(2,1)S(1)}, bf16[128,2176]{1,0:T(8,128)(2,1)S(1)}, u32[]{:S(2)}, u32[]{:S(2)}) collective-permute-start(bf16[128,2176]{1,0:T(8,128)(2,1)S(1)} %collective-permute-done.3.refs_1_), channel_id=1, source_target_pairs={{0,2},{1,3},{4,0},{5,1},{8,4},{9,5},{12,8},{13,9},{14,12},{15,13},... | collective-permute-start | bytes 1671176 | tf_op jit(solution)/shard_map/ppermute | solution.py:187
  49.7 7.5 %collective-permute-start.10 = (bf16[64,2176]{1,0:T(8,128)(2,1)S(1)}, bf16[64,2176]{1,0:T(8,128)(2,1)S(1)}, u32[]{:S(2)}, u32[]{:S(2)}) collective-permute-start(bf16[64,2176]{1,0:T(8,128)(2,1)S(1)} %slice.10), channel_id=1, source_target_pairs={{0,2},{1,3},{4,0},{5,1},{8,4},{9,5},{12,8},{13,9},{14,12},{15,13},... | collective-permute-start | bytes 835592 | tf_op jit(solution)/shard_map/ppermute | solution.py:187
  50.2 7.0 %collective-permute-start.9 = (bf16[64,2176]{1,0:T(8,128)(2,1)S(1)}, bf16[64,2176]{1,0:T(8,128)(2,1)S(1)}, u32[]{:S(2)}, u32[]{:S(2)}) collective-permute-start(bf16[64,2176]{1,0:T(8,128)(2,1)S(1)} %slice.9), channel_id=1, source_target_pairs={{0,4},{1,5},{4,8},{5,9},{8,12},{9,13},{12,14},{13,15},{14,10},{15,... | collective-permute-start | bytes 835592 | tf_op jit(solution)/shard_map/ppermute | solution.py:186
  57.2 7.9 %collective-permute-start.11 = (bf16[64,2048]{1,0:T(8,128)(2,1)S(1)}, bf16[64,2048]{1,0:T(8,128)(2,1)S(1)}, u32[]{:S(2)}, u32[]{:S(2)}) collective-permute-start(bf16[64,2048]{1,0:T(8,128)(2,1)S(1)} %get-tuple-element.73), channel_id=1, source_target_pairs={{0,2},{1,3},{4,0},{5,1},{8,4},{9,5},{12,8},{13,9},{14,12},{15,13},... | collective-permute-start | bytes 786440 | tf_op jit(solution)/shard_map/ppermute | solution.py:187
  60.5 9.3 %collective-permute-start.21 = (bf16[64,2048]{1,0:T(8,128)(2,1)S(1)}, bf16[64,2048]{1,0:T(8,128)(2,1)S(1)}, u32[]{:S(2)}, u32[]{:S(2)}) collective-permute-start(bf16[64,2048]{1,0:T(8,128)(2,1)S(1)} %get-tuple-element.91), channel_id=1, source_target_pairs={{0,4},{1,5},{4,8},{5,9},{8,12},{9,13},{12,14},{13,15},{14,10},{15,... | collective-permute-start | bytes 786440 | tf_op jit(solution)/shard_map/ppermute | solution.py:186
  62.1 13.3 %collective-permute-start.17 = (bf16[64,2048]{1,0:T(8,128)(2,1)S(1)}, bf16[64,2048]{1,0:T(8,128)(2,1)S(1)}, u32[]{:S(2)}, u32[]{:S(2)}) collective-permute-start(bf16[64,2048]{1,0:T(8,128)(2,1)S(1)} %get-tuple-element.84), channel_id=1, source_target_pairs={{0,4},{1,5},{4,8},{5,9},{8,12},{9,13},{12,14},{13,15},{14,10},{15,... | collective-permute-start | bytes 786440 | tf_op jit(solution)/shard_map/ppermute | solution.py:186
  63.7 25.2 %copy-start = (bf16[128,2176]{1,0:T(8,128)(2,1)S(1)}, bf16[128,2176]{1,0:T(8,128)(2,1)}, u32[]{:S(2)}) copy-start(bf16[128,2176]{1,0:T(8,128)(2,1)} %shard_map.85.refs_0_) | copy-start | bytes 1671172
  63.7 13.4 %collective-permute-start.13 = (bf16[64,2048]{1,0:T(8,128)(2,1)S(1)}, bf16[64,2048]{1,0:T(8,128)(2,1)S(1)}, u32[]{:S(2)}, u32[]{:S(2)}) collective-permute-start(bf16[64,2048]{1,0:T(8,128)(2,1)S(1)} %get-tuple-element.81), channel_id=1, source_target_pairs={{0,2},{1,3},{4,0},{5,1},{8,4},{9,5},{12,8},{13,9},{14,12},{15,13},... | collective-permute-start | bytes 786440 | tf_op jit(solution)/shard_map/ppermute | solution.py:187
  65.2 13.3 %collective-permute-start.12 = (bf16[64,2048]{1,0:T(8,128)(2,1)S(1)}, bf16[64,2048]{1,0:T(8,128)(2,1)S(1)}, u32[]{:S(2)}, u32[]{:S(2)}) collective-permute-start(bf16[64,2048]{1,0:T(8,128)(2,1)S(1)} %add_convert_fusion.9), channel_id=1, source_target_pairs={{0,2},{1,3},{4,0},{5,1},{8,4},{9,5},{12,8},{13,9},{14,12},{15,13},... | collective-permute-start | bytes 786440 | tf_op jit(solution)/shard_map/ppermute | solution.py:187
  69.8 11.2 %collective-permute-start.22 = (bf16[64,2048]{1,0:T(8,128)(2,1)S(1)}, bf16[64,2048]{1,0:T(8,128)(2,1)S(1)}, u32[]{:S(2)}, u32[]{:S(2)}) collective-permute-start(bf16[64,2048]{1,0:T(8,128)(2,1)S(1)} %add_convert_fusion.2), channel_id=1, source_target_pairs={{0,4},{1,5},{4,8},{5,9},{8,12},{9,13},{12,14},{13,15},{14,10},{15,... | collective-permute-start | bytes 786440 | tf_op jit(solution)/shard_map/ppermute | solution.py:186
  75.5 11.2 %collective-permute-start.18 = (bf16[64,2048]{1,0:T(8,128)(2,1)S(1)}, bf16[64,2048]{1,0:T(8,128)(2,1)S(1)}, u32[]{:S(2)}, u32[]{:S(2)}) collective-permute-start(bf16[64,2048]{1,0:T(8,128)(2,1)S(1)} %add_convert_fusion.5), channel_id=1, source_target_pairs={{0,4},{1,5},{4,8},{5,9},{8,12},{9,13},{12,14},{13,15},{14,10},{15,... | collective-permute-start | bytes 786440 | tf_op jit(solution)/shard_map/ppermute | solution.py:186
  77.2 11.2 %collective-permute-start.14 = (bf16[64,2048]{1,0:T(8,128)(2,1)S(1)}, bf16[64,2048]{1,0:T(8,128)(2,1)S(1)}, u32[]{:S(2)}, u32[]{:S(2)}) collective-permute-start(bf16[64,2048]{1,0:T(8,128)(2,1)S(1)} %add_convert_fusion.8), channel_id=1, source_target_pairs={{0,2},{1,3},{4,0},{5,1},{8,4},{9,5},{12,8},{13,9},{14,12},{15,13},... | collective-permute-start | bytes 786440 | tf_op jit(solution)/shard_map/ppermute | solution.py:187
  81.1 11.2 %collective-permute-start.23 = (bf16[64,2048]{1,0:T(8,128)(2,1)S(1)}, bf16[64,2048]{1,0:T(8,128)(2,1)S(1)}, u32[]{:S(2)}, u32[]{:S(2)}) collective-permute-start(bf16[64,2048]{1,0:T(8,128)(2,1)S(1)} %add_convert_fusion.1), channel_id=1, source_target_pairs={{0,4},{1,5},{4,8},{5,9},{8,12},{9,13},{12,14},{13,15},{14,10},{15,... | collective-permute-start | bytes 786440 | tf_op jit(solution)/shard_map/ppermute | solution.py:186
  82.8 15.6 %collective-permute-start.20 = (bf16[64,2048]{1,0:T(8,128)(2,1)S(1)}, bf16[64,2048]{1,0:T(8,128)(2,1)S(1)}, u32[]{:S(2)}, u32[]{:S(2)}) collective-permute-start(bf16[64,2048]{1,0:T(8,128)(2,1)S(1)} %add_convert_fusion.3), channel_id=1, source_target_pairs={{0,2},{1,3},{4,0},{5,1},{8,4},{9,5},{12,8},{13,9},{14,12},{15,13},... | collective-permute-start | bytes 786440 | tf_op jit(solution)/shard_map/ppermute | solution.py:187
  86.7 11.7 %collective-permute-start.19 = (bf16[64,2048]{1,0:T(8,128)(2,1)S(1)}, bf16[64,2048]{1,0:T(8,128)(2,1)S(1)}, u32[]{:S(2)}, u32[]{:S(2)}) collective-permute-start(bf16[64,2048]{1,0:T(8,128)(2,1)S(1)} %add_convert_fusion.4), channel_id=1, source_target_pairs={{0,4},{1,5},{4,8},{5,9},{8,12},{9,13},{12,14},{13,15},{14,10},{15,... | collective-permute-start | bytes 786440 | tf_op jit(solution)/shard_map/ppermute | solution.py:186
  88.4 6.4 %collective-permute-start.15 = (bf16[64,2048]{1,0:T(8,128)(2,1)S(1)}, bf16[64,2048]{1,0:T(8,128)(2,1)S(1)}, u32[]{:S(2)}, u32[]{:S(2)}) collective-permute-start(bf16[64,2048]{1,0:T(8,128)(2,1)S(1)} %add_convert_fusion.7), channel_id=1, source_target_pairs={{0,2},{1,3},{4,0},{5,1},{8,4},{9,5},{12,8},{13,9},{14,12},{15,13},... | collective-permute-start | bytes 786440 | tf_op jit(solution)/shard_map/ppermute | solution.py:187
  92.3 6.5 %collective-permute-start.24 = (bf16[64,2048]{1,0:T(8,128)(2,1)S(1)}, bf16[64,2048]{1,0:T(8,128)(2,1)S(1)}, u32[]{:S(2)}, u32[]{:S(2)}) collective-permute-start(bf16[64,2048]{1,0:T(8,128)(2,1)S(1)} %add_convert_fusion), channel_id=1, source_target_pairs={{0,4},{1,5},{4,8},{5,9},{8,12},{9,13},{12,14},{13,15},{14,10},{15,... | collective-permute-start | bytes 786440 | tf_op jit(solution)/shard_map/ppermute | solution.py:186
  94.9 6.4 %collective-permute-start.16 = (bf16[64,2048]{1,0:T(8,128)(2,1)S(1)}, bf16[64,2048]{1,0:T(8,128)(2,1)S(1)}, u32[]{:S(2)}, u32[]{:S(2)}) collective-permute-start(bf16[64,2048]{1,0:T(8,128)(2,1)S(1)} %add_convert_fusion.6), channel_id=1, source_target_pairs={{0,2},{1,3},{4,0},{5,1},{8,4},{9,5},{12,8},{13,9},{14,12},{15,13},... | collective-permute-start | bytes 786440 | tf_op jit(solution)/shard_map/ppermute | solution.py:187
  95.4 1.1 %collective-permute-start.25 = (f32[2,128]{1,0:T(2,128)S(1)}, f32[2,128]{1,0:T(2,128)S(1)}, u32[]{:S(2)}, u32[]{:S(2)}) collective-permute-start(f32[2,128]{1,0:T(2,128)S(1)} %add_add_fusion), channel_id=1, source_target_pairs={{0,1},{1,0},{2,3},{3,2},{4,5},{5,4},{6,7},{7,6},{8,9},{9,8},{10,11... | collective-permute-start | bytes 3080 | tf_op jit(solution)/shard_map/ppermute | solution.py:188

commit v8 on v7

--- a/solution.py
+++ b/solution.py
@@ -28,44 +28,61 @@
     return pairs
 
 
-def pack_kernel(experts, tokens_ref, ids_hbm, gates_hbm, out_ref, ids_ref, gates_ref, arrived):
-    rows, width = tokens_ref.shape
-    lanes = out_ref.shape[1] - width
+def turn(array):
+    return pltpu.roll(array, LANES // 2, 1)
+
+
+def pack_kernel(
+    tokens_hbm, ids_hbm, gates_hbm, out_ref, tokens_ref, ids_ref, gates_ref, arrived
+):
+    half = tokens_ref.shape[0] // 2
+    columns = tokens_ref.shape[1] // LANES
+    experts = out_ref.shape[1] - columns * half
     copies = [
-        pltpu.make_async_copy(ids_hbm, ids_ref, arrived.at[0]),
-        pltpu.make_async_copy(gates_hbm, gates_ref, arrived.at[1]),
-        pltpu.make_async_copy(tokens_ref, out_ref.at[:, pl.ds(0, width)], arrived.at[2]),
+        pltpu.make_async_copy(source, target, arrived.at[i])
+        for i, (source, target) in enumerate(
+            ((ids_hbm, ids_ref), (gates_hbm, gates_ref), (tokens_hbm, tokens_ref))
+        )
     ]
     for copy in copies:
         copy.start()
     copies[0].wait()
     copies[1].wait()
-    lane = lax.broadcasted_iota(jnp.int32, (lanes, rows), 0)
-    scores = jnp.zeros((lanes, rows), jnp.int32)
+    expert = lax.broadcasted_iota(jnp.int32, (experts, LANES), 0)
+    first = lax.broadcasted_iota(jnp.int32, (experts, LANES), 1) < LANES // 2
+    scores = jnp.zeros((experts, LANES), jnp.int32)
     for k in range(ids_ref.shape[0]):
-        at, gate = ids_ref[k : k + 1, :], gates_ref[k : k + 1, :]
-        scores = jnp.where(lane == at, gate >> 8, scores)
-        scores = jnp.where(lane == at + experts, gate & 255, scores)
-    out_ref[:, width:] = scores.astype(jnp.float32).T.astype(jnp.bfloat16)
+        scores = jnp.where(expert == ids_ref[k : k + 1, :], gates_ref[k : k + 1, :], scores)
+    high = (scores >> 8).astype(jnp.float32)
+    low = (scores & 255).astype(jnp.float32)
+    halves = jnp.where(first, high, turn(low)), jnp.where(first, turn(high), low)
+    for i in range(2):
+        out_ref[i, columns * half :, :] = halves[i].astype(jnp.bfloat16)
     copies[2].wait()
+    for i in range(2):
+        for j in range(columns):
+            out_ref[i, j * half : (j + 1) * half, :] = tokens_ref[
+                i * half : (i + 1) * half, j * LANES : (j + 1) * LANES
+            ]
 
 
 def pack(tokens, expert_ids, gate_fixed, experts):
     rows, width = tokens.shape
-    lanes = -(-2 * experts // LANES) * LANES
     per_token = expert_ids.shape[1]
-    return pl.pallas_call(
-        functools.partial(pack_kernel, experts),
-        out_shape=jax.ShapeDtypeStruct((rows, width + lanes), jnp.bfloat16),
+    height = rows // 2 * (width // LANES) + experts
+    return pl.pallas_call(
+        pack_kernel,
+        out_shape=jax.ShapeDtypeStruct((2, height, LANES), jnp.bfloat16),
         in_specs=[pl.BlockSpec(memory_space=pl.ANY)] * 3,
         out_specs=pl.BlockSpec(memory_space=pltpu.VMEM),
         scratch_shapes=[
+            pltpu.VMEM((rows, width), jnp.bfloat16),
             pltpu.VMEM((per_token, rows), jnp.int32),
             pltpu.VMEM((per_token, rows), jnp.int32),
             pltpu.SemaphoreType.DMA((3,)),
         ],
         cost_estimate=pl.CostEstimate(
-            flops=rows * lanes, bytes_accessed=4 * rows * width, transcendentals=0
+            flops=rows * LANES, bytes_accessed=4 * rows * width, transcendentals=0
         ),
     )(tokens, expert_ids.T, gate_fixed.T)
 
@@ -113,26 +130,42 @@
     )(*arrays)
 
 
-def expert_kernel(sizes, piece, *refs):
-    count = len(sizes)
-    blocks = refs[:count]
-    own_ref, join_ref = refs[count : count + 2]
-    experts = [refs[count + 2 + 3 * i : count + 5 + 3 * i] for i in range(CORES)]
-    refs = refs[count + 2 + 3 * CORES :]
-    *outs, stats_ref, hidden_ref = refs
+def expert_kernel(count, piece, *refs):
+    halves = []
+    for ref in refs[:count]:
+        halves += [ref] if len(ref.shape) == 2 else [ref.at[0], ref.at[1]]
+    own_ref = refs[count]
+    experts = [refs[count + 1 + 3 * i : count + 4 + 3 * i] for i in range(CORES)]
+    *outs, stats_ref, hidden_ref = refs[count + 1 + 3 * CORES :]
     width, hidden_width = experts[0][0].shape
-    lanes = join_ref.shape[0]
-
-    scores = jnp.concatenate([block[:, width:] for block in blocks], axis=0)
-    joined = jnp.dot(scores, join_ref[...], preferred_element_type=jnp.float32)
-    weights = joined[:, :lanes] / joined[:, lanes:]
+    columns = width // LANES
+
+    scores = [half[columns * piece :, :].astype(jnp.float32) for half in halves]
+    scores = [256.0 * score + turn(score) for score in scores]
+    first = lax.broadcasted_iota(jnp.int32, scores[0].shape, 1) < LANES // 2
+    scores = jnp.concatenate(
+        [
+            jnp.where(first, scores[i], turn(scores[i + 1]))
+            for i in range(0, len(scores), 2)
+        ],
+        axis=1,
+    )
+    dense = scores / jnp.sum(scores, axis=0, keepdims=True)
+    idle = jnp.zeros((LANES - dense.shape[0], dense.shape[1]), jnp.float32)
+    weights = jnp.concatenate([dense, idle], axis=0).T
     stats_ref[0:1, :] = jnp.sum((weights > 0).astype(jnp.float32), axis=0, keepdims=True)
     stats_ref[1:2, :] = jnp.sum(weights, axis=0, keepdims=True)
     scales = [
         jnp.sum(weights * own_ref[i : i + 1, :], axis=1, keepdims=True) for i in range(CORES)
     ]
 
-    rows = jnp.concatenate([block[:, :width] for block in blocks], axis=0)
+    rows = jnp.concatenate(
+        [
+            jnp.concatenate([half[j * piece : (j + 1) * piece, :] for half in halves], axis=0)
+            for j in range(columns)
+        ],
+        axis=1,
+    )
     for i, (gate_ref, up_ref, _) in enumerate(experts):
         for start in range(0, hidden_width, HIDDEN_CHUNK):
             at = slice(start, start + HIDDEN_CHUNK)
@@ -149,17 +182,16 @@
             out_ref[:, at] = total[i * piece : (i + 1) * piece].astype(jnp.bfloat16)
 
 
-def apply_experts(blocks, piece, own, join, weights):
+def apply_experts(blocks, piece, own, weights):
     width, hidden_width = weights[0].shape
-    sizes = tuple(block.shape[0] for block in blocks)
-    total = sum(sizes)
     count = len(blocks)
+    total = piece * sum(1 if block.ndim == 2 else 2 for block in blocks)
     in_vmem = pl.BlockSpec(memory_space=pltpu.VMEM)
     return pl.pallas_call(
-        functools.partial(expert_kernel, sizes, piece),
+        functools.partial(expert_kernel, count, piece),
         out_shape=[jax.ShapeDtypeStruct((piece, width), jnp.bfloat16)] * (total // piece)
         + [jax.ShapeDtypeStruct((2, own.shape[1]), jnp.float32)],
-        in_specs=[in_vmem] * (count + 2 + len(weights)),
+        in_specs=[in_vmem] * (count + 1 + len(weights)),
         out_specs=[in_vmem] * (total // piece + 1),
         scratch_shapes=[pltpu.VMEM((CORES, total, hidden_width), jnp.bfloat16)],
         compiler_params=pltpu.CompilerParams(vmem_limit_bytes=VMEM_LIMIT),
@@ -168,7 +200,7 @@
             bytes_accessed=4 * total * width,
             transcendentals=CORES * total * hidden_width,
         ),
-    )(*blocks, own, join, *weights)
+    )(*blocks, own, *weights)
 
 
 def body(tokens, expert_ids, gate_fixed, gate_weight, up_weight, down_weight):
@@ -193,18 +225,11 @@
     others = [sibling(weight) for weight in weights]
     weights = hold([pltpu.with_memory_space_constraint(w, pltpu.HBM) for w in weights + others])
     packed = pack(tokens, expert_ids, gate_fixed, expert_count)
-    lanes = packed.shape[1] - model_width
-    own = (jnp.arange(lanes)[None] == jnp.stack([node, node ^ 1])[:, None]).astype(jnp.float32)
-    source, target = jnp.arange(lanes)[:, None], jnp.arange(2 * lanes)[None]
-    is_low = source >= expert_count
-    to_expert = (target == jnp.where(is_low, source - expert_count, source)) | (target >= lanes)
-    join = jnp.where(
-        to_expert & (source < 2 * expert_count), jnp.where(is_low, 1.0, 256.0), 0.0
-    ).astype(jnp.bfloat16)
+    own = (jnp.arange(LANES)[None] == jnp.stack([node, node ^ 1])[:, None]).astype(jnp.float32)
     stats = []
 
     def run(blocks):
-        res = apply_experts(blocks, half, own, join, weights)
+        res = apply_experts(blocks, half, own, weights)
         stats.append(res[-1])
         return res[:-1]
 
@@ -222,7 +247,7 @@
         if k < far - 1:
             low, high = right(low), left(high)
         else:
-            low, high = right(low[:half]), left(high[half:])
+            low, high = right(low[0]), left(high[1])
         outs[k] = run(here)
     res = run(here)
 

time: 104 us -> 102 us (0.981)
  waiting for transfers between devices: 43.3 us -> 41.6 us
    ppermute x11, starting transfers between devices: 4.63 us -> 6.36 us  [body(): left = lambda a: lax.ppermute(a, 'node', to_left)]
    ppermute x11, starting transfers between devices: 19.3 us -> 17.8 us  [body(): right = lambda a: lax.ppermute(a, 'node', to_right)]
    ppermute x11, waiting for transfers between devices: 34.2 us -> 33.2 us  [body(): right = lambda a: lax.ppermute(a, 'node', to_right)]
  transfers between devices with their start and end apart: 26 -> 26, of which waited for: 16 -> 15; matrix products, arithmetic and copies ran while one was open for 2% -> 2% of each run, Pallas kernels for 28% -> 29%
where the time goes in v8:
time: 102 us
  waiting for transfers between devices  41.6 us (41%)
  Pallas kernels  30.5 us (30%)
  starting transfers between devices  25.2 us (25%)
  between operations  2.58 us (3%)
  other arithmetic  2 us (2%)
    ppermute x11, waiting for transfers between devices, body(): right = lambda a: lax.ppermute(a, 'node', to_right)  33.2 us
    pallas_call x5, Pallas kernels, apply_experts(): pl.pallas_call(functools.partial(expert_kernel, count, piece), out_shape=...  21 us
    ppermute x11, starting transfers between devices, body(): right = lambda a: lax.ppermute(a, 'node', to_right)  17.8 us
    ppermute x11, waiting for transfers between devices, body(): left = lambda a: lax.ppermute(a, 'node', to_left)  7.3 us
    pallas_call x1, Pallas kernels, hold(): pl.pallas_call(hold_kernel, out_shape=[pltpu.VMEM(array.shape, array.dtyp...  6.5 us
    ppermute x11, starting transfers between devices, body(): left = lambda a: lax.ppermute(a, 'node', to_left)  6.36 us
  transfers between devices with their start and end apart: 26, of which 15 were waited for; matrix products, arithmetic and copies ran while one was open for 2% of the time, Pallas kernels for 29%

profile of v8, /device:TPU:0, one launch (start us, length us, event | category | flops | bytes accessed | tf_op | source)
XLA Modules:
  0.0 101.9 jit_solution(1002970231369934982)
XLA Ops:
  0.6 0.5 collective-permute-start.4
  1.1 0.1 collective-permute-start.5
  1.2 0.4 collective-permute-start.6
  1.7 2.0 %shard_map.85.refs_0_ = bf16[2,1040,128]{2,1,0:T(8,128)(2,1)} custom-call(bf16[128,2048]{1,0:T(8,128)(2,1)} %tokens_hbm.1, s32[8,128]{1,0:T(8,128)} %bitcast.19, s32[8,128]{1,0:T(8,128)} %bitcast.20), custom_call_target="tpu_custom_call" | custom-call | flops 16384 | bytes 1048576 | tf_op jit(solution)/shard_map/pallas_call | solution.py:73
  3.6 2.7 %collective-permute-start = (bf16[2,1040,128]{2,1,0:T(8,128)(2,1)}, bf16[2,1040,128]{2,1,0:T(8,128)(2,1)S(1)}, u32[]{:S(2)}, u32[]{:S(2)}) collective-permute-start(bf16[2,1040,128]{2,1,0:T(8,128)(2,1)} %shard_map.85.refs_0_), channel_id=1, source_target_pairs={{0,4},{1,5},{4,8},{5,9},{8,12},{9,13},{12,14},{13,15},{14,10},{15,... | collective-permute-start | bytes 1597448 | tf_op jit(solution)/shard_map/ppermute | solution.py:218
  6.4 0.0 collective-permute-start.2
  6.4 0.1 pad_add_fusion
  6.4 12.8 %collective-permute-done.refs_0_ = bf16[2,1040,128]{2,1,0:T(8,128)(2,1)S(1)} collective-permute-done((bf16[2,1040,128]{2,1,0:T(8,128)(2,1)}, bf16[2,1040,128]{2,1,0:T(8,128)(2,1)S(1)}, u32[]{:S(2)}, u32[]{:S(2)}) %collective-permute-start) | collective-permute-done | bytes 532512 | tf_op jit(solution)/shard_map/ppermute | solution.py:218
  19.2 1.8 %collective-permute-start.1 = (bf16[2,1040,128]{2,1,0:T(8,128)(2,1)S(1)}, bf16[2,1040,128]{2,1,0:T(8,128)(2,1)S(1)}, u32[]{:S(2)}, u32[]{:S(2)}) collective-permute-start(bf16[2,1040,128]{2,1,0:T(8,128)(2,1)S(1)} %collective-permute-done.refs_0_), channel_id=1, source_target_pairs={{0,4},{1,5},{4,8},{5,9},{8,12},{9,13},{12,14},{13,15},{14,10},{15,... | collective-permute-start | bytes 1597448 | tf_op jit(solution)/shard_map/ppermute | solution.py:218
  21.0 0.0 collective-permute-done.2.refs_1_
  21.0 0.2 collective-permute-start.3
  21.2 0.1 compare_convert_fusion.refs_2_.refs_1_
  21.3 6.5 %shard_map.86 = (bf16[2048,768]{1,0:T(8,128)(2,1)S(1)}, bf16[2048,768]{1,0:T(8,128)(2,1)S(1)}, bf16[768,2048]{1,0:T(8,128)(2,1)S(1)}, bf16[2048,768]{1,0:T(8,128...) custom-call(bf16[2048,768]{1,0:T(8,128)(2,1)} %bitcast.14, bf16[2048,768]{1,0:T(8,128)(2,1)} %bitcast.16, ...), custom_call_target="tpu_custom_call" | custom-call | tf_op jit(solution)/shard_map/pallas_call | solution.py:123
  27.8 5.2 %shard_map.87 = (bf16[64,2048]{1,0:T(8,128)(2,1)S(1)}, bf16[64,2048]{1,0:T(8,128)(2,1)S(1)}, bf16[64,2048]{1,0:T(8,128)(2,1)S(1)}, bf16[64,2048]{1,0:T(8,128)(2,1)S(1)}, f32[2,128]{1,0:T(2,128)S(1)}) custom-call(bf16[2,1040,128]{2,1,0:T(8,128)(2,1)S(1)} %collective-permute-done.refs_0_, bf16[2,1040,128]{2,1,0:T(8,128)(2,1)S(1)} %collective-permute-done.2.refs_1_, ...), custom_call_target="tpu_custom_call" | custom-call | flops 4831838208 | bytes 2097152 | tf_op jit(solution)/shard_map/pallas_call | solution.py:190
  33.0 0.0 collective-permute-done.1.refs_0_
  33.1 1.3 %collective-permute-done.3.refs_1_ = bf16[2,1040,128]{2,1,0:T(8,128)(2,1)S(1)} collective-permute-done((bf16[2,1040,128]{2,1,0:T(8,128)(2,1)S(1)}, bf16[2,1040,128]{2,1,0:T(8,128)(2,1)S(1)}, u32[]{:S(2)}, u32[]{:S(2)}) %collective-permute-start.3) | collective-permute-done | bytes 532512 | tf_op jit(solution)/shard_map/ppermute | solution.py:219
  34.4 1.6 %collective-permute-start.7 = (bf16[2,1040,128]{2,1,0:T(8,128)(2,1)S(1)}, bf16[2,1040,128]{2,1,0:T(8,128)(2,1)S(1)}, u32[]{:S(2)}, u32[]{:S(2)}) collective-permute-start(bf16[2,1040,128]{2,1,0:T(8,128)(2,1)S(1)} %collective-permute-done.1.refs_0_), channel_id=1, source_target_pairs={{0,4},{1,5},{4,8},{5,9},{8,12},{9,13},{12,14},{13,15},{14,10},{15,... | collective-permute-start | bytes 1597448 | tf_op jit(solution)/shard_map/ppermute | solution.py:218
  36.0 0.4 collective-permute-start.8
  36.4 5.2 %shard_map.88 = (bf16[64,2048]{1,0:T(8,128)(2,1)S(1)}, bf16[64,2048]{1,0:T(8,128)(2,1)S(1)}, bf16[64,2048]{1,0:T(8,128)(2,1)S(1)}, bf16[64,2048]{1,0:T(8,128)(2,1)S(1)}, f32[2,128]{1,0:T(2,128)S(1)}) custom-call(bf16[2,1040,128]{2,1,0:T(8,128)(2,1)S(1)} %collective-permute-done.1.refs_0_, bf16[2,1040,128]{2,1,0:T(8,128)(2,1)S(1)} %collective-permute-done.3.refs_1_, ...), custom_call_target="tpu_custom_call" | custom-call | flops 4831838208 | bytes 2097152 | tf_op jit(solution)/shard_map/pallas_call | solution.py:190
  41.6 5.2 %collective-permute-done.7.refs_0_ = bf16[2,1040,128]{2,1,0:T(8,128)(2,1)S(1)} collective-permute-done((bf16[2,1040,128]{2,1,0:T(8,128)(2,1)S(1)}, bf16[2,1040,128]{2,1,0:T(8,128)(2,1)S(1)}, u32[]{:S(2)}, u32[]{:S(2)}) %collective-permute-start.7) | collective-permute-done | bytes 532512 | tf_op jit(solution)/shard_map/ppermute | solution.py:218
  46.8 1.3 %collective-permute-done.8.refs_1_ = bf16[2,1040,128]{2,1,0:T(8,128)(2,1)S(1)} collective-permute-done((bf16[2,1040,128]{2,1,0:T(8,128)(2,1)S(1)}, bf16[2,1040,128]{2,1,0:T(8,128)(2,1)S(1)}, u32[]{:S(2)}, u32[]{:S(2)}) %collective-permute-start.8) | collective-permute-done | bytes 532512 | tf_op jit(solution)/shard_map/ppermute | solution.py:219
  48.2 0.5 collective-permute-start.10
  48.7 1.8 %collective-permute-start.9 = (bf16[1040,128]{1,0:T(8,128)(2,1)S(1)}, bf16[1040,128]{1,0:T(8,128)(2,1)S(1)}, u32[]{:S(2)}, u32[]{:S(2)}) collective-permute-start(bf16[1040,128]{1,0:T(8,128)(2,1)S(1)} %slice_bitcast_fusion.1), channel_id=1, source_target_pairs={{0,4},{1,5},{4,8},{5,9},{8,12},{9,13},{12,14},{13,15},{14,10},{15,... | collective-permute-start | bytes 798728 | tf_op jit(solution)/shard_map/ppermute | solution.py:218
  50.5 5.2 %shard_map.89 = (bf16[64,2048]{1,0:T(8,128)(2,1)S(1)}, bf16[64,2048]{1,0:T(8,128)(2,1)S(1)}, bf16[64,2048]{1,0:T(8,128)(2,1)S(1)}, bf16[64,2048]{1,0:T(8,128)(2,1)S(1)}, f32[2,128]{1,0:T(2,128)S(1)}) custom-call(bf16[2,1040,128]{2,1,0:T(8,128)(2,1)S(1)} %collective-permute-done.7.refs_0_, bf16[2,1040,128]{2,1,0:T(8,128)(2,1)S(1)} %collective-permute-done.8.refs_1_, ...), custom_call_target="tpu_custom_call" | custom-call | flops 4831838208 | bytes 2097152 | tf_op jit(solution)/shard_map/pallas_call | solution.py:190
  55.7 0.7 collective-permute-start.11
  56.5 2.7 %shard_map.91 = (bf16[64,2048]{1,0:T(8,128)(2,1)S(1)}, bf16[64,2048]{1,0:T(8,128)(2,1)S(1)}, f32[2,128]{1,0:T(2,128)S(1)}) custom-call(bf16[1040,128]{1,0:T(8,128)(2,1)S(1)} %collective-permute-done.9.refs_0_, bf16[1040,128]{1,0:T(8,128)(2,1)S(1)} %collective-permute-done.10.refs_1_, f32[2,128]{1,0:T(2,128)S(1)} %compare_convert_fusion.refs_2_.refs_1_, ...), custom_call_target="tpu_custom_call" | custom-call | flops 2415919104 | bytes 1048576 | tf_op jit(solution)/shard_map/pallas_call | solution.py:190
  59.2 1.4 %collective-permute-start.21 = (bf16[64,2048]{1,0:T(8,128)(2,1)S(1)}, bf16[64,2048]{1,0:T(8,128)(2,1)S(1)}, u32[]{:S(2)}, u32[]{:S(2)}) collective-permute-start(bf16[64,2048]{1,0:T(8,128)(2,1)S(1)} %get-tuple-element.91), channel_id=1, source_target_pairs={{0,4},{1,5},{4,8},{5,9},{8,12},{9,13},{12,14},{13,15},{14,10},{15,... | collective-permute-start | bytes 786440 | tf_op jit(solution)/shard_map/ppermute | solution.py:218
  60.6 1.6 %collective-permute-start.17 = (bf16[64,2048]{1,0:T(8,128)(2,1)S(1)}, bf16[64,2048]{1,0:T(8,128)(2,1)S(1)}, u32[]{:S(2)}, u32[]{:S(2)}) collective-permute-start(bf16[64,2048]{1,0:T(8,128)(2,1)S(1)} %get-tuple-element.84), channel_id=1, source_target_pairs={{0,4},{1,5},{4,8},{5,9},{8,12},{9,13},{12,14},{13,15},{14,10},{15,... | collective-permute-start | bytes 786440 | tf_op jit(solution)/shard_map/ppermute | solution.py:218
  62.2 0.4 collective-permute-start.13
  62.6 1.0 %collective-permute-done.11 = bf16[64,2048]{1,0:T(8,128)(2,1)S(1)} collective-permute-done((bf16[64,2048]{1,0:T(8,128)(2,1)S(1)}, bf16[64,2048]{1,0:T(8,128)(2,1)S(1)}, u32[]{:S(2)}, u32[]{:S(2)}) %collective-permute-start.11) | collective-permute-done | bytes 262176 | tf_op jit(solution)/shard_map/ppermute | solution.py:219
  63.7 0.1 add_convert_fusion.9
  63.7 1.0 %collective-permute-start.12 = (bf16[64,2048]{1,0:T(8,128)(2,1)S(1)}, bf16[64,2048]{1,0:T(8,128)(2,1)S(1)}, u32[]{:S(2)}, u32[]{:S(2)}) collective-permute-start(bf16[64,2048]{1,0:T(8,128)(2,1)S(1)} %add_convert_fusion.9), channel_id=1, source_target_pairs={{0,2},{1,3},{4,0},{5,1},{8,4},{9,5},{12,8},{13,9},{14,12},{15,13},... | collective-permute-start | bytes 786440 | tf_op jit(solution)/shard_map/ppermute | solution.py:219
  64.8 3.7 %collective-permute-done.21 = bf16[64,2048]{1,0:T(8,128)(2,1)S(1)} collective-permute-done((bf16[64,2048]{1,0:T(8,128)(2,1)S(1)}, bf16[64,2048]{1,0:T(8,128)(2,1)S(1)}, u32[]{:S(2)}, u32[]{:S(2)}) %collective-permute-start.21) | collective-permute-done | bytes 262176 | tf_op jit(solution)/shard_map/ppermute | solution.py:218
  68.5 0.1 add_convert_fusion.2
  68.6 1.4 %collective-permute-start.22 = (bf16[64,2048]{1,0:T(8,128)(2,1)S(1)}, bf16[64,2048]{1,0:T(8,128)(2,1)S(1)}, u32[]{:S(2)}, u32[]{:S(2)}) collective-permute-start(bf16[64,2048]{1,0:T(8,128)(2,1)S(1)} %add_convert_fusion.2), channel_id=1, source_target_pairs={{0,4},{1,5},{4,8},{5,9},{8,12},{9,13},{12,14},{13,15},{14,10},{15,... | collective-permute-start | bytes 786440 | tf_op jit(solution)/shard_map/ppermute | solution.py:218
  69.9 4.2 %collective-permute-done.17 = bf16[64,2048]{1,0:T(8,128)(2,1)S(1)} collective-permute-done((bf16[64,2048]{1,0:T(8,128)(2,1)S(1)}, bf16[64,2048]{1,0:T(8,128)(2,1)S(1)}, u32[]{:S(2)}, u32[]{:S(2)}) %collective-permute-start.17) | collective-permute-done | bytes 262176 | tf_op jit(solution)/shard_map/ppermute | solution.py:218
  74.1 0.1 add_convert_fusion.5
  74.2 1.4 %collective-permute-start.18 = (bf16[64,2048]{1,0:T(8,128)(2,1)S(1)}, bf16[64,2048]{1,0:T(8,128)(2,1)S(1)}, u32[]{:S(2)}, u32[]{:S(2)}) collective-permute-start(bf16[64,2048]{1,0:T(8,128)(2,1)S(1)} %add_convert_fusion.5), channel_id=1, source_target_pairs={{0,4},{1,5},{4,8},{5,9},{8,12},{9,13},{12,14},{13,15},{14,10},{15,... | collective-permute-start | bytes 786440 | tf_op jit(solution)/shard_map/ppermute | solution.py:218
  75.6 0.1 add_convert_fusion.8
  75.6 0.7 collective-permute-start.14
  76.4 0.6 collective-permute-done.12
  77.0 2.7 %collective-permute-done.22 = bf16[64,2048]{1,0:T(8,128)(2,1)S(1)} collective-permute-done((bf16[64,2048]{1,0:T(8,128)(2,1)S(1)}, bf16[64,2048]{1,0:T(8,128)(2,1)S(1)}, u32[]{:S(2)}, u32[]{:S(2)}) %collective-permute-start.22) | collective-permute-done | bytes 262176 | tf_op jit(solution)/shard_map/ppermute | solution.py:218
  79.7 0.1 add_convert_fusion.1
  79.8 1.4 %collective-permute-start.23 = (bf16[64,2048]{1,0:T(8,128)(2,1)S(1)}, bf16[64,2048]{1,0:T(8,128)(2,1)S(1)}, u32[]{:S(2)}, u32[]{:S(2)}) collective-permute-start(bf16[64,2048]{1,0:T(8,128)(2,1)S(1)} %add_convert_fusion.1), channel_id=1, source_target_pairs={{0,4},{1,5},{4,8},{5,9},{8,12},{9,13},{12,14},{13,15},{14,10},{15,... | collective-permute-start | bytes 786440 | tf_op jit(solution)/shard_map/ppermute | solution.py:218
  81.2 0.1 add_convert_fusion.3
  81.2 0.7 collective-permute-start.20
  82.0 3.3 %collective-permute-done.18 = bf16[64,2048]{1,0:T(8,128)(2,1)S(1)} collective-permute-done((bf16[64,2048]{1,0:T(8,128)(2,1)S(1)}, bf16[64,2048]{1,0:T(8,128)(2,1)S(1)}, u32[]{:S(2)}, u32[]{:S(2)}) %collective-permute-start.18) | collective-permute-done | bytes 262176 | tf_op jit(solution)/shard_map/ppermute | solution.py:218
  85.3 0.1 add_convert_fusion.4
  85.4 1.4 %collective-permute-start.19 = (bf16[64,2048]{1,0:T(8,128)(2,1)S(1)}, bf16[64,2048]{1,0:T(8,128)(2,1)S(1)}, u32[]{:S(2)}, u32[]{:S(2)}) collective-permute-start(bf16[64,2048]{1,0:T(8,128)(2,1)S(1)} %add_convert_fusion.4), channel_id=1, source_target_pairs={{0,4},{1,5},{4,8},{5,9},{8,12},{9,13},{12,14},{13,15},{14,10},{15,... | collective-permute-start | bytes 786440 | tf_op jit(solution)/shard_map/ppermute | solution.py:218
  86.8 0.1 add_convert_fusion.7
  86.9 0.7 collective-permute-start.15
  87.6 2.7 %shard_map.90 = (bf16[64,2048]{1,0:T(8,128)(2,1)S(1)}, bf16[64,2048]{1,0:T(8,128)(2,1)S(1)}, f32[2,128]{1,0:T(2,128)S(1)}) custom-call(bf16[2,1040,128]{2,1,0:T(8,128)(2,1)S(1)} %copy-done, f32[2,128]{1,0:T(2,128)S(1)} %compare_convert_fusion.refs_2_.refs_1_, bf16[2048,768]{1,0:T(8,128)(2,1)S(1)} %get-tuple-element.50.refs_3_.refs_2_, ...), custom_call_target="tpu_custom_call" | custom-call | flops 2415919104 | bytes 1048576 | tf_op jit(solution)/shard_map/pallas_call | solution.py:190
  90.4 0.6 collective-permute-done.23
  91.0 0.1 add_convert_fusion
  91.0 1.4 %collective-permute-start.24 = (bf16[64,2048]{1,0:T(8,128)(2,1)S(1)}, bf16[64,2048]{1,0:T(8,128)(2,1)S(1)}, u32[]{:S(2)}, u32[]{:S(2)}) collective-permute-start(bf16[64,2048]{1,0:T(8,128)(2,1)S(1)} %add_convert_fusion), channel_id=1, source_target_pairs={{0,4},{1,5},{4,8},{5,9},{8,12},{9,13},{12,14},{13,15},{14,10},{15,... | collective-permute-start | bytes 786440 | tf_op jit(solution)/shard_map/ppermute | solution.py:218
  92.4 0.9 collective-permute-done.15
  93.3 0.1 add_convert_fusion.6
  93.4 0.7 collective-permute-start.16
  94.1 1.1 %collective-permute-done.25 = f32[2,128]{1,0:T(2,128)S(1)} collective-permute-done((f32[2,128]{1,0:T(2,128)S(1)}, f32[2,128]{1,0:T(2,128)S(1)}, u32[]{:S(2)}, u32[]{:S(2)}) %collective-permute-start.25) | collective-permute-done | bytes 1056 | tf_op jit(solution)/shard_map/ppermute | solution.py:220
  95.3 0.6 multiply_reduce_fusion
  95.9 0.6 fusion
  97.1 0.6 collective-permute-done.24.refs_5_
  97.8 2.1 %collective-permute-done.16.refs_1_ = bf16[64,2048]{1,0:T(8,128)(2,1)S(1)} collective-permute-done((bf16[64,2048]{1,0:T(8,128)(2,1)S(1)}, bf16[64,2048]{1,0:T(8,128)(2,1)S(1)}, u32[]{:S(2)}, u32[]{:S(2)}) %collective-permute-start.16) | collective-permute-done | bytes 262176 | tf_op jit(solution)/shard_map/ppermute | solution.py:219
  99.8 1.0 shard_map.92
  (16 shorter events, 0.1 us)
Async XLA Ops:
  0.6 20.7 %collective-permute-start.4 = (bf16[2048,768]{1,0:T(8,128)(2,1)}, bf16[2048,768]{1,0:T(8,128)(2,1)}, u32[]{:S(2)}, u32[]{:S(2)}) collective-permute-start(bf16[2048,768]{1,0:T(8,128)(2,1)} %bitcast.13), channel_id=1, source_target_pairs={{0,1},{1,0},{2,3},{3,2},{4,5},{5,4},{6,7},{7,6},{8,9},{9,8},{10,11... | collective-permute-start | bytes 9437192 | tf_op jit(solution)/shard_map/ppermute | solution.py:220
  1.1 20.2 %collective-permute-start.5 = (bf16[2048,768]{1,0:T(8,128)(2,1)}, bf16[2048,768]{1,0:T(8,128)(2,1)}, u32[]{:S(2)}, u32[]{:S(2)}) collective-permute-start(bf16[2048,768]{1,0:T(8,128)(2,1)} %bitcast.15), channel_id=1, source_target_pairs={{0,1},{1,0},{2,3},{3,2},{4,5},{5,4},{6,7},{7,6},{8,9},{9,8},{10,11... | collective-permute-start | bytes 9437192 | tf_op jit(solution)/shard_map/ppermute | solution.py:220
  1.2 20.1 %collective-permute-start.6 = (bf16[768,2048]{1,0:T(8,128)(2,1)}, bf16[768,2048]{1,0:T(8,128)(2,1)}, u32[]{:S(2)}, u32[]{:S(2)}) collective-permute-start(bf16[768,2048]{1,0:T(8,128)(2,1)} %bitcast.17), channel_id=1, source_target_pairs={{0,1},{1,0},{2,3},{3,2},{4,5},{5,4},{6,7},{7,6},{8,9},{9,8},{10,11... | collective-permute-start | bytes 9437192 | tf_op jit(solution)/shard_map/ppermute | solution.py:220
  3.6 15.6 %collective-permute-start = (bf16[2,1040,128]{2,1,0:T(8,128)(2,1)}, bf16[2,1040,128]{2,1,0:T(8,128)(2,1)S(1)}, u32[]{:S(2)}, u32[]{:S(2)}) collective-permute-start(bf16[2,1040,128]{2,1,0:T(8,128)(2,1)} %shard_map.85.refs_0_), channel_id=1, source_target_pairs={{0,4},{1,5},{4,8},{5,9},{8,12},{9,13},{12,14},{13,15},{14,10},{15,... | collective-permute-start | bytes 1597448 | tf_op jit(solution)/shard_map/ppermute | solution.py:218
  6.4 14.7 %collective-permute-start.2 = (bf16[2,1040,128]{2,1,0:T(8,128)(2,1)}, bf16[2,1040,128]{2,1,0:T(8,128)(2,1)S(1)}, u32[]{:S(2)}, u32[]{:S(2)}) collective-permute-start(bf16[2,1040,128]{2,1,0:T(8,128)(2,1)} %shard_map.85.refs_0_), channel_id=1, source_target_pairs={{0,2},{1,3},{4,0},{5,1},{8,4},{9,5},{12,8},{13,9},{14,12},{15,13},... | collective-permute-start | bytes 1597448 | tf_op jit(solution)/shard_map/ppermute | solution.py:219
  19.2 13.9 %collective-permute-start.1 = (bf16[2,1040,128]{2,1,0:T(8,128)(2,1)S(1)}, bf16[2,1040,128]{2,1,0:T(8,128)(2,1)S(1)}, u32[]{:S(2)}, u32[]{:S(2)}) collective-permute-start(bf16[2,1040,128]{2,1,0:T(8,128)(2,1)S(1)} %collective-permute-done.refs_0_), channel_id=1, source_target_pairs={{0,4},{1,5},{4,8},{5,9},{8,12},{9,13},{12,14},{13,15},{14,10},{15,... | collective-permute-start | bytes 1597448 | tf_op jit(solution)/shard_map/ppermute | solution.py:218
  21.0 13.4 %collective-permute-start.3 = (bf16[2,1040,128]{2,1,0:T(8,128)(2,1)S(1)}, bf16[2,1040,128]{2,1,0:T(8,128)(2,1)S(1)}, u32[]{:S(2)}, u32[]{:S(2)}) collective-permute-start(bf16[2,1040,128]{2,1,0:T(8,128)(2,1)S(1)} %collective-permute-done.2.refs_1_), channel_id=1, source_target_pairs={{0,2},{1,3},{4,0},{5,1},{8,4},{9,5},{12,8},{13,9},{14,12},{15,13},... | collective-permute-start | bytes 1597448 | tf_op jit(solution)/shard_map/ppermute | solution.py:219
  34.4 12.5 %collective-permute-start.7 = (bf16[2,1040,128]{2,1,0:T(8,128)(2,1)S(1)}, bf16[2,1040,128]{2,1,0:T(8,128)(2,1)S(1)}, u32[]{:S(2)}, u32[]{:S(2)}) collective-permute-start(bf16[2,1040,128]{2,1,0:T(8,128)(2,1)S(1)} %collective-permute-done.1.refs_0_), channel_id=1, source_target_pairs={{0,4},{1,5},{4,8},{5,9},{8,12},{9,13},{12,14},{13,15},{14,10},{15,... | collective-permute-start | bytes 1597448 | tf_op jit(solution)/shard_map/ppermute | solution.py:218
  36.0 12.2 %collective-permute-start.8 = (bf16[2,1040,128]{2,1,0:T(8,128)(2,1)S(1)}, bf16[2,1040,128]{2,1,0:T(8,128)(2,1)S(1)}, u32[]{:S(2)}, u32[]{:S(2)}) collective-permute-start(bf16[2,1040,128]{2,1,0:T(8,128)(2,1)S(1)} %collective-permute-done.3.refs_1_), channel_id=1, source_target_pairs={{0,2},{1,3},{4,0},{5,1},{8,4},{9,5},{12,8},{13,9},{14,12},{15,13},... | collective-permute-start | bytes 1597448 | tf_op jit(solution)/shard_map/ppermute | solution.py:219
  48.2 7.5 %collective-permute-start.10 = (bf16[1040,128]{1,0:T(8,128)(2,1)S(1)}, bf16[1040,128]{1,0:T(8,128)(2,1)S(1)}, u32[]{:S(2)}, u32[]{:S(2)}) collective-permute-start(bf16[1040,128]{1,0:T(8,128)(2,1)S(1)} %slice_bitcast_fusion), channel_id=1, source_target_pairs={{0,2},{1,3},{4,0},{5,1},{8,4},{9,5},{12,8},{13,9},{14,12},{15,13},... | collective-permute-start | bytes 798728 | tf_op jit(solution)/shard_map/ppermute | solution.py:219
  48.7 7.0 %collective-permute-start.9 = (bf16[1040,128]{1,0:T(8,128)(2,1)S(1)}, bf16[1040,128]{1,0:T(8,128)(2,1)S(1)}, u32[]{:S(2)}, u32[]{:S(2)}) collective-permute-start(bf16[1040,128]{1,0:T(8,128)(2,1)S(1)} %slice_bitcast_fusion.1), channel_id=1, source_target_pairs={{0,4},{1,5},{4,8},{5,9},{8,12},{9,13},{12,14},{13,15},{14,10},{15,... | collective-permute-start | bytes 798728 | tf_op jit(solution)/shard_map/ppermute | solution.py:218
  55.7 7.9 %collective-permute-start.11 = (bf16[64,2048]{1,0:T(8,128)(2,1)S(1)}, bf16[64,2048]{1,0:T(8,128)(2,1)S(1)}, u32[]{:S(2)}, u32[]{:S(2)}) collective-permute-start(bf16[64,2048]{1,0:T(8,128)(2,1)S(1)} %get-tuple-element.73), channel_id=1, source_target_pairs={{0,2},{1,3},{4,0},{5,1},{8,4},{9,5},{12,8},{13,9},{14,12},{15,13},... | collective-permute-start | bytes 786440 | tf_op jit(solution)/shard_map/ppermute | solution.py:219
  59.2 9.3 %collective-permute-start.21 = (bf16[64,2048]{1,0:T(8,128)(2,1)S(1)}, bf16[64,2048]{1,0:T(8,128)(2,1)S(1)}, u32[]{:S(2)}, u32[]{:S(2)}) collective-permute-start(bf16[64,2048]{1,0:T(8,128)(2,1)S(1)} %get-tuple-element.91), channel_id=1, source_target_pairs={{0,4},{1,5},{4,8},{5,9},{8,12},{9,13},{12,14},{13,15},{14,10},{15,... | collective-permute-start | bytes 786440 | tf_op jit(solution)/shard_map/ppermute | solution.py:218
  60.6 13.5 %collective-permute-start.17 = (bf16[64,2048]{1,0:T(8,128)(2,1)S(1)}, bf16[64,2048]{1,0:T(8,128)(2,1)S(1)}, u32[]{:S(2)}, u32[]{:S(2)}) collective-permute-start(bf16[64,2048]{1,0:T(8,128)(2,1)S(1)} %get-tuple-element.84), channel_id=1, source_target_pairs={{0,4},{1,5},{4,8},{5,9},{8,12},{9,13},{12,14},{13,15},{14,10},{15,... | collective-permute-start | bytes 786440 | tf_op jit(solution)/shard_map/ppermute | solution.py:218
  62.2 25.5 %copy-start = (bf16[2,1040,128]{2,1,0:T(8,128)(2,1)S(1)}, bf16[2,1040,128]{2,1,0:T(8,128)(2,1)}, u32[]{:S(2)}) copy-start(bf16[2,1040,128]{2,1,0:T(8,128)(2,1)} %shard_map.85.refs_0_) | copy-start | bytes 1597444
  62.2 13.4 %collective-permute-start.13 = (bf16[64,2048]{1,0:T(8,128)(2,1)S(1)}, bf16[64,2048]{1,0:T(8,128)(2,1)S(1)}, u32[]{:S(2)}, u32[]{:S(2)}) collective-permute-start(bf16[64,2048]{1,0:T(8,128)(2,1)S(1)} %get-tuple-element.81), channel_id=1, source_target_pairs={{0,2},{1,3},{4,0},{5,1},{8,4},{9,5},{12,8},{13,9},{14,12},{15,13},... | collective-permute-start | bytes 786440 | tf_op jit(solution)/shard_map/ppermute | solution.py:219
  63.7 13.3 %collective-permute-start.12 = (bf16[64,2048]{1,0:T(8,128)(2,1)S(1)}, bf16[64,2048]{1,0:T(8,128)(2,1)S(1)}, u32[]{:S(2)}, u32[]{:S(2)}) collective-permute-start(bf16[64,2048]{1,0:T(8,128)(2,1)S(1)} %add_convert_fusion.9), channel_id=1, source_target_pairs={{0,2},{1,3},{4,0},{5,1},{8,4},{9,5},{12,8},{13,9},{14,12},{15,13},... | collective-permute-start | bytes 786440 | tf_op jit(solution)/shard_map/ppermute | solution.py:219
  68.6 11.2 %collective-permute-start.22 = (bf16[64,2048]{1,0:T(8,128)(2,1)S(1)}, bf16[64,2048]{1,0:T(8,128)(2,1)S(1)}, u32[]{:S(2)}, u32[]{:S(2)}) collective-permute-start(bf16[64,2048]{1,0:T(8,128)(2,1)S(1)} %add_convert_fusion.2), channel_id=1, source_target_pairs={{0,4},{1,5},{4,8},{5,9},{8,12},{9,13},{12,14},{13,15},{14,10},{15,... | collective-permute-start | bytes 786440 | tf_op jit(solution)/shard_map/ppermute | solution.py:218
  74.2 11.2 %collective-permute-start.18 = (bf16[64,2048]{1,0:T(8,128)(2,1)S(1)}, bf16[64,2048]{1,0:T(8,128)(2,1)S(1)}, u32[]{:S(2)}, u32[]{:S(2)}) collective-permute-start(bf16[64,2048]{1,0:T(8,128)(2,1)S(1)} %add_convert_fusion.5), channel_id=1, source_target_pairs={{0,4},{1,5},{4,8},{5,9},{8,12},{9,13},{12,14},{13,15},{14,10},{15,... | collective-permute-start | bytes 786440 | tf_op jit(solution)/shard_map/ppermute | solution.py:218
  75.6 11.2 %collective-permute-start.14 = (bf16[64,2048]{1,0:T(8,128)(2,1)S(1)}, bf16[64,2048]{1,0:T(8,128)(2,1)S(1)}, u32[]{:S(2)}, u32[]{:S(2)}) collective-permute-start(bf16[64,2048]{1,0:T(8,128)(2,1)S(1)} %add_convert_fusion.8), channel_id=1, source_target_pairs={{0,2},{1,3},{4,0},{5,1},{8,4},{9,5},{12,8},{13,9},{14,12},{15,13},... | collective-permute-start | bytes 786440 | tf_op jit(solution)/shard_map/ppermute | solution.py:219
  79.8 11.2 %collective-permute-start.23 = (bf16[64,2048]{1,0:T(8,128)(2,1)S(1)}, bf16[64,2048]{1,0:T(8,128)(2,1)S(1)}, u32[]{:S(2)}, u32[]{:S(2)}) collective-permute-start(bf16[64,2048]{1,0:T(8,128)(2,1)S(1)} %add_convert_fusion.1), channel_id=1, source_target_pairs={{0,4},{1,5},{4,8},{5,9},{8,12},{9,13},{12,14},{13,15},{14,10},{15,... | collective-permute-start | bytes 786440 | tf_op jit(solution)/shard_map/ppermute | solution.py:218
  81.2 15.9 %collective-permute-start.20 = (bf16[64,2048]{1,0:T(8,128)(2,1)S(1)}, bf16[64,2048]{1,0:T(8,128)(2,1)S(1)}, u32[]{:S(2)}, u32[]{:S(2)}) collective-permute-start(bf16[64,2048]{1,0:T(8,128)(2,1)S(1)} %add_convert_fusion.3), channel_id=1, source_target_pairs={{0,2},{1,3},{4,0},{5,1},{8,4},{9,5},{12,8},{13,9},{14,12},{15,13},... | collective-permute-start | bytes 786440 | tf_op jit(solution)/shard_map/ppermute | solution.py:219
  85.4 11.7 %collective-permute-start.19 = (bf16[64,2048]{1,0:T(8,128)(2,1)S(1)}, bf16[64,2048]{1,0:T(8,128)(2,1)S(1)}, u32[]{:S(2)}, u32[]{:S(2)}) collective-permute-start(bf16[64,2048]{1,0:T(8,128)(2,1)S(1)} %add_convert_fusion.4), channel_id=1, source_target_pairs={{0,4},{1,5},{4,8},{5,9},{8,12},{9,13},{12,14},{13,15},{14,10},{15,... | collective-permute-start | bytes 786440 | tf_op jit(solution)/shard_map/ppermute | solution.py:218
  86.9 6.4 %collective-permute-start.15 = (bf16[64,2048]{1,0:T(8,128)(2,1)S(1)}, bf16[64,2048]{1,0:T(8,128)(2,1)S(1)}, u32[]{:S(2)}, u32[]{:S(2)}) collective-permute-start(bf16[64,2048]{1,0:T(8,128)(2,1)S(1)} %add_convert_fusion.7), channel_id=1, source_target_pairs={{0,2},{1,3},{4,0},{5,1},{8,4},{9,5},{12,8},{13,9},{14,12},{15,13},... | collective-permute-start | bytes 786440 | tf_op jit(solution)/shard_map/ppermute | solution.py:219
  91.0 6.7 %collective-permute-start.24 = (bf16[64,2048]{1,0:T(8,128)(2,1)S(1)}, bf16[64,2048]{1,0:T(8,128)(2,1)S(1)}, u32[]{:S(2)}, u32[]{:S(2)}) collective-permute-start(bf16[64,2048]{1,0:T(8,128)(2,1)S(1)} %add_convert_fusion), channel_id=1, source_target_pairs={{0,4},{1,5},{4,8},{5,9},{8,12},{9,13},{12,14},{13,15},{14,10},{15,... | collective-permute-start | bytes 786440 | tf_op jit(solution)/shard_map/ppermute | solution.py:218
  93.4 6.4 %collective-permute-start.16 = (bf16[64,2048]{1,0:T(8,128)(2,1)S(1)}, bf16[64,2048]{1,0:T(8,128)(2,1)S(1)}, u32[]{:S(2)}, u32[]{:S(2)}) collective-permute-start(bf16[64,2048]{1,0:T(8,128)(2,1)S(1)} %add_convert_fusion.6), channel_id=1, source_target_pairs={{0,2},{1,3},{4,0},{5,1},{8,4},{9,5},{12,8},{13,9},{14,12},{15,13},... | collective-permute-start | bytes 786440 | tf_op jit(solution)/shard_map/ppermute | solution.py:219
  94.1 1.1 %collective-permute-start.25 = (f32[2,128]{1,0:T(2,128)S(1)}, f32[2,128]{1,0:T(2,128)S(1)}, u32[]{:S(2)}, u32[]{:S(2)}) collective-permute-start(f32[2,128]{1,0:T(2,128)S(1)} %add_add_fusion), channel_id=1, source_target_pairs={{0,1},{1,0},{2,3},{3,2},{4,5},{5,4},{6,7},{7,6},{8,9},{9,8},{10,11... | collective-permute-start | bytes 3080 | tf_op jit(solution)/shard_map/ppermute | solution.py:220

commit v9 on v8

--- a/solution.py
+++ b/solution.py
@@ -253,13 +253,13 @@
 
     ways = (left, left, right, right)
     from_far = {0: res[0], 3: res[1]}
-    sums = [ways[i](from_far.get(i, outs[far - 1][i])) for i in (1, 2, 0, 3)]
-    sums = [sums[(1, 2, 0, 3).index(i)] for i in range(4)]
+    sums = [ways[i](from_far.get(i, outs[far - 1][i])) for i in (2, 1, 3, 0)]
+    sums = [sums[(2, 1, 3, 0).index(i)] for i in range(4)]
     for k in range(far - 1, 0, -1):
         if k == max(1, far - 2):
             packed, sums[1] = tie((packed, sums[1]))
             own_rows = run([packed])
-        for i in (1, 2, 0, 3):
+        for i in (2, 1, 3, 0):
             step = k if i in from_far else k - 1
             if step:
                 sums[i] = ways[i](add(outs[step][i], sums[i]))

time: 102 us -> 102 us (level)
  no operation moved by 1% of the time
where the time goes in v9:
time: 102 us
  waiting for transfers between devices  41.6 us (41%)
  Pallas kernels  30.5 us (30%)
  starting transfers between devices  25.2 us (25%)
  between operations  2.58 us (3%)
  other arithmetic  2 us (2%)
    ppermute x11, waiting for transfers between devices, body(): right = lambda a: lax.ppermute(a, 'node', to_right)  33.2 us
    pallas_call x5, Pallas kernels, apply_experts(): pl.pallas_call(functools.partial(expert_kernel, count, piece), out_shape=...  21 us
    ppermute x11, starting transfers between devices, body(): right = lambda a: lax.ppermute(a, 'node', to_right)  17.8 us
    ppermute x11, waiting for transfers between devices, body(): left = lambda a: lax.ppermute(a, 'node', to_left)  7.3 us
    pallas_call x1, Pallas kernels, hold(): pl.pallas_call(hold_kernel, out_shape=[pltpu.VMEM(array.shape, array.dtyp...  6.5 us
    ppermute x11, starting transfers between devices, body(): left = lambda a: lax.ppermute(a, 'node', to_left)  6.36 us
  transfers between devices with their start and end apart: 26, of which 15 were waited for; matrix products, arithmetic and copies ran while one was open for 2% of the time, Pallas kernels for 29%

profile of v9, /device:TPU:0, one launch (start us, length us, event | category | flops | bytes accessed | tf_op | source)
XLA Modules:
  0.0 101.9 jit_solution(1002970231369934982)
XLA Ops:
  0.6 0.5 collective-permute-start.4
  1.1 0.1 collective-permute-start.5
  1.2 0.4 collective-permute-start.6
  1.7 2.0 %shard_map.85.refs_0_ = bf16[2,1040,128]{2,1,0:T(8,128)(2,1)} custom-call(bf16[128,2048]{1,0:T(8,128)(2,1)} %tokens_hbm.1, s32[8,128]{1,0:T(8,128)} %bitcast.19, s32[8,128]{1,0:T(8,128)} %bitcast.20), custom_call_target="tpu_custom_call" | custom-call | flops 16384 | bytes 1048576 | tf_op jit(solution)/shard_map/pallas_call | solution.py:73
  3.6 2.7 %collective-permute-start = (bf16[2,1040,128]{2,1,0:T(8,128)(2,1)}, bf16[2,1040,128]{2,1,0:T(8,128)(2,1)S(1)}, u32[]{:S(2)}, u32[]{:S(2)}) collective-permute-start(bf16[2,1040,128]{2,1,0:T(8,128)(2,1)} %shard_map.85.refs_0_), channel_id=1, source_target_pairs={{0,4},{1,5},{4,8},{5,9},{8,12},{9,13},{12,14},{13,15},{14,10},{15,... | collective-permute-start | bytes 1597448 | tf_op jit(solution)/shard_map/ppermute | solution.py:218
  6.4 0.0 collective-permute-start.2
  6.4 0.1 pad_add_fusion
  6.4 12.8 %collective-permute-done.refs_0_ = bf16[2,1040,128]{2,1,0:T(8,128)(2,1)S(1)} collective-permute-done((bf16[2,1040,128]{2,1,0:T(8,128)(2,1)}, bf16[2,1040,128]{2,1,0:T(8,128)(2,1)S(1)}, u32[]{:S(2)}, u32[]{:S(2)}) %collective-permute-start) | collective-permute-done | bytes 532512 | tf_op jit(solution)/shard_map/ppermute | solution.py:218
  19.2 1.8 %collective-permute-start.1 = (bf16[2,1040,128]{2,1,0:T(8,128)(2,1)S(1)}, bf16[2,1040,128]{2,1,0:T(8,128)(2,1)S(1)}, u32[]{:S(2)}, u32[]{:S(2)}) collective-permute-start(bf16[2,1040,128]{2,1,0:T(8,128)(2,1)S(1)} %collective-permute-done.refs_0_), channel_id=1, source_target_pairs={{0,4},{1,5},{4,8},{5,9},{8,12},{9,13},{12,14},{13,15},{14,10},{15,... | collective-permute-start | bytes 1597448 | tf_op jit(solution)/shard_map/ppermute | solution.py:218
  21.0 0.0 collective-permute-done.2.refs_1_
  21.0 0.2 collective-permute-start.3
  21.2 0.1 compare_convert_fusion.refs_2_.refs_1_
  21.3 6.5 %shard_map.86 = (bf16[2048,768]{1,0:T(8,128)(2,1)S(1)}, bf16[2048,768]{1,0:T(8,128)(2,1)S(1)}, bf16[768,2048]{1,0:T(8,128)(2,1)S(1)}, bf16[2048,768]{1,0:T(8,128...) custom-call(bf16[2048,768]{1,0:T(8,128)(2,1)} %bitcast.14, bf16[2048,768]{1,0:T(8,128)(2,1)} %bitcast.16, ...), custom_call_target="tpu_custom_call" | custom-call | tf_op jit(solution)/shard_map/pallas_call | solution.py:123
  27.8 5.2 %shard_map.87 = (bf16[64,2048]{1,0:T(8,128)(2,1)S(1)}, bf16[64,2048]{1,0:T(8,128)(2,1)S(1)}, bf16[64,2048]{1,0:T(8,128)(2,1)S(1)}, bf16[64,2048]{1,0:T(8,128)(2,1)S(1)}, f32[2,128]{1,0:T(2,128)S(1)}) custom-call(bf16[2,1040,128]{2,1,0:T(8,128)(2,1)S(1)} %collective-permute-done.refs_0_, bf16[2,1040,128]{2,1,0:T(8,128)(2,1)S(1)} %collective-permute-done.2.refs_1_, ...), custom_call_target="tpu_custom_call" | custom-call | flops 4831838208 | bytes 2097152 | tf_op jit(solution)/shard_map/pallas_call | solution.py:190
  33.0 0.0 collective-permute-done.1.refs_0_
  33.1 1.3 %collective-permute-done.3.refs_1_ = bf16[2,1040,128]{2,1,0:T(8,128)(2,1)S(1)} collective-permute-done((bf16[2,1040,128]{2,1,0:T(8,128)(2,1)S(1)}, bf16[2,1040,128]{2,1,0:T(8,128)(2,1)S(1)}, u32[]{:S(2)}, u32[]{:S(2)}) %collective-permute-start.3) | collective-permute-done | bytes 532512 | tf_op jit(solution)/shard_map/ppermute | solution.py:219
  34.4 1.6 %collective-permute-start.7 = (bf16[2,1040,128]{2,1,0:T(8,128)(2,1)S(1)}, bf16[2,1040,128]{2,1,0:T(8,128)(2,1)S(1)}, u32[]{:S(2)}, u32[]{:S(2)}) collective-permute-start(bf16[2,1040,128]{2,1,0:T(8,128)(2,1)S(1)} %collective-permute-done.1.refs_0_), channel_id=1, source_target_pairs={{0,4},{1,5},{4,8},{5,9},{8,12},{9,13},{12,14},{13,15},{14,10},{15,... | collective-permute-start | bytes 1597448 | tf_op jit(solution)/shard_map/ppermute | solution.py:218
  36.0 0.4 collective-permute-start.8
  36.4 5.2 %shard_map.88 = (bf16[64,2048]{1,0:T(8,128)(2,1)S(1)}, bf16[64,2048]{1,0:T(8,128)(2,1)S(1)}, bf16[64,2048]{1,0:T(8,128)(2,1)S(1)}, bf16[64,2048]{1,0:T(8,128)(2,1)S(1)}, f32[2,128]{1,0:T(2,128)S(1)}) custom-call(bf16[2,1040,128]{2,1,0:T(8,128)(2,1)S(1)} %collective-permute-done.1.refs_0_, bf16[2,1040,128]{2,1,0:T(8,128)(2,1)S(1)} %collective-permute-done.3.refs_1_, ...), custom_call_target="tpu_custom_call" | custom-call | flops 4831838208 | bytes 2097152 | tf_op jit(solution)/shard_map/pallas_call | solution.py:190
  41.6 5.2 %collective-permute-done.7.refs_0_ = bf16[2,1040,128]{2,1,0:T(8,128)(2,1)S(1)} collective-permute-done((bf16[2,1040,128]{2,1,0:T(8,128)(2,1)S(1)}, bf16[2,1040,128]{2,1,0:T(8,128)(2,1)S(1)}, u32[]{:S(2)}, u32[]{:S(2)}) %collective-permute-start.7) | collective-permute-done | bytes 532512 | tf_op jit(solution)/shard_map/ppermute | solution.py:218
  46.8 1.3 %collective-permute-done.8.refs_1_ = bf16[2,1040,128]{2,1,0:T(8,128)(2,1)S(1)} collective-permute-done((bf16[2,1040,128]{2,1,0:T(8,128)(2,1)S(1)}, bf16[2,1040,128]{2,1,0:T(8,128)(2,1)S(1)}, u32[]{:S(2)}, u32[]{:S(2)}) %collective-permute-start.8) | collective-permute-done | bytes 532512 | tf_op jit(solution)/shard_map/ppermute | solution.py:219
  48.2 0.5 collective-permute-start.10
  48.7 1.8 %collective-permute-start.9 = (bf16[1040,128]{1,0:T(8,128)(2,1)S(1)}, bf16[1040,128]{1,0:T(8,128)(2,1)S(1)}, u32[]{:S(2)}, u32[]{:S(2)}) collective-permute-start(bf16[1040,128]{1,0:T(8,128)(2,1)S(1)} %slice_bitcast_fusion.1), channel_id=1, source_target_pairs={{0,4},{1,5},{4,8},{5,9},{8,12},{9,13},{12,14},{13,15},{14,10},{15,... | collective-permute-start | bytes 798728 | tf_op jit(solution)/shard_map/ppermute | solution.py:218
  50.5 5.2 %shard_map.89 = (bf16[64,2048]{1,0:T(8,128)(2,1)S(1)}, bf16[64,2048]{1,0:T(8,128)(2,1)S(1)}, bf16[64,2048]{1,0:T(8,128)(2,1)S(1)}, bf16[64,2048]{1,0:T(8,128)(2,1)S(1)}, f32[2,128]{1,0:T(2,128)S(1)}) custom-call(bf16[2,1040,128]{2,1,0:T(8,128)(2,1)S(1)} %collective-permute-done.7.refs_0_, bf16[2,1040,128]{2,1,0:T(8,128)(2,1)S(1)} %collective-permute-done.8.refs_1_, ...), custom_call_target="tpu_custom_call" | custom-call | flops 4831838208 | bytes 2097152 | tf_op jit(solution)/shard_map/pallas_call | solution.py:190
  55.7 0.7 collective-permute-start.11
  56.5 2.7 %shard_map.91 = (bf16[64,2048]{1,0:T(8,128)(2,1)S(1)}, bf16[64,2048]{1,0:T(8,128)(2,1)S(1)}, f32[2,128]{1,0:T(2,128)S(1)}) custom-call(bf16[1040,128]{1,0:T(8,128)(2,1)S(1)} %collective-permute-done.9.refs_0_, bf16[1040,128]{1,0:T(8,128)(2,1)S(1)} %collective-permute-done.10.refs_1_, f32[2,128]{1,0:T(2,128)S(1)} %compare_convert_fusion.refs_2_.refs_1_, ...), custom_call_target="tpu_custom_call" | custom-call | flops 2415919104 | bytes 1048576 | tf_op jit(solution)/shard_map/pallas_call | solution.py:190
  59.2 1.4 %collective-permute-start.21 = (bf16[64,2048]{1,0:T(8,128)(2,1)S(1)}, bf16[64,2048]{1,0:T(8,128)(2,1)S(1)}, u32[]{:S(2)}, u32[]{:S(2)}) collective-permute-start(bf16[64,2048]{1,0:T(8,128)(2,1)S(1)} %get-tuple-element.91), channel_id=1, source_target_pairs={{0,4},{1,5},{4,8},{5,9},{8,12},{9,13},{12,14},{13,15},{14,10},{15,... | collective-permute-start | bytes 786440 | tf_op jit(solution)/shard_map/ppermute | solution.py:218
  60.6 1.6 %collective-permute-start.17 = (bf16[64,2048]{1,0:T(8,128)(2,1)S(1)}, bf16[64,2048]{1,0:T(8,128)(2,1)S(1)}, u32[]{:S(2)}, u32[]{:S(2)}) collective-permute-start(bf16[64,2048]{1,0:T(8,128)(2,1)S(1)} %get-tuple-element.84), channel_id=1, source_target_pairs={{0,4},{1,5},{4,8},{5,9},{8,12},{9,13},{12,14},{13,15},{14,10},{15,... | collective-permute-start | bytes 786440 | tf_op jit(solution)/shard_map/ppermute | solution.py:218
  62.2 0.4 collective-permute-start.13
  62.6 1.0 %collective-permute-done.11 = bf16[64,2048]{1,0:T(8,128)(2,1)S(1)} collective-permute-done((bf16[64,2048]{1,0:T(8,128)(2,1)S(1)}, bf16[64,2048]{1,0:T(8,128)(2,1)S(1)}, u32[]{:S(2)}, u32[]{:S(2)}) %collective-permute-start.11) | collective-permute-done | bytes 262176 | tf_op jit(solution)/shard_map/ppermute | solution.py:219
  63.7 0.1 add_convert_fusion.9
  63.7 1.0 %collective-permute-start.12 = (bf16[64,2048]{1,0:T(8,128)(2,1)S(1)}, bf16[64,2048]{1,0:T(8,128)(2,1)S(1)}, u32[]{:S(2)}, u32[]{:S(2)}) collective-permute-start(bf16[64,2048]{1,0:T(8,128)(2,1)S(1)} %add_convert_fusion.9), channel_id=1, source_target_pairs={{0,2},{1,3},{4,0},{5,1},{8,4},{9,5},{12,8},{13,9},{14,12},{15,13},... | collective-permute-start | bytes 786440 | tf_op jit(solution)/shard_map/ppermute | solution.py:219
  64.8 3.7 %collective-permute-done.21 = bf16[64,2048]{1,0:T(8,128)(2,1)S(1)} collective-permute-done((bf16[64,2048]{1,0:T(8,128)(2,1)S(1)}, bf16[64,2048]{1,0:T(8,128)(2,1)S(1)}, u32[]{:S(2)}, u32[]{:S(2)}) %collective-permute-start.21) | collective-permute-done | bytes 262176 | tf_op jit(solution)/shard_map/ppermute | solution.py:218
  68.5 0.1 add_convert_fusion.2
  68.6 1.4 %collective-permute-start.22 = (bf16[64,2048]{1,0:T(8,128)(2,1)S(1)}, bf16[64,2048]{1,0:T(8,128)(2,1)S(1)}, u32[]{:S(2)}, u32[]{:S(2)}) collective-permute-start(bf16[64,2048]{1,0:T(8,128)(2,1)S(1)} %add_convert_fusion.2), channel_id=1, source_target_pairs={{0,4},{1,5},{4,8},{5,9},{8,12},{9,13},{12,14},{13,15},{14,10},{15,... | collective-permute-start | bytes 786440 | tf_op jit(solution)/shard_map/ppermute | solution.py:218
  69.9 4.2 %collective-permute-done.17 = bf16[64,2048]{1,0:T(8,128)(2,1)S(1)} collective-permute-done((bf16[64,2048]{1,0:T(8,128)(2,1)S(1)}, bf16[64,2048]{1,0:T(8,128)(2,1)S(1)}, u32[]{:S(2)}, u32[]{:S(2)}) %collective-permute-start.17) | collective-permute-done | bytes 262176 | tf_op jit(solution)/shard_map/ppermute | solution.py:218
  74.1 0.1 add_convert_fusion.5
  74.2 1.4 %collective-permute-start.18 = (bf16[64,2048]{1,0:T(8,128)(2,1)S(1)}, bf16[64,2048]{1,0:T(8,128)(2,1)S(1)}, u32[]{:S(2)}, u32[]{:S(2)}) collective-permute-start(bf16[64,2048]{1,0:T(8,128)(2,1)S(1)} %add_convert_fusion.5), channel_id=1, source_target_pairs={{0,4},{1,5},{4,8},{5,9},{8,12},{9,13},{12,14},{13,15},{14,10},{15,... | collective-permute-start | bytes 786440 | tf_op jit(solution)/shard_map/ppermute | solution.py:218
  75.6 0.1 add_convert_fusion.8
  75.6 0.7 collective-permute-start.14
  76.4 0.6 collective-permute-done.12
  77.0 2.7 %collective-permute-done.22 = bf16[64,2048]{1,0:T(8,128)(2,1)S(1)} collective-permute-done((bf16[64,2048]{1,0:T(8,128)(2,1)S(1)}, bf16[64,2048]{1,0:T(8,128)(2,1)S(1)}, u32[]{:S(2)}, u32[]{:S(2)}) %collective-permute-start.22) | collective-permute-done | bytes 262176 | tf_op jit(solution)/shard_map/ppermute | solution.py:218
  79.7 0.1 add_convert_fusion.1
  79.8 1.4 %collective-permute-start.23 = (bf16[64,2048]{1,0:T(8,128)(2,1)S(1)}, bf16[64,2048]{1,0:T(8,128)(2,1)S(1)}, u32[]{:S(2)}, u32[]{:S(2)}) collective-permute-start(bf16[64,2048]{1,0:T(8,128)(2,1)S(1)} %add_convert_fusion.1), channel_id=1, source_target_pairs={{0,4},{1,5},{4,8},{5,9},{8,12},{9,13},{12,14},{13,15},{14,10},{15,... | collective-permute-start | bytes 786440 | tf_op jit(solution)/shard_map/ppermute | solution.py:218
  81.2 0.1 add_convert_fusion.3
  81.2 0.7 collective-permute-start.20
  82.0 3.3 %collective-permute-done.18 = bf16[64,2048]{1,0:T(8,128)(2,1)S(1)} collective-permute-done((bf16[64,2048]{1,0:T(8,128)(2,1)S(1)}, bf16[64,2048]{1,0:T(8,128)(2,1)S(1)}, u32[]{:S(2)}, u32[]{:S(2)}) %collective-permute-start.18) | collective-permute-done | bytes 262176 | tf_op jit(solution)/shard_map/ppermute | solution.py:218
  85.3 0.1 add_convert_fusion.4
  85.4 1.4 %collective-permute-start.19 = (bf16[64,2048]{1,0:T(8,128)(2,1)S(1)}, bf16[64,2048]{1,0:T(8,128)(2,1)S(1)}, u32[]{:S(2)}, u32[]{:S(2)}) collective-permute-start(bf16[64,2048]{1,0:T(8,128)(2,1)S(1)} %add_convert_fusion.4), channel_id=1, source_target_pairs={{0,4},{1,5},{4,8},{5,9},{8,12},{9,13},{12,14},{13,15},{14,10},{15,... | collective-permute-start | bytes 786440 | tf_op jit(solution)/shard_map/ppermute | solution.py:218
  86.8 0.1 add_convert_fusion.7
  86.9 0.7 collective-permute-start.15
  87.6 2.7 %shard_map.90 = (bf16[64,2048]{1,0:T(8,128)(2,1)S(1)}, bf16[64,2048]{1,0:T(8,128)(2,1)S(1)}, f32[2,128]{1,0:T(2,128)S(1)}) custom-call(bf16[2,1040,128]{2,1,0:T(8,128)(2,1)S(1)} %copy-done, f32[2,128]{1,0:T(2,128)S(1)} %compare_convert_fusion.refs_2_.refs_1_, bf16[2048,768]{1,0:T(8,128)(2,1)S(1)} %get-tuple-element.50.refs_3_.refs_2_, ...), custom_call_target="tpu_custom_call" | custom-call | flops 2415919104 | bytes 1048576 | tf_op jit(solution)/shard_map/pallas_call | solution.py:190
  90.4 0.6 collective-permute-done.23
  91.0 0.1 add_convert_fusion
  91.0 1.4 %collective-permute-start.24 = (bf16[64,2048]{1,0:T(8,128)(2,1)S(1)}, bf16[64,2048]{1,0:T(8,128)(2,1)S(1)}, u32[]{:S(2)}, u32[]{:S(2)}) collective-permute-start(bf16[64,2048]{1,0:T(8,128)(2,1)S(1)} %add_convert_fusion), channel_id=1, source_target_pairs={{0,4},{1,5},{4,8},{5,9},{8,12},{9,13},{12,14},{13,15},{14,10},{15,... | collective-permute-start | bytes 786440 | tf_op jit(solution)/shard_map/ppermute | solution.py:218
  92.4 0.9 collective-permute-done.15
  93.3 0.1 add_convert_fusion.6
  93.4 0.7 collective-permute-start.16
  94.1 1.1 %collective-permute-done.25 = f32[2,128]{1,0:T(2,128)S(1)} collective-permute-done((f32[2,128]{1,0:T(2,128)S(1)}, f32[2,128]{1,0:T(2,128)S(1)}, u32[]{:S(2)}, u32[]{:S(2)}) %collective-permute-start.25) | collective-permute-done | bytes 1056 | tf_op jit(solution)/shard_map/ppermute | solution.py:220
  95.3 0.6 multiply_reduce_fusion
  95.9 0.6 fusion
  97.1 0.6 collective-permute-done.24.refs_5_
  97.8 2.1 %collective-permute-done.16.refs_1_ = bf16[64,2048]{1,0:T(8,128)(2,1)S(1)} collective-permute-done((bf16[64,2048]{1,0:T(8,128)(2,1)S(1)}, bf16[64,2048]{1,0:T(8,128)(2,1)S(1)}, u32[]{:S(2)}, u32[]{:S(2)}) %collective-permute-start.16) | collective-permute-done | bytes 262176 | tf_op jit(solution)/shard_map/ppermute | solution.py:219
  99.8 1.0 shard_map.92
  (16 shorter events, 0.1 us)
Async XLA Ops:
  0.6 20.7 %collective-permute-start.4 = (bf16[2048,768]{1,0:T(8,128)(2,1)}, bf16[2048,768]{1,0:T(8,128)(2,1)}, u32[]{:S(2)}, u32[]{:S(2)}) collective-permute-start(bf16[2048,768]{1,0:T(8,128)(2,1)} %bitcast.13), channel_id=1, source_target_pairs={{0,1},{1,0},{2,3},{3,2},{4,5},{5,4},{6,7},{7,6},{8,9},{9,8},{10,11... | collective-permute-start | bytes 9437192 | tf_op jit(solution)/shard_map/ppermute | solution.py:220
  1.1 20.2 %collective-permute-start.5 = (bf16[2048,768]{1,0:T(8,128)(2,1)}, bf16[2048,768]{1,0:T(8,128)(2,1)}, u32[]{:S(2)}, u32[]{:S(2)}) collective-permute-start(bf16[2048,768]{1,0:T(8,128)(2,1)} %bitcast.15), channel_id=1, source_target_pairs={{0,1},{1,0},{2,3},{3,2},{4,5},{5,4},{6,7},{7,6},{8,9},{9,8},{10,11... | collective-permute-start | bytes 9437192 | tf_op jit(solution)/shard_map/ppermute | solution.py:220
  1.2 20.1 %collective-permute-start.6 = (bf16[768,2048]{1,0:T(8,128)(2,1)}, bf16[768,2048]{1,0:T(8,128)(2,1)}, u32[]{:S(2)}, u32[]{:S(2)}) collective-permute-start(bf16[768,2048]{1,0:T(8,128)(2,1)} %bitcast.17), channel_id=1, source_target_pairs={{0,1},{1,0},{2,3},{3,2},{4,5},{5,4},{6,7},{7,6},{8,9},{9,8},{10,11... | collective-permute-start | bytes 9437192 | tf_op jit(solution)/shard_map/ppermute | solution.py:220
  3.6 15.6 %collective-permute-start = (bf16[2,1040,128]{2,1,0:T(8,128)(2,1)}, bf16[2,1040,128]{2,1,0:T(8,128)(2,1)S(1)}, u32[]{:S(2)}, u32[]{:S(2)}) collective-permute-start(bf16[2,1040,128]{2,1,0:T(8,128)(2,1)} %shard_map.85.refs_0_), channel_id=1, source_target_pairs={{0,4},{1,5},{4,8},{5,9},{8,12},{9,13},{12,14},{13,15},{14,10},{15,... | collective-permute-start | bytes 1597448 | tf_op jit(solution)/shard_map/ppermute | solution.py:218
  6.4 14.7 %collective-permute-start.2 = (bf16[2,1040,128]{2,1,0:T(8,128)(2,1)}, bf16[2,1040,128]{2,1,0:T(8,128)(2,1)S(1)}, u32[]{:S(2)}, u32[]{:S(2)}) collective-permute-start(bf16[2,1040,128]{2,1,0:T(8,128)(2,1)} %shard_map.85.refs_0_), channel_id=1, source_target_pairs={{0,2},{1,3},{4,0},{5,1},{8,4},{9,5},{12,8},{13,9},{14,12},{15,13},... | collective-permute-start | bytes 1597448 | tf_op jit(solution)/shard_map/ppermute | solution.py:219
  19.2 13.9 %collective-permute-start.1 = (bf16[2,1040,128]{2,1,0:T(8,128)(2,1)S(1)}, bf16[2,1040,128]{2,1,0:T(8,128)(2,1)S(1)}, u32[]{:S(2)}, u32[]{:S(2)}) collective-permute-start(bf16[2,1040,128]{2,1,0:T(8,128)(2,1)S(1)} %collective-permute-done.refs_0_), channel_id=1, source_target_pairs={{0,4},{1,5},{4,8},{5,9},{8,12},{9,13},{12,14},{13,15},{14,10},{15,... | collective-permute-start | bytes 1597448 | tf_op jit(solution)/shard_map/ppermute | solution.py:218
  21.0 13.4 %collective-permute-start.3 = (bf16[2,1040,128]{2,1,0:T(8,128)(2,1)S(1)}, bf16[2,1040,128]{2,1,0:T(8,128)(2,1)S(1)}, u32[]{:S(2)}, u32[]{:S(2)}) collective-permute-start(bf16[2,1040,128]{2,1,0:T(8,128)(2,1)S(1)} %collective-permute-done.2.refs_1_), channel_id=1, source_target_pairs={{0,2},{1,3},{4,0},{5,1},{8,4},{9,5},{12,8},{13,9},{14,12},{15,13},... | collective-permute-start | bytes 1597448 | tf_op jit(solution)/shard_map/ppermute | solution.py:219
  34.4 12.5 %collective-permute-start.7 = (bf16[2,1040,128]{2,1,0:T(8,128)(2,1)S(1)}, bf16[2,1040,128]{2,1,0:T(8,128)(2,1)S(1)}, u32[]{:S(2)}, u32[]{:S(2)}) collective-permute-start(bf16[2,1040,128]{2,1,0:T(8,128)(2,1)S(1)} %collective-permute-done.1.refs_0_), channel_id=1, source_target_pairs={{0,4},{1,5},{4,8},{5,9},{8,12},{9,13},{12,14},{13,15},{14,10},{15,... | collective-permute-start | bytes 1597448 | tf_op jit(solution)/shard_map/ppermute | solution.py:218
  36.0 12.2 %collective-permute-start.8 = (bf16[2,1040,128]{2,1,0:T(8,128)(2,1)S(1)}, bf16[2,1040,128]{2,1,0:T(8,128)(2,1)S(1)}, u32[]{:S(2)}, u32[]{:S(2)}) collective-permute-start(bf16[2,1040,128]{2,1,0:T(8,128)(2,1)S(1)} %collective-permute-done.3.refs_1_), channel_id=1, source_target_pairs={{0,2},{1,3},{4,0},{5,1},{8,4},{9,5},{12,8},{13,9},{14,12},{15,13},... | collective-permute-start | bytes 1597448 | tf_op jit(solution)/shard_map/ppermute | solution.py:219
  48.2 7.5 %collective-permute-start.10 = (bf16[1040,128]{1,0:T(8,128)(2,1)S(1)}, bf16[1040,128]{1,0:T(8,128)(2,1)S(1)}, u32[]{:S(2)}, u32[]{:S(2)}) collective-permute-start(bf16[1040,128]{1,0:T(8,128)(2,1)S(1)} %slice_bitcast_fusion), channel_id=1, source_target_pairs={{0,2},{1,3},{4,0},{5,1},{8,4},{9,5},{12,8},{13,9},{14,12},{15,13},... | collective-permute-start | bytes 798728 | tf_op jit(solution)/shard_map/ppermute | solution.py:219
  48.7 7.0 %collective-permute-start.9 = (bf16[1040,128]{1,0:T(8,128)(2,1)S(1)}, bf16[1040,128]{1,0:T(8,128)(2,1)S(1)}, u32[]{:S(2)}, u32[]{:S(2)}) collective-permute-start(bf16[1040,128]{1,0:T(8,128)(2,1)S(1)} %slice_bitcast_fusion.1), channel_id=1, source_target_pairs={{0,4},{1,5},{4,8},{5,9},{8,12},{9,13},{12,14},{13,15},{14,10},{15,... | collective-permute-start | bytes 798728 | tf_op jit(solution)/shard_map/ppermute | solution.py:218
  55.7 7.9 %collective-permute-start.11 = (bf16[64,2048]{1,0:T(8,128)(2,1)S(1)}, bf16[64,2048]{1,0:T(8,128)(2,1)S(1)}, u32[]{:S(2)}, u32[]{:S(2)}) collective-permute-start(bf16[64,2048]{1,0:T(8,128)(2,1)S(1)} %get-tuple-element.73), channel_id=1, source_target_pairs={{0,2},{1,3},{4,0},{5,1},{8,4},{9,5},{12,8},{13,9},{14,12},{15,13},... | collective-permute-start | bytes 786440 | tf_op jit(solution)/shard_map/ppermute | solution.py:219
  59.2 9.3 %collective-permute-start.21 = (bf16[64,2048]{1,0:T(8,128)(2,1)S(1)}, bf16[64,2048]{1,0:T(8,128)(2,1)S(1)}, u32[]{:S(2)}, u32[]{:S(2)}) collective-permute-start(bf16[64,2048]{1,0:T(8,128)(2,1)S(1)} %get-tuple-element.91), channel_id=1, source_target_pairs={{0,4},{1,5},{4,8},{5,9},{8,12},{9,13},{12,14},{13,15},{14,10},{15,... | collective-permute-start | bytes 786440 | tf_op jit(solution)/shard_map/ppermute | solution.py:218
  60.6 13.5 %collective-permute-start.17 = (bf16[64,2048]{1,0:T(8,128)(2,1)S(1)}, bf16[64,2048]{1,0:T(8,128)(2,1)S(1)}, u32[]{:S(2)}, u32[]{:S(2)}) collective-permute-start(bf16[64,2048]{1,0:T(8,128)(2,1)S(1)} %get-tuple-element.84), channel_id=1, source_target_pairs={{0,4},{1,5},{4,8},{5,9},{8,12},{9,13},{12,14},{13,15},{14,10},{15,... | collective-permute-start | bytes 786440 | tf_op jit(solution)/shard_map/ppermute | solution.py:218
  62.2 25.5 %copy-start = (bf16[2,1040,128]{2,1,0:T(8,128)(2,1)S(1)}, bf16[2,1040,128]{2,1,0:T(8,128)(2,1)}, u32[]{:S(2)}) copy-start(bf16[2,1040,128]{2,1,0:T(8,128)(2,1)} %shard_map.85.refs_0_) | copy-start | bytes 1597444
  62.2 13.4 %collective-permute-start.13 = (bf16[64,2048]{1,0:T(8,128)(2,1)S(1)}, bf16[64,2048]{1,0:T(8,128)(2,1)S(1)}, u32[]{:S(2)}, u32[]{:S(2)}) collective-permute-start(bf16[64,2048]{1,0:T(8,128)(2,1)S(1)} %get-tuple-element.81), channel_id=1, source_target_pairs={{0,2},{1,3},{4,0},{5,1},{8,4},{9,5},{12,8},{13,9},{14,12},{15,13},... | collective-permute-start | bytes 786440 | tf_op jit(solution)/shard_map/ppermute | solution.py:219
  63.7 13.3 %collective-permute-start.12 = (bf16[64,2048]{1,0:T(8,128)(2,1)S(1)}, bf16[64,2048]{1,0:T(8,128)(2,1)S(1)}, u32[]{:S(2)}, u32[]{:S(2)}) collective-permute-start(bf16[64,2048]{1,0:T(8,128)(2,1)S(1)} %add_convert_fusion.9), channel_id=1, source_target_pairs={{0,2},{1,3},{4,0},{5,1},{8,4},{9,5},{12,8},{13,9},{14,12},{15,13},... | collective-permute-start | bytes 786440 | tf_op jit(solution)/shard_map/ppermute | solution.py:219
  68.6 11.2 %collective-permute-start.22 = (bf16[64,2048]{1,0:T(8,128)(2,1)S(1)}, bf16[64,2048]{1,0:T(8,128)(2,1)S(1)}, u32[]{:S(2)}, u32[]{:S(2)}) collective-permute-start(bf16[64,2048]{1,0:T(8,128)(2,1)S(1)} %add_convert_fusion.2), channel_id=1, source_target_pairs={{0,4},{1,5},{4,8},{5,9},{8,12},{9,13},{12,14},{13,15},{14,10},{15,... | collective-permute-start | bytes 786440 | tf_op jit(solution)/shard_map/ppermute | solution.py:218
  74.2 11.2 %collective-permute-start.18 = (bf16[64,2048]{1,0:T(8,128)(2,1)S(1)}, bf16[64,2048]{1,0:T(8,128)(2,1)S(1)}, u32[]{:S(2)}, u32[]{:S(2)}) collective-permute-start(bf16[64,2048]{1,0:T(8,128)(2,1)S(1)} %add_convert_fusion.5), channel_id=1, source_target_pairs={{0,4},{1,5},{4,8},{5,9},{8,12},{9,13},{12,14},{13,15},{14,10},{15,... | collective-permute-start | bytes 786440 | tf_op jit(solution)/shard_map/ppermute | solution.py:218
  75.6 11.2 %collective-permute-start.14 = (bf16[64,2048]{1,0:T(8,128)(2,1)S(1)}, bf16[64,2048]{1,0:T(8,128)(2,1)S(1)}, u32[]{:S(2)}, u32[]{:S(2)}) collective-permute-start(bf16[64,2048]{1,0:T(8,128)(2,1)S(1)} %add_convert_fusion.8), channel_id=1, source_target_pairs={{0,2},{1,3},{4,0},{5,1},{8,4},{9,5},{12,8},{13,9},{14,12},{15,13},... | collective-permute-start | bytes 786440 | tf_op jit(solution)/shard_map/ppermute | solution.py:219
  79.8 11.2 %collective-permute-start.23 = (bf16[64,2048]{1,0:T(8,128)(2,1)S(1)}, bf16[64,2048]{1,0:T(8,128)(2,1)S(1)}, u32[]{:S(2)}, u32[]{:S(2)}) collective-permute-start(bf16[64,2048]{1,0:T(8,128)(2,1)S(1)} %add_convert_fusion.1), channel_id=1, source_target_pairs={{0,4},{1,5},{4,8},{5,9},{8,12},{9,13},{12,14},{13,15},{14,10},{15,... | collective-permute-start | bytes 786440 | tf_op jit(solution)/shard_map/ppermute | solution.py:218
  81.2 15.9 %collective-permute-start.20 = (bf16[64,2048]{1,0:T(8,128)(2,1)S(1)}, bf16[64,2048]{1,0:T(8,128)(2,1)S(1)}, u32[]{:S(2)}, u32[]{:S(2)}) collective-permute-start(bf16[64,2048]{1,0:T(8,128)(2,1)S(1)} %add_convert_fusion.3), channel_id=1, source_target_pairs={{0,2},{1,3},{4,0},{5,1},{8,4},{9,5},{12,8},{13,9},{14,12},{15,13},... | collective-permute-start | bytes 786440 | tf_op jit(solution)/shard_map/ppermute | solution.py:219
  85.4 11.7 %collective-permute-start.19 = (bf16[64,2048]{1,0:T(8,128)(2,1)S(1)}, bf16[64,2048]{1,0:T(8,128)(2,1)S(1)}, u32[]{:S(2)}, u32[]{:S(2)}) collective-permute-start(bf16[64,2048]{1,0:T(8,128)(2,1)S(1)} %add_convert_fusion.4), channel_id=1, source_target_pairs={{0,4},{1,5},{4,8},{5,9},{8,12},{9,13},{12,14},{13,15},{14,10},{15,... | collective-permute-start | bytes 786440 | tf_op jit(solution)/shard_map/ppermute | solution.py:218
  86.9 6.4 %collective-permute-start.15 = (bf16[64,2048]{1,0:T(8,128)(2,1)S(1)}, bf16[64,2048]{1,0:T(8,128)(2,1)S(1)}, u32[]{:S(2)}, u32[]{:S(2)}) collective-permute-start(bf16[64,2048]{1,0:T(8,128)(2,1)S(1)} %add_convert_fusion.7), channel_id=1, source_target_pairs={{0,2},{1,3},{4,0},{5,1},{8,4},{9,5},{12,8},{13,9},{14,12},{15,13},... | collective-permute-start | bytes 786440 | tf_op jit(solution)/shard_map/ppermute | solution.py:219
  91.0 6.7 %collective-permute-start.24 = (bf16[64,2048]{1,0:T(8,128)(2,1)S(1)}, bf16[64,2048]{1,0:T(8,128)(2,1)S(1)}, u32[]{:S(2)}, u32[]{:S(2)}) collective-permute-start(bf16[64,2048]{1,0:T(8,128)(2,1)S(1)} %add_convert_fusion), channel_id=1, source_target_pairs={{0,4},{1,5},{4,8},{5,9},{8,12},{9,13},{12,14},{13,15},{14,10},{15,... | collective-permute-start | bytes 786440 | tf_op jit(solution)/shard_map/ppermute | solution.py:218
  93.4 6.4 %collective-permute-start.16 = (bf16[64,2048]{1,0:T(8,128)(2,1)S(1)}, bf16[64,2048]{1,0:T(8,128)(2,1)S(1)}, u32[]{:S(2)}, u32[]{:S(2)}) collective-permute-start(bf16[64,2048]{1,0:T(8,128)(2,1)S(1)} %add_convert_fusion.6), channel_id=1, source_target_pairs={{0,2},{1,3},{4,0},{5,1},{8,4},{9,5},{12,8},{13,9},{14,12},{15,13},... | collective-permute-start | bytes 786440 | tf_op jit(solution)/shard_map/ppermute | solution.py:219
  94.1 1.1 %collective-permute-start.25 = (f32[2,128]{1,0:T(2,128)S(1)}, f32[2,128]{1,0:T(2,128)S(1)}, u32[]{:S(2)}, u32[]{:S(2)}) collective-permute-start(f32[2,128]{1,0:T(2,128)S(1)} %add_add_fusion), channel_id=1, source_target_pairs={{0,1},{1,0},{2,3},{3,2},{4,5},{5,4},{6,7},{7,6},{8,9},{9,8},{10,11... | collective-permute-start | bytes 3080 | tf_op jit(solution)/shard_map/ppermute | solution.py:220

commit v10 on v8

--- a/solution.py
+++ b/solution.py
@@ -108,8 +108,9 @@
 
 
 def hold_kernel(*refs):
-    count = len(refs) // 2
-    arrived = refs[-1]
+    count = len(refs) // 2 - 1
+    mark_ref, arrived = refs[-2:]
+    mark_ref[...] = jnp.zeros(mark_ref.shape, mark_ref.dtype)
     copies = [
         pltpu.make_async_copy(refs[i], refs[count + i], arrived.at[i]) for i in range(count)
     ]
@@ -122,9 +123,10 @@
 def hold(arrays):
     return pl.pallas_call(
         hold_kernel,
-        out_shape=[pltpu.VMEM(array.shape, array.dtype) for array in arrays],
+        out_shape=[pltpu.VMEM(array.shape, array.dtype) for array in arrays]
+        + [jax.ShapeDtypeStruct((2, LANES), jnp.float32)],
         in_specs=[pl.BlockSpec(memory_space=pl.ANY)] * len(arrays),
-        out_specs=[pl.BlockSpec(memory_space=pltpu.VMEM)] * len(arrays),
+        out_specs=[pl.BlockSpec(memory_space=pltpu.VMEM)] * (len(arrays) + 1),
         scratch_shapes=[pltpu.SemaphoreType.DMA((len(arrays),))],
         compiler_params=pltpu.CompilerParams(vmem_limit_bytes=VMEM_LIMIT),
     )(*arrays)
@@ -223,10 +225,10 @@
 
     weights = [gate_weight[0], up_weight[0], down_weight[0]]
     others = [sibling(weight) for weight in weights]
-    weights = hold([pltpu.with_memory_space_constraint(w, pltpu.HBM) for w in weights + others])
+    *weights, held = hold([pltpu.with_memory_space_constraint(w, pltpu.HBM) for w in weights + others])
     packed = pack(tokens, expert_ids, gate_fixed, expert_count)
     own = (jnp.arange(LANES)[None] == jnp.stack([node, node ^ 1])[:, None]).astype(jnp.float32)
-    stats = []
+    stats = [held]
 
     def run(blocks):
         res = apply_experts(blocks, half, own, weights)
@@ -237,18 +239,22 @@
         return sum(term.astype(jnp.float32) for term in terms).astype(jnp.bfloat16)
 
     low, high = right(packed), left(packed)
-    outs = {}
+    blocks, outs, fresh = {}, {}, {}
     for k in range(1, far + 1):
-        if k > 1:
-            low, high, outs[k - 1] = tie((low, high, outs[k - 1]))
-        here = low, high
+        if k == 2:
+            low, high, stats[0] = tie((low, high, stats[0]))
+        elif k > 2:
+            low, high, fresh = tie((low, high, fresh))
+            outs.update(fresh)
+        here = blocks[k] = [low, high]
         if k == far:
             break
         if k < far - 1:
             low, high = right(low), left(high)
         else:
             low, high = right(low[0]), left(high[1])
-        outs[k] = run(here)
+        ready = [i for i in blocks if i not in outs] if k >= min(2, far - 1) else []
+        fresh = {i: run(blocks[i]) for i in ready}
     res = run(here)
 
     ways = (left, left, right, right)

time: 102 us -> 102 us (level)
    ppermute x11, starting transfers between devices: 6.36 us -> 4.62 us  [body(): left = lambda a: lax.ppermute(a, 'node', to_left)]
    ppermute x11, starting transfers between devices: 17.8 us -> 19.3 us  [body(): right = lambda a: lax.ppermute(a, 'node', to_right)]
where the time goes in v10:
time: 102 us
  waiting for transfers between devices  41.8 us (41%)
  Pallas kernels  30.5 us (30%)
  starting transfers between devices  24.9 us (24%)
  between operations  2.59 us (3%)
  other arithmetic  2.01 us (2%)
    ppermute x11, waiting for transfers between devices, body(): right = lambda a: lax.ppermute(a, 'node', to_right)  32.7 us
    pallas_call x5, Pallas kernels, apply_experts(): pl.pallas_call(functools.partial(expert_kernel, count, piece), out_shape=...  21.1 us
    ppermute x11, starting transfers between devices, body(): right = lambda a: lax.ppermute(a, 'node', to_right)  19.3 us
    ppermute x11, waiting for transfers between devices, body(): left = lambda a: lax.ppermute(a, 'node', to_left)  7.96 us
    pallas_call x1, Pallas kernels, hold(): pl.pallas_call(hold_kernel, out_shape=[pltpu.VMEM(array.shape, array.dtyp...  6.5 us
    ppermute x11, starting transfers between devices, body(): left = lambda a: lax.ppermute(a, 'node', to_left)  4.62 us
  transfers between devices with their start and end apart: 26, of which 15 were waited for; matrix products, arithmetic and copies ran while one was open for 2% of the time, Pallas kernels for 29%

profile of v10, /device:TPU:0, one launch (start us, length us, event | category | flops | bytes accessed | tf_op | source)
XLA Modules:
  0.0 101.9 jit_solution(5937505714721736387)
XLA Ops:
  0.6 0.5 collective-permute-start.4
  1.1 0.1 collective-permute-start.5
  1.2 0.4 collective-permute-start.6
  1.7 2.0 %shard_map.85.refs_0_ = bf16[2,1040,128]{2,1,0:T(8,128)(2,1)} custom-call(bf16[128,2048]{1,0:T(8,128)(2,1)} %tokens_hbm.1, s32[8,128]{1,0:T(8,128)} %bitcast.19, s32[8,128]{1,0:T(8,128)} %bitcast.20), custom_call_target="tpu_custom_call" | custom-call | flops 16384 | bytes 1048576 | tf_op jit(solution)/shard_map/pallas_call | solution.py:73
  3.6 2.7 %collective-permute-start = (bf16[2,1040,128]{2,1,0:T(8,128)(2,1)}, bf16[2,1040,128]{2,1,0:T(8,128)(2,1)S(1)}, u32[]{:S(2)}, u32[]{:S(2)}) collective-permute-start(bf16[2,1040,128]{2,1,0:T(8,128)(2,1)} %shard_map.85.refs_0_), channel_id=1, source_target_pairs={{0,4},{1,5},{4,8},{5,9},{8,12},{9,13},{12,14},{13,15},{14,10},{15,... | collective-permute-start | bytes 1597448 | tf_op jit(solution)/shard_map/ppermute | solution.py:220
  6.4 0.0 collective-permute-start.2
  6.4 12.8 %collective-permute-done.refs_0_ = bf16[2,1040,128]{2,1,0:T(8,128)(2,1)S(1)} collective-permute-done((bf16[2,1040,128]{2,1,0:T(8,128)(2,1)}, bf16[2,1040,128]{2,1,0:T(8,128)(2,1)S(1)}, u32[]{:S(2)}, u32[]{:S(2)}) %collective-permute-start) | collective-permute-done | bytes 532512 | tf_op jit(solution)/shard_map/ppermute | solution.py:220
  19.2 1.8 %collective-permute-start.1 = (bf16[2,1040,128]{2,1,0:T(8,128)(2,1)S(1)}, bf16[2,1040,128]{2,1,0:T(8,128)(2,1)S(1)}, u32[]{:S(2)}, u32[]{:S(2)}) collective-permute-start(bf16[2,1040,128]{2,1,0:T(8,128)(2,1)S(1)} %collective-permute-done.refs_0_), channel_id=1, source_target_pairs={{0,4},{1,5},{4,8},{5,9},{8,12},{9,13},{12,14},{13,15},{14,10},{15,... | collective-permute-start | bytes 1597448 | tf_op jit(solution)/shard_map/ppermute | solution.py:220
  21.0 0.2 collective-permute-start.3
  21.2 0.1 pad_add_fusion
  21.3 0.1 compare_convert_fusion.refs_2_.refs_1_
  21.4 0.0 collective-permute-done.5.refs_4_
  21.4 0.0 collective-permute-done.6.refs_5_
  21.4 6.5 %shard_map.86 = (bf16[2048,768]{1,0:T(8,128)(2,1)S(1)}, bf16[2048,768]{1,0:T(8,128)(2,1)S(1)}, bf16[768,2048]{1,0:T(8,128)(2,1)S(1)}, bf16[2048,768]{1,0:T(8,128...) custom-call(bf16[2048,768]{1,0:T(8,128)(2,1)} %bitcast.14, ...), custom_call_target="tpu_custom_call" | custom-call | tf_op jit(solution)/shard_map/pallas_call | solution.py:124
  27.9 5.2 %collective-permute-done.1.refs_0_ = bf16[2,1040,128]{2,1,0:T(8,128)(2,1)S(1)} collective-permute-done((bf16[2,1040,128]{2,1,0:T(8,128)(2,1)S(1)}, bf16[2,1040,128]{2,1,0:T(8,128)(2,1)S(1)}, u32[]{:S(2)}, u32[]{:S(2)}) %collective-permute-start.1) | collective-permute-done | bytes 532512 | tf_op jit(solution)/shard_map/ppermute | solution.py:220
  33.1 1.3 %collective-permute-done.3.refs_1_ = bf16[2,1040,128]{2,1,0:T(8,128)(2,1)S(1)} collective-permute-done((bf16[2,1040,128]{2,1,0:T(8,128)(2,1)S(1)}, bf16[2,1040,128]{2,1,0:T(8,128)(2,1)S(1)}, u32[]{:S(2)}, u32[]{:S(2)}) %collective-permute-start.3) | collective-permute-done | bytes 532512 | tf_op jit(solution)/shard_map/ppermute | solution.py:221
  34.4 1.6 %collective-permute-start.7 = (bf16[2,1040,128]{2,1,0:T(8,128)(2,1)S(1)}, bf16[2,1040,128]{2,1,0:T(8,128)(2,1)S(1)}, u32[]{:S(2)}, u32[]{:S(2)}) collective-permute-start(bf16[2,1040,128]{2,1,0:T(8,128)(2,1)S(1)} %collective-permute-done.1.refs_0_), channel_id=1, source_target_pairs={{0,4},{1,5},{4,8},{5,9},{8,12},{9,13},{12,14},{13,15},{14,10},{15,... | collective-permute-start | bytes 1597448 | tf_op jit(solution)/shard_map/ppermute | solution.py:220
  36.0 0.4 collective-permute-start.8
  36.4 5.2 %shard_map.88 = (bf16[64,2048]{1,0:T(8,128)(2,1)S(1)}, bf16[64,2048]{1,0:T(8,128)(2,1)S(1)}, bf16[64,2048]{1,0:T(8,128)(2,1)S(1)}, bf16[64,2048]{1,0:T(8,128)(2,1)S(1)}, f32[2,128]{1,0:T(2,128)S(1)}) custom-call(bf16[2,1040,128]{2,1,0:T(8,128)(2,1)S(1)} %collective-permute-done.1.refs_0_, bf16[2,1040,128]{2,1,0:T(8,128)(2,1)S(1)} %collective-permute-done.3.refs_1_, ...), custom_call_target="tpu_custom_call" | custom-call | flops 4831838208 | bytes 2097152 | tf_op jit(solution)/shard_map/pallas_call | solution.py:192
  41.6 5.2 %shard_map.87 = (bf16[64,2048]{1,0:T(8,128)(2,1)S(1)}, bf16[64,2048]{1,0:T(8,128)(2,1)S(1)}, bf16[64,2048]{1,0:T(8,128)(2,1)S(1)}, bf16[64,2048]{1,0:T(8,128)(2,1)S(1)}, f32[2,128]{1,0:T(2,128)S(1)}) custom-call(bf16[2,1040,128]{2,1,0:T(8,128)(2,1)S(1)} %collective-permute-done.refs_0_, bf16[2,1040,128]{2,1,0:T(8,128)(2,1)S(1)} %collective-permute-done.2.refs_1_, ...), custom_call_target="tpu_custom_call" | custom-call | flops 4831838208 | bytes 2097152 | tf_op jit(solution)/shard_map/pallas_call | solution.py:192
  46.9 1.3 %collective-permute-done.8.refs_1_ = bf16[2,1040,128]{2,1,0:T(8,128)(2,1)S(1)} collective-permute-done((bf16[2,1040,128]{2,1,0:T(8,128)(2,1)S(1)}, bf16[2,1040,128]{2,1,0:T(8,128)(2,1)S(1)}, u32[]{:S(2)}, u32[]{:S(2)}) %collective-permute-start.8) | collective-permute-done | bytes 532512 | tf_op jit(solution)/shard_map/ppermute | solution.py:221
  48.2 0.5 collective-permute-start.10
  48.7 1.8 %collective-permute-start.9 = (bf16[1040,128]{1,0:T(8,128)(2,1)S(1)}, bf16[1040,128]{1,0:T(8,128)(2,1)S(1)}, u32[]{:S(2)}, u32[]{:S(2)}) collective-permute-start(bf16[1040,128]{1,0:T(8,128)(2,1)S(1)} %slice_bitcast_fusion.1), channel_id=1, source_target_pairs={{0,4},{1,5},{4,8},{5,9},{8,12},{9,13},{12,14},{13,15},{14,10},{15,... | collective-permute-start | bytes 798728 | tf_op jit(solution)/shard_map/ppermute | solution.py:220
  50.5 5.2 %shard_map.89 = (bf16[64,2048]{1,0:T(8,128)(2,1)S(1)}, bf16[64,2048]{1,0:T(8,128)(2,1)S(1)}, bf16[64,2048]{1,0:T(8,128)(2,1)S(1)}, bf16[64,2048]{1,0:T(8,128)(2,1)S(1)}, f32[2,128]{1,0:T(2,128)S(1)}) custom-call(bf16[2,1040,128]{2,1,0:T(8,128)(2,1)S(1)} %collective-permute-done.7.refs_0_, bf16[2,1040,128]{2,1,0:T(8,128)(2,1)S(1)} %collective-permute-done.8.refs_1_, ...), custom_call_target="tpu_custom_call" | custom-call | flops 4831838208 | bytes 2097152 | tf_op jit(solution)/shard_map/pallas_call | solution.py:192
  55.7 0.5 collective-permute-start.11
  56.2 2.7 %shard_map.91 = (bf16[64,2048]{1,0:T(8,128)(2,1)S(1)}, bf16[64,2048]{1,0:T(8,128)(2,1)S(1)}, f32[2,128]{1,0:T(2,128)S(1)}) custom-call(bf16[1040,128]{1,0:T(8,128)(2,1)S(1)} %collective-permute-done.9.refs_0_, bf16[1040,128]{1,0:T(8,128)(2,1)S(1)} %collective-permute-done.10.refs_1_, f32[2,128]{1,0:T(2,128)S(1)} %compare_convert_fusion.refs_2_.refs_1_, ...), custom_call_target="tpu_custom_call" | custom-call | flops 2415919104 | bytes 1048576 | tf_op jit(solution)/shard_map/pallas_call | solution.py:192
  58.9 1.6 %collective-permute-start.21 = (bf16[64,2048]{1,0:T(8,128)(2,1)S(1)}, bf16[64,2048]{1,0:T(8,128)(2,1)S(1)}, u32[]{:S(2)}, u32[]{:S(2)}) collective-permute-start(bf16[64,2048]{1,0:T(8,128)(2,1)S(1)} %get-tuple-element.94), channel_id=1, source_target_pairs={{0,4},{1,5},{4,8},{5,9},{8,12},{9,13},{12,14},{13,15},{14,10},{15,... | collective-permute-start | bytes 786440 | tf_op jit(solution)/shard_map/ppermute | solution.py:220
  60.6 1.6 %collective-permute-start.17 = (bf16[64,2048]{1,0:T(8,128)(2,1)S(1)}, bf16[64,2048]{1,0:T(8,128)(2,1)S(1)}, u32[]{:S(2)}, u32[]{:S(2)}) collective-permute-start(bf16[64,2048]{1,0:T(8,128)(2,1)S(1)} %get-tuple-element.87), channel_id=1, source_target_pairs={{0,4},{1,5},{4,8},{5,9},{8,12},{9,13},{12,14},{13,15},{14,10},{15,... | collective-permute-start | bytes 786440 | tf_op jit(solution)/shard_map/ppermute | solution.py:220
  62.2 0.4 collective-permute-start.13
  62.6 1.0 %collective-permute-done.11 = bf16[64,2048]{1,0:T(8,128)(2,1)S(1)} collective-permute-done((bf16[64,2048]{1,0:T(8,128)(2,1)S(1)}, bf16[64,2048]{1,0:T(8,128)(2,1)S(1)}, u32[]{:S(2)}, u32[]{:S(2)}) %collective-permute-start.11) | collective-permute-done | bytes 262176 | tf_op jit(solution)/shard_map/ppermute | solution.py:221
  63.7 0.1 add_convert_fusion.9
  63.7 0.5 collective-permute-start.12
  64.2 4.0 %collective-permute-done.21 = bf16[64,2048]{1,0:T(8,128)(2,1)S(1)} collective-permute-done((bf16[64,2048]{1,0:T(8,128)(2,1)S(1)}, bf16[64,2048]{1,0:T(8,128)(2,1)S(1)}, u32[]{:S(2)}, u32[]{:S(2)}) %collective-permute-start.21) | collective-permute-done | bytes 262176 | tf_op jit(solution)/shard_map/ppermute | solution.py:220
  68.2 0.1 add_convert_fusion.2
  68.3 1.6 %collective-permute-start.22 = (bf16[64,2048]{1,0:T(8,128)(2,1)S(1)}, bf16[64,2048]{1,0:T(8,128)(2,1)S(1)}, u32[]{:S(2)}, u32[]{:S(2)}) collective-permute-start(bf16[64,2048]{1,0:T(8,128)(2,1)S(1)} %add_convert_fusion.2), channel_id=1, source_target_pairs={{0,4},{1,5},{4,8},{5,9},{8,12},{9,13},{12,14},{13,15},{14,10},{15,... | collective-permute-start | bytes 786440 | tf_op jit(solution)/shard_map/ppermute | solution.py:220
  70.0 3.9 %collective-permute-done.17 = bf16[64,2048]{1,0:T(8,128)(2,1)S(1)} collective-permute-done((bf16[64,2048]{1,0:T(8,128)(2,1)S(1)}, bf16[64,2048]{1,0:T(8,128)(2,1)S(1)}, u32[]{:S(2)}, u32[]{:S(2)}) %collective-permute-start.17) | collective-permute-done | bytes 262176 | tf_op jit(solution)/shard_map/ppermute | solution.py:220
  73.9 0.1 add_convert_fusion.5
  73.9 1.6 %collective-permute-start.18 = (bf16[64,2048]{1,0:T(8,128)(2,1)S(1)}, bf16[64,2048]{1,0:T(8,128)(2,1)S(1)}, u32[]{:S(2)}, u32[]{:S(2)}) collective-permute-start(bf16[64,2048]{1,0:T(8,128)(2,1)S(1)} %add_convert_fusion.5), channel_id=1, source_target_pairs={{0,4},{1,5},{4,8},{5,9},{8,12},{9,13},{12,14},{13,15},{14,10},{15,... | collective-permute-start | bytes 786440 | tf_op jit(solution)/shard_map/ppermute | solution.py:220
  75.6 0.1 add_convert_fusion.8
  75.6 0.5 collective-permute-start.14
  76.1 0.9 collective-permute-done.12
  77.0 2.5 %collective-permute-done.22 = bf16[64,2048]{1,0:T(8,128)(2,1)S(1)} collective-permute-done((bf16[64,2048]{1,0:T(8,128)(2,1)S(1)}, bf16[64,2048]{1,0:T(8,128)(2,1)S(1)}, u32[]{:S(2)}, u32[]{:S(2)}) %collective-permute-start.22) | collective-permute-done | bytes 262176 | tf_op jit(solution)/shard_map/ppermute | solution.py:220
  79.5 0.1 add_convert_fusion.1
  79.6 1.6 %collective-permute-start.23 = (bf16[64,2048]{1,0:T(8,128)(2,1)S(1)}, bf16[64,2048]{1,0:T(8,128)(2,1)S(1)}, u32[]{:S(2)}, u32[]{:S(2)}) collective-permute-start(bf16[64,2048]{1,0:T(8,128)(2,1)S(1)} %add_convert_fusion.1), channel_id=1, source_target_pairs={{0,4},{1,5},{4,8},{5,9},{8,12},{9,13},{12,14},{13,15},{14,10},{15,... | collective-permute-start | bytes 786440 | tf_op jit(solution)/shard_map/ppermute | solution.py:220
  81.2 0.1 add_convert_fusion.3
  81.3 0.5 collective-permute-start.20
  81.8 3.3 %collective-permute-done.18 = bf16[64,2048]{1,0:T(8,128)(2,1)S(1)} collective-permute-done((bf16[64,2048]{1,0:T(8,128)(2,1)S(1)}, bf16[64,2048]{1,0:T(8,128)(2,1)S(1)}, u32[]{:S(2)}, u32[]{:S(2)}) %collective-permute-start.18) | collective-permute-done | bytes 262176 | tf_op jit(solution)/shard_map/ppermute | solution.py:220
  85.1 0.1 add_convert_fusion.4
  85.2 1.6 %collective-permute-start.19 = (bf16[64,2048]{1,0:T(8,128)(2,1)S(1)}, bf16[64,2048]{1,0:T(8,128)(2,1)S(1)}, u32[]{:S(2)}, u32[]{:S(2)}) collective-permute-start(bf16[64,2048]{1,0:T(8,128)(2,1)S(1)} %add_convert_fusion.4), channel_id=1, source_target_pairs={{0,4},{1,5},{4,8},{5,9},{8,12},{9,13},{12,14},{13,15},{14,10},{15,... | collective-permute-start | bytes 786440 | tf_op jit(solution)/shard_map/ppermute | solution.py:220
  86.8 0.1 add_convert_fusion.7
  86.9 0.5 collective-permute-start.15
  87.4 2.7 %shard_map.90 = (bf16[64,2048]{1,0:T(8,128)(2,1)S(1)}, bf16[64,2048]{1,0:T(8,128)(2,1)S(1)}, f32[2,128]{1,0:T(2,128)S(1)}) custom-call(bf16[2,1040,128]{2,1,0:T(8,128)(2,1)S(1)} %copy-done, f32[2,128]{1,0:T(2,128)S(1)} %compare_convert_fusion.refs_2_.refs_1_, bf16[2048,768]{1,0:T(8,128)(2,1)S(1)} %get-tuple-element.55.refs_3_.refs_2_, ...), custom_call_target="tpu_custom_call" | custom-call | flops 2415919104 | bytes 1048576 | tf_op jit(solution)/shard_map/pallas_call | solution.py:192
  90.1 0.6 collective-permute-done.23
  90.7 0.1 add_convert_fusion
  90.8 1.6 %collective-permute-start.24 = (bf16[64,2048]{1,0:T(8,128)(2,1)S(1)}, bf16[64,2048]{1,0:T(8,128)(2,1)S(1)}, u32[]{:S(2)}, u32[]{:S(2)}) collective-permute-start(bf16[64,2048]{1,0:T(8,128)(2,1)S(1)} %add_convert_fusion), channel_id=1, source_target_pairs={{0,4},{1,5},{4,8},{5,9},{8,12},{9,13},{12,14},{13,15},{14,10},{15,... | collective-permute-start | bytes 786440 | tf_op jit(solution)/shard_map/ppermute | solution.py:220
  92.4 0.9 collective-permute-done.15
  93.3 0.1 add_convert_fusion.6
  93.4 0.5 collective-permute-start.16
  93.9 1.1 %collective-permute-done.25 = f32[2,128]{1,0:T(2,128)S(1)} collective-permute-done((f32[2,128]{1,0:T(2,128)S(1)}, f32[2,128]{1,0:T(2,128)S(1)}, u32[]{:S(2)}, u32[]{:S(2)}) %collective-permute-start.25) | collective-permute-done | bytes 1056 | tf_op jit(solution)/shard_map/ppermute | solution.py:222
  95.0 0.6 multiply_reduce_fusion
  95.6 0.6 fusion
  96.9 0.4 collective-permute-done.24.refs_5_
  97.3 2.5 %collective-permute-done.16.refs_1_ = bf16[64,2048]{1,0:T(8,128)(2,1)S(1)} collective-permute-done((bf16[64,2048]{1,0:T(8,128)(2,1)S(1)}, bf16[64,2048]{1,0:T(8,128)(2,1)S(1)}, u32[]{:S(2)}, u32[]{:S(2)}) %collective-permute-start.16) | collective-permute-done | bytes 262176 | tf_op jit(solution)/shard_map/ppermute | solution.py:221
  99.8 1.0 shard_map.92
  (16 shorter events, 0.1 us)
Async XLA Ops:
  0.6 20.8 %collective-permute-start.4 = (bf16[2048,768]{1,0:T(8,128)(2,1)}, bf16[2048,768]{1,0:T(8,128)(2,1)}, u32[]{:S(2)}, u32[]{:S(2)}) collective-permute-start(bf16[2048,768]{1,0:T(8,128)(2,1)} %bitcast.13), channel_id=1, source_target_pairs={{0,1},{1,0},{2,3},{3,2},{4,5},{5,4},{6,7},{7,6},{8,9},{9,8},{10,11... | collective-permute-start | bytes 9437192 | tf_op jit(solution)/shard_map/ppermute | solution.py:222
  1.1 20.2 %collective-permute-start.5 = (bf16[2048,768]{1,0:T(8,128)(2,1)}, bf16[2048,768]{1,0:T(8,128)(2,1)}, u32[]{:S(2)}, u32[]{:S(2)}) collective-permute-start(bf16[2048,768]{1,0:T(8,128)(2,1)} %bitcast.15), channel_id=1, source_target_pairs={{0,1},{1,0},{2,3},{3,2},{4,5},{5,4},{6,7},{7,6},{8,9},{9,8},{10,11... | collective-permute-start | bytes 9437192 | tf_op jit(solution)/shard_map/ppermute | solution.py:222
  1.2 20.2 %collective-permute-start.6 = (bf16[768,2048]{1,0:T(8,128)(2,1)}, bf16[768,2048]{1,0:T(8,128)(2,1)}, u32[]{:S(2)}, u32[]{:S(2)}) collective-permute-start(bf16[768,2048]{1,0:T(8,128)(2,1)} %bitcast.17), channel_id=1, source_target_pairs={{0,1},{1,0},{2,3},{3,2},{4,5},{5,4},{6,7},{7,6},{8,9},{9,8},{10,11... | collective-permute-start | bytes 9437192 | tf_op jit(solution)/shard_map/ppermute | solution.py:222
  3.6 15.6 %collective-permute-start = (bf16[2,1040,128]{2,1,0:T(8,128)(2,1)}, bf16[2,1040,128]{2,1,0:T(8,128)(2,1)S(1)}, u32[]{:S(2)}, u32[]{:S(2)}) collective-permute-start(bf16[2,1040,128]{2,1,0:T(8,128)(2,1)} %shard_map.85.refs_0_), channel_id=1, source_target_pairs={{0,4},{1,5},{4,8},{5,9},{8,12},{9,13},{12,14},{13,15},{14,10},{15,... | collective-permute-start | bytes 1597448 | tf_op jit(solution)/shard_map/ppermute | solution.py:220
  6.4 14.7 %collective-permute-start.2 = (bf16[2,1040,128]{2,1,0:T(8,128)(2,1)}, bf16[2,1040,128]{2,1,0:T(8,128)(2,1)S(1)}, u32[]{:S(2)}, u32[]{:S(2)}) collective-permute-start(bf16[2,1040,128]{2,1,0:T(8,128)(2,1)} %shard_map.85.refs_0_), channel_id=1, source_target_pairs={{0,2},{1,3},{4,0},{5,1},{8,4},{9,5},{12,8},{13,9},{14,12},{15,13},... | collective-permute-start | bytes 1597448 | tf_op jit(solution)/shard_map/ppermute | solution.py:221
  19.2 13.9 %collective-permute-start.1 = (bf16[2,1040,128]{2,1,0:T(8,128)(2,1)S(1)}, bf16[2,1040,128]{2,1,0:T(8,128)(2,1)S(1)}, u32[]{:S(2)}, u32[]{:S(2)}) collective-permute-start(bf16[2,1040,128]{2,1,0:T(8,128)(2,1)S(1)} %collective-permute-done.refs_0_), channel_id=1, source_target_pairs={{0,4},{1,5},{4,8},{5,9},{8,12},{9,13},{12,14},{13,15},{14,10},{15,... | collective-permute-start | bytes 1597448 | tf_op jit(solution)/shard_map/ppermute | solution.py:220
  21.0 13.4 %collective-permute-start.3 = (bf16[2,1040,128]{2,1,0:T(8,128)(2,1)S(1)}, bf16[2,1040,128]{2,1,0:T(8,128)(2,1)S(1)}, u32[]{:S(2)}, u32[]{:S(2)}) collective-permute-start(bf16[2,1040,128]{2,1,0:T(8,128)(2,1)S(1)} %collective-permute-done.2.refs_1_), channel_id=1, source_target_pairs={{0,2},{1,3},{4,0},{5,1},{8,4},{9,5},{12,8},{13,9},{14,12},{15,13},... | collective-permute-start | bytes 1597448 | tf_op jit(solution)/shard_map/ppermute | solution.py:221
  34.4 12.5 %collective-permute-start.7 = (bf16[2,1040,128]{2,1,0:T(8,128)(2,1)S(1)}, bf16[2,1040,128]{2,1,0:T(8,128)(2,1)S(1)}, u32[]{:S(2)}, u32[]{:S(2)}) collective-permute-start(bf16[2,1040,128]{2,1,0:T(8,128)(2,1)S(1)} %collective-permute-done.1.refs_0_), channel_id=1, source_target_pairs={{0,4},{1,5},{4,8},{5,9},{8,12},{9,13},{12,14},{13,15},{14,10},{15,... | collective-permute-start | bytes 1597448 | tf_op jit(solution)/shard_map/ppermute | solution.py:220
  36.0 12.2 %collective-permute-start.8 = (bf16[2,1040,128]{2,1,0:T(8,128)(2,1)S(1)}, bf16[2,1040,128]{2,1,0:T(8,128)(2,1)S(1)}, u32[]{:S(2)}, u32[]{:S(2)}) collective-permute-start(bf16[2,1040,128]{2,1,0:T(8,128)(2,1)S(1)} %collective-permute-done.3.refs_1_), channel_id=1, source_target_pairs={{0,2},{1,3},{4,0},{5,1},{8,4},{9,5},{12,8},{13,9},{14,12},{15,13},... | collective-permute-start | bytes 1597448 | tf_op jit(solution)/shard_map/ppermute | solution.py:221
  48.2 7.5 %collective-permute-start.10 = (bf16[1040,128]{1,0:T(8,128)(2,1)S(1)}, bf16[1040,128]{1,0:T(8,128)(2,1)S(1)}, u32[]{:S(2)}, u32[]{:S(2)}) collective-permute-start(bf16[1040,128]{1,0:T(8,128)(2,1)S(1)} %slice_bitcast_fusion), channel_id=1, source_target_pairs={{0,2},{1,3},{4,0},{5,1},{8,4},{9,5},{12,8},{13,9},{14,12},{15,13},... | collective-permute-start | bytes 798728 | tf_op jit(solution)/shard_map/ppermute | solution.py:221
  48.7 7.0 %collective-permute-start.9 = (bf16[1040,128]{1,0:T(8,128)(2,1)S(1)}, bf16[1040,128]{1,0:T(8,128)(2,1)S(1)}, u32[]{:S(2)}, u32[]{:S(2)}) collective-permute-start(bf16[1040,128]{1,0:T(8,128)(2,1)S(1)} %slice_bitcast_fusion.1), channel_id=1, source_target_pairs={{0,4},{1,5},{4,8},{5,9},{8,12},{9,13},{12,14},{13,15},{14,10},{15,... | collective-permute-start | bytes 798728 | tf_op jit(solution)/shard_map/ppermute | solution.py:220
  55.7 7.9 %collective-permute-start.11 = (bf16[64,2048]{1,0:T(8,128)(2,1)S(1)}, bf16[64,2048]{1,0:T(8,128)(2,1)S(1)}, u32[]{:S(2)}, u32[]{:S(2)}) collective-permute-start(bf16[64,2048]{1,0:T(8,128)(2,1)S(1)} %get-tuple-element.76), channel_id=1, source_target_pairs={{0,2},{1,3},{4,0},{5,1},{8,4},{9,5},{12,8},{13,9},{14,12},{15,13},... | collective-permute-start | bytes 786440 | tf_op jit(solution)/shard_map/ppermute | solution.py:221
  58.9 9.3 %collective-permute-start.21 = (bf16[64,2048]{1,0:T(8,128)(2,1)S(1)}, bf16[64,2048]{1,0:T(8,128)(2,1)S(1)}, u32[]{:S(2)}, u32[]{:S(2)}) collective-permute-start(bf16[64,2048]{1,0:T(8,128)(2,1)S(1)} %get-tuple-element.94), channel_id=1, source_target_pairs={{0,4},{1,5},{4,8},{5,9},{8,12},{9,13},{12,14},{13,15},{14,10},{15,... | collective-permute-start | bytes 786440 | tf_op jit(solution)/shard_map/ppermute | solution.py:220
  60.6 13.3 %collective-permute-start.17 = (bf16[64,2048]{1,0:T(8,128)(2,1)S(1)}, bf16[64,2048]{1,0:T(8,128)(2,1)S(1)}, u32[]{:S(2)}, u32[]{:S(2)}) collective-permute-start(bf16[64,2048]{1,0:T(8,128)(2,1)S(1)} %get-tuple-element.87), channel_id=1, source_target_pairs={{0,4},{1,5},{4,8},{5,9},{8,12},{9,13},{12,14},{13,15},{14,10},{15,... | collective-permute-start | bytes 786440 | tf_op jit(solution)/shard_map/ppermute | solution.py:220
  62.2 25.2 %copy-start = (bf16[2,1040,128]{2,1,0:T(8,128)(2,1)S(1)}, bf16[2,1040,128]{2,1,0:T(8,128)(2,1)}, u32[]{:S(2)}) copy-start(bf16[2,1040,128]{2,1,0:T(8,128)(2,1)} %shard_map.85.refs_0_) | copy-start | bytes 1597444
  62.2 13.4 %collective-permute-start.13 = (bf16[64,2048]{1,0:T(8,128)(2,1)S(1)}, bf16[64,2048]{1,0:T(8,128)(2,1)S(1)}, u32[]{:S(2)}, u32[]{:S(2)}) collective-permute-start(bf16[64,2048]{1,0:T(8,128)(2,1)S(1)} %get-tuple-element.84), channel_id=1, source_target_pairs={{0,2},{1,3},{4,0},{5,1},{8,4},{9,5},{12,8},{13,9},{14,12},{15,13},... | collective-permute-start | bytes 786440 | tf_op jit(solution)/shard_map/ppermute | solution.py:221
  63.7 13.3 %collective-permute-start.12 = (bf16[64,2048]{1,0:T(8,128)(2,1)S(1)}, bf16[64,2048]{1,0:T(8,128)(2,1)S(1)}, u32[]{:S(2)}, u32[]{:S(2)}) collective-permute-start(bf16[64,2048]{1,0:T(8,128)(2,1)S(1)} %add_convert_fusion.9), channel_id=1, source_target_pairs={{0,2},{1,3},{4,0},{5,1},{8,4},{9,5},{12,8},{13,9},{14,12},{15,13},... | collective-permute-start | bytes 786440 | tf_op jit(solution)/shard_map/ppermute | solution.py:221
  68.3 11.2 %collective-permute-start.22 = (bf16[64,2048]{1,0:T(8,128)(2,1)S(1)}, bf16[64,2048]{1,0:T(8,128)(2,1)S(1)}, u32[]{:S(2)}, u32[]{:S(2)}) collective-permute-start(bf16[64,2048]{1,0:T(8,128)(2,1)S(1)} %add_convert_fusion.2), channel_id=1, source_target_pairs={{0,4},{1,5},{4,8},{5,9},{8,12},{9,13},{12,14},{13,15},{14,10},{15,... | collective-permute-start | bytes 786440 | tf_op jit(solution)/shard_map/ppermute | solution.py:220
  73.9 11.2 %collective-permute-start.18 = (bf16[64,2048]{1,0:T(8,128)(2,1)S(1)}, bf16[64,2048]{1,0:T(8,128)(2,1)S(1)}, u32[]{:S(2)}, u32[]{:S(2)}) collective-permute-start(bf16[64,2048]{1,0:T(8,128)(2,1)S(1)} %add_convert_fusion.5), channel_id=1, source_target_pairs={{0,4},{1,5},{4,8},{5,9},{8,12},{9,13},{12,14},{13,15},{14,10},{15,... | collective-permute-start | bytes 786440 | tf_op jit(solution)/shard_map/ppermute | solution.py:220
  75.6 11.2 %collective-permute-start.14 = (bf16[64,2048]{1,0:T(8,128)(2,1)S(1)}, bf16[64,2048]{1,0:T(8,128)(2,1)S(1)}, u32[]{:S(2)}, u32[]{:S(2)}) collective-permute-start(bf16[64,2048]{1,0:T(8,128)(2,1)S(1)} %add_convert_fusion.8), channel_id=1, source_target_pairs={{0,2},{1,3},{4,0},{5,1},{8,4},{9,5},{12,8},{13,9},{14,12},{15,13},... | collective-permute-start | bytes 786440 | tf_op jit(solution)/shard_map/ppermute | solution.py:221
  79.6 11.2 %collective-permute-start.23 = (bf16[64,2048]{1,0:T(8,128)(2,1)S(1)}, bf16[64,2048]{1,0:T(8,128)(2,1)S(1)}, u32[]{:S(2)}, u32[]{:S(2)}) collective-permute-start(bf16[64,2048]{1,0:T(8,128)(2,1)S(1)} %add_convert_fusion.1), channel_id=1, source_target_pairs={{0,4},{1,5},{4,8},{5,9},{8,12},{9,13},{12,14},{13,15},{14,10},{15,... | collective-permute-start | bytes 786440 | tf_op jit(solution)/shard_map/ppermute | solution.py:220
  81.3 15.6 %collective-permute-start.20 = (bf16[64,2048]{1,0:T(8,128)(2,1)S(1)}, bf16[64,2048]{1,0:T(8,128)(2,1)S(1)}, u32[]{:S(2)}, u32[]{:S(2)}) collective-permute-start(bf16[64,2048]{1,0:T(8,128)(2,1)S(1)} %add_convert_fusion.3), channel_id=1, source_target_pairs={{0,2},{1,3},{4,0},{5,1},{8,4},{9,5},{12,8},{13,9},{14,12},{15,13},... | collective-permute-start | bytes 786440 | tf_op jit(solution)/shard_map/ppermute | solution.py:221
  85.2 11.7 %collective-permute-start.19 = (bf16[64,2048]{1,0:T(8,128)(2,1)S(1)}, bf16[64,2048]{1,0:T(8,128)(2,1)S(1)}, u32[]{:S(2)}, u32[]{:S(2)}) collective-permute-start(bf16[64,2048]{1,0:T(8,128)(2,1)S(1)} %add_convert_fusion.4), channel_id=1, source_target_pairs={{0,4},{1,5},{4,8},{5,9},{8,12},{9,13},{12,14},{13,15},{14,10},{15,... | collective-permute-start | bytes 786440 | tf_op jit(solution)/shard_map/ppermute | solution.py:220
  86.9 6.4 %collective-permute-start.15 = (bf16[64,2048]{1,0:T(8,128)(2,1)S(1)}, bf16[64,2048]{1,0:T(8,128)(2,1)S(1)}, u32[]{:S(2)}, u32[]{:S(2)}) collective-permute-start(bf16[64,2048]{1,0:T(8,128)(2,1)S(1)} %add_convert_fusion.7), channel_id=1, source_target_pairs={{0,2},{1,3},{4,0},{5,1},{8,4},{9,5},{12,8},{13,9},{14,12},{15,13},... | collective-permute-start | bytes 786440 | tf_op jit(solution)/shard_map/ppermute | solution.py:221
  90.8 6.5 %collective-permute-start.24 = (bf16[64,2048]{1,0:T(8,128)(2,1)S(1)}, bf16[64,2048]{1,0:T(8,128)(2,1)S(1)}, u32[]{:S(2)}, u32[]{:S(2)}) collective-permute-start(bf16[64,2048]{1,0:T(8,128)(2,1)S(1)} %add_convert_fusion), channel_id=1, source_target_pairs={{0,4},{1,5},{4,8},{5,9},{8,12},{9,13},{12,14},{13,15},{14,10},{15,... | collective-permute-start | bytes 786440 | tf_op jit(solution)/shard_map/ppermute | solution.py:220
  93.4 6.4 %collective-permute-start.16 = (bf16[64,2048]{1,0:T(8,128)(2,1)S(1)}, bf16[64,2048]{1,0:T(8,128)(2,1)S(1)}, u32[]{:S(2)}, u32[]{:S(2)}) collective-permute-start(bf16[64,2048]{1,0:T(8,128)(2,1)S(1)} %add_convert_fusion.6), channel_id=1, source_target_pairs={{0,2},{1,3},{4,0},{5,1},{8,4},{9,5},{12,8},{13,9},{14,12},{15,13},... | collective-permute-start | bytes 786440 | tf_op jit(solution)/shard_map/ppermute | solution.py:221
  93.9 1.1 %collective-permute-start.25 = (f32[2,128]{1,0:T(2,128)S(1)}, f32[2,128]{1,0:T(2,128)S(1)}, u32[]{:S(2)}, u32[]{:S(2)}) collective-permute-start(f32[2,128]{1,0:T(2,128)S(1)} %add_add_fusion), channel_id=1, source_target_pairs={{0,1},{1,0},{2,3},{3,2},{4,5},{5,4},{6,7},{7,6},{8,9},{9,8},{10,11... | collective-permute-start | bytes 3080 | tf_op jit(solution)/shard_map/ppermute | solution.py:222
